TPU v7x, 32 devices: a whole 2x2x4 slice. The times are simulated.
32 devices in a mesh: dp: 4 (over z), space: 8 (over y, x, core).
Axes of the slice: x: 2, y: 2, z: 4, core: 2. Of those that a mesh axis runs over, the one named last changes fastest.
Arguments:
- pre_act: bfloat16 [4, 64, 128, 320], P('dp', 'space'), may hold values from -6 to 6
- out_grad: bfloat16 [4, 64, 128, 320], P('dp', 'space'), may hold values from -6 to 6
- kernel: bfloat16 [3, 3, 320, 320], replicated, may hold values from -0.109375 to 0.109375
Outputs:
- in_grad: bfloat16 [4, 64, 128, 320], P('dp', 'space')
- kernel_grad: float32 [2880, 320], P('dp')
All inputs are finite; a program needn't handle non-finite values.
Results may differ from a plain program's by a relative error of at most 0.0029.
Values may be sent and summed in bfloat16 or wider, within the bound.
No kernel may reach another device: no remote copies, remote signals or barrier semaphores. Data moves between devices by JAX's collectives and lax.ppermute only.
A program may use at most 64 MiB of HBM per device.

v0:
```python
import jax
import jax.numpy as jnp
from jax import lax
from jax.sharding import PartitionSpec as P


def with_halo(cells, sides, width):
    for axis, dim in sides:
        count = lax.axis_size(axis)
        ends = count - 1
        head = lax.slice_in_dim(cells, 0, width, axis=dim)
        tail = lax.slice_in_dim(cells, cells.shape[dim] - width, cells.shape[dim], axis=dim)
        cells = jnp.concatenate(
            [
                lax.ppermute(tail, axis, [(i, (i + 1) % count) for i in range(ends)]),
                cells,
                lax.ppermute(head, axis, [((i + 1) % count, i) for i in range(ends)]),
            ],
            axis=dim,
        )
    return cells


def shards(pre_act, out_grad, kernel):
    images = pre_act.shape[0]
    rows = pre_act.shape[1]
    width = pre_act.shape[2]
    chans = pre_act.shape[3]
    count_rows = images * rows * width
    pixels = count_rows * lax.axis_size("dp") * lax.axis_size("space")
    factor = float(pixels) ** (-0.5)
    stacked = jnp.stack([pre_act, out_grad])
    padded = with_halo(stacked, (("space", 2),), 1)
    padded = jnp.pad(padded, ((0, 0), (0, 0), (0, 0), (1, 1), (0, 0)))
    act_pad = jax.nn.silu(padded[0].astype(jnp.float32)).astype(jnp.bfloat16)
    grad_pad = padded[1]
    grad_taps = []
    for tap_a in range(3):
        for tap_b in range(3):
            grad_taps.append(
                grad_pad[:, 2 - tap_a : 2 - tap_a + rows, 2 - tap_b : 2 - tap_b + width, :]
            )
    grad_cols = jnp.stack(grad_taps, axis=3).reshape(count_rows, 9, chans)
    kernel_taps = kernel.reshape(9, chans, chans)
    act_grad = jnp.einsum("mtd,tcd->mc", grad_cols, kernel_taps, preferred_element_type=jnp.float32)
    pre_f = pre_act.astype(jnp.float32)
    sig = jax.nn.sigmoid(pre_f)
    deriv = sig * (1.0 + pre_f * (1.0 - sig))
    in_grad = (act_grad.reshape(images, rows, width, chans) * deriv).astype(jnp.bfloat16)
    g_flat = out_grad.reshape(count_rows, chans)
    span = 9 * chans // 9
    act_taps = []
    for tap_a in range(3):
        for tap_b in range(3):
            act_taps.append(act_pad[:, tap_a : tap_a + rows, tap_b : tap_b + width, :])
    patches = jnp.stack(act_taps, axis=3).reshape(count_rows, 9, span)
    term = jnp.einsum("mtc,md->ctd", patches, g_flat, preferred_element_type=jnp.float32)
    local_term = term.reshape(span * 9, chans) * factor
    summed = lax.psum(local_term, "space")
    kernel_grad = lax.psum_scatter(summed, "dp", scatter_dimension=0, tiled=True)
    return (in_grad, kernel_grad)


def solution(mesh):
    placed = (P("dp", "space", None, None), P("dp", "space", None, None), P())
    return jax.shard_map(
        shards,
        mesh=mesh,
        in_specs=placed,
        out_specs=(P("dp", "space", None, None), P("dp", None)),
        check_vma=False,
    )
```

profile of v0, /device:TPU:0, one launch (start us, length us, event | category | flops | bytes accessed | tf_op | source)
XLA Modules:
  0.0 194.9 jit_solution(12554800603256581409)
XLA Ops:
  8.4 2.4 %collective-permute-start = (bf16[2,1,1,128,320]{3,4,2,1,0:T(8,128)(2,1)S(1)}, bf16[2,1,1,128,320]{3,4,2,1,0:T(8,128)(2,1)S(1)}, u32[]{:S(2)}, u32[]{:S(2)}) collective-permute-start(bf16[2,1,1,128,320]{3,4,2,1,0:T(8,128)(2,1)S(1)} %get-tuple-element.13), channel_id=1, source_target_pairs={{0,1},{1,2},{2,3},{3,4},{4,5},{5,6},{6,7},{8,9},{9,10},{10,11},{11... | collective-permute-start | bytes 491528 | tf_op jit(solution)/shard_map/ppermute | solution.py:15
  12.1 4.1 %collective-permute-done.1 = bf16[2,1,1,128,320]{3,4,2,1,0:T(8,128)(2,1)S(1)} collective-permute-done((bf16[2,1,1,128,320]{3,4,2,1,0:T(8,128)(2,1)S(1)}, bf16[2,1,1,128,320]{3,4,2,1,0:T(8,128)(2,1)S(1)}, u32[]{:S(2)}, u32[]{:S(2)}) %collective-permute-start.1) | collective-permute-done | bytes 163872 | tf_op jit(solution)/shard_map/ppermute | solution.py:17
  16.2 3.7 %select_maximum_fusion = bf16[2,1,10,130,320]{3,4,2,1,0:T(8,128)(2,1)S(1)} fusion(bf16[2,1,1,128,320]{3,4,2,1,0:T(8,128)(2,1)S(1)} %collective-permute-done.1, bf16[2,1,1,128,320]{3,4,2,1,0:T(8,128)(2,1)S(1)} %collective-permute-done, bf16[1,1,8,128,320]{3,4,2,1,0:T(8,128)(2,1)} %bitcast.125, bf16[1,1,8,128,320]{3,4,2,1,0:T(8,128)(2,1)} %bitcast.127), kind=kLoop, calls=%fused_computation.16 | loop fusion | flops 12480000 | bytes 3302400 | tf_op jit(solution)/shard_map/concatenate | solution.py:13
  23.4 3.3 %fusion.6 = f32[320,9,320]{2,0,1:T(8,128)S(1)} fusion(bf16[1,8,128,9,320]{2,4,1,3,0:T(8,128)(2,1)S(1)} %fusion.30, bf16[1,8,128,320]{2,3,1,0:T(8,128)(2,1)S(1)} %copy-done.2), kind=kOutput, calls=%fused_computation.9 | convolution fusion | flops 1888358400 | bytes 10240000 | tf_op jit(solution)/shard_map/mtc,md->ctd/dot_general | solution.py:57
  26.6 5.8 %copy.15 = f32[320,9,320]{2,1,0:T(8,128)} copy(f32[320,9,320]{2,0,1:T(8,128)S(1)} %fusion.6) | data formatting | bytes 7372800 | tf_op jit(solution)/shard_map/mul | solution.py:58
  32.5 6.8 %mul.40 = f32[2880,320]{1,0:T(8,128)} reshape(f32[320,9,320]{2,1,0:T(8,128)} %copy.15) | data formatting | bytes 7372800 | tf_op jit(solution)/shard_map/mul | solution.py:58
  41.0 3.1 %fusion.40 = (bf16[1,8,128,320]{2,3,1,0:T(8,128)(2,1)S(1)}, bf16[1,8,128,320]{2,3,1,0:T(8,128)(2,1)S(1)}, bf16[1,8,128,320]{2,3,1,0:T(8,128)(2,1)}, bf16[1,8,128...) fusion(bf16[1,10,130,320]{2,3,1,0:T(8,128)(2,1)S(1)} %slice_bit, ...), kind=kLoop, calls=%fused_computation.63 | loop fusion | bytes 11796480 | tf_op jit(solution)/shard_map/slice | solution.py:41
  45.4 2.1 %stack.72 = bf16[1024,1,320]{0,2,1:T(8,128)(2,1)} reshape(bf16[1,8,128,320]{2,1,3,0:T(8,128)(2,1)} %copy.5) | data formatting | bytes 1310720 | tf_op jit(solution)/shard_map/stack | solution.py:43
  47.5 2.4 %copy.6 = bf16[1,8,128,320]{2,1,3,0:T(8,128)(2,1)} copy(bf16[1,8,128,320]{2,3,1,0:T(8,128)(2,1)} %get-tuple-element.11) | data formatting | bytes 1310720 | tf_op jit(solution)/shard_map/slice | solution.py:41
  49.8 2.3 %stack.73 = bf16[1024,1,320]{0,2,1:T(8,128)(2,1)} reshape(bf16[1,8,128,320]{2,1,3,0:T(8,128)(2,1)} %copy.6) | data formatting | bytes 1310720 | tf_op jit(solution)/shard_map/stack | solution.py:43
  52.1 2.4 %copy.7 = bf16[1,8,128,320]{2,1,3,0:T(8,128)(2,1)} copy(bf16[1,8,128,320]{2,3,1,0:T(8,128)(2,1)} %get-tuple-element.10) | data formatting | bytes 1310720 | tf_op jit(solution)/shard_map/slice | solution.py:41
  54.5 2.2 %stack.74 = bf16[1024,1,320]{0,2,1:T(8,128)(2,1)} reshape(bf16[1,8,128,320]{2,1,3,0:T(8,128)(2,1)} %copy.7) | data formatting | bytes 1310720 | tf_op jit(solution)/shard_map/stack | solution.py:43
  56.6 2.3 %copy.8 = bf16[1,8,128,320]{2,1,3,0:T(8,128)(2,1)} copy(bf16[1,8,128,320]{2,3,1,0:T(8,128)(2,1)} %get-tuple-element.9) | data formatting | bytes 1310720 | tf_op jit(solution)/shard_map/slice | solution.py:41
  59.0 2.2 %stack.75 = bf16[1024,1,320]{0,2,1:T(8,128)(2,1)} reshape(bf16[1,8,128,320]{2,1,3,0:T(8,128)(2,1)} %copy.8) | data formatting | bytes 1310720 | tf_op jit(solution)/shard_map/stack | solution.py:43
  61.1 2.4 %copy.9 = bf16[1,8,128,320]{2,1,3,0:T(8,128)(2,1)} copy(bf16[1,8,128,320]{2,3,1,0:T(8,128)(2,1)} %get-tuple-element.8) | data formatting | bytes 1310720 | tf_op jit(solution)/shard_map/slice | solution.py:41
  63.5 2.1 %stack.76 = bf16[1024,1,320]{0,2,1:T(8,128)(2,1)} reshape(bf16[1,8,128,320]{2,1,3,0:T(8,128)(2,1)} %copy.9) | data formatting | bytes 1310720 | tf_op jit(solution)/shard_map/stack | solution.py:43
  65.6 2.4 %copy.10 = bf16[1,8,128,320]{2,1,3,0:T(8,128)(2,1)} copy(bf16[1,8,128,320]{2,3,1,0:T(8,128)(2,1)} %get-tuple-element.7) | data formatting | bytes 1310720 | tf_op jit(solution)/shard_map/slice | solution.py:41
  70.1 2.4 %copy.11 = bf16[1,8,128,320]{2,1,3,0:T(8,128)(2,1)} copy(bf16[1,8,128,320]{2,3,1,0:T(8,128)(2,1)} %get-tuple-element.6) | data formatting | bytes 1310720 | tf_op jit(solution)/shard_map/slice | solution.py:41
  75.8 2.2 %stack.79 = bf16[1024,1,320]{0,2,1:T(8,128)(2,1)} reshape(bf16[1,8,128,320]{2,1,3,0:T(8,128)(2,1)} %copy.12) | data formatting | bytes 1310720 | tf_op jit(solution)/shard_map/stack | solution.py:43
  79.3 2.1 %stack.80 = bf16[1024,1,320]{0,2,1:T(8,128)(2,1)} reshape(bf16[1,8,128,320]{2,1,3,0:T(8,128)(2,1)} %copy.13) | data formatting | bytes 1310720 | tf_op jit(solution)/shard_map/stack | solution.py:43
  95.2 29.4 %reduce-scatter.2.cloned.1.call-done = f32[720,320]{1,0:T(8,128)} async-done(((f32[2880,320]{1,0:T(8,128)}), f32[720,320]{1,0:T(8,128)}) %reduce-scatter.2.cloned.1.call-update) | async-done | bytes 921616 | tf_op jit(solution)/shard_map/reduce_scatter | solution.py:60
  124.6 5.9 %fusion.22 = bf16[1,8,128,320]{2,3,1,0:T(8,128)(2,1)} fusion(bf16[9,320,320,1]{2,1,0,3:T(8,128)(2,1)S(1)} %bitcast.123, bf16[1,8,128,320]{2,3,1,0:T(8,128)(2,1)S(1)} %copy-done.3, bf16[1024,9,320]{0,2,1:T(8,128)(2,1)} %constant_dynamic-update-slice_fusion), kind=kOutput, calls=%fused_computation.27 | convolution fusion | flops 1890713600 | bytes 9052160 | tf_op jit(solution)/shard_map/mtd,tcd->mc/dot_general | solution.py:45
  130.5 55.0 %all-reduce.3.cloned.1.call-done = f32[720,320]{1,0:T(8,128)} async-done(((f32[720,320]{1,0:T(8,128)}), f32[720,320]{1,0:T(8,128)}) %all-reduce.3.cloned.1.call-update) | async-done | bytes 921616 | tf_op jit(solution)/shard_map/psum | solution.py:59
  185.5 2.5 %copy.16 = f32[720,320]{0,1:T(8,128)} copy(f32[720,320]{1,0:T(8,128)} %all-reduce.3.cloned.1.call-done) | data formatting | bytes 1843200
  (48 shorter events, 29.4 us)
Async XLA Ops:
  7.2 117.4 %copy-start = (bf16[3,3,320,320]{3,2,1,0:T(8,128)(2,1)S(1)}, bf16[3,3,320,320]{3,2,1,0:T(8,128)(2,1)}, u32[]{:S(2)}) copy-start(bf16[3,3,320,320]{3,2,1,0:T(8,128)(2,1)} %param.5) | copy-start | bytes 5529604
  7.2 117.4 %reduce-scatter.2.cloned.1.call-start = ((), (), s32[]{:S(2)}) async-start(), calls=%async_computation.1 | async-start | bytes 5529600 | tf_op jit(solution)/shard_map/reduce_scatter | solution.py:60
  8.4 3.7 %collective-permute-start = (bf16[2,1,1,128,320]{3,4,2,1,0:T(8,128)(2,1)S(1)}, bf16[2,1,1,128,320]{3,4,2,1,0:T(8,128)(2,1)S(1)}, u32[]{:S(2)}, u32[]{:S(2)}) collective-permute-start(bf16[2,1,1,128,320]{3,4,2,1,0:T(8,128)(2,1)S(1)} %get-tuple-element.13), channel_id=1, source_target_pairs={{0,1},{1,2},{2,3},{3,4},{4,5},{5,6},{6,7},{8,9},{9,10},{10,11},{11... | collective-permute-start | bytes 491528 | tf_op jit(solution)/shard_map/ppermute | solution.py:15
  10.8 5.4 %collective-permute-start.1 = (bf16[2,1,1,128,320]{3,4,2,1,0:T(8,128)(2,1)S(1)}, bf16[2,1,1,128,320]{3,4,2,1,0:T(8,128)(2,1)S(1)}, u32[]{:S(2)}, u32[]{:S(2)}) collective-permute-start(bf16[2,1,1,128,320]{3,4,2,1,0:T(8,128)(2,1)S(1)} %get-tuple-element.14), channel_id=1, source_target_pairs={{1,0},{2,1},{3,2},{4,3},{5,4},{6,5},{7,6},{9,8},{10,9},{11,10},{12... | collective-permute-start | bytes 491528 | tf_op jit(solution)/shard_map/ppermute | solution.py:17
  19.9 2.8 %copy-start.1 = (bf16[2,1,10,130,320]{3,4,2,1,0:T(8,128)(2,1)}, bf16[2,1,10,130,320]{3,4,2,1,0:T(8,128)(2,1)S(1)}, u32[]{:S(2)}) copy-start(bf16[2,1,10,130,320]{3,4,2,1,0:T(8,128)(2,1)S(1)} %select_maximum_fusion) | copy-start | bytes 4992004
  20.8 2.5 %copy-start.2 = (bf16[1,8,128,320]{2,3,1,0:T(8,128)(2,1)S(1)}, bf16[1,8,128,320]{2,3,1,0:T(8,128)(2,1)}, u32[]{:S(2)}) copy-start(bf16[1,8,128,320]{2,3,1,0:T(8,128)(2,1)} %param.4) | copy-start | bytes 1966084
  39.2 146.3 %all-reduce.3.cloned.1.call-start = ((), (), s32[]{:S(2)}) async-start(), calls=%async_computation.2 | async-start | bytes 2211840 | tf_op jit(solution)/shard_map/psum | solution.py:59
  75.8 9.8 %copy-start.4 = (bf16[1024,1,320]{0,2,1:T(8,128)(2,1)S(1)}, bf16[1024,1,320]{0,2,1:T(8,128)(2,1)}, u32[]{:S(2)}) copy-start(bf16[1024,1,320]{0,2,1:T(8,128)(2,1)} %stack.74) | copy-start | bytes 1966084
  81.4 9.0 %copy-start.5 = (bf16[1024,1,320]{0,2,1:T(8,128)(2,1)S(1)}, bf16[1024,1,320]{0,2,1:T(8,128)(2,1)}, u32[]{:S(2)}) copy-start(bf16[1024,1,320]{0,2,1:T(8,128)(2,1)} %stack.77) | copy-start | bytes 1966084
  81.4 9.9 %copy-start.6 = (bf16[1024,1,320]{0,2,1:T(8,128)(2,1)S(1)}, bf16[1024,1,320]{0,2,1:T(8,128)(2,1)}, u32[]{:S(2)}) copy-start(bf16[1024,1,320]{0,2,1:T(8,128)(2,1)} %stack.78) | copy-start | bytes 1966084
  81.4 12.8 %copy-start.7 = (bf16[1024,1,320]{0,2,1:T(8,128)(2,1)S(1)}, bf16[1024,1,320]{0,2,1:T(8,128)(2,1)}, u32[]{:S(2)}) copy-start(bf16[1024,1,320]{0,2,1:T(8,128)(2,1)} %stack.80) | copy-start | bytes 1966084
  83.5 41.1 %copy-start.3 = (bf16[1,8,128,320]{2,3,1,0:T(8,128)(2,1)S(1)}, bf16[1,8,128,320]{2,3,1,0:T(8,128)(2,1)}, u32[]{:S(2)}) copy-start(bf16[1,8,128,320]{2,3,1,0:T(8,128)(2,1)} %param.3) | copy-start | bytes 1966084
Sparse Core Ops, SparseCore 0:
  39.4 85.1 reduce-scatter.1
  128.1 57.4 all-reduce.2
where the time goes:
time: 196 us; the launch traced here: 195 us
  waiting for transfers between devices  88.5 us (45%)
  local copies, waits for them, and re-layouts  73.3 us (37%)
  between operations  14.2 us (7%)
  matrix products  9.16 us (5%)
  other arithmetic  5.81 us (3%)
  starting transfers between devices  3.92 us (2%)
    psum x1, waiting for transfers between devices, shards(): summed = lax.psum(local_term, 'space')  55 us
    reduce_scatter x1, waiting for transfers between devices, shards(): lax.psum_scatter(summed, 'dp', scatter_dimension=0, tiled=True)  29.4 us
    slice x10, local copies, waits for them, and re-layouts, shards(): grad_pad[:, 2 - tap_a:2 - tap_a + rows, 2 - tap_b:2 - tap_b + width, :]  21 us
    another operation x10, local copies, waits for them, and re-layouts, shards(): grad_cols = jnp.stack(grad_taps, axis=3).reshape(count_rows, 9, chans)  20.3 us
    unnamed x33, local copies, waits for them, and re-layouts  17.5 us
    mul x2, local copies, waits for them, and re-layouts, shards(): local_term = term.reshape(span * 9, chans) * factor  12.6 us
    dot_general x1, matrix products, shards(): jnp.einsum('mtd,tcd->mc', grad_cols, kernel_taps, preferred_element_type=...  5.91 us
    ppermute x1, waiting for transfers between devices, with_halo(): lax.ppermute(head, axis, [((i + 1) % count, i) for i in range(ends)])  4.08 us
  transfers between devices with their start and end apart: 4, of which 3 were waited for; matrix products, arithmetic and copies ran while one was open for 32% of the time, Pallas kernels for 0%

commit v1 on v0

v1 whole, which is shorter than its diff:
```python
import functools

import jax
import jax.numpy as jnp
from jax import lax
from jax.experimental import pallas as pl
from jax.experimental.pallas import tpu as pltpu
from jax.sharding import PartitionSpec as P

F32 = jnp.float32
BF16 = jnp.bfloat16
LANES = 128
PAIR = 2
PLANE = 4
VMEM_LIMIT = 48 * 1024 * 1024


def vmem():
    return pl.BlockSpec(memory_space=pltpu.VMEM)


def column_shifts(row):
    wide = row.astype(F32)
    width = wide.shape[1]
    at = lax.broadcasted_iota(jnp.int32, wide.shape, 1)
    ahead = jnp.where(at == width - 1, 0.0, pltpu.roll(wide, width - 1, 1))
    behind = jnp.where(at == 0, 0.0, pltpu.roll(wide, 1, 1))
    return ahead.astype(BF16), row, behind.astype(BF16)


def weight_kernel(blocks, pre_ref, grad_ref, up_ref, down_ref, own_ref, send_ref, act_s, taps_s):
    rows, chans, width = pre_ref.shape
    half = chans // PAIR
    core = lax.rem(lax.axis_index("space"), PAIR)
    block = chans // blocks
    for h in range(PAIR):
        taps_s[h, 3 * half :, :] = jnp.zeros((taps_s.shape[1] - 3 * half, taps_s.shape[2]), BF16)
    for r in range(rows + 2):
        row = up_ref[...] if r == 0 else down_ref[...] if r == rows + 1 else grad_ref[r - 1]
        for b, shifted in enumerate(column_shifts(row)):
            for h in range(PAIR):
                taps_s[h, b * half : (b + 1) * half, r * width : (r + 1) * width] = shifted[h * half : (h + 1) * half]
    for r in range(rows):
        x = pre_ref[r].astype(F32)
        act_s[:, r * width : (r + 1) * width] = (x / (1.0 + jnp.exp(-x))).astype(BF16)
    for slot, out_ref in enumerate((send_ref, own_ref)):
        h = core if slot else 1 - core
        for a in range(3):
            at = (2 - a) * width
            term = lax.dot_general(
                act_s[...],
                taps_s[h, :, at : at + rows * width],
                (((1,), (1,)), ((), ())),
                preferred_element_type=F32,
            )
            for p in range(PLANE):
                for z in range(blocks):
                    out_ref[p, z, a] = term[z * block : (z + 1) * block, p * LANES : (p + 1) * LANES].astype(out_ref.dtype)


def input_kernel(pre_ref, grad_ref, up_ref, down_ref, kernel_ref, out_ref, taps_s):
    rows, chans, width = pre_ref.shape
    for r in range(rows + 2):
        row = up_ref[...] if r == 0 else down_ref[...] if r == rows + 1 else grad_ref[r - 1]
        for b, shifted in enumerate(column_shifts(row)):
            taps_s[b, :, r * width : (r + 1) * width] = shifted
    step = 2
    for first in range(0, rows, step):
        total = jnp.zeros((chans, step * width), F32)
        for a in range(3):
            at = (first + 2 - a) * width
            for b in range(3):
                total += jnp.dot(kernel_ref[a, b], taps_s[b, :, at : at + step * width], preferred_element_type=F32)
        for r in range(step):
            x = pre_ref[first + r].astype(F32)
            sig = 1.0 / (1.0 + jnp.exp(-x))
            deriv = sig * (1.0 + x * (1.0 - sig))
            out_ref[first + r] = (total[:, r * width : (r + 1) * width] * deriv).astype(out_ref.dtype)


def place_kernel(parts_ref, out_ref, rows_s):
    _, _, block, _ = parts_ref.shape
    chans = out_ref.shape[0]
    half = chans // PAIR
    for h in range(PAIR):
        for a in range(3):
            wide = jnp.concatenate([parts_ref[q * PAIR + h, a].astype(F32) for q in range(PLANE)], axis=1)
            for b in range(3):
                t = 3 * a + b
                rows_s[t * block : (t + 1) * block, h * half : (h + 1) * half] = wide[:, b * half : (b + 1) * half]
    k = lax.broadcasted_iota(jnp.int32, (block, 9 * block), 0)
    j = lax.broadcasted_iota(jnp.int32, (block, 9 * block), 1)
    pick = jnp.concatenate([jnp.where(j - 9 * k == t, 1.0, 0.0) for t in range(9)], axis=0)
    pick = pick.astype(BF16)
    high = rows_s[...].astype(BF16)
    low = (rows_s[...] - high.astype(F32)).astype(BF16)
    dims = (((0,), (0,)), ((), ()))
    out_ref[...] = lax.dot_general(high, pick, dims, preferred_element_type=F32) + lax.dot_general(
        low, pick, dims, preferred_element_type=F32
    )


def shards(pre_act, out_grad, kernel):
    images, rows, width, chans = pre_act.shape
    assert images == 1
    space, blocks = lax.axis_size("space"), lax.axis_size("dp")
    inner = PAIR * PLANE
    outer = space // inner
    block = chans // blocks
    factor = float(images * rows * width * space * blocks) ** (-0.5)
    params = pltpu.CompilerParams(vmem_limit_bytes=VMEM_LIMIT)

    pre = jnp.swapaxes(pre_act[0], 1, 2)
    grad = jnp.swapaxes(out_grad[0], 1, 2)
    up = lax.ppermute(grad[rows - 1], "space", [(i, i + 1) for i in range(space - 1)])
    down = lax.ppermute(grad[0], "space", [(i + 1, i) for i in range(space - 1)])

    piece = jax.ShapeDtypeStruct((PLANE, blocks, 3, block, LANES), F32)
    flops = 2 * 9 * chans * chans * rows * width
    own, send = pl.pallas_call(
        functools.partial(weight_kernel, blocks),
        out_shape=(piece, piece),
        in_specs=[vmem()] * 4,
        out_specs=(vmem(), vmem()),
        scratch_shapes=[
            pltpu.VMEM((chans, rows * width), BF16),
            pltpu.VMEM((PAIR, PLANE * LANES, (rows + 2) * width), BF16),
        ],
        compiler_params=params,
        cost_estimate=pl.CostEstimate(flops=flops, bytes_accessed=6000000, transcendentals=rows * width * chans),
        name="weight_terms",
    )(pre, grad, up, down)
    recv = lax.ppermute(send, "space", [(i, i + 1 - 2 * (i % 2)) for i in range(space)])
    pair_sum = (own + recv).astype(BF16)

    in_grad = pl.pallas_call(
        input_kernel,
        out_shape=jax.ShapeDtypeStruct((rows, chans, width), BF16),
        in_specs=[vmem()] * 5,
        out_specs=vmem(),
        scratch_shapes=[pltpu.VMEM((3, chans, (rows + 2) * width), BF16)],
        compiler_params=params,
        cost_estimate=pl.CostEstimate(flops=flops, bytes_accessed=4000000, transcendentals=rows * width * chans),
        name="input_grad",
    )(pre, grad, up, down, kernel)

    planes = [[first + PAIR * p + c for p in range(PLANE)] for first in range(0, space, inner) for c in range(PAIR)]
    terms = lax.all_to_all(pair_sum, "space", 0, 0, axis_index_groups=planes, tiled=True)
    plane_sum = jnp.sum(terms.astype(F32), axis=0)
    terms = lax.all_to_all(plane_sum.astype(BF16), "dp", 0, 0, tiled=True)
    total = jnp.sum(terms.astype(F32), axis=0) * factor
    if outer > 1:
        total = lax.psum(total, "space", axis_index_groups=[[o * inner + i for o in range(outer)] for i in range(inner)])
    inners = [[first + i for i in range(inner)] for first in range(0, space, inner)]
    spread = jnp.broadcast_to(total[None], (inner, 3, block, LANES))
    parts = lax.all_to_all(spread, "space", 0, 0, axis_index_groups=inners, tiled=True)

    placed = pl.pallas_call(
        place_kernel,
        out_shape=jax.ShapeDtypeStruct((chans, 9 * block), F32),
        in_specs=[vmem()],
        out_specs=vmem(),
        scratch_shapes=[pltpu.VMEM((9 * block, chans), F32)],
        compiler_params=params,
        cost_estimate=pl.CostEstimate(flops=2 * 81 * block * block * chans, bytes_accessed=2000000, transcendentals=0),
        name="place_rows",
    )(parts)
    return jnp.swapaxes(in_grad, 1, 2)[None], placed.T


def solution(mesh):
    placed = (P("dp", "space", None, None), P("dp", "space", None, None), P())
    return jax.shard_map(
        shards,
        mesh=mesh,
        in_specs=placed,
        out_specs=(P("dp", "space", None, None), P("dp", None)),
        check_vma=False,
    )
```

time: 196 us -> 73.7 us (0.38)
  waiting for transfers between devices: 88.5 us -> 16.2 us
  local copies, waits for them, and re-layouts: 73.3 us -> 5.75 us
  blocking collectives: 0 us -> 29.9 us
  between operations: 14.2 us -> 0.72 us
  Pallas kernels: 0 us -> 9.91 us
  matrix products: 9.16 us -> 0 us
  starting transfers between devices: 3.92 us -> 10.4 us
  other arithmetic: 5.81 us -> 0.42 us
    psum x1 -> x0, waiting for transfers between devices: 55 us -> none  [shards(): summed = lax.psum(local_term, 'space')]
    all_to_all x0 -> x2, blocking collectives: none -> 29.9 us  [the longest x1 17.6 us: shards(): lax.all_to_all(pair_sum, 'space', 0, 0, axis_index_groups=planes, tiled=T...]
    reduce_scatter x1 -> x0, waiting for transfers between devices: 29.4 us -> none  [shards(): lax.psum_scatter(summed, 'dp', scatter_dimension=0, tiled=True)]
    slice x10 -> x0, local copies, waits for them, and re-layouts: 21 us -> none  [shards(): grad_pad[:, 2 - tap_a:2 - tap_a + rows, 2 - tap_b:2 - tap_b + width, :]]
    another operation x11 -> x0, local copies, waits for them, and re-layouts: 20.6 us -> none  [the longest x10 20.3 us: shards(): grad_cols = jnp.stack(grad_taps, axis=3).reshape(count_rows, 9, chans)]
    unnamed x33 -> x10, local copies, waits for them, and re-layouts: 17.5 us -> 3.8 us
    mul x2 -> x0, local copies, waits for them, and re-layouts: 12.6 us -> none  [shards(): local_term = term.reshape(span * 9, chans) * factor]
    pallas_call x0 -> x3, Pallas kernels: none -> 9.91 us  [the longest x1 4.4 us: shards(): pl.pallas_call(input_kernel, out_shape=jax.ShapeDtypeStruct((rows, chans,...]
  transfers between devices with their start and end apart: 4 -> 4, of which waited for: 3 -> 3; matrix products, arithmetic and copies ran while one was open for 32% -> 0% of each run, Pallas kernels for 0% -> 6%
where the time goes in v1:
time: 73.7 us; the launch traced here: 73.2 us
  blocking collectives  29.9 us (41%)
  waiting for transfers between devices  16.2 us (22%)
  starting transfers between devices  10.4 us (14%)
  Pallas kernels  9.91 us (13%)
  local copies, waits for them, and re-layouts  5.75 us (8%)
    all_to_all x1, blocking collectives, shards(): lax.all_to_all(pair_sum, 'space', 0, 0, axis_index_groups=planes, tiled=T...  17.6 us
    all_to_all x1, blocking collectives, shards(): terms = lax.all_to_all(plane_sum.astype(BF16), 'dp', 0, 0, tiled=True)  12.3 us
    all_to_all x1, waiting for transfers between devices, shards(): lax.all_to_all(spread, 'space', 0, 0, axis_index_groups=inners, tiled=True)  8.59 us
    pallas_call x1, Pallas kernels, shards(): pl.pallas_call(input_kernel, out_shape=jax.ShapeDtypeStruct((rows, chans,...  4.4 us
    ppermute x1, waiting for transfers between devices, shards(): lax.ppermute(grad[0], 'space', [(i + 1, i) for i in range(space - 1)])  3.96 us
    unnamed x10, local copies, waits for them, and re-layouts  3.8 us
    ppermute x1, waiting for transfers between devices, shards(): lax.ppermute(send, 'space', [(i, i + 1 - 2 * (i % 2)) for i in range(spac...  3.6 us
    all_to_all x1, starting transfers between devices, shards(): lax.all_to_all(spread, 'space', 0, 0, axis_index_groups=inners, tiled=True)  3.56 us
  transfers between devices with their start and end apart: 4, of which 3 were waited for; matrix products, arithmetic and copies ran while one was open for 0% of the time, Pallas kernels for 6%

profile of v1, /device:TPU:0, one launch (start us, length us, event | category | flops | bytes accessed | tf_op | source)
XLA Modules:
  0.0 73.2 jit_solution(7518400665647621037)
XLA Ops:
  0.6 0.9 %slice_bitcast_fusion = (bf16[320,128]{1,0:T(8,128)(2,1)S(1)}, bf16[320,128]{1,0:T(8,128)(2,1)S(1)}) fusion(bf16[8,320,128]{2,1,0:T(8,128)(2,1)} %bitcast.14), kind=kLoop, calls=%fused_computation.2 | loop fusion | bytes 327680 | tf_op jit(solution)/shard_map/squeeze | solution.py:116
  1.6 2.4 %collective-permute-start = (bf16[320,128]{1,0:T(8,128)(2,1)S(1)}, bf16[320,128]{1,0:T(8,128)(2,1)S(1)}, u32[]{:S(2)}, u32[]{:S(2)}) collective-permute-start(bf16[320,128]{1,0:T(8,128)(2,1)S(1)} %get-tuple-element.7), channel_id=1, source_target_pairs={{0,1},{1,2},{2,3},{3,4},{4,5},{5,6},{6,7},{8,9},{9,10},{10,11},{11... | collective-permute-start | bytes 245768 | tf_op jit(solution)/shard_map/ppermute | solution.py:115
  3.9 1.3 %collective-permute-start.1 = (bf16[320,128]{1,0:T(8,128)(2,1)S(1)}, bf16[320,128]{1,0:T(8,128)(2,1)S(1)}, u32[]{:S(2)}, u32[]{:S(2)}) collective-permute-start(bf16[320,128]{1,0:T(8,128)(2,1)S(1)} %get-tuple-element.6), channel_id=1, source_target_pairs={{1,0},{2,1},{3,2},{4,3},{5,4},{6,5},{7,6},{9,8},{10,9},{11,10},{12... | collective-permute-start | bytes 245768 | tf_op jit(solution)/shard_map/ppermute | solution.py:116
  5.2 0.0 collective-permute-done.up_ref
  5.3 4.0 %collective-permute-done.1.down_ref = bf16[320,128]{1,0:T(8,128)(2,1)S(1)} collective-permute-done((bf16[320,128]{1,0:T(8,128)(2,1)S(1)}, bf16[320,128]{1,0:T(8,128)(2,1)S(1)}, u32[]{:S(2)}, u32[]{:S(2)}) %collective-permute-start.1) | collective-permute-done | bytes 81952 | tf_op jit(solution)/shard_map/ppermute | solution.py:116
  9.2 0.0 copy-start
  9.2 1.1 %copy-done = bf16[1,8,128,320]{2,3,1,0:T(8,128)(2,1)S(1)} copy-done((bf16[1,8,128,320]{2,3,1,0:T(8,128)(2,1)S(1)}, bf16[1,8,128,320]{2,3,1,0:T(8,128)(2,1)}, u32[]{:S(2)}) %copy-start) | copy-done | bytes 655384
  10.3 1.1 %copy-done.3 = bf16[1,8,128,320]{2,3,1,0:T(8,128)(2,1)S(1)} copy-done((bf16[1,8,128,320]{2,3,1,0:T(8,128)(2,1)S(1)}, bf16[1,8,128,320]{2,3,1,0:T(8,128)(2,1)}, u32[]{:S(2)}) %copy-start.3) | copy-done | bytes 655384
  11.4 3.2 %weight_terms.1 = (f32[4,4,3,80,128]{4,3,2,1,0:T(8,128)S(1)}, f32[4,4,3,80,128]{4,3,2,1,0:T(8,128)S(1)}) custom-call(bf16[8,320,128]{2,1,0:T(8,128)(2,1)S(1)} %bitcast.17, bf16[8,320,128]{2,1,0:T(8,128)(2,1)S(1)} %bitcast.15, bf16[320,128]{1,0:T(8,128)(2,1)S(1)} %collective-permute-done.up_ref, bf16[320,128]{1,0:T(8,128)(2,1)S(1)} %collective-permute-done.1.down_ref), custom_call_target="tpu_custom_call" | custom-call | flops 1887436800 | bytes 6000000 | tf_op jit(solution)/shard_map/weight_terms/pallas_call | solution.py:120
  14.6 3.1 %collective-permute-start.2 = (f32[4,4,3,80,128]{4,3,2,1,0:T(8,128)S(1)}, f32[4,4,3,80,128]{4,3,2,1,0:T(8,128)S(1)}, u32[]{:S(2)}, u32[]{:S(2)}) collective-permute-start(f32[4,4,3,80,128]{4,3,2,1,0:T(8,128)S(1)} %get-tuple-element.5), channel_id=1, source_target_pairs={{0,1},{1,0},{2,3},{3,2},{4,5},{5,4},{6,7},{7,6},{8,9},{9,8},{10,11... | collective-permute-start | bytes 5898248 | tf_op jit(solution)/shard_map/ppermute | solution.py:133
  17.7 3.6 %collective-permute-done.2 = f32[4,4,3,80,128]{4,3,2,1,0:T(8,128)S(1)} collective-permute-done((f32[4,4,3,80,128]{4,3,2,1,0:T(8,128)S(1)}, f32[4,4,3,80,128]{4,3,2,1,0:T(8,128)S(1)}, u32[]{:S(2)}, u32[]{:S(2)}) %collective-permute-start.2) | collective-permute-done | bytes 1966112 | tf_op jit(solution)/shard_map/ppermute | solution.py:133
  21.3 0.2 add_convert_fusion
  21.6 17.6 %all_to_all.15 = bf16[4,4,3,80,128]{4,3,2,1,0:T(8,128)(2,1)S(1)} all-to-all(bf16[4,4,3,80,128]{4,3,2,1,0:T(8,128)(2,1)S(1)} %add_convert_fusion), channel_id=1, replica_groups={{0,2,4,6},{1,3,5,7},{8,10,12,14},{9,11,13,15},{16,18,20,22},{17,19,21,2..., dimensions={0} | all-to-all | bytes 1966080 | tf_op jit(solution)/shard_map/all_to_all | solution.py:148
  39.2 0.2 reduce_sum.21
  39.3 12.3 %all_to_all.16 = bf16[4,3,80,128]{3,2,1,0:T(8,128)(2,1)S(1)} all-to-all(bf16[4,3,80,128]{3,2,1,0:T(8,128)(2,1)S(1)} %reduce_sum.21), channel_id=1, replica_groups=mesh['dp'=4,'space'=8] {'dp'}, dimensions={0} | all-to-all | bytes 491520 | tf_op jit(solution)/shard_map/all_to_all | solution.py:150
  51.7 1.0 %broadcast_in_dim.10 = f32[8,3,80,128]{3,2,1,0:T(8,128)} broadcast(f32[3,80,128]{2,1,0:T(8,128)S(1)} %broadcast_multiply_fusion), dimensions={1,2,3} | broadcast | bytes 1105920 | tf_op jit(solution)/shard_map/broadcast_in_dim | solution.py:155
  52.7 3.6 %all-to-all-start.2 = ((f32[8,3,80,128]{3,2,1,0:T(8,128)}), f32[8,3,80,128]{3,2,1,0:T(8,128)S(1)}, u32[]{:S(2)}, u32[]{:S(2)}) async-start(f32[8,3,80,128]{3,2,1,0:T(8,128)} %broadcast_in_dim.10), calls=%async_computation.2 | async-start | bytes 1966080 | tf_op jit(solution)/shard_map/all_to_all | solution.py:156
  56.3 0.0 copy-done.1
  56.3 0.0 copy-done.4
  56.3 0.0 copy-start.2
  56.3 1.6 %copy-done.2 = bf16[3,3,320,320]{3,2,1,0:T(8,128)(2,1)S(1)} copy-done((bf16[3,3,320,320]{3,2,1,0:T(8,128)(2,1)S(1)}, bf16[3,3,320,320]{3,2,1,0:T(8,128)(2,1)}, u32[]{:S(2)}) %copy-start.2) | copy-done | bytes 1843224
  57.9 4.4 %input_grad.1 = bf16[8,320,128]{2,1,0:T(8,128)(2,1)} custom-call(bf16[8,320,128]{2,1,0:T(8,128)(2,1)S(1)} %bitcast.18, bf16[8,320,128]{2,1,0:T(8,128)(2,1)S(1)} %bitcast.16, bf16[320,128]{1,0:T(8,128)(2,1)S(1)} %collective-permute-done.up_ref, bf16[320,128]{1,0:T(8,128)(2,1)S(1)} %collective-permute-done.1.down_ref, bf16[3,3,320,320]{3,2,1,0:T(8,128)(2,1)S(1)} %copy-done.2), custom_call_target="tpu_custom_call" | custom-call | flops 1887436800 | bytes 4000000 | tf_op jit(solution)/shard_map/input_grad/pallas_call | solution.py:136
  62.3 8.6 %all-to-all-done.2.parts_ref = f32[8,3,80,128]{3,2,1,0:T(8,128)S(1)} async-done(((f32[8,3,80,128]{3,2,1,0:T(8,128)}), f32[8,3,80,128]{3,2,1,0:T(8,128)S(1)}, u32[]{:S(2)}, u32[]{:S(2)}) %all-to-all-start.2) | async-done | bytes 983072 | tf_op jit(solution)/shard_map/all_to_all | solution.py:156
  70.9 2.3 %place_rows.1 = f32[320,720]{1,0:T(8,128)} custom-call(f32[8,3,80,128]{3,2,1,0:T(8,128)S(1)} %all-to-all-done.2.parts_ref), custom_call_target="tpu_custom_call" | custom-call | flops 331776000 | bytes 2000000 | tf_op jit(solution)/shard_map/place_rows/pallas_call | solution.py:158
  (5 shorter events, 0.0 us)
Async XLA Ops:
  1.6 3.7 %collective-permute-start = (bf16[320,128]{1,0:T(8,128)(2,1)S(1)}, bf16[320,128]{1,0:T(8,128)(2,1)S(1)}, u32[]{:S(2)}, u32[]{:S(2)}) collective-permute-start(bf16[320,128]{1,0:T(8,128)(2,1)S(1)} %get-tuple-element.7), channel_id=1, source_target_pairs={{0,1},{1,2},{2,3},{3,4},{4,5},{5,6},{6,7},{8,9},{9,10},{10,11},{11... | collective-permute-start | bytes 245768 | tf_op jit(solution)/shard_map/ppermute | solution.py:115
  3.9 5.3 %collective-permute-start.1 = (bf16[320,128]{1,0:T(8,128)(2,1)S(1)}, bf16[320,128]{1,0:T(8,128)(2,1)S(1)}, u32[]{:S(2)}, u32[]{:S(2)}) collective-permute-start(bf16[320,128]{1,0:T(8,128)(2,1)S(1)} %get-tuple-element.6), channel_id=1, source_target_pairs={{1,0},{2,1},{3,2},{4,3},{5,4},{6,5},{7,6},{9,8},{10,9},{11,10},{12... | collective-permute-start | bytes 245768 | tf_op jit(solution)/shard_map/ppermute | solution.py:116
  9.2 1.1 %copy-start = (bf16[1,8,128,320]{2,3,1,0:T(8,128)(2,1)S(1)}, bf16[1,8,128,320]{2,3,1,0:T(8,128)(2,1)}, u32[]{:S(2)}) copy-start(bf16[1,8,128,320]{2,3,1,0:T(8,128)(2,1)} %param.4) | copy-start | bytes 1966084
  10.3 1.1 %copy-start.3 = (bf16[1,8,128,320]{2,3,1,0:T(8,128)(2,1)S(1)}, bf16[1,8,128,320]{2,3,1,0:T(8,128)(2,1)}, u32[]{:S(2)}) copy-start(bf16[1,8,128,320]{2,3,1,0:T(8,128)(2,1)} %param.3) | copy-start | bytes 1966084
  14.6 6.7 %collective-permute-start.2 = (f32[4,4,3,80,128]{4,3,2,1,0:T(8,128)S(1)}, f32[4,4,3,80,128]{4,3,2,1,0:T(8,128)S(1)}, u32[]{:S(2)}, u32[]{:S(2)}) collective-permute-start(f32[4,4,3,80,128]{4,3,2,1,0:T(8,128)S(1)} %get-tuple-element.5), channel_id=1, source_target_pairs={{0,1},{1,0},{2,3},{3,2},{4,5},{5,4},{6,7},{7,6},{8,9},{9,8},{10,11... | collective-permute-start | bytes 5898248 | tf_op jit(solution)/shard_map/ppermute | solution.py:133
  51.6 4.6 %copy-start.1 = (bf16[1,8,128,320]{2,3,1,0:T(8,128)(2,1)S(1)}, bf16[1,8,128,320]{2,3,1,0:T(8,128)(2,1)}, u32[]{:S(2)}) copy-start(bf16[1,8,128,320]{2,3,1,0:T(8,128)(2,1)} %param.4) | copy-start | bytes 1966084
  51.6 4.6 %copy-start.4 = (bf16[1,8,128,320]{2,3,1,0:T(8,128)(2,1)S(1)}, bf16[1,8,128,320]{2,3,1,0:T(8,128)(2,1)}, u32[]{:S(2)}) copy-start(bf16[1,8,128,320]{2,3,1,0:T(8,128)(2,1)} %param.3) | copy-start | bytes 1966084
  52.7 18.2 %all-to-all-start.2 = ((f32[8,3,80,128]{3,2,1,0:T(8,128)}), f32[8,3,80,128]{3,2,1,0:T(8,128)S(1)}, u32[]{:S(2)}, u32[]{:S(2)}) async-start(f32[8,3,80,128]{3,2,1,0:T(8,128)} %broadcast_in_dim.10), calls=%async_computation.2 | async-start | bytes 1966080 | tf_op jit(solution)/shard_map/all_to_all | solution.py:156
  56.3 1.6 %copy-start.2 = (bf16[3,3,320,320]{3,2,1,0:T(8,128)(2,1)S(1)}, bf16[3,3,320,320]{3,2,1,0:T(8,128)(2,1)}, u32[]{:S(2)}) copy-start(bf16[3,3,320,320]{3,2,1,0:T(8,128)(2,1)} %kernel_ref.1) | copy-start | bytes 5529604

commit v2 on v1

v2 whole, which is shorter than its diff:
```python
import jax
import jax.numpy as jnp
from jax import lax
from jax.experimental import pallas as pl
from jax.experimental.pallas import tpu as pltpu
from jax.sharding import PartitionSpec as P

F32 = jnp.float32
BF16 = jnp.bfloat16
LANES = 128
PAIR = 2
PLANE = 4
NEAR = 2
VMEM_LIMIT = 48 * 1024 * 1024
NT = (((1,), (1,)), ((), ()))


def vmem():
    return pl.BlockSpec(memory_space=pltpu.VMEM)


def column_shifts(row):
    wide = row.astype(F32)
    width = wide.shape[1]
    at = lax.broadcasted_iota(jnp.int32, wide.shape, 1)
    ahead = jnp.where(at == width - 1, 0.0, pltpu.roll(wide, width - 1, 1))
    behind = jnp.where(at == 0, 0.0, pltpu.roll(wide, 1, 1))
    return ahead.astype(BF16), row, behind.astype(BF16)


def put_taps(taps_s, slot, row):
    half, width = row.shape
    for b, shifted in enumerate(column_shifts(row)):
        taps_s[b * half : (b + 1) * half, slot * width : (slot + 1) * width] = shifted


def silu(v):
    x = v.astype(F32)
    return (x / (1.0 + jnp.exp(-x))).astype(BF16)


def my_core():
    return lax.rem(lax.axis_index("space"), PAIR)


def own_kernel(pre_ref, grad_ref, term_ref, act_s, taps_s):
    rows, chans, width = pre_ref.shape
    half = chans // PAIR
    mine = pl.ds(pl.multiple_of(my_core() * half, half), half)
    zero = jnp.zeros((half, width), BF16)
    taps_s[3 * half :, :] = jnp.zeros((taps_s.shape[0] - 3 * half, taps_s.shape[1]), BF16)
    for r in range(rows + 2):
        put_taps(taps_s, r, grad_ref[r - 1, mine, :] if 0 < r <= rows else zero)
    for r in range(rows):
        act_s[:, r * width : (r + 1) * width] = silu(pre_ref[r])
    for a in range(3):
        at = (2 - a) * width
        term_ref[a] = lax.dot_general(act_s[...], taps_s[:, at : at + rows * width], NT, preferred_element_type=F32)


def pair_kernel(term_ref, pre_ref, grad_ref, their_pre_ref, their_grad_ref, near_ref, far_ref, out_ref, act_s, taps_s):
    rows, chans, width = pre_ref.shape
    half = chans // PAIR
    _, _, outers, _, block, _ = out_ref.shape
    core = my_core()
    first = core == 0
    mine = pl.ds(pl.multiple_of(core * half, half), half)
    taps_s[3 * half :, :] = jnp.zeros((taps_s.shape[0] - 3 * half, taps_s.shape[1]), BF16)
    put_taps(taps_s, 0, jnp.where(first, near_ref[mine, :], their_grad_ref[rows - 1, mine, :]))
    put_taps(taps_s, 1, jnp.where(first, grad_ref[rows - 1, mine, :], far_ref[...]))
    for r in range(rows):
        put_taps(taps_s, 2 + r, their_grad_ref[r, mine, :])
    put_taps(taps_s, rows + 2, jnp.where(first, far_ref[...], grad_ref[0, mine, :]))
    put_taps(taps_s, rows + 3, jnp.where(first, their_grad_ref[0, mine, :], near_ref[mine, :]))
    act_s[:, :width] = silu(pre_ref[0])
    for r in range(rows):
        act_s[:, (r + 1) * width : (r + 2) * width] = silu(their_pre_ref[r])
    act_s[:, (rows + 1) * width :] = silu(pre_ref[rows - 1])
    for a, (left, right, at) in enumerate(((1, rows + 2, 3), (1, rows + 1, 2), (0, rows + 1, 0))):
        term = term_ref[a] + lax.dot_general(
            act_s[:, left * width : right * width],
            taps_s[:, at * width : (at + right - left) * width],
            NT,
            preferred_element_type=F32,
        )
        for p in range(PLANE):
            for z in range(NEAR * outers):
                out_ref[z % NEAR, p, z // NEAR, a] = term[
                    z * block : (z + 1) * block, p * LANES : (p + 1) * LANES
                ].astype(out_ref.dtype)


def input_kernel(pre_ref, grad_ref, their_grad_ref, near_ref, kernel_ref, out_ref, taps_s):
    rows, chans, width = pre_ref.shape
    first = my_core() == 0
    for r in range(rows + 2):
        if r == 0:
            row = jnp.where(first, near_ref[...], their_grad_ref[rows - 1])
        elif r == rows + 1:
            row = jnp.where(first, their_grad_ref[0], near_ref[...])
        else:
            row = grad_ref[r - 1]
        put_taps(taps_s, r, row)
    step = 2
    for top in range(0, rows, step):
        total = jnp.zeros((chans, step * width), F32)
        for a in range(3):
            at = (top + 2 - a) * width
            for b in range(3):
                taps = taps_s[b * chans : (b + 1) * chans, at : at + step * width]
                total += jnp.dot(kernel_ref[a, b], taps, preferred_element_type=F32)
        for r in range(step):
            x = pre_ref[top + r].astype(F32)
            sig = 1.0 / (1.0 + jnp.exp(-x))
            deriv = sig * (1.0 + x * (1.0 - sig))
            out_ref[top + r] = (total[:, r * width : (r + 1) * width] * deriv).astype(out_ref.dtype)


def place_kernel(parts_ref, out_ref, rows_s):
    _, _, block, _ = parts_ref.shape
    chans = out_ref.shape[0]
    half = chans // PAIR
    for h in range(PAIR):
        for a in range(3):
            wide = jnp.concatenate([parts_ref[q * PAIR + h, a].astype(F32) for q in range(PLANE)], axis=1)
            for b in range(3):
                t = 3 * a + b
                rows_s[t * block : (t + 1) * block, h * half : (h + 1) * half] = wide[:, b * half : (b + 1) * half]
    k = lax.broadcasted_iota(jnp.int32, (block, 9 * block), 0)
    j = lax.broadcasted_iota(jnp.int32, (block, 9 * block), 1)
    pick = jnp.concatenate([jnp.where(j - 9 * k == t, 1.0, 0.0) for t in range(9)], axis=0).astype(BF16)
    dims = (((0,), (0,)), ((), ()))
    out_ref[...] = lax.dot_general(rows_s[...].astype(BF16), pick, dims, preferred_element_type=F32)


def shards(pre_act, out_grad, kernel):
    images, rows, width, chans = pre_act.shape
    assert images == 1
    space, blocks = lax.axis_size("space"), lax.axis_size("dp")
    inner = PAIR * PLANE
    outer = space // inner
    block = chans // blocks
    half = chans // PAIR
    far = blocks // NEAR
    factor = float(images * rows * width * space * blocks) ** (-0.5)
    params = pltpu.CompilerParams(vmem_limit_bytes=VMEM_LIMIT)
    core = my_core()
    flops = 2 * 9 * chans * chans * rows * width

    pre = jnp.swapaxes(pre_act[0], 1, 2)
    grad = jnp.swapaxes(out_grad[0], 1, 2)
    edge = lax.dynamic_index_in_dim(grad, core * (rows - 1), 0, keepdims=False)
    edge_half = lax.dynamic_slice_in_dim(edge, core * half, half, 0)
    beyond = [(i, i + 1 if i % 2 else i - 1) for i in range(space)]
    beyond_two = [(i, i + 2 if i % 2 else i - 2) for i in range(space)]
    pairs = [(i, i + 1 - 2 * (i % 2)) for i in range(space)]

    def inside(moves):
        return [(i, j) for i, j in moves if 0 <= j < space]

    near_row = lax.ppermute(edge, "space", inside(beyond))
    far_row = lax.ppermute(edge_half, "space", inside(beyond_two))
    their_grad = lax.ppermute(grad, "space", pairs)
    their_pre = lax.ppermute(pre, "space", pairs)

    own = pl.pallas_call(
        own_kernel,
        out_shape=jax.ShapeDtypeStruct((3, chans, PLANE * LANES), F32),
        in_specs=[vmem()] * 2,
        out_specs=vmem(),
        scratch_shapes=[
            pltpu.VMEM((chans, rows * width), BF16),
            pltpu.VMEM((PLANE * LANES, (rows + 2) * width), BF16),
        ],
        compiler_params=params,
        cost_estimate=pl.CostEstimate(flops=flops, bytes_accessed=4000000, transcendentals=rows * width * chans),
        name="own_terms",
    )(pre, grad)
    terms = pl.pallas_call(
        pair_kernel,
        out_shape=jax.ShapeDtypeStruct((NEAR, PLANE, far, 3, block, LANES), BF16),
        in_specs=[vmem()] * 7,
        out_specs=vmem(),
        scratch_shapes=[
            pltpu.VMEM((chans, (rows + 2) * width), BF16),
            pltpu.VMEM((PLANE * LANES, (rows + 4) * width), BF16),
        ],
        compiler_params=params,
        cost_estimate=pl.CostEstimate(flops=flops, bytes_accessed=4000000, transcendentals=rows * width * chans),
        name="pair_terms",
    )(own, pre, grad, their_pre, their_grad, near_row, far_row)

    in_grad = pl.pallas_call(
        input_kernel,
        out_shape=jax.ShapeDtypeStruct((rows, chans, width), BF16),
        in_specs=[vmem()] * 5,
        out_specs=vmem(),
        scratch_shapes=[pltpu.VMEM((3 * chans, (rows + 2) * width), BF16)],
        compiler_params=params,
        cost_estimate=pl.CostEstimate(flops=flops, bytes_accessed=4000000, transcendentals=rows * width * chans),
        name="input_grad",
    )(pre, grad, their_grad, near_row, kernel)

    groups = [
        [(NEAR * f + n) * space + first + PAIR * p + c for n in range(NEAR) for p in range(PLANE)]
        for f in range(far)
        for first in range(0, space, inner)
        for c in range(PAIR)
    ]
    terms = terms.reshape(NEAR * PLANE, far, 3, block, LANES)
    got = lax.all_to_all(terms, ("dp", "space"), 0, 0, axis_index_groups=groups, tiled=True)
    near_sum = jnp.sum(got.astype(F32), axis=0)
    mine = lax.axis_index("dp") // NEAR
    total = lax.dynamic_index_in_dim(near_sum, mine, 0, keepdims=False)
    for k in range(1, far):
        theirs = lax.dynamic_index_in_dim(near_sum, mine ^ k, 0, keepdims=False).astype(BF16)
        moves = [(z, z ^ (k * NEAR)) for z in range(blocks)]
        total = total + lax.ppermute(theirs, "dp", moves).astype(F32)
    total = total * factor
    if outer > 1:
        total = lax.psum(total, "space", axis_index_groups=[[o * inner + i for o in range(outer)] for i in range(inner)])
    inners = [[first + i for i in range(inner)] for first in range(0, space, inner)]
    spread = jnp.broadcast_to(total.astype(BF16)[None], (inner, 3, block, LANES))
    parts = lax.all_to_all(spread, "space", 0, 0, axis_index_groups=inners, tiled=True)

    placed = pl.pallas_call(
        place_kernel,
        out_shape=jax.ShapeDtypeStruct((chans, 9 * block), F32),
        in_specs=[vmem()],
        out_specs=vmem(),
        scratch_shapes=[pltpu.VMEM((9 * block, chans), F32)],
        compiler_params=params,
        cost_estimate=pl.CostEstimate(flops=2 * 81 * block * block * chans, bytes_accessed=2000000, transcendentals=0),
        name="place_rows",
    )(parts)
    return jnp.swapaxes(in_grad, 1, 2)[None], placed.T


def solution(mesh):
    placed = (P("dp", "space", None, None), P("dp", "space", None, None), P())
    return jax.shard_map(
        shards,
        mesh=mesh,
        in_specs=placed,
        out_specs=(P("dp", "space", None, None), P("dp", None)),
        check_vma=False,
    )
```

time: 73.7 us -> 60.2 us (0.82)
  blocking collectives: 29.9 us -> 0 us
  waiting for transfers between devices: 16.2 us -> 24.5 us
  starting transfers between devices: 10.4 us -> 15.5 us
  local copies, waits for them, and re-layouts: 5.75 us -> 6.91 us
  other arithmetic: 0.42 us -> 1.38 us
    all_to_all x2 -> x0, blocking collectives: 29.9 us -> none  [the longest x1 17.6 us: shards(): lax.all_to_all(pair_sum, 'space', 0, 0, axis_index_groups=planes, tiled=T...]
    all_to_all x0 -> x1, waiting for transfers between devices: none -> 15 us  [shards(): lax.all_to_all(terms, ('dp', 'space'), 0, 0, axis_index_groups=groups, ti...]
    all_to_all x0 -> x1, starting transfers between devices: none -> 6.65 us  [shards(): lax.all_to_all(terms, ('dp', 'space'), 0, 0, axis_index_groups=groups, ti...]
    all_to_all x1, waiting for transfers between devices: 8.59 us -> 2.78 us  [shards(): lax.all_to_all(spread, 'space', 0, 0, axis_index_groups=inners, tiled=True)]
    ppermute x3 -> x5, starting transfers between devices: 6.8 us -> 5.2 us  [the longest x1 2.66 us: shards(): total = total + lax.ppermute(theirs, 'dp', moves).astype(F32)]
    reduce_sum x2 -> x1, other arithmetic: 0.18 us -> 1.36 us  [shards(): near_sum = jnp.sum(got.astype(F32), axis=0)]
    pallas_call x1 -> x2, Pallas kernels: 3.19 us -> 4.2 us  [the longest x1 2.68 us: shards(): pl.pallas_call(pair_kernel, out_shape=jax.ShapeDtypeStruct((NEAR, PLANE,...]
    dynamic_slice x0 -> x1, local copies, waits for them, and re-layouts: none -> 0.81 us  [shards(): edge_half = lax.dynamic_slice_in_dim(edge, core * half, half, 0)]
  transfers between devices with their start and end apart: 4 -> 7, of which waited for: 3 -> 4; matrix products, arithmetic and copies ran while one was open for 0% -> 3% of each run, Pallas kernels for 6% -> 10%
where the time goes in v2:
time: 60.2 us; the launch traced here: 59.6 us
  waiting for transfers between devices  24.5 us (41%)
  starting transfers between devices  15.5 us (26%)
  Pallas kernels  10.5 us (17%)
  local copies, waits for them, and re-layouts  6.91 us (11%)
  other arithmetic  1.38 us (2%)
  between operations  0.77 us (1%)
    all_to_all x1, waiting for transfers between devices, shards(): lax.all_to_all(terms, ('dp', 'space'), 0, 0, axis_index_groups=groups, ti...  15 us
    all_to_all x1, starting transfers between devices, shards(): lax.all_to_all(terms, ('dp', 'space'), 0, 0, axis_index_groups=groups, ti...  6.65 us
    pallas_call x1, Pallas kernels, shards(): pl.pallas_call(input_kernel, out_shape=jax.ShapeDtypeStruct((rows, chans,...  4.42 us
    unnamed x14, local copies, waits for them, and re-layouts  4.35 us
    ppermute x1, waiting for transfers between devices, shards(): total = total + lax.ppermute(theirs, 'dp', moves).astype(F32)  3.75 us
    all_to_all x1, starting transfers between devices, shards(): lax.all_to_all(spread, 'space', 0, 0, axis_index_groups=inners, tiled=True)  3.63 us
    ppermute x1, waiting for transfers between devices, shards(): far_row = lax.ppermute(edge_half, 'space', inside(beyond_two))  3.05 us
    all_to_all x1, waiting for transfers between devices, shards(): lax.all_to_all(spread, 'space', 0, 0, axis_index_groups=inners, tiled=True)  2.78 us
  transfers between devices with their start and end apart: 7, of which 4 were waited for; matrix products, arithmetic and copies ran while one was open for 3% of the time, Pallas kernels for 10%

profile of v2, /device:TPU:0, one launch (start us, length us, event | category | flops | bytes accessed | tf_op | source)
XLA Modules:
  0.0 59.6 jit_solution(14634308006220438942)
XLA Ops:
  0.6 0.5 collective-permute-start
  1.1 0.1 collective-permute-start.2
  1.2 0.9 %dynamic-slice_bitcast_fusion = bf16[320,128]{1,0:T(8,128)(2,1)S(1)} fusion(bf16[1,8,128,320]{2,3,1,0:T(8,128)(2,1)} %param.4, s32[]{:T(128)S(6)} %select_n.23), kind=kLoop, calls=%fused_computation.5 | loop fusion | bytes 163844 | tf_op jit(solution)/shard_map/jit(dynamic_index_in_dim)/squeeze | solution.py:152
  2.1 0.7 %collective-permute-start.1 = (bf16[320,128]{1,0:T(8,128)(2,1)S(1)}, bf16[320,128]{1,0:T(8,128)(2,1)S(1)}, u32[]{:S(2)}, u32[]{:S(2)}) collective-permute-start(bf16[320,128]{1,0:T(8,128)(2,1)S(1)} %dynamic-slice_bitcast_fusion), channel_id=1, source_target_pairs={{1,2},{2,1},{3,4},{4,3},{5,6},{6,5},{9,10},{10,9},{11,12},{12,11},... | collective-permute-start | bytes 245768 | tf_op jit(solution)/shard_map/ppermute | solution.py:161
  2.8 0.8 %dynamic-slice_bitcast_fusion.1 = bf16[160,128]{1,0:T(8,128)(2,1)S(1)} fusion(bf16[1,8,128,320]{2,3,1,0:T(8,128)(2,1)} %param.4, s32[]{:T(128)S(6)} %select_n.24, s32[]{:T(128)S(6)} %select_n.26), kind=kLoop, calls=%fused_computation.7 | loop fusion | bytes 81928 | tf_op jit(solution)/shard_map/dynamic_slice | solution.py:153
  3.6 1.3 %collective-permute-start.3 = (bf16[160,128]{1,0:T(8,128)(2,1)S(1)}, bf16[160,128]{1,0:T(8,128)(2,1)S(1)}, u32[]{:S(2)}, u32[]{:S(2)}) collective-permute-start(bf16[160,128]{1,0:T(8,128)(2,1)S(1)} %dynamic-slice_bitcast_fusion.1), channel_id=1, source_target_pairs={{1,3},{2,0},{3,5},{4,2},{5,7},{6,4},{9,11},{10,8},{11,13},{12,10},... | collective-permute-start | bytes 122888 | tf_op jit(solution)/shard_map/ppermute | solution.py:162
  4.9 0.0 copy-start
  4.9 1.1 %copy-done = bf16[1,8,128,320]{2,3,1,0:T(8,128)(2,1)S(1)} copy-done((bf16[1,8,128,320]{2,3,1,0:T(8,128)(2,1)S(1)}, bf16[1,8,128,320]{2,3,1,0:T(8,128)(2,1)}, u32[]{:S(2)}) %copy-start) | copy-done | bytes 655384
  6.0 1.1 %copy-done.3 = bf16[1,8,128,320]{2,3,1,0:T(8,128)(2,1)S(1)} copy-done((bf16[1,8,128,320]{2,3,1,0:T(8,128)(2,1)S(1)}, bf16[1,8,128,320]{2,3,1,0:T(8,128)(2,1)}, u32[]{:S(2)}) %copy-start.3) | copy-done | bytes 655384
  7.1 1.5 %own_terms.1.term_ref = f32[3,320,512]{2,1,0:T(8,128)S(1)} custom-call(bf16[8,320,128]{2,1,0:T(8,128)(2,1)S(1)} %bitcast.36, bf16[8,320,128]{2,1,0:T(8,128)(2,1)S(1)} %bitcast.32), custom_call_target="tpu_custom_call" | custom-call | flops 1887436800 | bytes 4000000 | tf_op jit(solution)/shard_map/own_terms/pallas_call | solution.py:166
  8.6 3.1 %collective-permute-done.3.far_ref = bf16[160,128]{1,0:T(8,128)(2,1)S(1)} collective-permute-done((bf16[160,128]{1,0:T(8,128)(2,1)S(1)}, bf16[160,128]{1,0:T(8,128)(2,1)S(1)}, u32[]{:S(2)}, u32[]{:S(2)}) %collective-permute-start.3) | collective-permute-done | bytes 40992 | tf_op jit(solution)/shard_map/ppermute | solution.py:162
  11.7 2.7 %pair_terms.1 = bf16[2,4,2,3,80,128]{5,4,3,2,1,0:T(8,128)(2,1)} custom-call(f32[3,320,512]{2,1,0:T(8,128)S(1)} %own_terms.1.term_ref, bf16[8,320,128]{2,1,0:T(8,128)(2,1)S(1)} %bitcast.37, bf16[8,320,128]{2,1,0:T(8,128)(2,1)S(1)} %bitcast.33, bf16[8,320,128]{2,1,0:T(8,128)(2,1)S(1)} %collective-permute-done.2.their_pre_ref, ...), custom_call_target="tpu_custom_call" | custom-call | flops 1887436800 | bytes 4000000 | tf_op jit(solution)/shard_map/pair_terms/pallas_call | solution.py:179
  14.4 6.7 %all-to-all-start = ((bf16[8,2,3,80,128]{4,3,2,1,0:T(8,128)(2,1)}), bf16[8,2,3,80,128]{4,3,2,1,0:T(8,128)(2,1)}, u32[]{:S(2)}, u32[]{:S(2)}) async-start(bf16[8,2,3,80,128]{4,3,2,1,0:T(8,128)(2,1)} %bitcast.14), calls=%async_computation | async-start | bytes 1966080 | tf_op jit(solution)/shard_map/all_to_all | solution.py:211
  21.1 15.0 %all-to-all-done = bf16[8,2,3,80,128]{4,3,2,1,0:T(8,128)(2,1)} async-done(((bf16[8,2,3,80,128]{4,3,2,1,0:T(8,128)(2,1)}), bf16[8,2,3,80,128]{4,3,2,1,0:T(8,128)(2,1)}, u32[]{:S(2)}, u32[]{:S(2)}) %all-to-all-start) | async-done | bytes 983072 | tf_op jit(solution)/shard_map/all_to_all | solution.py:211
  36.0 1.4 %convert_reduce_fusion = f32[2,3,80,128]{3,2,1,0:T(8,128)S(1)} fusion(bf16[8,2,3,80,128]{4,3,2,1,0:T(8,128)(2,1)} %all-to-all-done), kind=kLoop, calls=%fused_computation | loop fusion | flops 921600 | bytes 1228800 | tf_op jit(solution)/shard_map/reduce_sum | solution.py:212
  37.4 2.7 %collective-permute-start.4 = (bf16[3,80,128]{2,1,0:T(8,128)(2,1)S(1)}, bf16[3,80,128]{2,1,0:T(8,128)(2,1)S(1)}, u32[]{:S(2)}, u32[]{:S(2)}) collective-permute-start(bf16[3,80,128]{2,1,0:T(8,128)(2,1)S(1)} %fusion.2), channel_id=1, source_target_pairs={{0,16},{8,24},{16,0},{24,8},{1,17},{9,25},{17,1},{25,9},{2,18},{10... | collective-permute-start | bytes 184328 | tf_op jit(solution)/shard_map/ppermute | solution.py:218
  40.1 3.7 %collective-permute-done.4 = bf16[3,80,128]{2,1,0:T(8,128)(2,1)S(1)} collective-permute-done((bf16[3,80,128]{2,1,0:T(8,128)(2,1)S(1)}, bf16[3,80,128]{2,1,0:T(8,128)(2,1)S(1)}, u32[]{:S(2)}, u32[]{:S(2)}) %collective-permute-start.4) | collective-permute-done | bytes 61472 | tf_op jit(solution)/shard_map/ppermute | solution.py:218
  43.8 0.8 %broadcast_in_dim.10 = bf16[8,3,80,128]{3,2,1,0:T(8,128)(2,1)} broadcast(bf16[3,80,128]{2,1,0:T(8,128)(2,1)S(1)} %fusion.1), dimensions={1,2,3} | broadcast | bytes 552960 | tf_op jit(solution)/shard_map/broadcast_in_dim | solution.py:223
  44.7 3.6 %all-to-all-start.1 = ((bf16[8,3,80,128]{3,2,1,0:T(8,128)(2,1)}), bf16[8,3,80,128]{3,2,1,0:T(8,128)(2,1)S(1)}, u32[]{:S(2)}, u32[]{:S(2)}) async-start(bf16[8,3,80,128]{3,2,1,0:T(8,128)(2,1)} %broadcast_in_dim.10), calls=%async_computation.1 | async-start | bytes 983040 | tf_op jit(solution)/shard_map/all_to_all | solution.py:224
  48.3 1.1 %copy-done.4 = bf16[1,8,128,320]{2,3,1,0:T(8,128)(2,1)S(1)} copy-done((bf16[1,8,128,320]{2,3,1,0:T(8,128)(2,1)S(1)}, bf16[1,8,128,320]{2,3,1,0:T(8,128)(2,1)}, u32[]{:S(2)}) %copy-start.4) | copy-done | bytes 655384
  49.4 1.1 %copy-done.6 = bf16[8,320,128]{2,1,0:T(8,128)(2,1)S(1)} copy-done((bf16[8,320,128]{2,1,0:T(8,128)(2,1)S(1)}, bf16[8,320,128]{2,1,0:T(8,128)(2,1)}, u32[]{:S(2)}) %copy-start.6) | copy-done | bytes 655384
  50.5 4.4 %input_grad.1 = bf16[8,320,128]{2,1,0:T(8,128)(2,1)} custom-call(bf16[8,320,128]{2,1,0:T(8,128)(2,1)S(1)} %bitcast.38, bf16[8,320,128]{2,1,0:T(8,128)(2,1)S(1)} %bitcast.34, bf16[8,320,128]{2,1,0:T(8,128)(2,1)S(1)} %copy-done.6, bf16[320,128]{1,0:T(8,128)(2,1)S(1)} %collective-permute-done.1.near_ref, bf16[3,3,320,320]{3,2,1,0:T(8,128)(2,1)S(1)} %copy-done.2), custom_call_target="tpu_custom_call" | custom-call | flops 1887436800 | bytes 4000000 | tf_op jit(solution)/shard_map/input_grad/pallas_call | solution.py:193
  54.9 2.8 %all-to-all-done.1.parts_ref = bf16[8,3,80,128]{3,2,1,0:T(8,128)(2,1)S(1)} async-done(((bf16[8,3,80,128]{3,2,1,0:T(8,128)(2,1)}), bf16[8,3,80,128]{3,2,1,0:T(8,128)(2,1)S(1)}, u32[]{:S(2)}, u32[]{:S(2)}) %all-to-all-start.1) | async-done | bytes 491552 | tf_op jit(solution)/shard_map/all_to_all | solution.py:224
  57.7 1.9 %place_rows.1 = f32[320,720]{1,0:T(8,128)} custom-call(bf16[8,3,80,128]{3,2,1,0:T(8,128)(2,1)S(1)} %all-to-all-done.1.parts_ref), custom_call_target="tpu_custom_call" | custom-call | flops 331776000 | bytes 2000000 | tf_op jit(solution)/shard_map/place_rows/pallas_call | solution.py:226
  (14 shorter events, 0.1 us)
Async XLA Ops:
  0.6 11.0 %collective-permute-start = (bf16[8,320,128]{2,1,0:T(8,128)(2,1)}, bf16[8,320,128]{2,1,0:T(8,128)(2,1)S(1)}, u32[]{:S(2)}, u32[]{:S(2)}) collective-permute-start(bf16[8,320,128]{2,1,0:T(8,128)(2,1)} %bitcast.31), channel_id=1, source_target_pairs={{0,1},{1,0},{2,3},{3,2},{4,5},{5,4},{6,7},{7,6},{8,9},{9,8},{10,11... | collective-permute-start | bytes 1966088 | tf_op jit(solution)/shard_map/ppermute | solution.py:163
  1.1 10.5 %collective-permute-start.2 = (bf16[8,320,128]{2,1,0:T(8,128)(2,1)}, bf16[8,320,128]{2,1,0:T(8,128)(2,1)S(1)}, u32[]{:S(2)}, u32[]{:S(2)}) collective-permute-start(bf16[8,320,128]{2,1,0:T(8,128)(2,1)} %bitcast.35), channel_id=1, source_target_pairs={{0,1},{1,0},{2,3},{3,2},{4,5},{5,4},{6,7},{7,6},{8,9},{9,8},{10,11... | collective-permute-start | bytes 1966088 | tf_op jit(solution)/shard_map/ppermute | solution.py:164
  2.1 9.5 %collective-permute-start.1 = (bf16[320,128]{1,0:T(8,128)(2,1)S(1)}, bf16[320,128]{1,0:T(8,128)(2,1)S(1)}, u32[]{:S(2)}, u32[]{:S(2)}) collective-permute-start(bf16[320,128]{1,0:T(8,128)(2,1)S(1)} %dynamic-slice_bitcast_fusion), channel_id=1, source_target_pairs={{1,2},{2,1},{3,4},{4,3},{5,6},{6,5},{9,10},{10,9},{11,12},{12,11},... | collective-permute-start | bytes 245768 | tf_op jit(solution)/shard_map/ppermute | solution.py:161
  3.6 8.1 %collective-permute-start.3 = (bf16[160,128]{1,0:T(8,128)(2,1)S(1)}, bf16[160,128]{1,0:T(8,128)(2,1)S(1)}, u32[]{:S(2)}, u32[]{:S(2)}) collective-permute-start(bf16[160,128]{1,0:T(8,128)(2,1)S(1)} %dynamic-slice_bitcast_fusion.1), channel_id=1, source_target_pairs={{1,3},{2,0},{3,5},{4,2},{5,7},{6,4},{9,11},{10,8},{11,13},{12,10},... | collective-permute-start | bytes 122888 | tf_op jit(solution)/shard_map/ppermute | solution.py:162
  4.9 1.1 %copy-start = (bf16[1,8,128,320]{2,3,1,0:T(8,128)(2,1)S(1)}, bf16[1,8,128,320]{2,3,1,0:T(8,128)(2,1)}, u32[]{:S(2)}) copy-start(bf16[1,8,128,320]{2,3,1,0:T(8,128)(2,1)} %param.4) | copy-start | bytes 1966084
  6.0 1.1 %copy-start.3 = (bf16[1,8,128,320]{2,3,1,0:T(8,128)(2,1)S(1)}, bf16[1,8,128,320]{2,3,1,0:T(8,128)(2,1)}, u32[]{:S(2)}) copy-start(bf16[1,8,128,320]{2,3,1,0:T(8,128)(2,1)} %param.3) | copy-start | bytes 1966084
  11.7 2.7 %copy-start.5 = (bf16[8,320,128]{2,1,0:T(8,128)(2,1)}, bf16[8,320,128]{2,1,0:T(8,128)(2,1)S(1)}, u32[]{:S(2)}) copy-start(bf16[8,320,128]{2,1,0:T(8,128)(2,1)S(1)} %collective-permute-done.their_grad_ref) | copy-start | bytes 1966084
  14.4 21.6 %all-to-all-start = ((bf16[8,2,3,80,128]{4,3,2,1,0:T(8,128)(2,1)}), bf16[8,2,3,80,128]{4,3,2,1,0:T(8,128)(2,1)}, u32[]{:S(2)}, u32[]{:S(2)}) async-start(bf16[8,2,3,80,128]{4,3,2,1,0:T(8,128)(2,1)} %bitcast.14), calls=%async_computation | async-start | bytes 1966080 | tf_op jit(solution)/shard_map/all_to_all | solution.py:211
  21.0 27.3 %copy-start.1 = (bf16[1,8,128,320]{2,3,1,0:T(8,128)(2,1)S(1)}, bf16[1,8,128,320]{2,3,1,0:T(8,128)(2,1)}, u32[]{:S(2)}) copy-start(bf16[1,8,128,320]{2,3,1,0:T(8,128)(2,1)} %param.4) | copy-start | bytes 1966084
  21.0 27.3 %copy-start.2 = (bf16[3,3,320,320]{3,2,1,0:T(8,128)(2,1)S(1)}, bf16[3,3,320,320]{3,2,1,0:T(8,128)(2,1)}, u32[]{:S(2)}) copy-start(bf16[3,3,320,320]{3,2,1,0:T(8,128)(2,1)} %kernel_ref.1) | copy-start | bytes 5529604
  37.4 6.4 %collective-permute-start.4 = (bf16[3,80,128]{2,1,0:T(8,128)(2,1)S(1)}, bf16[3,80,128]{2,1,0:T(8,128)(2,1)S(1)}, u32[]{:S(2)}, u32[]{:S(2)}) collective-permute-start(bf16[3,80,128]{2,1,0:T(8,128)(2,1)S(1)} %fusion.2), channel_id=1, source_target_pairs={{0,16},{8,24},{16,0},{24,8},{1,17},{9,25},{17,1},{25,9},{2,18},{10... | collective-permute-start | bytes 184328 | tf_op jit(solution)/shard_map/ppermute | solution.py:218
  44.7 13.0 %all-to-all-start.1 = ((bf16[8,3,80,128]{3,2,1,0:T(8,128)(2,1)}), bf16[8,3,80,128]{3,2,1,0:T(8,128)(2,1)S(1)}, u32[]{:S(2)}, u32[]{:S(2)}) async-start(bf16[8,3,80,128]{3,2,1,0:T(8,128)(2,1)} %broadcast_in_dim.10), calls=%async_computation.1 | async-start | bytes 983040 | tf_op jit(solution)/shard_map/all_to_all | solution.py:224
  48.3 1.1 %copy-start.4 = (bf16[1,8,128,320]{2,3,1,0:T(8,128)(2,1)S(1)}, bf16[1,8,128,320]{2,3,1,0:T(8,128)(2,1)}, u32[]{:S(2)}) copy-start(bf16[1,8,128,320]{2,3,1,0:T(8,128)(2,1)} %param.3) | copy-start | bytes 1966084
  49.4 1.1 %copy-start.6 = (bf16[8,320,128]{2,1,0:T(8,128)(2,1)S(1)}, bf16[8,320,128]{2,1,0:T(8,128)(2,1)}, u32[]{:S(2)}) copy-start(bf16[8,320,128]{2,1,0:T(8,128)(2,1)} %copy-done.5) | copy-start | bytes 1966084

commit v3 on v2

v3 whole, which is shorter than its diff:
```python
import jax
import jax.numpy as jnp
from jax import lax
from jax.experimental import pallas as pl
from jax.experimental.pallas import tpu as pltpu
from jax.sharding import PartitionSpec as P

F32 = jnp.float32
BF16 = jnp.bfloat16
LANES = 128
PAIR = 2
PLANE = 4
NEAR = 2
VMEM_LIMIT = 48 * 1024 * 1024
NT = (((1,), (1,)), ((), ()))


def vmem():
    return pl.BlockSpec(memory_space=pltpu.VMEM)


def anywhere():
    return pl.BlockSpec(memory_space=pltpu.HBM)


def column_shifts(row):
    wide = row.astype(F32)
    width = wide.shape[1]
    at = lax.broadcasted_iota(jnp.int32, wide.shape, 1)
    ahead = jnp.where(at == width - 1, 0.0, pltpu.roll(wide, width - 1, 1))
    behind = jnp.where(at == 0, 0.0, pltpu.roll(wide, 1, 1))
    return ahead.astype(BF16), row, behind.astype(BF16)


def put_taps(taps_s, slot, row):
    half, width = row.shape
    for b, shifted in enumerate(column_shifts(row)):
        taps_s[b * half : (b + 1) * half, slot * width : (slot + 1) * width] = shifted


def plane_index():
    return lax.rem(lax.axis_index("space") // PAIR, PLANE)


def near_index():
    return lax.rem(lax.axis_index("dp"), NEAR) * PLANE + plane_index()


def silu(v):
    x = v.astype(F32)
    return (x / (1.0 + jnp.exp(-x))).astype(BF16)


def my_core():
    return lax.rem(lax.axis_index("space"), PAIR)


def fetch(pairs, sem):
    copies = [pltpu.make_async_copy(src, dst, sem.at[i]) for i, (src, dst) in enumerate(pairs)]
    for copy in copies:
        copy.start()
    return copies


def own_kernel(pre_hbm, grad_hbm, term_ref, act_edge_ref, grad_edge_ref, pre_ref, grad_ref, act_s, taps_s, sem):
    rows, chans, width = pre_ref.shape
    half = chans // PAIR
    order = [(grad_hbm.at[r], grad_ref.at[r]) for r in range(rows)] + [(pre_hbm.at[r], pre_ref.at[r]) for r in range(rows)]
    copies = fetch(order, sem)
    mine = pl.ds(pl.multiple_of(my_core() * half, half), half)
    zero = jnp.zeros((half, width), BF16)
    taps_s[3 * half :, :] = jnp.zeros((taps_s.shape[0] - 3 * half, taps_s.shape[1]), BF16)
    put_taps(taps_s, 0, zero)
    put_taps(taps_s, rows + 1, zero)
    for r in range(rows):
        copies[r].wait()
        put_taps(taps_s, r + 1, grad_ref[r, mine, :])
    for r in range(rows):
        copies[rows + r].wait()
        act_s[:, r * width : (r + 1) * width] = silu(pre_ref[r])
    for i, r in enumerate((0, rows - 1)):
        act_edge_ref[i] = act_s[:, r * width : (r + 1) * width]
        grad_edge_ref[i] = grad_ref[r, mine, :]
    for a in range(3):
        at = (2 - a) * width
        term_ref[a] = lax.dot_general(act_s[...], taps_s[:, at : at + rows * width], NT, preferred_element_type=F32)


def pair_kernel(term_ref, act_edge_ref, grad_edge_ref, their_pre_ref, their_grad_ref, near_ref, far_ref, *refs):
    out_refs, (act_s, taps_s, term_s) = refs[: PLANE * NEAR], refs[PLANE * NEAR :]
    rows, chans, width = their_pre_ref.shape
    half = chans // PAIR
    outers, _, block, _ = out_refs[0].shape
    core = my_core()
    first = core == 0
    mine = pl.ds(pl.multiple_of(core * half, half), half)
    taps_s[3 * half :, :] = jnp.zeros((taps_s.shape[0] - 3 * half, taps_s.shape[1]), BF16)
    put_taps(taps_s, 0, jnp.where(first, near_ref[mine, :], their_grad_ref[rows - 1, mine, :]))
    put_taps(taps_s, 1, jnp.where(first, grad_edge_ref[1], far_ref[mine, :]))
    for r in range(rows):
        put_taps(taps_s, 2 + r, their_grad_ref[r, mine, :])
    put_taps(taps_s, rows + 2, jnp.where(first, far_ref[mine, :], grad_edge_ref[0]))
    put_taps(taps_s, rows + 3, jnp.where(first, their_grad_ref[0, mine, :], near_ref[mine, :]))
    act_s[:, :width] = act_edge_ref[0]
    for r in range(rows):
        act_s[:, (r + 1) * width : (r + 2) * width] = silu(their_pre_ref[r])
    act_s[:, (rows + 1) * width :] = act_edge_ref[1]
    for a, (left, right, at) in enumerate(((1, rows + 2, 3), (1, rows + 1, 2), (0, rows + 1, 0))):
        term = term_ref[a] + lax.dot_general(
            act_s[:, left * width : right * width],
            taps_s[:, at * width : (at + right - left) * width],
            NT,
            preferred_element_type=F32,
        )
        for p in range(PLANE):
            for z in range(NEAR * outers):
                term_s[z % NEAR * PLANE + p, z // NEAR, a] = term[
                    z * block : (z + 1) * block, p * LANES : (p + 1) * LANES
                ].astype(term_s.dtype)
    at, outer_at = near_index(), lax.axis_index("dp") // NEAR
    for k, out_ref in enumerate(out_refs):
        for j in range(outers):
            out_ref[j] = term_s[at ^ k, outer_at ^ j]


def input_kernel(pre_hbm, grad_hbm, their_grad_ref, near_ref, kernel_hbm, out_ref, pre_ref, grad_ref, kernel_ref, taps_s, sem):
    rows, chans, width = pre_ref.shape
    first = my_core() == 0
    order = [(grad_hbm.at[r], grad_ref.at[r]) for r in range(rows)]
    order += [(kernel_hbm.at[a], kernel_ref.at[a]) for a in range(3)]
    order += [(pre_hbm.at[r], pre_ref.at[r]) for r in range(rows)]
    copies = fetch(order, sem)
    for copy in copies:
        copy.wait()
    for r in range(rows + 2):
        if r == 0:
            row = jnp.where(first, near_ref[...], their_grad_ref[rows - 1])
        elif r == rows + 1:
            row = jnp.where(first, their_grad_ref[0], near_ref[...])
        else:
            row = grad_ref[r - 1]
        put_taps(taps_s, r, row)
    step = 2
    for top in range(0, rows, step):
        total = jnp.zeros((chans, step * width), F32)
        for a in range(3):
            at = (top + 2 - a) * width
            for b in range(3):
                taps = taps_s[b * chans : (b + 1) * chans, at : at + step * width]
                total += jnp.dot(kernel_ref[a, b], taps, preferred_element_type=F32)
        for r in range(step):
            x = pre_ref[top + r].astype(F32)
            sig = 1.0 / (1.0 + jnp.exp(-x))
            deriv = sig * (1.0 + x * (1.0 - sig))
            out_ref[top + r] = (total[:, r * width : (r + 1) * width] * deriv).astype(out_ref.dtype)


def place_kernel(*refs):
    parts, (out_ref, wide_s, rows_s) = refs[: PAIR * PLANE], refs[PAIR * PLANE :]
    _, block, _ = parts[0].shape
    chans = out_ref.shape[0]
    half = chans // PAIR
    core, at = my_core(), plane_index()
    for i, part in enumerate(parts):
        lanes = pl.ds(pl.multiple_of((at ^ (i % PLANE)) * LANES, LANES), LANES)
        wide_s[core ^ (i // PLANE), :, :, lanes] = part[...].astype(F32)
    for h in range(PAIR):
        for a in range(3):
            for b in range(3):
                t = 3 * a + b
                rows_s[t * block : (t + 1) * block, h * half : (h + 1) * half] = wide_s[h, a, :, b * half : (b + 1) * half]
    k = lax.broadcasted_iota(jnp.int32, (block, 9 * block), 0)
    j = lax.broadcasted_iota(jnp.int32, (block, 9 * block), 1)
    pick = jnp.concatenate([jnp.where(j - 9 * k == t, 1.0, 0.0) for t in range(9)], axis=0).astype(BF16)
    dims = (((0,), (0,)), ((), ()))
    out_ref[...] = lax.dot_general(rows_s[...].astype(BF16), pick, dims, preferred_element_type=F32)


def shards(pre_act, out_grad, kernel):
    images, rows, width, chans = pre_act.shape
    assert images == 1
    space, blocks = lax.axis_size("space"), lax.axis_size("dp")
    inner = PAIR * PLANE
    outer = space // inner
    block = chans // blocks
    half = chans // PAIR
    far = blocks // NEAR
    factor = float(images * rows * width * space * blocks) ** (-0.5)
    params = pltpu.CompilerParams(vmem_limit_bytes=VMEM_LIMIT)
    core = my_core()
    flops = 2 * 9 * chans * chans * rows * width

    pre = jnp.swapaxes(pre_act[0], 1, 2)
    grad = jnp.swapaxes(out_grad[0], 1, 2)
    edge = lax.dynamic_index_in_dim(grad, core * (rows - 1), 0, keepdims=False)
    beyond = [(i, i + 1 if i % 2 else i - 1) for i in range(space)]
    beyond_two = [(i, i + 2 if i % 2 else i - 2) for i in range(space)]
    pairs = [(i, i + 1 - 2 * (i % 2)) for i in range(space)]

    def inside(moves):
        return [(i, j) for i, j in moves if 0 <= j < space]

    near_row = lax.ppermute(edge, "space", inside(beyond))
    far_row = lax.ppermute(edge, "space", inside(beyond_two))
    their_grad = lax.ppermute(grad, "space", pairs)
    their_pre = lax.ppermute(pre, "space", pairs)

    row_block = pltpu.VMEM((rows, chans, width), BF16)
    own, act_edge, grad_edge = pl.pallas_call(
        own_kernel,
        out_shape=(
            jax.ShapeDtypeStruct((3, chans, PLANE * LANES), F32),
            jax.ShapeDtypeStruct((2, chans, width), BF16),
            jax.ShapeDtypeStruct((2, half, width), BF16),
        ),
        in_specs=[anywhere()] * 2,
        out_specs=(vmem(),) * 3,
        scratch_shapes=[
            row_block,
            row_block,
            pltpu.VMEM((chans, rows * width), BF16),
            pltpu.VMEM((PLANE * LANES, (rows + 2) * width), BF16),
            pltpu.SemaphoreType.DMA((2 * rows,)),
        ],
        compiler_params=params,
        cost_estimate=pl.CostEstimate(flops=flops, bytes_accessed=4000000, transcendentals=rows * width * chans),
        name="own_terms",
    )(pre, grad)
    piece = jax.ShapeDtypeStruct((far, 3, block, LANES), BF16)
    terms = pl.pallas_call(
        pair_kernel,
        out_shape=(piece,) * (NEAR * PLANE),
        in_specs=[vmem()] * 7,
        out_specs=(vmem(),) * (NEAR * PLANE),
        scratch_shapes=[
            pltpu.VMEM((chans, (rows + 2) * width), BF16),
            pltpu.VMEM((PLANE * LANES, (rows + 4) * width), BF16),
            pltpu.VMEM((NEAR * PLANE, far, 3, block, LANES), BF16),
        ],
        compiler_params=params,
        cost_estimate=pl.CostEstimate(flops=flops, bytes_accessed=4000000, transcendentals=rows * width * chans),
        name="pair_terms",
    )(own, act_edge, grad_edge, their_pre, their_grad, near_row, far_row)

    got = [terms[0]]
    for k in range(NEAR * PLANE - 1, 0, -1):
        moves = []
        for z in range(blocks):
            for i in range(space):
                to_z, to_i = z ^ (k // PLANE), i ^ (k % PLANE * PAIR)
                moves.append((z * space + i, to_z * space + to_i))
        got.append(lax.ppermute(terms[k], ("dp", "space"), moves))

    in_grad = pl.pallas_call(
        input_kernel,
        out_shape=jax.ShapeDtypeStruct((rows, chans, width), BF16),
        in_specs=[anywhere(), anywhere(), vmem(), vmem(), anywhere()],
        out_specs=vmem(),
        scratch_shapes=[
            row_block,
            row_block,
            pltpu.VMEM(kernel.shape, BF16),
            pltpu.VMEM((3 * chans, (rows + 2) * width), BF16),
            pltpu.SemaphoreType.DMA((2 * rows + 3,)),
        ],
        compiler_params=params,
        cost_estimate=pl.CostEstimate(flops=flops, bytes_accessed=4000000, transcendentals=rows * width * chans),
        name="input_grad",
    )(pre, grad, their_grad, near_row, kernel)
    *got, in_grad = lax.optimization_barrier((*got, in_grad))

    near_sum = sum(part.astype(F32) for part in got)
    total = near_sum[0]
    for k in range(1, far):
        moves = [(z, z ^ (k * NEAR)) for z in range(blocks)]
        total = total + lax.ppermute(near_sum[k].astype(BF16), "dp", moves).astype(F32)
    total = total * factor
    if outer > 1:
        total = lax.psum(total, "space", axis_index_groups=[[o * inner + i for o in range(outer)] for i in range(inner)])
    final = total.astype(BF16)
    parts = [final]
    for k in range(1, PLANE):
        parts.append(lax.ppermute(final, "space", [(i, i ^ (k * PAIR)) for i in range(space)]))
    parts += [lax.ppermute(part, "space", pairs) for part in parts]

    placed = pl.pallas_call(
        place_kernel,
        out_shape=jax.ShapeDtypeStruct((chans, 9 * block), F32),
        in_specs=[vmem()] * inner,
        out_specs=vmem(),
        scratch_shapes=[
            pltpu.VMEM((PAIR, 3, block, PLANE * LANES), F32),
            pltpu.VMEM((9 * block, chans), F32),
        ],
        compiler_params=params,
        cost_estimate=pl.CostEstimate(flops=2 * 81 * block * block * chans, bytes_accessed=2000000, transcendentals=0),
        name="place_rows",
    )(*parts)
    return jnp.swapaxes(in_grad, 1, 2)[None], placed.T


def solution(mesh):
    placed = (P("dp", "space", None, None), P("dp", "space", None, None), P())
    return jax.shard_map(
        shards,
        mesh=mesh,
        in_specs=placed,
        out_specs=(P("dp", "space", None, None), P("dp", None)),
        check_vma=False,
    )
```

time: 60.2 us -> 51.7 us (0.86)
  waiting for transfers between devices: 24.5 us -> 8.38 us
  starting transfers between devices: 15.5 us -> 23.7 us
  Pallas kernels: 10.5 us -> 15.4 us
  local copies, waits for them, and re-layouts: 6.91 us -> 3.09 us
  other arithmetic: 1.38 us -> 0.16 us
    ppermute x2 -> x16, starting transfers between devices: 3.95 us -> 22.4 us  [the longest x7 14.9 us: shards(): got.append(lax.ppermute(terms[k], ('dp', 'space'), moves))]
    all_to_all x2 -> x0, waiting for transfers between devices: 17.7 us -> none  [the longest x1 15 us: shards(): lax.all_to_all(terms, ('dp', 'space'), 0, 0, axis_index_groups=groups, ti...]
    all_to_all x2 -> x0, starting transfers between devices: 10.3 us -> none  [the longest x1 6.65 us: shards(): lax.all_to_all(terms, ('dp', 'space'), 0, 0, axis_index_groups=groups, ti...]
    pallas_call x1, Pallas kernels: 4.42 us -> 7.23 us  [shards(): pl.pallas_call(input_kernel, out_shape=jax.ShapeDtypeStruct((rows, chans,...]
    unnamed x14 -> x10, local copies, waits for them, and re-layouts: 4.35 us -> 2.19 us
    pallas_call x2, Pallas kernels: 4.2 us -> 6.13 us  [the longest x1 4.34 us: shards(): pl.pallas_call(own_kernel, out_shape=(jax.ShapeDtypeStruct((3, chans, PLA...]
    ppermute x2 -> x16, waiting for transfers between devices: 6.8 us -> 8.38 us  [the longest x3 3.94 us: shards(): lax.ppermute(final, 'space', [(i, i ^ k * PAIR) for i in range(space)])]
    reduce_sum x1 -> x0, other arithmetic: 1.36 us -> none  [shards(): near_sum = jnp.sum(got.astype(F32), axis=0)]
  transfers between devices with their start and end apart: 7 -> 19, of which waited for: 4 -> 6; matrix products, arithmetic and copies ran while one was open for 3% -> 2% of each run, Pallas kernels for 10% -> 22%
where the time goes in v3:
time: 51.7 us; the launch traced here: 51.5 us
  starting transfers between devices  23.7 us (46%)
  Pallas kernels  15.4 us (30%)
  waiting for transfers between devices  8.38 us (16%)
  local copies, waits for them, and re-layouts  3.09 us (6%)
  between operations  0.79 us (2%)
    ppermute x7, starting transfers between devices, shards(): got.append(lax.ppermute(terms[k], ('dp', 'space'), moves))  14.9 us
    pallas_call x1, Pallas kernels, shards(): pl.pallas_call(input_kernel, out_shape=jax.ShapeDtypeStruct((rows, chans,...  7.23 us
    pallas_call x1, Pallas kernels, shards(): pl.pallas_call(own_kernel, out_shape=(jax.ShapeDtypeStruct((3, chans, PLA...  4.34 us
    ppermute x3, waiting for transfers between devices, shards(): lax.ppermute(final, 'space', [(i, i ^ k * PAIR) for i in range(space)])  3.94 us
    ppermute x3, starting transfers between devices, shards(): lax.ppermute(final, 'space', [(i, i ^ k * PAIR) for i in range(space)])  3.55 us
    ppermute x1, starting transfers between devices, shards(): lax.ppermute(near_sum[k].astype(BF16), 'dp', moves).astype(F32)  2.66 us
    ppermute x1, waiting for transfers between devices, shards(): lax.ppermute(near_sum[k].astype(BF16), 'dp', moves).astype(F32)  2.53 us
    unnamed x10, local copies, waits for them, and re-layouts  2.19 us
  transfers between devices with their start and end apart: 19, of which 6 were waited for; matrix products, arithmetic and copies ran while one was open for 2% of the time, Pallas kernels for 22%

profile of v3, /device:TPU:0, one launch (start us, length us, event | category | flops | bytes accessed | tf_op | source)
XLA Modules:
  0.0 51.5 jit_solution(2847829341853172011)
XLA Ops:
  0.6 0.5 %collective-permute-start.1 = (bf16[8,320,128]{2,1,0:T(8,128)(2,1)}, bf16[8,320,128]{2,1,0:T(8,128)(2,1)S(1)}, u32[]{:S(2)}, u32[]{:S(2)}) collective-permute-start(bf16[8,320,128]{2,1,0:T(8,128)(2,1)} %bitcast.26), channel_id=1, source_target_pairs={{0,1},{1,0},{2,3},{3,2},{4,5},{5,4},{6,7},{7,6},{8,9},{9,8},{10,11... | collective-permute-start | bytes 1966088 | tf_op jit(solution)/shard_map/ppermute | solution.py:205
  1.2 0.9 %dynamic-slice_bitcast_fusion = bf16[320,128]{1,0:T(8,128)(2,1)S(1)} fusion(bf16[1,8,128,320]{2,3,1,0:T(8,128)(2,1)} %param.4, s32[]{:T(128)S(6)} %select_n.4), kind=kLoop, calls=%fused_computation.6 | loop fusion | bytes 163844 | tf_op jit(solution)/shard_map/jit(dynamic_index_in_dim)/squeeze | solution.py:195
  2.1 0.7 %collective-permute-start.2 = (bf16[320,128]{1,0:T(8,128)(2,1)S(1)}, bf16[320,128]{1,0:T(8,128)(2,1)S(1)}, u32[]{:S(2)}, u32[]{:S(2)}) collective-permute-start(bf16[320,128]{1,0:T(8,128)(2,1)S(1)} %dynamic-slice_bitcast_fusion), channel_id=1, source_target_pairs={{1,2},{2,1},{3,4},{4,3},{5,6},{6,5},{9,10},{10,9},{11,12},{12,11},... | collective-permute-start | bytes 245768 | tf_op jit(solution)/shard_map/ppermute | solution.py:203
  2.8 1.3 %collective-permute-start.3 = (bf16[320,128]{1,0:T(8,128)(2,1)S(1)}, bf16[320,128]{1,0:T(8,128)(2,1)S(1)}, u32[]{:S(2)}, u32[]{:S(2)}) collective-permute-start(bf16[320,128]{1,0:T(8,128)(2,1)S(1)} %dynamic-slice_bitcast_fusion), channel_id=1, source_target_pairs={{1,3},{2,0},{3,5},{4,2},{5,7},{6,4},{9,11},{10,8},{11,13},{12,10},... | collective-permute-start | bytes 245768 | tf_op jit(solution)/shard_map/ppermute | solution.py:204
  4.1 1.1 %copy-done = bf16[1,8,128,320]{2,3,1,0:T(8,128)(2,1)S(1)} copy-done((bf16[1,8,128,320]{2,3,1,0:T(8,128)(2,1)S(1)}, bf16[1,8,128,320]{2,3,1,0:T(8,128)(2,1)}, u32[]{:S(2)}) %copy-start) | copy-done | bytes 655384
  5.2 1.1 %copy-done.3 = bf16[1,8,128,320]{2,3,1,0:T(8,128)(2,1)S(1)} copy-done((bf16[1,8,128,320]{2,3,1,0:T(8,128)(2,1)S(1)}, bf16[1,8,128,320]{2,3,1,0:T(8,128)(2,1)}, u32[]{:S(2)}) %copy-start.3) | copy-done | bytes 655384
  6.3 4.3 %own_terms.1 = (f32[3,320,512]{2,1,0:T(8,128)S(1)}, bf16[2,320,128]{2,1,0:T(8,128)(2,1)S(1)}, bf16[2,160,128]{2,1,0:T(8,128)(2,1)S(1)}) custom-call(bf16[8,320,128]{2,1,0:T(8,128)(2,1)S(1)} %bitcast.30, bf16[8,320,128]{2,1,0:T(8,128)(2,1)S(1)} %bitcast.27), custom_call_target="tpu_custom_call" | custom-call | flops 1887436800 | bytes 4000000 | tf_op jit(solution)/shard_map/own_terms/pallas_call | solution.py:209
  10.6 0.7 %collective-permute-done.3.far_ref = bf16[320,128]{1,0:T(8,128)(2,1)S(1)} collective-permute-done((bf16[320,128]{1,0:T(8,128)(2,1)S(1)}, bf16[320,128]{1,0:T(8,128)(2,1)S(1)}, u32[]{:S(2)}, u32[]{:S(2)}) %collective-permute-start.3) | collective-permute-done | bytes 81952 | tf_op jit(solution)/shard_map/ppermute | solution.py:204
  11.3 1.8 %pair_terms.1 = (bf16[2,3,80,128]{3,2,1,0:T(8,128)(2,1)S(1)}, bf16[2,3,80,128]{3,2,1,0:T(8,128)(2,1)S(1)}, bf16[2,3,80,128]{3,2,1,0:T(8,128)(2,1)S(1)}, bf16[2,3...) custom-call(f32[3,320,512]{2,1,0:T(8,128)S(1)} %get-tuple-element.22, ...), custom_call_target="tpu_custom_call" | custom-call | flops 1887436800 | bytes 4000000 | tf_op jit(solution)/shard_map/pair_terms/pallas_call | solution.py:230
  13.1 4.2 %collective-permute-start.10 = (bf16[2,3,80,128]{3,2,1,0:T(8,128)(2,1)S(1)}, bf16[2,3,80,128]{3,2,1,0:T(8,128)(2,1)S(1)}, u32[]{:S(2)}, u32[]{:S(2)}) collective-permute-start(bf16[2,3,80,128]{3,2,1,0:T(8,128)(2,1)S(1)} %get-tuple-element.32), channel_id=1, source_target_pairs={{0,2},{1,3},{2,0},{3,1},{4,6},{5,7},{6,4},{7,5},{8,10},{9,11},{10,... | collective-permute-start | bytes 368648 | tf_op jit(solution)/shard_map/ppermute | solution.py:252
  17.3 4.1 %collective-permute-start.4 = (bf16[2,3,80,128]{3,2,1,0:T(8,128)(2,1)S(1)}, bf16[2,3,80,128]{3,2,1,0:T(8,128)(2,1)S(1)}, u32[]{:S(2)}, u32[]{:S(2)}) collective-permute-start(bf16[2,3,80,128]{3,2,1,0:T(8,128)(2,1)S(1)} %get-tuple-element.26), channel_id=1, source_target_pairs={{0,14},{1,15},{2,12},{3,13},{4,10},{5,11},{6,8},{7,9},{8,6},{9,7},... | collective-permute-start | bytes 368648 | tf_op jit(solution)/shard_map/ppermute | solution.py:252
  21.5 1.4 %collective-permute-start.6 = (bf16[2,3,80,128]{3,2,1,0:T(8,128)(2,1)S(1)}, bf16[2,3,80,128]{3,2,1,0:T(8,128)(2,1)S(1)}, u32[]{:S(2)}, u32[]{:S(2)}) collective-permute-start(bf16[2,3,80,128]{3,2,1,0:T(8,128)(2,1)S(1)} %get-tuple-element.28), channel_id=1, source_target_pairs={{0,10},{1,11},{2,8},{3,9},{4,14},{5,15},{6,12},{7,13},{8,2},{9,3},... | collective-permute-start | bytes 368648 | tf_op jit(solution)/shard_map/ppermute | solution.py:252
  23.0 1.5 %collective-permute-start.7 = (bf16[2,3,80,128]{3,2,1,0:T(8,128)(2,1)S(1)}, bf16[2,3,80,128]{3,2,1,0:T(8,128)(2,1)S(1)}, u32[]{:S(2)}, u32[]{:S(2)}) collective-permute-start(bf16[2,3,80,128]{3,2,1,0:T(8,128)(2,1)S(1)} %get-tuple-element.29), channel_id=1, source_target_pairs={{0,8},{1,9},{2,10},{3,11},{4,12},{5,13},{6,14},{7,15},{8,0},{9,1},... | collective-permute-start | bytes 368648 | tf_op jit(solution)/shard_map/ppermute | solution.py:252
  24.4 3.0 %collective-permute-start.8 = (bf16[2,3,80,128]{3,2,1,0:T(8,128)(2,1)S(1)}, bf16[2,3,80,128]{3,2,1,0:T(8,128)(2,1)S(1)}, u32[]{:S(2)}, u32[]{:S(2)}) collective-permute-start(bf16[2,3,80,128]{3,2,1,0:T(8,128)(2,1)S(1)} %get-tuple-element.30), channel_id=1, source_target_pairs={{0,6},{1,7},{2,4},{3,5},{4,2},{5,3},{6,0},{7,1},{8,14},{9,15},{10,... | collective-permute-start | bytes 368648 | tf_op jit(solution)/shard_map/ppermute | solution.py:252
  27.4 0.6 %collective-permute-start.9 = (bf16[2,3,80,128]{3,2,1,0:T(8,128)(2,1)S(1)}, bf16[2,3,80,128]{3,2,1,0:T(8,128)(2,1)S(1)}, u32[]{:S(2)}, u32[]{:S(2)}) collective-permute-start(bf16[2,3,80,128]{3,2,1,0:T(8,128)(2,1)S(1)} %get-tuple-element.31), channel_id=1, source_target_pairs={{0,4},{1,5},{2,6},{3,7},{4,0},{5,1},{6,2},{7,3},{8,12},{9,13},{10,... | collective-permute-start | bytes 368648 | tf_op jit(solution)/shard_map/ppermute | solution.py:252
  28.0 7.2 %input_grad.1 = bf16[8,320,128]{2,1,0:T(8,128)(2,1)} custom-call(bf16[8,320,128]{2,1,0:T(8,128)(2,1)S(1)} %bitcast.31, bf16[8,320,128]{2,1,0:T(8,128)(2,1)S(1)} %bitcast.28, bf16[8,320,128]{2,1,0:T(8,128)(2,1)S(1)} %collective-permute-done.1.their_grad_ref, bf16[320,128]{1,0:T(8,128)(2,1)S(1)} %collective-permute-done.2.near_ref, ...), custom_call_target="tpu_custom_call" | custom-call | flops 1887436800 | bytes 4000000 | tf_op jit(solution)/shard_map/input_grad/pallas_call | solution.py:254
  35.5 2.7 %collective-permute-start.11 = (bf16[3,80,128]{2,1,0:T(8,128)(2,1)S(1)}, bf16[3,80,128]{2,1,0:T(8,128)(2,1)S(1)}, u32[]{:S(2)}, u32[]{:S(2)}) collective-permute-start(bf16[3,80,128]{2,1,0:T(8,128)(2,1)S(1)} %fusion.3), channel_id=1, source_target_pairs={{0,16},{8,24},{16,0},{24,8},{1,17},{9,25},{17,1},{25,9},{2,18},{10... | collective-permute-start | bytes 184328 | tf_op jit(solution)/shard_map/ppermute | solution.py:276
  38.1 2.5 %collective-permute-done.11 = bf16[3,80,128]{2,1,0:T(8,128)(2,1)S(1)} collective-permute-done((bf16[3,80,128]{2,1,0:T(8,128)(2,1)S(1)}, bf16[3,80,128]{2,1,0:T(8,128)(2,1)S(1)}, u32[]{:S(2)}, u32[]{:S(2)}) %collective-permute-start.11) | collective-permute-done | bytes 61472 | tf_op jit(solution)/shard_map/ppermute | solution.py:276
  41.1 1.9 %collective-permute-start.13 = (bf16[3,80,128]{2,1,0:T(8,128)(2,1)S(1)}, bf16[3,80,128]{2,1,0:T(8,128)(2,1)S(1)}, u32[]{:S(2)}, u32[]{:S(2)}) collective-permute-start(bf16[3,80,128]{2,1,0:T(8,128)(2,1)S(1)} %fusion.2.refs_0_), channel_id=1, source_target_pairs={{0,4},{1,5},{2,6},{3,7},{4,0},{5,1},{6,2},{7,3},{8,12},{9,13},{10,... | collective-permute-start | bytes 184328 | tf_op jit(solution)/shard_map/ppermute | solution.py:283
  43.1 1.2 %collective-permute-start.14 = (bf16[3,80,128]{2,1,0:T(8,128)(2,1)S(1)}, bf16[3,80,128]{2,1,0:T(8,128)(2,1)S(1)}, u32[]{:S(2)}, u32[]{:S(2)}) collective-permute-start(bf16[3,80,128]{2,1,0:T(8,128)(2,1)S(1)} %fusion.2.refs_0_), channel_id=1, source_target_pairs={{0,6},{1,7},{2,4},{3,5},{4,2},{5,3},{6,0},{7,1},{8,14},{9,15},{10,... | collective-permute-start | bytes 184328 | tf_op jit(solution)/shard_map/ppermute | solution.py:283
  44.2 0.8 %collective-permute-done.12.refs_1_ = bf16[3,80,128]{2,1,0:T(8,128)(2,1)S(1)} collective-permute-done((bf16[3,80,128]{2,1,0:T(8,128)(2,1)S(1)}, bf16[3,80,128]{2,1,0:T(8,128)(2,1)S(1)}, u32[]{:S(2)}, u32[]{:S(2)}) %collective-permute-start.12) | collective-permute-done | bytes 61472 | tf_op jit(solution)/shard_map/ppermute | solution.py:283
  45.6 2.6 %collective-permute-done.14.refs_3_ = bf16[3,80,128]{2,1,0:T(8,128)(2,1)S(1)} collective-permute-done((bf16[3,80,128]{2,1,0:T(8,128)(2,1)S(1)}, bf16[3,80,128]{2,1,0:T(8,128)(2,1)S(1)}, u32[]{:S(2)}, u32[]{:S(2)}) %collective-permute-start.14) | collective-permute-done | bytes 61472 | tf_op jit(solution)/shard_map/ppermute | solution.py:283
  48.2 1.2 %collective-permute-done.18.refs_7_ = bf16[3,80,128]{2,1,0:T(8,128)(2,1)S(1)} collective-permute-done((bf16[3,80,128]{2,1,0:T(8,128)(2,1)S(1)}, bf16[3,80,128]{2,1,0:T(8,128)(2,1)S(1)}, u32[]{:S(2)}, u32[]{:S(2)}) %collective-permute-start.18) | collective-permute-done | bytes 61472 | tf_op jit(solution)/shard_map/ppermute | solution.py:284
  49.4 2.0 %place_rows.1 = f32[320,720]{1,0:T(8,128)} custom-call(bf16[3,80,128]{2,1,0:T(8,128)(2,1)S(1)} %fusion.2.refs_0_, bf16[3,80,128]{2,1,0:T(8,128)(2,1)S(1)} %collective-permute-done.12.refs_1_, bf16[3,80,128]{2,1,0:T(8,128)(2,1)S(1)} %collective-permute-done.13.refs_2_, bf16[3,80,128]{2,1,0:T(8,128)(2,1)S(1)} %collective-permute-done.14.refs_3_, ...), custom_call_target="tpu_custom_call" | custom-call | flops 331776000 | bytes 2000000 | tf_op jit(solution)/shard_map/place_rows/pallas_call | solution.py:286
  (32 shorter events, 1.3 us)
Async XLA Ops:
  0.6 10.6 %collective-permute-start.1 = (bf16[8,320,128]{2,1,0:T(8,128)(2,1)}, bf16[8,320,128]{2,1,0:T(8,128)(2,1)S(1)}, u32[]{:S(2)}, u32[]{:S(2)}) collective-permute-start(bf16[8,320,128]{2,1,0:T(8,128)(2,1)} %bitcast.26), channel_id=1, source_target_pairs={{0,1},{1,0},{2,3},{3,2},{4,5},{5,4},{6,7},{7,6},{8,9},{9,8},{10,11... | collective-permute-start | bytes 1966088 | tf_op jit(solution)/shard_map/ppermute | solution.py:205
  1.1 10.1 %collective-permute-start = (bf16[8,320,128]{2,1,0:T(8,128)(2,1)}, bf16[8,320,128]{2,1,0:T(8,128)(2,1)S(1)}, u32[]{:S(2)}, u32[]{:S(2)}) collective-permute-start(bf16[8,320,128]{2,1,0:T(8,128)(2,1)} %bitcast.29), channel_id=1, source_target_pairs={{0,1},{1,0},{2,3},{3,2},{4,5},{5,4},{6,7},{7,6},{8,9},{9,8},{10,11... | collective-permute-start | bytes 1966088 | tf_op jit(solution)/shard_map/ppermute | solution.py:206
  2.1 8.5 %collective-permute-start.2 = (bf16[320,128]{1,0:T(8,128)(2,1)S(1)}, bf16[320,128]{1,0:T(8,128)(2,1)S(1)}, u32[]{:S(2)}, u32[]{:S(2)}) collective-permute-start(bf16[320,128]{1,0:T(8,128)(2,1)S(1)} %dynamic-slice_bitcast_fusion), channel_id=1, source_target_pairs={{1,2},{2,1},{3,4},{4,3},{5,6},{6,5},{9,10},{10,9},{11,12},{12,11},... | collective-permute-start | bytes 245768 | tf_op jit(solution)/shard_map/ppermute | solution.py:203
  2.8 8.5 %collective-permute-start.3 = (bf16[320,128]{1,0:T(8,128)(2,1)S(1)}, bf16[320,128]{1,0:T(8,128)(2,1)S(1)}, u32[]{:S(2)}, u32[]{:S(2)}) collective-permute-start(bf16[320,128]{1,0:T(8,128)(2,1)S(1)} %dynamic-slice_bitcast_fusion), channel_id=1, source_target_pairs={{1,3},{2,0},{3,5},{4,2},{5,7},{6,4},{9,11},{10,8},{11,13},{12,10},... | collective-permute-start | bytes 245768 | tf_op jit(solution)/shard_map/ppermute | solution.py:204
  4.1 1.1 %copy-start = (bf16[1,8,128,320]{2,3,1,0:T(8,128)(2,1)S(1)}, bf16[1,8,128,320]{2,3,1,0:T(8,128)(2,1)}, u32[]{:S(2)}) copy-start(bf16[1,8,128,320]{2,3,1,0:T(8,128)(2,1)} %param.4) | copy-start | bytes 1966084
  5.2 1.1 %copy-start.3 = (bf16[1,8,128,320]{2,3,1,0:T(8,128)(2,1)S(1)}, bf16[1,8,128,320]{2,3,1,0:T(8,128)(2,1)}, u32[]{:S(2)}) copy-start(bf16[1,8,128,320]{2,3,1,0:T(8,128)(2,1)} %param.3) | copy-start | bytes 1966084
  11.3 16.7 %copy-start.1 = (bf16[1,8,128,320]{2,3,1,0:T(8,128)(2,1)S(1)}, bf16[1,8,128,320]{2,3,1,0:T(8,128)(2,1)}, u32[]{:S(2)}) copy-start(bf16[1,8,128,320]{2,3,1,0:T(8,128)(2,1)} %param.4) | copy-start | bytes 1966084
  11.3 16.7 %copy-start.2 = (bf16[3,3,320,320]{3,2,1,0:T(8,128)(2,1)S(1)}, bf16[3,3,320,320]{3,2,1,0:T(8,128)(2,1)}, u32[]{:S(2)}) copy-start(bf16[3,3,320,320]{3,2,1,0:T(8,128)(2,1)} %kernel_hbm.1) | copy-start | bytes 5529604
  11.3 16.7 %copy-start.4 = (bf16[1,8,128,320]{2,3,1,0:T(8,128)(2,1)S(1)}, bf16[1,8,128,320]{2,3,1,0:T(8,128)(2,1)}, u32[]{:S(2)}) copy-start(bf16[1,8,128,320]{2,3,1,0:T(8,128)(2,1)} %param.3) | copy-start | bytes 1966084
  13.1 11.3 %collective-permute-start.10 = (bf16[2,3,80,128]{3,2,1,0:T(8,128)(2,1)S(1)}, bf16[2,3,80,128]{3,2,1,0:T(8,128)(2,1)S(1)}, u32[]{:S(2)}, u32[]{:S(2)}) collective-permute-start(bf16[2,3,80,128]{3,2,1,0:T(8,128)(2,1)S(1)} %get-tuple-element.32), channel_id=1, source_target_pairs={{0,2},{1,3},{2,0},{3,1},{4,6},{5,7},{6,4},{7,5},{8,10},{9,11},{10,... | collective-permute-start | bytes 368648 | tf_op jit(solution)/shard_map/ppermute | solution.py:252
  17.3 10.1 %collective-permute-start.4 = (bf16[2,3,80,128]{3,2,1,0:T(8,128)(2,1)S(1)}, bf16[2,3,80,128]{3,2,1,0:T(8,128)(2,1)S(1)}, u32[]{:S(2)}, u32[]{:S(2)}) collective-permute-start(bf16[2,3,80,128]{3,2,1,0:T(8,128)(2,1)S(1)} %get-tuple-element.26), channel_id=1, source_target_pairs={{0,14},{1,15},{2,12},{3,13},{4,10},{5,11},{6,8},{7,9},{8,6},{9,7},... | collective-permute-start | bytes 368648 | tf_op jit(solution)/shard_map/ppermute | solution.py:252
  21.5 13.8 %collective-permute-start.5 = (bf16[2,3,80,128]{3,2,1,0:T(8,128)(2,1)S(1)}, bf16[2,3,80,128]{3,2,1,0:T(8,128)(2,1)S(1)}, u32[]{:S(2)}, u32[]{:S(2)}) collective-permute-start(bf16[2,3,80,128]{3,2,1,0:T(8,128)(2,1)S(1)} %get-tuple-element.27), channel_id=1, source_target_pairs={{0,12},{1,13},{2,14},{3,15},{4,8},{5,9},{6,10},{7,11},{8,4},{9,5},... | collective-permute-start | bytes 368648 | tf_op jit(solution)/shard_map/ppermute | solution.py:252
  21.5 13.8 %collective-permute-start.6 = (bf16[2,3,80,128]{3,2,1,0:T(8,128)(2,1)S(1)}, bf16[2,3,80,128]{3,2,1,0:T(8,128)(2,1)S(1)}, u32[]{:S(2)}, u32[]{:S(2)}) collective-permute-start(bf16[2,3,80,128]{3,2,1,0:T(8,128)(2,1)S(1)} %get-tuple-element.28), channel_id=1, source_target_pairs={{0,10},{1,11},{2,8},{3,9},{4,14},{5,15},{6,12},{7,13},{8,2},{9,3},... | collective-permute-start | bytes 368648 | tf_op jit(solution)/shard_map/ppermute | solution.py:252
  23.0 12.3 %collective-permute-start.7 = (bf16[2,3,80,128]{3,2,1,0:T(8,128)(2,1)S(1)}, bf16[2,3,80,128]{3,2,1,0:T(8,128)(2,1)S(1)}, u32[]{:S(2)}, u32[]{:S(2)}) collective-permute-start(bf16[2,3,80,128]{3,2,1,0:T(8,128)(2,1)S(1)} %get-tuple-element.29), channel_id=1, source_target_pairs={{0,8},{1,9},{2,10},{3,11},{4,12},{5,13},{6,14},{7,15},{8,0},{9,1},... | collective-permute-start | bytes 368648 | tf_op jit(solution)/shard_map/ppermute | solution.py:252
  24.4 10.9 %collective-permute-start.8 = (bf16[2,3,80,128]{3,2,1,0:T(8,128)(2,1)S(1)}, bf16[2,3,80,128]{3,2,1,0:T(8,128)(2,1)S(1)}, u32[]{:S(2)}, u32[]{:S(2)}) collective-permute-start(bf16[2,3,80,128]{3,2,1,0:T(8,128)(2,1)S(1)} %get-tuple-element.30), channel_id=1, source_target_pairs={{0,6},{1,7},{2,4},{3,5},{4,2},{5,3},{6,0},{7,1},{8,14},{9,15},{10,... | collective-permute-start | bytes 368648 | tf_op jit(solution)/shard_map/ppermute | solution.py:252
  27.4 7.9 %collective-permute-start.9 = (bf16[2,3,80,128]{3,2,1,0:T(8,128)(2,1)S(1)}, bf16[2,3,80,128]{3,2,1,0:T(8,128)(2,1)S(1)}, u32[]{:S(2)}, u32[]{:S(2)}) collective-permute-start(bf16[2,3,80,128]{3,2,1,0:T(8,128)(2,1)S(1)} %get-tuple-element.31), channel_id=1, source_target_pairs={{0,4},{1,5},{2,6},{3,7},{4,0},{5,1},{6,2},{7,3},{8,12},{9,13},{10,... | collective-permute-start | bytes 368648 | tf_op jit(solution)/shard_map/ppermute | solution.py:252
  35.5 5.2 %collective-permute-start.11 = (bf16[3,80,128]{2,1,0:T(8,128)(2,1)S(1)}, bf16[3,80,128]{2,1,0:T(8,128)(2,1)S(1)}, u32[]{:S(2)}, u32[]{:S(2)}) collective-permute-start(bf16[3,80,128]{2,1,0:T(8,128)(2,1)S(1)} %fusion.3), channel_id=1, source_target_pairs={{0,16},{8,24},{16,0},{24,8},{1,17},{9,25},{17,1},{25,9},{2,18},{10... | collective-permute-start | bytes 184328 | tf_op jit(solution)/shard_map/ppermute | solution.py:276
  40.7 4.4 %collective-permute-start.12 = (bf16[3,80,128]{2,1,0:T(8,128)(2,1)S(1)}, bf16[3,80,128]{2,1,0:T(8,128)(2,1)S(1)}, u32[]{:S(2)}, u32[]{:S(2)}) collective-permute-start(bf16[3,80,128]{2,1,0:T(8,128)(2,1)S(1)} %fusion.2.refs_0_), channel_id=1, source_target_pairs={{0,2},{1,3},{2,0},{3,1},{4,6},{5,7},{6,4},{7,5},{8,10},{9,11},{10,... | collective-permute-start | bytes 184328 | tf_op jit(solution)/shard_map/ppermute | solution.py:283
  41.1 4.5 %collective-permute-start.13 = (bf16[3,80,128]{2,1,0:T(8,128)(2,1)S(1)}, bf16[3,80,128]{2,1,0:T(8,128)(2,1)S(1)}, u32[]{:S(2)}, u32[]{:S(2)}) collective-permute-start(bf16[3,80,128]{2,1,0:T(8,128)(2,1)S(1)} %fusion.2.refs_0_), channel_id=1, source_target_pairs={{0,4},{1,5},{2,6},{3,7},{4,0},{5,1},{6,2},{7,3},{8,12},{9,13},{10,... | collective-permute-start | bytes 184328 | tf_op jit(solution)/shard_map/ppermute | solution.py:283
  43.1 5.1 %collective-permute-start.14 = (bf16[3,80,128]{2,1,0:T(8,128)(2,1)S(1)}, bf16[3,80,128]{2,1,0:T(8,128)(2,1)S(1)}, u32[]{:S(2)}, u32[]{:S(2)}) collective-permute-start(bf16[3,80,128]{2,1,0:T(8,128)(2,1)S(1)} %fusion.2.refs_0_), channel_id=1, source_target_pairs={{0,6},{1,7},{2,4},{3,5},{4,2},{5,3},{6,0},{7,1},{8,14},{9,15},{10,... | collective-permute-start | bytes 184328 | tf_op jit(solution)/shard_map/ppermute | solution.py:283
  44.2 4.0 %collective-permute-start.15 = (bf16[3,80,128]{2,1,0:T(8,128)(2,1)S(1)}, bf16[3,80,128]{2,1,0:T(8,128)(2,1)S(1)}, u32[]{:S(2)}, u32[]{:S(2)}) collective-permute-start(bf16[3,80,128]{2,1,0:T(8,128)(2,1)S(1)} %fusion.2.refs_0_), channel_id=1, source_target_pairs={{0,1},{1,0},{2,3},{3,2},{4,5},{5,4},{6,7},{7,6},{8,9},{9,8},{10,11... | collective-permute-start | bytes 184328 | tf_op jit(solution)/shard_map/ppermute | solution.py:284
  45.1 3.1 %collective-permute-start.16 = (bf16[3,80,128]{2,1,0:T(8,128)(2,1)S(1)}, bf16[3,80,128]{2,1,0:T(8,128)(2,1)S(1)}, u32[]{:S(2)}, u32[]{:S(2)}) collective-permute-start(bf16[3,80,128]{2,1,0:T(8,128)(2,1)S(1)} %collective-permute-done.12.refs_1_), channel_id=1, source_target_pairs={{0,1},{1,0},{2,3},{3,2},{4,5},{5,4},{6,7},{7,6},{8,9},{9,8},{10,11... | collective-permute-start | bytes 184328 | tf_op jit(solution)/shard_map/ppermute | solution.py:284
  45.6 2.6 %collective-permute-start.17 = (bf16[3,80,128]{2,1,0:T(8,128)(2,1)S(1)}, bf16[3,80,128]{2,1,0:T(8,128)(2,1)S(1)}, u32[]{:S(2)}, u32[]{:S(2)}) collective-permute-start(bf16[3,80,128]{2,1,0:T(8,128)(2,1)S(1)} %collective-permute-done.13.refs_2_), channel_id=1, source_target_pairs={{0,1},{1,0},{2,3},{3,2},{4,5},{5,4},{6,7},{7,6},{8,9},{9,8},{10,11... | collective-permute-start | bytes 184328 | tf_op jit(solution)/shard_map/ppermute | solution.py:284
  48.2 1.2 %collective-permute-start.18 = (bf16[3,80,128]{2,1,0:T(8,128)(2,1)S(1)}, bf16[3,80,128]{2,1,0:T(8,128)(2,1)S(1)}, u32[]{:S(2)}, u32[]{:S(2)}) collective-permute-start(bf16[3,80,128]{2,1,0:T(8,128)(2,1)S(1)} %collective-permute-done.14.refs_3_), channel_id=1, source_target_pairs={{0,1},{1,0},{2,3},{3,2},{4,5},{5,4},{6,7},{7,6},{8,9},{9,8},{10,11... | collective-permute-start | bytes 184328 | tf_op jit(solution)/shard_map/ppermute | solution.py:284

commit v4 on v3

v4 whole, which is shorter than its diff:
```python
import functools

import jax
import jax.numpy as jnp
from jax import lax
from jax.experimental import pallas as pl
from jax.experimental.pallas import tpu as pltpu
from jax.sharding import PartitionSpec as P

F32 = jnp.float32
BF16 = jnp.bfloat16
LANES = 128
PAIR = 2
PLANE = 4
NEAR = 2
VMEM_LIMIT = 48 * 1024 * 1024
NT = (((1,), (1,)), ((), ()))


def vmem():
    return pl.BlockSpec(memory_space=pltpu.VMEM)


def anywhere():
    return pl.BlockSpec(memory_space=pl.ANY)


def column_shifts(row):
    wide = row.astype(F32)
    width = wide.shape[1]
    at = lax.broadcasted_iota(jnp.int32, wide.shape, 1)
    ahead = jnp.where(at == width - 1, 0.0, pltpu.roll(wide, width - 1, 1))
    behind = jnp.where(at == 0, 0.0, pltpu.roll(wide, 1, 1))
    return ahead.astype(BF16), row, behind.astype(BF16)


def put_taps(taps_s, slot, row):
    half, width = row.shape
    for b, shifted in enumerate(column_shifts(row)):
        taps_s[b * half : (b + 1) * half, slot * width : (slot + 1) * width] = shifted


def plane_index():
    return lax.rem(lax.axis_index("space") // PAIR, PLANE)


def near_index():
    return lax.rem(lax.axis_index("dp"), NEAR) * PLANE + plane_index()


def silu(v):
    x = v.astype(F32)
    return (x / (1.0 + jnp.exp(-x))).astype(BF16)


def my_core():
    return lax.rem(lax.axis_index("space"), PAIR)


def edge_kernel(pre_ref, grad_ref, out_ref):
    row = my_core() * (pre_ref.shape[0] - 1)
    out_ref[0] = grad_ref[row]
    out_ref[1] = pre_ref[row]


def own_kernel(pre_ref, grad_ref, term_ref, act_edge_ref, grad_edge_ref, act_s, taps_s):
    rows, chans, width = pre_ref.shape
    half = chans // PAIR
    mine = pl.ds(pl.multiple_of(my_core() * half, half), half)
    zero = jnp.zeros((half, width), BF16)
    taps_s[3 * half :, :] = jnp.zeros((taps_s.shape[0] - 3 * half, taps_s.shape[1]), BF16)
    for r in range(rows + 2):
        put_taps(taps_s, r, grad_ref[r - 1, mine, :] if 0 < r <= rows else zero)
    for r in range(rows):
        act_s[:, r * width : (r + 1) * width] = silu(pre_ref[r])
    for i, r in enumerate((0, rows - 1)):
        act_edge_ref[i] = act_s[:, r * width : (r + 1) * width]
        grad_edge_ref[i] = grad_ref[r, mine, :]
    for a in range(3):
        at = (2 - a) * width
        term_ref[a] = lax.dot_general(act_s[...], taps_s[:, at : at + rows * width], NT, preferred_element_type=F32)


def pair_kernel(term_ref, act_edge_ref, grad_edge_ref, their_pre_ref, their_grad_ref, near_ref, *refs):
    out_refs, (act_s, taps_s, term_s) = refs[: PLANE * NEAR], refs[PLANE * NEAR :]
    rows, chans, width = their_pre_ref.shape
    half = chans // PAIR
    outers, _, block, _ = out_refs[0].shape
    core = my_core()
    first = core == 0
    mine = pl.ds(pl.multiple_of(core * half, half), half)
    taps_s[3 * half :, :] = jnp.zeros((taps_s.shape[0] - 3 * half, taps_s.shape[1]), BF16)
    for r in range(rows):
        act_s[:, (2 + r) * width : (3 + r) * width] = silu(their_pre_ref[r])
    near_act = silu(near_ref[1])
    their_top = act_s[:, 2 * width : 3 * width]
    their_end = act_s[:, (rows + 1) * width : (rows + 2) * width]
    extra = ((0, their_top, act_edge_ref[0]), (1, act_edge_ref[0], near_act))
    extra += ((rows + 2, act_edge_ref[1], their_end), (rows + 3, near_act, act_edge_ref[1]))
    for slot, if_first, if_second in extra:
        act_s[:, slot * width : (slot + 1) * width] = jnp.where(first, if_first, if_second)
    near_grad = near_ref[0, mine, :]
    their_top, their_end = their_grad_ref[0, mine, :], their_grad_ref[rows - 1, mine, :]
    zero = jnp.zeros((half, width), BF16)
    put_taps(taps_s, 0, jnp.where(first, grad_edge_ref[1], their_end))
    put_taps(taps_s, 1, jnp.where(first, near_grad, grad_edge_ref[1]))
    put_taps(taps_s, 2, zero)
    for r in range(rows):
        put_taps(taps_s, 3 + r, their_grad_ref[r, mine, :])
    put_taps(taps_s, rows + 3, zero)
    put_taps(taps_s, rows + 4, jnp.where(first, their_top, grad_edge_ref[0]))
    put_taps(taps_s, rows + 5, jnp.where(first, grad_edge_ref[0], near_grad))
    for a, (left, right, at) in enumerate(((2, rows + 4, 4), (2, rows + 2, 3), (0, rows + 2, 0))):
        term = term_ref[a] + lax.dot_general(
            act_s[:, left * width : right * width],
            taps_s[:, at * width : (at + right - left) * width],
            NT,
            preferred_element_type=F32,
        )
        for p in range(PLANE):
            for z in range(NEAR * outers):
                term_s[z % NEAR * PLANE + p, z // NEAR, a] = term[
                    z * block : (z + 1) * block, p * LANES : (p + 1) * LANES
                ].astype(term_s.dtype)
    at, outer_at = near_index(), lax.axis_index("dp") // NEAR
    for k, out_ref in enumerate(out_refs):
        for j in range(outers):
            out_ref[j] = term_s[at ^ k, outer_at ^ j]


def input_kernel(start, pre_ref, grad_ref, their_grad_ref, near_ref, kernel_ref, *refs):
    out_ref, taps_s = refs[-2:]
    rows, chans, width = pre_ref.shape
    count = out_ref.shape[0]
    first = my_core() == 0
    for r in range(count + 2):
        at = start + r
        if at == 0:
            row = jnp.where(first, near_ref[0], their_grad_ref[rows - 1])
        elif at == rows + 1:
            row = jnp.where(first, their_grad_ref[0], near_ref[0])
        else:
            row = grad_ref[at - 1]
        put_taps(taps_s, r, row)
    step = 2
    for top in range(0, count, step):
        total = jnp.zeros((chans, step * width), F32)
        for a in range(3):
            at = (top + 2 - a) * width
            for b in range(3):
                taps = taps_s[b * chans : (b + 1) * chans, at : at + step * width]
                total += jnp.dot(kernel_ref[a, b], taps, preferred_element_type=F32)
        for r in range(step):
            x = pre_ref[start + top + r].astype(F32)
            sig = 1.0 / (1.0 + jnp.exp(-x))
            deriv = sig * (1.0 + x * (1.0 - sig))
            out_ref[top + r] = (total[:, r * width : (r + 1) * width] * deriv).astype(out_ref.dtype)


def pick_kernel(out_ref):
    taps = 9
    block = out_ref.shape[0] // taps
    k = lax.broadcasted_iota(jnp.int32, (block, taps * block), 0)
    j = lax.broadcasted_iota(jnp.int32, (block, taps * block), 1)
    for t in range(taps):
        out_ref[t * block : (t + 1) * block, :] = jnp.where(j - taps * k == t, 1.0, 0.0).astype(BF16)


def place_kernel(flip, parts_ref, pick_ref, *refs):
    out_hbm, wide_s, rows_s, out_s, sem = refs[-5:]
    _, _, block, _ = parts_ref.shape
    half = out_s.shape[0]
    for k in range(PLANE):
        lanes = pl.ds(pl.multiple_of((plane_index() ^ k) * LANES, LANES), LANES)
        wide_s[:, :, lanes] = parts_ref[k].astype(F32)
    for a in range(3):
        for b in range(3):
            t = 3 * a + b
            rows_s[t * block : (t + 1) * block, :] = wide_s[a, :, b * half : (b + 1) * half]
    dims = (((0,), (0,)), ((), ()))
    out_s[...] = lax.dot_general(rows_s[...].astype(BF16), pick_ref[...], dims, preferred_element_type=F32)
    count = sem.shape[0]
    step = half // count
    first = (my_core() ^ flip) * half
    copies = []
    for i in range(count):
        to = pl.ds(pl.multiple_of(first + i * step, 8), step)
        copies.append(pltpu.make_async_copy(out_s.at[pl.ds(i * step, step)], out_hbm.at[to], sem.at[i]))
        copies[-1].start()
    for copy in copies:
        copy.wait()


def shards(pre_act, out_grad, kernel):
    images, rows, width, chans = pre_act.shape
    assert images == 1
    space, blocks = lax.axis_size("space"), lax.axis_size("dp")
    inner = PAIR * PLANE
    outer = space // inner
    block = chans // blocks
    half = chans // PAIR
    far = blocks // NEAR
    factor = float(images * rows * width * space * blocks) ** (-0.5)
    params = pltpu.CompilerParams(vmem_limit_bytes=VMEM_LIMIT)
    flops = 2 * 9 * chans * chans * rows * width

    pre = jnp.swapaxes(pre_act[0], 1, 2)
    grad = jnp.swapaxes(out_grad[0], 1, 2)
    edge = pl.pallas_call(
        edge_kernel,
        out_shape=jax.ShapeDtypeStruct((2, chans, width), BF16),
        in_specs=[vmem()] * 2,
        out_specs=vmem(),
        compiler_params=params,
        name="edge_rows",
    )(pre, grad)
    beyond = [(i, i + 1 if i % 2 else i - 1) for i in range(space)]
    pairs = [(i, i + 1 - 2 * (i % 2)) for i in range(space)]

    def inside(moves):
        return [(i, j) for i, j in moves if 0 <= j < space]

    near_row = lax.ppermute(edge, "space", inside(beyond))
    their_grad = lax.ppermute(grad, "space", pairs)
    their_pre = lax.ppermute(pre, "space", pairs)

    own, act_edge, grad_edge = pl.pallas_call(
        own_kernel,
        out_shape=(
            jax.ShapeDtypeStruct((3, chans, PLANE * LANES), F32),
            jax.ShapeDtypeStruct((2, chans, width), BF16),
            jax.ShapeDtypeStruct((2, half, width), BF16),
        ),
        in_specs=[vmem()] * 2,
        out_specs=(vmem(),) * 3,
        scratch_shapes=[
            pltpu.VMEM((chans, rows * width), BF16),
            pltpu.VMEM((PLANE * LANES, (rows + 2) * width), BF16),
        ],
        compiler_params=params,
        cost_estimate=pl.CostEstimate(flops=flops, bytes_accessed=4000000, transcendentals=rows * width * chans),
        name="own_terms",
    )(pre, grad)
    piece = jax.ShapeDtypeStruct((far, 3, block, LANES), BF16)
    terms = pl.pallas_call(
        pair_kernel,
        out_shape=(piece,) * (NEAR * PLANE),
        in_specs=[vmem()] * 6,
        out_specs=(vmem(),) * (NEAR * PLANE),
        scratch_shapes=[
            pltpu.VMEM((chans, (rows + 4) * width), BF16),
            pltpu.VMEM((PLANE * LANES, (rows + 6) * width), BF16),
            pltpu.VMEM((NEAR * PLANE, far, 3, block, LANES), BF16),
        ],
        compiler_params=params,
        cost_estimate=pl.CostEstimate(flops=flops, bytes_accessed=4000000, transcendentals=rows * width * chans),
        name="pair_terms",
    )(own, act_edge, grad_edge, their_pre, their_grad, near_row)

    got = [terms[0]]
    for k in range(NEAR * PLANE - 1, 0, -1):
        moves = []
        for z in range(blocks):
            for i in range(space):
                to_z, to_i = z ^ (k // PLANE), i ^ (k % PLANE * PAIR)
                moves.append((z * space + i, to_z * space + to_i))
        got.append(lax.ppermute(terms[k], ("dp", "space"), moves))

    def input_part(part, *before):
        count = rows // 2
        return pl.pallas_call(
            functools.partial(input_kernel, part * count),
            grid=(1,),
            out_shape=jax.ShapeDtypeStruct((rows, chans, width), BF16),
            in_specs=[vmem()] * 5 + [anywhere()] * len(before),
            out_specs=pl.BlockSpec((count, chans, width), lambda i: (part, 0, 0)),
            scratch_shapes=[pltpu.VMEM((3 * chans, (count + 2) * width), BF16)],
            input_output_aliases={5: 0} if before else {},
            compiler_params=params,
            cost_estimate=pl.CostEstimate(
                flops=flops // 2, bytes_accessed=3000000, transcendentals=rows * width * chans // 2
            ),
            name="input_grad",
        )(pre, grad, their_grad, near_row, kernel, *before)

    pick = pl.pallas_call(
        pick_kernel,
        out_shape=jax.ShapeDtypeStruct((9 * block, 9 * block), BF16),
        out_specs=vmem(),
        name="pick_rows",
    )()
    in_grad = input_part(0)
    *got, in_grad, pick = lax.optimization_barrier((*got, in_grad, pick))

    near_sum = sum(part.astype(F32) for part in got)
    others = []
    for k in range(1, far):
        moves = [(z, z ^ (k * NEAR)) for z in range(blocks)]
        others.append(lax.ppermute(near_sum[k].astype(BF16), "dp", moves))
    in_grad = input_part(1, in_grad)
    *others, in_grad = lax.optimization_barrier((*others, in_grad))
    total = near_sum[0] + sum(other.astype(F32) for other in others)
    total = total * factor
    if outer > 1:
        total = lax.psum(total, "space", axis_index_groups=[[o * inner + i for o in range(outer)] for i in range(inner)])
    final = total.astype(BF16)
    parts = [final]
    for k in range(1, PLANE):
        parts.append(lax.ppermute(final, "space", [(i, i ^ (k * PAIR)) for i in range(space)]))
    parts = jnp.stack(parts)
    their_parts = lax.ppermute(parts, "space", pairs)

    def place(flip, parts, *before):
        return pl.pallas_call(
            functools.partial(place_kernel, flip),
            out_shape=jax.ShapeDtypeStruct((chans, 9 * block), F32),
            in_specs=[vmem()] * 2 + [anywhere()] * len(before),
            out_specs=anywhere(),
            scratch_shapes=[
                pltpu.VMEM((3, block, PLANE * LANES), F32),
                pltpu.VMEM((9 * block, half), F32),
                pltpu.VMEM((half, 9 * block), F32),
                pltpu.SemaphoreType.DMA((4,)),
            ],
            input_output_aliases={2: 0} if before else {},
            compiler_params=params,
            cost_estimate=pl.CostEstimate(flops=81 * block * block * chans, bytes_accessed=1000000, transcendentals=0),
            name="place_rows",
        )(parts, pick, *before)

    placed = place(1, their_parts, place(0, parts))
    return jnp.swapaxes(in_grad, 1, 2)[None], placed.T


def solution(mesh):
    placed = (P("dp", "space", None, None), P("dp", "space", None, None), P())
    return jax.shard_map(
        shards,
        mesh=mesh,
        in_specs=placed,
        out_specs=(P("dp", "space", None, None), P("dp", None)),
        check_vma=False,
    )
```

time: 51.7 us -> 53.3 us (1.031)
  waiting for transfers between devices: 8.38 us -> 5.67 us
  starting transfers between devices: 23.7 us -> 26.2 us
  local copies, waits for them, and re-layouts: 3.09 us -> 5.53 us
  Pallas kernels: 15.4 us -> 13.5 us
  other arithmetic: 0.16 us -> 1.33 us
    ppermute x6 -> x2, waiting for transfers between devices: 4.42 us -> 0.01 us  [the longest x1 0.01 us: shards(): others.append(lax.ppermute(near_sum[k].astype(BF16), 'dp', moves))]
    unnamed x10 -> x32, local copies, waits for them, and re-layouts: 2.19 us -> 5.51 us
    ppermute x7, starting transfers between devices: 14.9 us -> 18.2 us  [shards(): got.append(lax.ppermute(terms[k], ('dp', 'space'), moves))]
    pallas_call x1, Pallas kernels: 4.34 us -> 1.53 us  [shards(): pl.pallas_call(own_kernel, out_shape=(jax.ShapeDtypeStruct((3, chans, PLA...]
    ppermute x6 -> x2, starting transfers between devices: 3.96 us -> 2.81 us  [the longest x1 2.74 us: shards(): others.append(lax.ppermute(near_sum[k].astype(BF16), 'dp', moves))]
    add x1, other arithmetic: 0.13 us -> 1.27 us  [shards(): near_sum = sum((part.astype(F32) for part in got))]
    ppermute x3, waiting for transfers between devices: 3.94 us -> 4.99 us  [shards(): lax.ppermute(final, 'space', [(i, i ^ k * PAIR) for i in range(space)])]
    squeeze x1 -> x0, local copies, waits for them, and re-layouts: 0.89 us -> none  [shards(): edge = lax.dynamic_index_in_dim(grad, core * (rows - 1), 0, keepdims=False)]
  transfers between devices with their start and end apart: 19 -> 15, of which waited for: 6 -> 4; matrix products, arithmetic and copies ran while one was open for 2% -> 0% of each run, Pallas kernels for 22% -> 18%
where the time goes in v4:
time: 53.3 us; the launch traced here: 53 us
  starting transfers between devices  26.2 us (49%)
  Pallas kernels  13.5 us (25%)
  waiting for transfers between devices  5.67 us (11%)
  local copies, waits for them, and re-layouts  5.53 us (10%)
  other arithmetic  1.33 us (2%)
  between operations  0.84 us (2%)
    ppermute x7, starting transfers between devices, shards(): got.append(lax.ppermute(terms[k], ('dp', 'space'), moves))  18.2 us
    unnamed x32, local copies, waits for them, and re-layouts  5.51 us
    pallas_call x2, Pallas kernels, input_part(): pl.pallas_call(functools.partial(input_kernel, part * count), grid=(1,),...  5.13 us
    ppermute x3, waiting for transfers between devices, shards(): lax.ppermute(final, 'space', [(i, i ^ k * PAIR) for i in range(space)])  4.99 us
    ppermute x3, starting transfers between devices, shards(): lax.ppermute(final, 'space', [(i, i ^ k * PAIR) for i in range(space)])  3.92 us
    pallas_call x2, Pallas kernels, place(): pl.pallas_call(functools.partial(place_kernel, flip), out_shape=jax.Shape...  2.96 us
    ppermute x1, starting transfers between devices, shards(): others.append(lax.ppermute(near_sum[k].astype(BF16), 'dp', moves))  2.74 us
    pallas_call x1, Pallas kernels, shards(): pl.pallas_call(pair_kernel, out_shape=(piece,) * (NEAR * PLANE), in_specs...  2.63 us
  transfers between devices with their start and end apart: 15, of which 4 were waited for; matrix products, arithmetic and copies ran while one was open for 0% of the time, Pallas kernels for 18%

profile of v4, /device:TPU:0, one launch (start us, length us, event | category | flops | bytes accessed | tf_op | source)
XLA Modules:
  0.0 53.0 jit_solution(15698262499067180175)
XLA Ops:
  1.2 1.1 %copy-done.2 = bf16[1,8,128,320]{2,3,1,0:T(8,128)(2,1)S(1)} copy-done((bf16[1,8,128,320]{2,3,1,0:T(8,128)(2,1)S(1)}, bf16[1,8,128,320]{2,3,1,0:T(8,128)(2,1)}, u32[]{:S(2)}) %copy-start.2) | copy-done | bytes 655384
  2.3 1.1 %copy-done.4 = bf16[1,8,128,320]{2,3,1,0:T(8,128)(2,1)S(1)} copy-done((bf16[1,8,128,320]{2,3,1,0:T(8,128)(2,1)S(1)}, bf16[1,8,128,320]{2,3,1,0:T(8,128)(2,1)}, u32[]{:S(2)}) %copy-start.4) | copy-done | bytes 655384
  3.4 0.7 %collective-permute-start.2 = (bf16[2,320,128]{2,1,0:T(8,128)(2,1)S(1)}, bf16[2,320,128]{2,1,0:T(8,128)(2,1)S(1)}, u32[]{:S(2)}, u32[]{:S(2)}) collective-permute-start(bf16[2,320,128]{2,1,0:T(8,128)(2,1)S(1)} %edge_rows.1), channel_id=1, source_target_pairs={{1,2},{2,1},{3,4},{4,3},{5,6},{6,5},{9,10},{10,9},{11,12},{12,11},... | collective-permute-start | bytes 491528 | tf_op jit(solution)/shard_map/ppermute | solution.py:223
  4.1 1.5 %own_terms.1 = (f32[3,320,512]{2,1,0:T(8,128)S(1)}, bf16[2,320,128]{2,1,0:T(8,128)(2,1)S(1)}, bf16[2,160,128]{2,1,0:T(8,128)(2,1)S(1)}) custom-call(bf16[8,320,128]{2,1,0:T(8,128)(2,1)S(1)} %bitcast.26, bf16[8,320,128]{2,1,0:T(8,128)(2,1)S(1)} %bitcast.31), custom_call_target="tpu_custom_call" | custom-call | flops 1887436800 | bytes 4000000 | tf_op jit(solution)/shard_map/own_terms/pallas_call | solution.py:227
  5.7 2.6 %pair_terms.1 = (bf16[2,3,80,128]{3,2,1,0:T(8,128)(2,1)S(1)}, bf16[2,3,80,128]{3,2,1,0:T(8,128)(2,1)}, bf16[2,3,80,128]{3,2,1,0:T(8,128)(2,1)}, bf16[2,3,80,128]...) custom-call(f32[3,320,512]{2,1,0:T(8,128)S(1)} %get-tuple-element.25, ...), custom_call_target="tpu_custom_call" | custom-call | flops 1887436800 | bytes 4000000 | tf_op jit(solution)/shard_map/pair_terms/pallas_call | solution.py:245
  9.0 10.8 %collective-permute-start.3 = (bf16[2,3,80,128]{3,2,1,0:T(8,128)(2,1)S(1)}, bf16[2,3,80,128]{3,2,1,0:T(8,128)(2,1)S(1)}, u32[]{:S(2)}, u32[]{:S(2)}) collective-permute-start(bf16[2,3,80,128]{3,2,1,0:T(8,128)(2,1)S(1)} %get-tuple-element.29), channel_id=1, source_target_pairs={{0,14},{1,15},{2,12},{3,13},{4,10},{5,11},{6,8},{7,9},{8,6},{9,7},... | collective-permute-start | bytes 368648 | tf_op jit(solution)/shard_map/ppermute | solution.py:267
  19.8 0.7 %collective-permute-start.5 = (bf16[2,3,80,128]{3,2,1,0:T(8,128)(2,1)}, bf16[2,3,80,128]{3,2,1,0:T(8,128)(2,1)}, u32[]{:S(2)}, u32[]{:S(2)}) collective-permute-start(bf16[2,3,80,128]{3,2,1,0:T(8,128)(2,1)} %get-tuple-element.31), channel_id=1, source_target_pairs={{0,10},{1,11},{2,8},{3,9},{4,14},{5,15},{6,12},{7,13},{8,2},{9,3},... | collective-permute-start | bytes 368648 | tf_op jit(solution)/shard_map/ppermute | solution.py:267
  20.5 1.8 %collective-permute-start.6 = (bf16[2,3,80,128]{3,2,1,0:T(8,128)(2,1)}, bf16[2,3,80,128]{3,2,1,0:T(8,128)(2,1)}, u32[]{:S(2)}, u32[]{:S(2)}) collective-permute-start(bf16[2,3,80,128]{3,2,1,0:T(8,128)(2,1)} %get-tuple-element.32), channel_id=1, source_target_pairs={{0,8},{1,9},{2,10},{3,11},{4,12},{5,13},{6,14},{7,15},{8,0},{9,1},... | collective-permute-start | bytes 368648 | tf_op jit(solution)/shard_map/ppermute | solution.py:267
  22.2 2.4 %collective-permute-start.7 = (bf16[2,3,80,128]{3,2,1,0:T(8,128)(2,1)}, bf16[2,3,80,128]{3,2,1,0:T(8,128)(2,1)}, u32[]{:S(2)}, u32[]{:S(2)}) collective-permute-start(bf16[2,3,80,128]{3,2,1,0:T(8,128)(2,1)} %get-tuple-element.33), channel_id=1, source_target_pairs={{0,6},{1,7},{2,4},{3,5},{4,2},{5,3},{6,0},{7,1},{8,14},{9,15},{10,... | collective-permute-start | bytes 368648 | tf_op jit(solution)/shard_map/ppermute | solution.py:267
  24.7 2.0 %collective-permute-start.8 = (bf16[2,3,80,128]{3,2,1,0:T(8,128)(2,1)}, bf16[2,3,80,128]{3,2,1,0:T(8,128)(2,1)}, u32[]{:S(2)}, u32[]{:S(2)}) collective-permute-start(bf16[2,3,80,128]{3,2,1,0:T(8,128)(2,1)} %get-tuple-element.34), channel_id=1, source_target_pairs={{0,4},{1,5},{2,6},{3,7},{4,0},{5,1},{6,2},{7,3},{8,12},{9,13},{10,... | collective-permute-start | bytes 368648 | tf_op jit(solution)/shard_map/ppermute | solution.py:267
  26.7 0.7 %collective-permute-done.4 = bf16[2,3,80,128]{3,2,1,0:T(8,128)(2,1)S(1)} collective-permute-done((bf16[2,3,80,128]{3,2,1,0:T(8,128)(2,1)S(1)}, bf16[2,3,80,128]{3,2,1,0:T(8,128)(2,1)S(1)}, u32[]{:S(2)}, u32[]{:S(2)}) %collective-permute-start.4) | collective-permute-done | bytes 122912 | tf_op jit(solution)/shard_map/ppermute | solution.py:267
  28.5 1.2 %pick_rows.1.pick_ref = bf16[720,720]{1,0:T(8,128)(2,1)} custom-call(), custom_call_target="tpu_custom_call" | custom-call | tf_op jit(solution)/shard_map/pick_rows/pallas_call | solution.py:286
  29.7 1.1 %copy-done.7 = bf16[8,320,128]{2,1,0:T(8,128)(2,1)S(1)} copy-done((bf16[8,320,128]{2,1,0:T(8,128)(2,1)S(1)}, bf16[8,320,128]{2,1,0:T(8,128)(2,1)}, u32[]{:S(2)}) %copy-start.7) | copy-done | bytes 655384
  30.8 0.9 %copy-done.9 = bf16[2,320,128]{2,1,0:T(8,128)(2,1)S(1)} copy-done((bf16[2,320,128]{2,1,0:T(8,128)(2,1)S(1)}, bf16[2,320,128]{2,1,0:T(8,128)(2,1)}, u32[]{:S(2)}) %copy-start.9) | copy-done | bytes 163864
  31.7 2.6 %input_grad.2.refs_0_ = bf16[8,320,128]{2,1,0:T(8,128)(2,1)} custom-call(bf16[8,320,128]{2,1,0:T(8,128)(2,1)S(1)} %bitcast.27, bf16[8,320,128]{2,1,0:T(8,128)(2,1)S(1)} %bitcast.32, bf16[8,320,128]{2,1,0:T(8,128)(2,1)S(1)} %copy-done.7, bf16[2,320,128]{2,1,0:T(8,128)(2,1)S(1)} %copy-done.9, bf16[3,3,320,320]{3,2,1,0:T(8,128)(2,1)S(1)} %copy-done.1), custom_call_target="tpu_custom_call" | custom-call | flops 943718400 | bytes 3000000 | tf_op jit(solution)/shard_map/input_grad/pallas_call | solution.py:271
  34.4 1.3 %convert_add_fusion = f32[2,3,80,128]{3,2,1,0:T(8,128)S(1)} fusion(bf16[2,3,80,128]{3,2,1,0:T(8,128)(2,1)} %collective-permute-done.9, bf16[2,3,80,128]{3,2,1,0:T(8,128)(2,1)} %collective-permute-done.8, bf16[2,3,80,128]{3,2,1,0:T(8,128)(2,1)} %collective-permute-done.7, bf16[2,3,80,128]{3,2,1,0:T(8,128)(2,1)} %collective-permute-done.6, ...), kind=kLoop, calls=%fused_computation.1 | loop fusion | flops 921600 | bytes 1228800 | tf_op jit(solution)/shard_map/add | solution.py:295
  35.7 2.7 %collective-permute-start.10 = (bf16[3,80,128]{2,1,0:T(8,128)(2,1)S(1)}, bf16[3,80,128]{2,1,0:T(8,128)(2,1)S(1)}, u32[]{:S(2)}, u32[]{:S(2)}) collective-permute-start(bf16[3,80,128]{2,1,0:T(8,128)(2,1)S(1)} %fusion.3), channel_id=1, source_target_pairs={{0,16},{8,24},{16,0},{24,8},{1,17},{9,25},{17,1},{25,9},{2,18},{10... | collective-permute-start | bytes 184328 | tf_op jit(solution)/shard_map/ppermute | solution.py:299
  38.4 2.6 %input_grad.3 = bf16[8,320,128]{2,1,0:T(8,128)(2,1)} custom-call(bf16[8,320,128]{2,1,0:T(8,128)(2,1)S(1)} %bitcast.28, bf16[8,320,128]{2,1,0:T(8,128)(2,1)S(1)} %bitcast.33, bf16[8,320,128]{2,1,0:T(8,128)(2,1)S(1)} %copy-done.7, bf16[2,320,128]{2,1,0:T(8,128)(2,1)S(1)} %copy-done.9, ...), custom_call_target="tpu_custom_call", output_to_operand_aliasing={{}: (5, {})} | custom-call | flops 943718400 | bytes 3000000 | tf_op jit(solution)/shard_map/input_grad/pallas_call | solution.py:271
  41.0 1.7 %collective-permute-start.11 = (bf16[3,80,128]{2,1,0:T(8,128)(2,1)S(1)}, bf16[3,80,128]{2,1,0:T(8,128)(2,1)S(1)}, u32[]{:S(2)}, u32[]{:S(2)}) collective-permute-start(bf16[3,80,128]{2,1,0:T(8,128)(2,1)S(1)} %fusion.2), channel_id=1, source_target_pairs={{0,2},{1,3},{2,0},{3,1},{4,6},{5,7},{6,4},{7,5},{8,10},{9,11},{10,... | collective-permute-start | bytes 184328 | tf_op jit(solution)/shard_map/ppermute | solution.py:309
  42.6 2.1 %collective-permute-start.12 = (bf16[3,80,128]{2,1,0:T(8,128)(2,1)S(1)}, bf16[3,80,128]{2,1,0:T(8,128)(2,1)S(1)}, u32[]{:S(2)}, u32[]{:S(2)}) collective-permute-start(bf16[3,80,128]{2,1,0:T(8,128)(2,1)S(1)} %fusion.2), channel_id=1, source_target_pairs={{0,4},{1,5},{2,6},{3,7},{4,0},{5,1},{6,2},{7,3},{8,12},{9,13},{10,... | collective-permute-start | bytes 184328 | tf_op jit(solution)/shard_map/ppermute | solution.py:309
  45.4 2.2 %collective-permute-done.12 = bf16[3,80,128]{2,1,0:T(8,128)(2,1)S(1)} collective-permute-done((bf16[3,80,128]{2,1,0:T(8,128)(2,1)S(1)}, bf16[3,80,128]{2,1,0:T(8,128)(2,1)S(1)}, u32[]{:S(2)}, u32[]{:S(2)}) %collective-permute-start.12) | collective-permute-done | bytes 61472 | tf_op jit(solution)/shard_map/ppermute | solution.py:309
  47.6 2.3 %collective-permute-done.13 = bf16[3,80,128]{2,1,0:T(8,128)(2,1)S(1)} collective-permute-done((bf16[3,80,128]{2,1,0:T(8,128)(2,1)S(1)}, bf16[3,80,128]{2,1,0:T(8,128)(2,1)S(1)}, u32[]{:S(2)}, u32[]{:S(2)}) %collective-permute-start.13) | collective-permute-done | bytes 61472 | tf_op jit(solution)/shard_map/ppermute | solution.py:309
  50.0 1.5 %place_rows.2.refs_0_ = f32[320,720]{1,0:T(8,128)} custom-call(bf16[4,3,80,128]{3,2,1,0:T(8,128)(2,1)S(1)} %pad_maximum_fusion.parts_ref, bf16[720,720]{1,0:T(8,128)(2,1)S(1)} %copy-done), custom_call_target="tpu_custom_call" | custom-call | flops 165888000 | bytes 1000000 | tf_op jit(solution)/shard_map/place_rows/pallas_call | solution.py:314
  51.5 1.5 %place_rows.3 = f32[320,720]{1,0:T(8,128)} custom-call(bf16[4,3,80,128]{3,2,1,0:T(8,128)(2,1)S(1)} %collective-permute-done.14.parts_ref, bf16[720,720]{1,0:T(8,128)(2,1)S(1)} %copy-done, f32[320,720]{1,0:T(8,128)} %place_rows.2.refs_0_), custom_call_target="tpu_custom_call", output_to_operand_aliasing={{}: (2, {})} | custom-call | flops 165888000 | bytes 1000000 | tf_op jit(solution)/shard_map/place_rows/pallas_call | solution.py:314
  (50 shorter events, 3.3 us)
Async XLA Ops:
  0.6 5.0 %collective-permute-start.1 = (bf16[8,320,128]{2,1,0:T(8,128)(2,1)}, bf16[8,320,128]{2,1,0:T(8,128)(2,1)S(1)}, u32[]{:S(2)}, u32[]{:S(2)}) collective-permute-start(bf16[8,320,128]{2,1,0:T(8,128)(2,1)} %bitcast.29), channel_id=1, source_target_pairs={{0,1},{1,0},{2,3},{3,2},{4,5},{5,4},{6,7},{7,6},{8,9},{9,8},{10,11... | collective-permute-start | bytes 1966088 | tf_op jit(solution)/shard_map/ppermute | solution.py:224
  1.1 4.5 %collective-permute-start = (bf16[8,320,128]{2,1,0:T(8,128)(2,1)}, bf16[8,320,128]{2,1,0:T(8,128)(2,1)S(1)}, u32[]{:S(2)}, u32[]{:S(2)}) collective-permute-start(bf16[8,320,128]{2,1,0:T(8,128)(2,1)} %bitcast.24), channel_id=1, source_target_pairs={{0,1},{1,0},{2,3},{3,2},{4,5},{5,4},{6,7},{7,6},{8,9},{9,8},{10,11... | collective-permute-start | bytes 1966088 | tf_op jit(solution)/shard_map/ppermute | solution.py:225
  3.4 2.2 %collective-permute-start.2 = (bf16[2,320,128]{2,1,0:T(8,128)(2,1)S(1)}, bf16[2,320,128]{2,1,0:T(8,128)(2,1)S(1)}, u32[]{:S(2)}, u32[]{:S(2)}) collective-permute-start(bf16[2,320,128]{2,1,0:T(8,128)(2,1)S(1)} %edge_rows.1), channel_id=1, source_target_pairs={{1,2},{2,1},{3,4},{4,3},{5,6},{6,5},{9,10},{10,9},{11,12},{12,11},... | collective-permute-start | bytes 491528 | tf_op jit(solution)/shard_map/ppermute | solution.py:223
  5.6 2.7 %copy-start.8 = (bf16[2,320,128]{2,1,0:T(8,128)(2,1)}, bf16[2,320,128]{2,1,0:T(8,128)(2,1)S(1)}, u32[]{:S(2)}) copy-start(bf16[2,320,128]{2,1,0:T(8,128)(2,1)S(1)} %collective-permute-done.2.near_ref) | copy-start | bytes 491524
  5.7 2.7 %copy-start.6 = (bf16[8,320,128]{2,1,0:T(8,128)(2,1)}, bf16[8,320,128]{2,1,0:T(8,128)(2,1)S(1)}, u32[]{:S(2)}) copy-start(bf16[8,320,128]{2,1,0:T(8,128)(2,1)S(1)} %collective-permute-done.1.their_grad_ref) | copy-start | bytes 1966084
  5.7 24.0 %copy-start.1 = (bf16[3,3,320,320]{3,2,1,0:T(8,128)(2,1)S(1)}, bf16[3,3,320,320]{3,2,1,0:T(8,128)(2,1)}, u32[]{:S(2)}) copy-start(bf16[3,3,320,320]{3,2,1,0:T(8,128)(2,1)} %kernel_ref.3) | copy-start | bytes 5529604
  5.7 24.0 %copy-start.3 = (bf16[1,8,128,320]{2,3,1,0:T(8,128)(2,1)S(1)}, bf16[1,8,128,320]{2,3,1,0:T(8,128)(2,1)}, u32[]{:S(2)}) copy-start(bf16[1,8,128,320]{2,3,1,0:T(8,128)(2,1)} %param.3) | copy-start | bytes 1966084
  5.7 24.0 %copy-start.5 = (bf16[1,8,128,320]{2,3,1,0:T(8,128)(2,1)S(1)}, bf16[1,8,128,320]{2,3,1,0:T(8,128)(2,1)}, u32[]{:S(2)}) copy-start(bf16[1,8,128,320]{2,3,1,0:T(8,128)(2,1)} %param.4) | copy-start | bytes 1966084
  9.0 15.7 %collective-permute-start.3 = (bf16[2,3,80,128]{3,2,1,0:T(8,128)(2,1)S(1)}, bf16[2,3,80,128]{3,2,1,0:T(8,128)(2,1)S(1)}, u32[]{:S(2)}, u32[]{:S(2)}) collective-permute-start(bf16[2,3,80,128]{3,2,1,0:T(8,128)(2,1)S(1)} %get-tuple-element.29), channel_id=1, source_target_pairs={{0,14},{1,15},{2,12},{3,13},{4,10},{5,11},{6,8},{7,9},{8,6},{9,7},... | collective-permute-start | bytes 368648 | tf_op jit(solution)/shard_map/ppermute | solution.py:267
  19.8 7.5 %collective-permute-start.4 = (bf16[2,3,80,128]{3,2,1,0:T(8,128)(2,1)S(1)}, bf16[2,3,80,128]{3,2,1,0:T(8,128)(2,1)S(1)}, u32[]{:S(2)}, u32[]{:S(2)}) collective-permute-start(bf16[2,3,80,128]{3,2,1,0:T(8,128)(2,1)S(1)} %get-tuple-element.30), channel_id=1, source_target_pairs={{0,12},{1,13},{2,14},{3,15},{4,8},{5,9},{6,10},{7,11},{8,4},{9,5},... | collective-permute-start | bytes 368648 | tf_op jit(solution)/shard_map/ppermute | solution.py:267
  19.8 14.5 %collective-permute-start.5 = (bf16[2,3,80,128]{3,2,1,0:T(8,128)(2,1)}, bf16[2,3,80,128]{3,2,1,0:T(8,128)(2,1)}, u32[]{:S(2)}, u32[]{:S(2)}) collective-permute-start(bf16[2,3,80,128]{3,2,1,0:T(8,128)(2,1)} %get-tuple-element.31), channel_id=1, source_target_pairs={{0,10},{1,11},{2,8},{3,9},{4,14},{5,15},{6,12},{7,13},{8,2},{9,3},... | collective-permute-start | bytes 368648 | tf_op jit(solution)/shard_map/ppermute | solution.py:267
  20.5 13.8 %collective-permute-start.6 = (bf16[2,3,80,128]{3,2,1,0:T(8,128)(2,1)}, bf16[2,3,80,128]{3,2,1,0:T(8,128)(2,1)}, u32[]{:S(2)}, u32[]{:S(2)}) collective-permute-start(bf16[2,3,80,128]{3,2,1,0:T(8,128)(2,1)} %get-tuple-element.32), channel_id=1, source_target_pairs={{0,8},{1,9},{2,10},{3,11},{4,12},{5,13},{6,14},{7,15},{8,0},{9,1},... | collective-permute-start | bytes 368648 | tf_op jit(solution)/shard_map/ppermute | solution.py:267
  22.2 12.1 %collective-permute-start.7 = (bf16[2,3,80,128]{3,2,1,0:T(8,128)(2,1)}, bf16[2,3,80,128]{3,2,1,0:T(8,128)(2,1)}, u32[]{:S(2)}, u32[]{:S(2)}) collective-permute-start(bf16[2,3,80,128]{3,2,1,0:T(8,128)(2,1)} %get-tuple-element.33), channel_id=1, source_target_pairs={{0,6},{1,7},{2,4},{3,5},{4,2},{5,3},{6,0},{7,1},{8,14},{9,15},{10,... | collective-permute-start | bytes 368648 | tf_op jit(solution)/shard_map/ppermute | solution.py:267
  24.7 2.7 %copy-start.12 = (bf16[2,3,80,128]{3,2,1,0:T(8,128)(2,1)}, bf16[2,3,80,128]{3,2,1,0:T(8,128)(2,1)S(1)}, u32[]{:S(2)}) copy-start(bf16[2,3,80,128]{3,2,1,0:T(8,128)(2,1)S(1)} %collective-permute-done.3) | copy-start | bytes 368644
  24.7 9.6 %collective-permute-start.8 = (bf16[2,3,80,128]{3,2,1,0:T(8,128)(2,1)}, bf16[2,3,80,128]{3,2,1,0:T(8,128)(2,1)}, u32[]{:S(2)}, u32[]{:S(2)}) collective-permute-start(bf16[2,3,80,128]{3,2,1,0:T(8,128)(2,1)} %get-tuple-element.34), channel_id=1, source_target_pairs={{0,4},{1,5},{2,6},{3,7},{4,0},{5,1},{6,2},{7,3},{8,12},{9,13},{10,... | collective-permute-start | bytes 368648 | tf_op jit(solution)/shard_map/ppermute | solution.py:267
  28.0 6.3 %collective-permute-start.9 = (bf16[2,3,80,128]{3,2,1,0:T(8,128)(2,1)}, bf16[2,3,80,128]{3,2,1,0:T(8,128)(2,1)}, u32[]{:S(2)}, u32[]{:S(2)}) collective-permute-start(bf16[2,3,80,128]{3,2,1,0:T(8,128)(2,1)} %get-tuple-element.35), channel_id=1, source_target_pairs={{0,2},{1,3},{2,0},{3,1},{4,6},{5,7},{6,4},{7,5},{8,10},{9,11},{10,... | collective-permute-start | bytes 368648 | tf_op jit(solution)/shard_map/ppermute | solution.py:267
  31.7 2.6 %copy-start.13 = (bf16[2,3,80,128]{3,2,1,0:T(8,128)(2,1)S(1)}, bf16[2,3,80,128]{3,2,1,0:T(8,128)(2,1)}, u32[]{:S(2)}) copy-start(bf16[2,3,80,128]{3,2,1,0:T(8,128)(2,1)} %copy-done.12) | copy-start | bytes 368644
  31.7 2.6 %copy-start.15 = (bf16[2,3,80,128]{3,2,1,0:T(8,128)(2,1)S(1)}, bf16[2,3,80,128]{3,2,1,0:T(8,128)(2,1)}, u32[]{:S(2)}) copy-start(bf16[2,3,80,128]{3,2,1,0:T(8,128)(2,1)} %copy-done.14) | copy-start | bytes 368644
  35.6 14.4 %copy-start = (bf16[720,720]{1,0:T(8,128)(2,1)S(1)}, bf16[720,720]{1,0:T(8,128)(2,1)}, u32[]{:S(2)}) copy-start(bf16[720,720]{1,0:T(8,128)(2,1)} %pick_rows.1.pick_ref) | copy-start | bytes 3110404
  35.7 5.3 %collective-permute-start.10 = (bf16[3,80,128]{2,1,0:T(8,128)(2,1)S(1)}, bf16[3,80,128]{2,1,0:T(8,128)(2,1)S(1)}, u32[]{:S(2)}, u32[]{:S(2)}) collective-permute-start(bf16[3,80,128]{2,1,0:T(8,128)(2,1)S(1)} %fusion.3), channel_id=1, source_target_pairs={{0,16},{8,24},{16,0},{24,8},{1,17},{9,25},{17,1},{25,9},{2,18},{10... | collective-permute-start | bytes 184328 | tf_op jit(solution)/shard_map/ppermute | solution.py:299
  41.0 4.4 %collective-permute-start.11 = (bf16[3,80,128]{2,1,0:T(8,128)(2,1)S(1)}, bf16[3,80,128]{2,1,0:T(8,128)(2,1)S(1)}, u32[]{:S(2)}, u32[]{:S(2)}) collective-permute-start(bf16[3,80,128]{2,1,0:T(8,128)(2,1)S(1)} %fusion.2), channel_id=1, source_target_pairs={{0,2},{1,3},{2,0},{3,1},{4,6},{5,7},{6,4},{7,5},{8,10},{9,11},{10,... | collective-permute-start | bytes 184328 | tf_op jit(solution)/shard_map/ppermute | solution.py:309
  42.6 5.0 %collective-permute-start.12 = (bf16[3,80,128]{2,1,0:T(8,128)(2,1)S(1)}, bf16[3,80,128]{2,1,0:T(8,128)(2,1)S(1)}, u32[]{:S(2)}, u32[]{:S(2)}) collective-permute-start(bf16[3,80,128]{2,1,0:T(8,128)(2,1)S(1)} %fusion.2), channel_id=1, source_target_pairs={{0,4},{1,5},{2,6},{3,7},{4,0},{5,1},{6,2},{7,3},{8,12},{9,13},{10,... | collective-permute-start | bytes 184328 | tf_op jit(solution)/shard_map/ppermute | solution.py:309
  44.8 5.1 %collective-permute-start.13 = (bf16[3,80,128]{2,1,0:T(8,128)(2,1)S(1)}, bf16[3,80,128]{2,1,0:T(8,128)(2,1)S(1)}, u32[]{:S(2)}, u32[]{:S(2)}) collective-permute-start(bf16[3,80,128]{2,1,0:T(8,128)(2,1)S(1)} %fusion.2), channel_id=1, source_target_pairs={{0,6},{1,7},{2,4},{3,5},{4,2},{5,3},{6,0},{7,1},{8,14},{9,15},{10,... | collective-permute-start | bytes 184328 | tf_op jit(solution)/shard_map/ppermute | solution.py:309
  49.9 1.6 %collective-permute-start.14 = (bf16[4,3,80,128]{3,2,1,0:T(8,128)(2,1)S(1)}, bf16[4,3,80,128]{3,2,1,0:T(8,128)(2,1)S(1)}, u32[]{:S(2)}, u32[]{:S(2)}) collective-permute-start(bf16[4,3,80,128]{3,2,1,0:T(8,128)(2,1)S(1)} %pad_maximum_fusion.parts_ref), channel_id=1, source_target_pairs={{0,1},{1,0},{2,3},{3,2},{4,5},{5,4},{6,7},{7,6},{8,9},{9,8},{10,11... | collective-permute-start | bytes 737288 | tf_op jit(solution)/shard_map/ppermute | solution.py:311
  (7 other events, 8.1 us)

commit v5 on v4

--- a/solution.py
+++ b/solution.py
@@ -13,7 +13,7 @@
 PAIR = 2
 PLANE = 4
 NEAR = 2
-VMEM_LIMIT = 48 * 1024 * 1024
+VMEM_LIMIT = 16 * 1024 * 1024
 NT = (((1,), (1,)), ((), ()))
 
 
@@ -55,12 +55,6 @@
 
 def my_core():
     return lax.rem(lax.axis_index("space"), PAIR)
-
-
-def edge_kernel(pre_ref, grad_ref, out_ref):
-    row = my_core() * (pre_ref.shape[0] - 1)
-    out_ref[0] = grad_ref[row]
-    out_ref[1] = pre_ref[row]
 
 
 def own_kernel(pre_ref, grad_ref, term_ref, act_edge_ref, grad_edge_ref, act_s, taps_s):
@@ -128,21 +122,18 @@
             out_ref[j] = term_s[at ^ k, outer_at ^ j]
 
 
-def input_kernel(start, pre_ref, grad_ref, their_grad_ref, near_ref, kernel_ref, *refs):
-    out_ref, taps_s = refs[-2:]
+def input_kernel(side, pre_ref, grad_ref, edge_ref, kernel_ref, *refs):
+    out_hbm, taps_s, out_s, sem = refs[-4:]
     rows, chans, width = pre_ref.shape
-    count = out_ref.shape[0]
-    first = my_core() == 0
-    for r in range(count + 2):
-        at = start + r
-        if at == 0:
-            row = jnp.where(first, near_ref[0], their_grad_ref[rows - 1])
-        elif at == rows + 1:
-            row = jnp.where(first, their_grad_ref[0], near_ref[0])
-        else:
-            row = grad_ref[at - 1]
-        put_taps(taps_s, r, row)
+    count = rows // 2
+    upper = my_core() == side
+    start = jnp.where(upper, 0, count)
+    put_taps(taps_s, 0, jnp.where(upper, edge_ref[0], grad_ref[count - 1]))
+    for r in range(count):
+        put_taps(taps_s, r + 1, grad_ref[start + r])
+    put_taps(taps_s, count + 1, jnp.where(upper, grad_ref[count], edge_ref[0]))
     step = 2
+    copies = []
     for top in range(0, count, step):
         total = jnp.zeros((chans, step * width), F32)
         for a in range(3):
@@ -154,10 +145,18 @@
             x = pre_ref[start + top + r].astype(F32)
             sig = 1.0 / (1.0 + jnp.exp(-x))
             deriv = sig * (1.0 + x * (1.0 - sig))
-            out_ref[top + r] = (total[:, r * width : (r + 1) * width] * deriv).astype(out_ref.dtype)
-
-
-def pick_kernel(out_ref):
+            out_s[top + r] = (total[:, r * width : (r + 1) * width] * deriv).astype(out_s.dtype)
+        copies.append(
+            pltpu.make_async_copy(
+                out_s.at[pl.ds(top, step)], out_hbm.at[pl.ds(start + top, step)], sem.at[top // step]
+            )
+        )
+        copies[-1].start()
+    for copy in copies:
+        copy.wait()
+
+
+def pick_kernel(after_ref, out_ref):
     taps = 9
     block = out_ref.shape[0] // taps
     k = lax.broadcasted_iota(jnp.int32, (block, taps * block), 0)
@@ -206,24 +205,24 @@
 
     pre = jnp.swapaxes(pre_act[0], 1, 2)
     grad = jnp.swapaxes(out_grad[0], 1, 2)
-    edge = pl.pallas_call(
-        edge_kernel,
-        out_shape=jax.ShapeDtypeStruct((2, chans, width), BF16),
-        in_specs=[vmem()] * 2,
+    row = my_core() * (rows - 1)
+    edge = jnp.stack([lax.dynamic_index_in_dim(grad, row, 0, False), lax.dynamic_index_in_dim(pre, row, 0, False)])
+    beyond = [(i, i + 1 if i % 2 else i - 1) for i in range(space)]
+    pairs = [(i, i + 1 - 2 * (i % 2)) for i in range(space)]
+
+    def inside(moves):
+        return [(i, j) for i, j in moves if 0 <= j < space]
+
+    near_row = lax.ppermute(edge, "space", inside(beyond))
+    pick = pl.pallas_call(
+        pick_kernel,
+        out_shape=jax.ShapeDtypeStruct((9 * block, 9 * block), BF16),
+        in_specs=[anywhere()],
         out_specs=vmem(),
         compiler_params=params,
-        name="edge_rows",
-    )(pre, grad)
-    beyond = [(i, i + 1 if i % 2 else i - 1) for i in range(space)]
-    pairs = [(i, i + 1 - 2 * (i % 2)) for i in range(space)]
-
-    def inside(moves):
-        return [(i, j) for i, j in moves if 0 <= j < space]
-
-    near_row = lax.ppermute(edge, "space", inside(beyond))
-    their_grad = lax.ppermute(grad, "space", pairs)
-    their_pre = lax.ppermute(pre, "space", pairs)
-
+        cost_estimate=pl.CostEstimate(flops=flops, bytes_accessed=4000000, transcendentals=0),
+        name="pick_rows",
+    )(edge)
     own, act_edge, grad_edge = pl.pallas_call(
         own_kernel,
         out_shape=(
@@ -241,6 +240,33 @@
         cost_estimate=pl.CostEstimate(flops=flops, bytes_accessed=4000000, transcendentals=rows * width * chans),
         name="own_terms",
     )(pre, grad)
+    near_row, pick, own, act_edge, grad_edge, my_pre, my_grad = lax.optimization_barrier(
+        (near_row, pick, own, act_edge, grad_edge, pre, grad)
+    )
+    their_grad = lax.ppermute(my_grad, "space", pairs)
+    their_pre = lax.ppermute(my_pre, "space", pairs)
+    def input_part(side, edge_rows, *before):
+        count = rows // 2
+        return pl.pallas_call(
+            functools.partial(input_kernel, side),
+            out_shape=jax.ShapeDtypeStruct((rows, chans, width), BF16),
+            in_specs=[vmem()] * 4 + [anywhere()] * len(before),
+            out_specs=anywhere(),
+            scratch_shapes=[
+                pltpu.VMEM((3 * chans, (count + 2) * width), BF16),
+                pltpu.VMEM((count, chans, width), BF16),
+                pltpu.SemaphoreType.DMA((count // 2,)),
+            ],
+            input_output_aliases={4: 0} if before else {},
+            compiler_params=params,
+            cost_estimate=pl.CostEstimate(
+                flops=flops // 2, bytes_accessed=3000000, transcendentals=rows * width * chans // 2
+            ),
+            name="input_grad",
+        )(pre, grad, edge_rows, kernel, *before)
+
+    in_grad = input_part(0, near_row)
+    their_grad, their_pre, in_grad = lax.optimization_barrier((their_grad, their_pre, in_grad))
     piece = jax.ShapeDtypeStruct((far, 3, block, LANES), BF16)
     terms = pl.pallas_call(
         pair_kernel,
@@ -266,39 +292,16 @@
                 moves.append((z * space + i, to_z * space + to_i))
         got.append(lax.ppermute(terms[k], ("dp", "space"), moves))
 
-    def input_part(part, *before):
-        count = rows // 2
-        return pl.pallas_call(
-            functools.partial(input_kernel, part * count),
-            grid=(1,),
-            out_shape=jax.ShapeDtypeStruct((rows, chans, width), BF16),
-            in_specs=[vmem()] * 5 + [anywhere()] * len(before),
-            out_specs=pl.BlockSpec((count, chans, width), lambda i: (part, 0, 0)),
-            scratch_shapes=[pltpu.VMEM((3 * chans, (count + 2) * width), BF16)],
-            input_output_aliases={5: 0} if before else {},
-            compiler_params=params,
-            cost_estimate=pl.CostEstimate(
-                flops=flops // 2, bytes_accessed=3000000, transcendentals=rows * width * chans // 2
-            ),
-            name="input_grad",
-        )(pre, grad, their_grad, near_row, kernel, *before)
-
-    pick = pl.pallas_call(
-        pick_kernel,
-        out_shape=jax.ShapeDtypeStruct((9 * block, 9 * block), BF16),
-        out_specs=vmem(),
-        name="pick_rows",
-    )()
-    in_grad = input_part(0)
-    *got, in_grad, pick = lax.optimization_barrier((*got, in_grad, pick))
+
+    their_edge = lax.dynamic_index_in_dim(their_grad, my_core() * (rows - 1), 0)
+    in_grad = input_part(1, their_edge, in_grad)
+    *got, in_grad = lax.optimization_barrier((*got, in_grad))
 
     near_sum = sum(part.astype(F32) for part in got)
     others = []
     for k in range(1, far):
         moves = [(z, z ^ (k * NEAR)) for z in range(blocks)]
         others.append(lax.ppermute(near_sum[k].astype(BF16), "dp", moves))
-    in_grad = input_part(1, in_grad)
-    *others, in_grad = lax.optimization_barrier((*others, in_grad))
     total = near_sum[0] + sum(other.astype(F32) for other in others)
     total = total * factor
     if outer > 1:

time: 53.3 us -> 50.3 us (0.944)
  waiting for transfers between devices: 5.67 us -> 10.6 us
  local copies, waits for them, and re-layouts: 5.53 us -> 1.23 us
  Pallas kernels: 13.5 us -> 11.7 us
  other arithmetic: 1.33 us -> 0.21 us
  starting transfers between devices: 26.2 us -> 25.5 us
    ppermute x7, starting transfers between devices: 18.2 us -> 12.3 us  [shards(): got.append(lax.ppermute(terms[k], ('dp', 'space'), moves))]
    ppermute x2, starting transfers between devices: 0.6 us -> 6.14 us  [the longest x1 6.13 us: shards(): their_grad = lax.ppermute(my_grad, 'space', pairs)]
    unnamed x32 -> x6, local copies, waits for them, and re-layouts: 5.51 us -> 0.26 us
    ppermute x7, waiting for transfers between devices: 0.67 us -> 3.35 us  [shards(): got.append(lax.ppermute(terms[k], ('dp', 'space'), moves))]
    ppermute x1, waiting for transfers between devices: 0.01 us -> 2.54 us  [shards(): others.append(lax.ppermute(near_sum[k].astype(BF16), 'dp', moves))]
    add x1, other arithmetic: 1.27 us -> 0.13 us  [shards(): near_sum = sum((part.astype(F32) for part in got))]
    pallas_call x1, Pallas kernels: 1.2 us -> 0.19 us  [shards(): pl.pallas_call(pick_kernel, out_shape=jax.ShapeDtypeStruct((9 * block, 9...]
    dynamic_slice x0 -> x2, local copies, waits for them, and re-layouts: none -> 0.95 us  [the longest x1 0.95 us: shards(): lax.dynamic_index_in_dim(pre, row, 0, False)]
  transfers between devices with their start and end apart: 15 -> 15, of which waited for: 4 -> 7; matrix products, arithmetic and copies ran while one was open for 0% -> 0% of each run, Pallas kernels for 18% -> 17%
where the time goes in v5:
time: 50.3 us; the launch traced here: 50.1 us
  starting transfers between devices  25.5 us (51%)
  Pallas kernels  11.7 us (23%)
  waiting for transfers between devices  10.6 us (21%)
  local copies, waits for them, and re-layouts  1.23 us (2%)
  between operations  0.8 us (2%)
    ppermute x7, starting transfers between devices, shards(): got.append(lax.ppermute(terms[k], ('dp', 'space'), moves))  12.3 us
    ppermute x1, starting transfers between devices, shards(): their_grad = lax.ppermute(my_grad, 'space', pairs)  6.13 us
    pallas_call x2, Pallas kernels, input_part(): pl.pallas_call(functools.partial(input_kernel, side), out_shape=jax.Shape...  5.22 us
    ppermute x3, waiting for transfers between devices, shards(): lax.ppermute(final, 'space', [(i, i ^ k * PAIR) for i in range(space)])  4.71 us
    ppermute x3, starting transfers between devices, shards(): lax.ppermute(final, 'space', [(i, i ^ k * PAIR) for i in range(space)])  3.55 us
    ppermute x7, waiting for transfers between devices, shards(): got.append(lax.ppermute(terms[k], ('dp', 'space'), moves))  3.35 us
    pallas_call x2, Pallas kernels, place(): pl.pallas_call(functools.partial(place_kernel, flip), out_shape=jax.Shape...  2.96 us
    ppermute x1, starting transfers between devices, shards(): others.append(lax.ppermute(near_sum[k].astype(BF16), 'dp', moves))  2.65 us
  transfers between devices with their start and end apart: 15, of which 7 were waited for; matrix products, arithmetic and copies ran while one was open for 0% of the time, Pallas kernels for 17%

profile of v5, /device:TPU:0, one launch (start us, length us, event | category | flops | bytes accessed | tf_op | source)
XLA Modules:
  0.0 50.1 jit_solution(419784011429490412)
XLA Ops:
  0.6 0.9 %dynamic-slice_bitcast_fusion = (bf16[1,320,128]{2,1,0:T(8,128)(2,1)S(1)}, bf16[1,320,128]{2,1,0:T(8,128)(2,1)S(1)}) fusion(bf16[1,8,128,320]{2,3,1,0:T(8,128)(2,1)} %param.3, s32[]{:T(128)S(6)} %select_n.7, bf16[1,8,128,320]{2,3,1,0:T(8,128)(2,1)} %param.4), kind=kLoop, calls=%fused_computation.8 | loop fusion | bytes 327684 | tf_op jit(solution)/shard_map/jit(dynamic_index_in_dim)/dynamic_slice | solution.py:209
  1.6 0.8 %collective-permute-start = (bf16[2,320,128]{2,1,0:T(8,128)(2,1)S(1)}, bf16[2,320,128]{2,1,0:T(8,128)(2,1)S(1)}, u32[]{:S(2)}, u32[]{:S(2)}) collective-permute-start(bf16[2,320,128]{2,1,0:T(8,128)(2,1)S(1)} %pad_maximum_fusion.1.after_ref), channel_id=1, source_target_pairs={{1,2},{2,1},{3,4},{4,3},{5,6},{6,5},{9,10},{10,9},{11,12},{12,11},... | collective-permute-start | bytes 491528 | tf_op jit(solution)/shard_map/ppermute | solution.py:216
  2.9 1.5 %own_terms.1 = (f32[3,320,512]{2,1,0:T(8,128)S(1)}, bf16[2,320,128]{2,1,0:T(8,128)(2,1)S(1)}, bf16[2,160,128]{2,1,0:T(8,128)(2,1)S(1)}) custom-call(bf16[8,320,128]{2,1,0:T(8,128)(2,1)S(1)} %bitcast.32, bf16[8,320,128]{2,1,0:T(8,128)(2,1)S(1)} %bitcast.36), custom_call_target="tpu_custom_call" | custom-call | flops 1887436800 | bytes 4000000 | tf_op jit(solution)/shard_map/own_terms/pallas_call | solution.py:226
  4.5 6.1 %collective-permute-start.1 = (bf16[8,320,128]{2,1,0:T(8,128)(2,1)S(1)}, bf16[8,320,128]{2,1,0:T(8,128)(2,1)S(1)}, u32[]{:S(2)}, u32[]{:S(2)}) collective-permute-start(bf16[8,320,128]{2,1,0:T(8,128)(2,1)S(1)} %bitcast.37), channel_id=1, source_target_pairs={{0,1},{1,0},{2,3},{3,2},{4,5},{5,4},{6,7},{7,6},{8,9},{9,8},{10,11... | collective-permute-start | bytes 1966088 | tf_op jit(solution)/shard_map/ppermute | solution.py:246
  10.6 2.6 %input_grad.2.refs_0_ = bf16[8,320,128]{2,1,0:T(8,128)(2,1)} custom-call(bf16[8,320,128]{2,1,0:T(8,128)(2,1)S(1)} %bitcast.34, bf16[8,320,128]{2,1,0:T(8,128)(2,1)S(1)} %bitcast.38, bf16[2,320,128]{2,1,0:T(8,128)(2,1)S(1)} %collective-permute-done.edge_ref.near_ref, bf16[3,3,320,320]{3,2,1,0:T(8,128)(2,1)S(1)} %copy-done), custom_call_target="tpu_custom_call" | custom-call | flops 943718400 | bytes 3000000 | tf_op jit(solution)/shard_map/input_grad/pallas_call | solution.py:250
  13.3 1.8 %pair_terms.1 = (bf16[2,3,80,128]{3,2,1,0:T(8,128)(2,1)S(1)}, bf16[2,3,80,128]{3,2,1,0:T(8,128)(2,1)S(1)}, bf16[2,3,80,128]{3,2,1,0:T(8,128)(2,1)S(1)}, bf16[2,3...) custom-call(f32[3,320,512]{2,1,0:T(8,128)S(1)} %get-tuple-element.35, ...), custom_call_target="tpu_custom_call" | custom-call | flops 1887436800 | bytes 4000000 | tf_op jit(solution)/shard_map/pair_terms/pallas_call | solution.py:271
  15.1 5.0 %collective-permute-start.3 = (bf16[2,3,80,128]{3,2,1,0:T(8,128)(2,1)S(1)}, bf16[2,3,80,128]{3,2,1,0:T(8,128)(2,1)S(1)}, u32[]{:S(2)}, u32[]{:S(2)}) collective-permute-start(bf16[2,3,80,128]{3,2,1,0:T(8,128)(2,1)S(1)} %get-tuple-element.44), channel_id=1, source_target_pairs={{0,14},{1,15},{2,12},{3,13},{4,10},{5,11},{6,8},{7,9},{8,6},{9,7},... | collective-permute-start | bytes 368648 | tf_op jit(solution)/shard_map/ppermute | solution.py:293
  20.1 0.6 %collective-permute-start.4 = (bf16[2,3,80,128]{3,2,1,0:T(8,128)(2,1)S(1)}, bf16[2,3,80,128]{3,2,1,0:T(8,128)(2,1)S(1)}, u32[]{:S(2)}, u32[]{:S(2)}) collective-permute-start(bf16[2,3,80,128]{3,2,1,0:T(8,128)(2,1)S(1)} %get-tuple-element.45), channel_id=1, source_target_pairs={{0,12},{1,13},{2,14},{3,15},{4,8},{5,9},{6,10},{7,11},{8,4},{9,5},... | collective-permute-start | bytes 368648 | tf_op jit(solution)/shard_map/ppermute | solution.py:293
  20.7 1.6 %collective-permute-start.6 = (bf16[2,3,80,128]{3,2,1,0:T(8,128)(2,1)S(1)}, bf16[2,3,80,128]{3,2,1,0:T(8,128)(2,1)S(1)}, u32[]{:S(2)}, u32[]{:S(2)}) collective-permute-start(bf16[2,3,80,128]{3,2,1,0:T(8,128)(2,1)S(1)} %get-tuple-element.47), channel_id=1, source_target_pairs={{0,8},{1,9},{2,10},{3,11},{4,12},{5,13},{6,14},{7,15},{8,0},{9,1},... | collective-permute-start | bytes 368648 | tf_op jit(solution)/shard_map/ppermute | solution.py:293
  22.3 2.6 %collective-permute-start.7 = (bf16[2,3,80,128]{3,2,1,0:T(8,128)(2,1)S(1)}, bf16[2,3,80,128]{3,2,1,0:T(8,128)(2,1)S(1)}, u32[]{:S(2)}, u32[]{:S(2)}) collective-permute-start(bf16[2,3,80,128]{3,2,1,0:T(8,128)(2,1)S(1)} %get-tuple-element.48), channel_id=1, source_target_pairs={{0,6},{1,7},{2,4},{3,5},{4,2},{5,3},{6,0},{7,1},{8,14},{9,15},{10,... | collective-permute-start | bytes 368648 | tf_op jit(solution)/shard_map/ppermute | solution.py:293
  24.9 1.4 %collective-permute-start.8 = (bf16[2,3,80,128]{3,2,1,0:T(8,128)(2,1)S(1)}, bf16[2,3,80,128]{3,2,1,0:T(8,128)(2,1)S(1)}, u32[]{:S(2)}, u32[]{:S(2)}) collective-permute-start(bf16[2,3,80,128]{3,2,1,0:T(8,128)(2,1)S(1)} %get-tuple-element.49), channel_id=1, source_target_pairs={{0,4},{1,5},{2,6},{3,7},{4,0},{5,1},{6,2},{7,3},{8,12},{9,13},{10,... | collective-permute-start | bytes 368648 | tf_op jit(solution)/shard_map/ppermute | solution.py:293
  26.3 2.1 %collective-permute-done.4 = bf16[2,3,80,128]{3,2,1,0:T(8,128)(2,1)S(1)} collective-permute-done((bf16[2,3,80,128]{3,2,1,0:T(8,128)(2,1)S(1)}, bf16[2,3,80,128]{3,2,1,0:T(8,128)(2,1)S(1)}, u32[]{:S(2)}, u32[]{:S(2)}) %collective-permute-start.4) | collective-permute-done | bytes 122912 | tf_op jit(solution)/shard_map/ppermute | solution.py:293
  28.5 1.0 %collective-permute-start.9 = (bf16[2,3,80,128]{3,2,1,0:T(8,128)(2,1)S(1)}, bf16[2,3,80,128]{3,2,1,0:T(8,128)(2,1)S(1)}, u32[]{:S(2)}, u32[]{:S(2)}) collective-permute-start(bf16[2,3,80,128]{3,2,1,0:T(8,128)(2,1)S(1)} %get-tuple-element.50), channel_id=1, source_target_pairs={{0,2},{1,3},{2,0},{3,1},{4,6},{5,7},{6,4},{7,5},{8,10},{9,11},{10,... | collective-permute-start | bytes 368648 | tf_op jit(solution)/shard_map/ppermute | solution.py:293
  29.5 2.6 %input_grad.3 = bf16[8,320,128]{2,1,0:T(8,128)(2,1)} custom-call(bf16[8,320,128]{2,1,0:T(8,128)(2,1)S(1)} %bitcast.35, bf16[8,320,128]{2,1,0:T(8,128)(2,1)S(1)} %bitcast.39, bf16[1,320,128]{2,1,0:T(8,128)(2,1)S(1)} %constant_dynamic-slice_fusion.edge_ref, bf16[3,3,320,320]{3,2,1,0:T(8,128)(2,1)S(1)} %copy-done, ...), custom_call_target="tpu_custom_call", output_to_operand_aliasing={{}: (4, {})} | custom-call | flops 943718400 | bytes 3000000 | tf_op jit(solution)/shard_map/input_grad/pallas_call | solution.py:250
  32.3 1.0 %collective-permute-done.9 = bf16[2,3,80,128]{3,2,1,0:T(8,128)(2,1)S(1)} collective-permute-done((bf16[2,3,80,128]{3,2,1,0:T(8,128)(2,1)S(1)}, bf16[2,3,80,128]{3,2,1,0:T(8,128)(2,1)S(1)}, u32[]{:S(2)}, u32[]{:S(2)}) %collective-permute-start.9) | collective-permute-done | bytes 122912 | tf_op jit(solution)/shard_map/ppermute | solution.py:293
  33.5 2.6 %collective-permute-start.10 = (bf16[3,80,128]{2,1,0:T(8,128)(2,1)S(1)}, bf16[3,80,128]{2,1,0:T(8,128)(2,1)S(1)}, u32[]{:S(2)}, u32[]{:S(2)}) collective-permute-start(bf16[3,80,128]{2,1,0:T(8,128)(2,1)S(1)} %fusion.3), channel_id=1, source_target_pairs={{0,16},{8,24},{16,0},{24,8},{1,17},{9,25},{17,1},{25,9},{2,18},{10... | collective-permute-start | bytes 184328 | tf_op jit(solution)/shard_map/ppermute | solution.py:304
  36.1 2.5 %collective-permute-done.10 = bf16[3,80,128]{2,1,0:T(8,128)(2,1)S(1)} collective-permute-done((bf16[3,80,128]{2,1,0:T(8,128)(2,1)S(1)}, bf16[3,80,128]{2,1,0:T(8,128)(2,1)S(1)}, u32[]{:S(2)}, u32[]{:S(2)}) %collective-permute-start.10) | collective-permute-done | bytes 61472 | tf_op jit(solution)/shard_map/ppermute | solution.py:304
  38.7 1.3 %collective-permute-start.11 = (bf16[3,80,128]{2,1,0:T(8,128)(2,1)S(1)}, bf16[3,80,128]{2,1,0:T(8,128)(2,1)S(1)}, u32[]{:S(2)}, u32[]{:S(2)}) collective-permute-start(bf16[3,80,128]{2,1,0:T(8,128)(2,1)S(1)} %fusion.2), channel_id=1, source_target_pairs={{0,2},{1,3},{2,0},{3,1},{4,6},{5,7},{6,4},{7,5},{8,10},{9,11},{10,... | collective-permute-start | bytes 184328 | tf_op jit(solution)/shard_map/ppermute | solution.py:312
  40.0 1.9 %collective-permute-start.12 = (bf16[3,80,128]{2,1,0:T(8,128)(2,1)S(1)}, bf16[3,80,128]{2,1,0:T(8,128)(2,1)S(1)}, u32[]{:S(2)}, u32[]{:S(2)}) collective-permute-start(bf16[3,80,128]{2,1,0:T(8,128)(2,1)S(1)} %fusion.2), channel_id=1, source_target_pairs={{0,4},{1,5},{2,6},{3,7},{4,0},{5,1},{6,2},{7,3},{8,12},{9,13},{10,... | collective-permute-start | bytes 184328 | tf_op jit(solution)/shard_map/ppermute | solution.py:312
  42.3 0.7 %collective-permute-done.11 = bf16[3,80,128]{2,1,0:T(8,128)(2,1)S(1)} collective-permute-done((bf16[3,80,128]{2,1,0:T(8,128)(2,1)S(1)}, bf16[3,80,128]{2,1,0:T(8,128)(2,1)S(1)}, u32[]{:S(2)}, u32[]{:S(2)}) %collective-permute-start.11) | collective-permute-done | bytes 61472 | tf_op jit(solution)/shard_map/ppermute | solution.py:312
  43.0 1.2 %collective-permute-done.12 = bf16[3,80,128]{2,1,0:T(8,128)(2,1)S(1)} collective-permute-done((bf16[3,80,128]{2,1,0:T(8,128)(2,1)S(1)}, bf16[3,80,128]{2,1,0:T(8,128)(2,1)S(1)}, u32[]{:S(2)}, u32[]{:S(2)}) %collective-permute-start.12) | collective-permute-done | bytes 61472 | tf_op jit(solution)/shard_map/ppermute | solution.py:312
  44.2 2.8 %collective-permute-done.13 = bf16[3,80,128]{2,1,0:T(8,128)(2,1)S(1)} collective-permute-done((bf16[3,80,128]{2,1,0:T(8,128)(2,1)S(1)}, bf16[3,80,128]{2,1,0:T(8,128)(2,1)S(1)}, u32[]{:S(2)}, u32[]{:S(2)}) %collective-permute-start.13) | collective-permute-done | bytes 61472 | tf_op jit(solution)/shard_map/ppermute | solution.py:312
  47.1 1.5 %place_rows.2.refs_0_ = f32[320,720]{1,0:T(8,128)} custom-call(bf16[4,3,80,128]{3,2,1,0:T(8,128)(2,1)S(1)} %pad_maximum_fusion.parts_ref, bf16[720,720]{1,0:T(8,128)(2,1)S(1)} %pick_rows.1.pick_ref), custom_call_target="tpu_custom_call" | custom-call | flops 165888000 | bytes 1000000 | tf_op jit(solution)/shard_map/place_rows/pallas_call | solution.py:317
  48.6 1.5 %place_rows.3 = f32[320,720]{1,0:T(8,128)} custom-call(bf16[4,3,80,128]{3,2,1,0:T(8,128)(2,1)S(1)} %collective-permute-done.14.parts_ref, bf16[720,720]{1,0:T(8,128)(2,1)S(1)} %pick_rows.1.pick_ref, f32[320,720]{1,0:T(8,128)} %place_rows.2.refs_0_), custom_call_target="tpu_custom_call", output_to_operand_aliasing={{}: (2, {})} | custom-call | flops 165888000 | bytes 1000000 | tf_op jit(solution)/shard_map/place_rows/pallas_call | solution.py:317
  (26 shorter events, 1.4 us)
Async XLA Ops:
  1.6 1.1 %copy-start.1 = (bf16[1,8,128,320]{2,3,1,0:T(8,128)(2,1)S(1)}, bf16[1,8,128,320]{2,3,1,0:T(8,128)(2,1)}, u32[]{:S(2)}) copy-start(bf16[1,8,128,320]{2,3,1,0:T(8,128)(2,1)} %param.3) | copy-start | bytes 1966084
  1.6 1.3 %copy-start.2 = (bf16[1,8,128,320]{2,3,1,0:T(8,128)(2,1)S(1)}, bf16[1,8,128,320]{2,3,1,0:T(8,128)(2,1)}, u32[]{:S(2)}) copy-start(bf16[1,8,128,320]{2,3,1,0:T(8,128)(2,1)} %param.4) | copy-start | bytes 1966084
  1.6 2.8 %collective-permute-start = (bf16[2,320,128]{2,1,0:T(8,128)(2,1)S(1)}, bf16[2,320,128]{2,1,0:T(8,128)(2,1)S(1)}, u32[]{:S(2)}, u32[]{:S(2)}) collective-permute-start(bf16[2,320,128]{2,1,0:T(8,128)(2,1)S(1)} %pad_maximum_fusion.1.after_ref), channel_id=1, source_target_pairs={{1,2},{2,1},{3,4},{4,3},{5,6},{6,5},{9,10},{10,9},{11,12},{12,11},... | collective-permute-start | bytes 491528 | tf_op jit(solution)/shard_map/ppermute | solution.py:216
  2.9 7.7 %copy-start = (bf16[3,3,320,320]{3,2,1,0:T(8,128)(2,1)S(1)}, bf16[3,3,320,320]{3,2,1,0:T(8,128)(2,1)}, u32[]{:S(2)}) copy-start(bf16[3,3,320,320]{3,2,1,0:T(8,128)(2,1)} %kernel_ref.3) | copy-start | bytes 5529604
  4.5 8.8 %collective-permute-start.1 = (bf16[8,320,128]{2,1,0:T(8,128)(2,1)S(1)}, bf16[8,320,128]{2,1,0:T(8,128)(2,1)S(1)}, u32[]{:S(2)}, u32[]{:S(2)}) collective-permute-start(bf16[8,320,128]{2,1,0:T(8,128)(2,1)S(1)} %bitcast.37), channel_id=1, source_target_pairs={{0,1},{1,0},{2,3},{3,2},{4,5},{5,4},{6,7},{7,6},{8,9},{9,8},{10,11... | collective-permute-start | bytes 1966088 | tf_op jit(solution)/shard_map/ppermute | solution.py:246
  10.6 2.7 %collective-permute-start.2 = (bf16[8,320,128]{2,1,0:T(8,128)(2,1)S(1)}, bf16[8,320,128]{2,1,0:T(8,128)(2,1)S(1)}, u32[]{:S(2)}, u32[]{:S(2)}) collective-permute-start(bf16[8,320,128]{2,1,0:T(8,128)(2,1)S(1)} %bitcast.33), channel_id=1, source_target_pairs={{0,1},{1,0},{2,3},{3,2},{4,5},{5,4},{6,7},{7,6},{8,9},{9,8},{10,11... | collective-permute-start | bytes 1966088 | tf_op jit(solution)/shard_map/ppermute | solution.py:247
  15.1 9.8 %collective-permute-start.3 = (bf16[2,3,80,128]{3,2,1,0:T(8,128)(2,1)S(1)}, bf16[2,3,80,128]{3,2,1,0:T(8,128)(2,1)S(1)}, u32[]{:S(2)}, u32[]{:S(2)}) collective-permute-start(bf16[2,3,80,128]{3,2,1,0:T(8,128)(2,1)S(1)} %get-tuple-element.44), channel_id=1, source_target_pairs={{0,14},{1,15},{2,12},{3,13},{4,10},{5,11},{6,8},{7,9},{8,6},{9,7},... | collective-permute-start | bytes 368648 | tf_op jit(solution)/shard_map/ppermute | solution.py:293
  20.1 8.4 %collective-permute-start.4 = (bf16[2,3,80,128]{3,2,1,0:T(8,128)(2,1)S(1)}, bf16[2,3,80,128]{3,2,1,0:T(8,128)(2,1)S(1)}, u32[]{:S(2)}, u32[]{:S(2)}) collective-permute-start(bf16[2,3,80,128]{3,2,1,0:T(8,128)(2,1)S(1)} %get-tuple-element.45), channel_id=1, source_target_pairs={{0,12},{1,13},{2,14},{3,15},{4,8},{5,9},{6,10},{7,11},{8,4},{9,5},... | collective-permute-start | bytes 368648 | tf_op jit(solution)/shard_map/ppermute | solution.py:293
  20.7 11.4 %collective-permute-start.5 = (bf16[2,3,80,128]{3,2,1,0:T(8,128)(2,1)S(1)}, bf16[2,3,80,128]{3,2,1,0:T(8,128)(2,1)S(1)}, u32[]{:S(2)}, u32[]{:S(2)}) collective-permute-start(bf16[2,3,80,128]{3,2,1,0:T(8,128)(2,1)S(1)} %get-tuple-element.46), channel_id=1, source_target_pairs={{0,10},{1,11},{2,8},{3,9},{4,14},{5,15},{6,12},{7,13},{8,2},{9,3},... | collective-permute-start | bytes 368648 | tf_op jit(solution)/shard_map/ppermute | solution.py:293
  20.7 11.4 %collective-permute-start.6 = (bf16[2,3,80,128]{3,2,1,0:T(8,128)(2,1)S(1)}, bf16[2,3,80,128]{3,2,1,0:T(8,128)(2,1)S(1)}, u32[]{:S(2)}, u32[]{:S(2)}) collective-permute-start(bf16[2,3,80,128]{3,2,1,0:T(8,128)(2,1)S(1)} %get-tuple-element.47), channel_id=1, source_target_pairs={{0,8},{1,9},{2,10},{3,11},{4,12},{5,13},{6,14},{7,15},{8,0},{9,1},... | collective-permute-start | bytes 368648 | tf_op jit(solution)/shard_map/ppermute | solution.py:293
  22.3 9.9 %collective-permute-start.7 = (bf16[2,3,80,128]{3,2,1,0:T(8,128)(2,1)S(1)}, bf16[2,3,80,128]{3,2,1,0:T(8,128)(2,1)S(1)}, u32[]{:S(2)}, u32[]{:S(2)}) collective-permute-start(bf16[2,3,80,128]{3,2,1,0:T(8,128)(2,1)S(1)} %get-tuple-element.48), channel_id=1, source_target_pairs={{0,6},{1,7},{2,4},{3,5},{4,2},{5,3},{6,0},{7,1},{8,14},{9,15},{10,... | collective-permute-start | bytes 368648 | tf_op jit(solution)/shard_map/ppermute | solution.py:293
  24.9 7.4 %collective-permute-start.8 = (bf16[2,3,80,128]{3,2,1,0:T(8,128)(2,1)S(1)}, bf16[2,3,80,128]{3,2,1,0:T(8,128)(2,1)S(1)}, u32[]{:S(2)}, u32[]{:S(2)}) collective-permute-start(bf16[2,3,80,128]{3,2,1,0:T(8,128)(2,1)S(1)} %get-tuple-element.49), channel_id=1, source_target_pairs={{0,4},{1,5},{2,6},{3,7},{4,0},{5,1},{6,2},{7,3},{8,12},{9,13},{10,... | collective-permute-start | bytes 368648 | tf_op jit(solution)/shard_map/ppermute | solution.py:293
  28.5 4.9 %collective-permute-start.9 = (bf16[2,3,80,128]{3,2,1,0:T(8,128)(2,1)S(1)}, bf16[2,3,80,128]{3,2,1,0:T(8,128)(2,1)S(1)}, u32[]{:S(2)}, u32[]{:S(2)}) collective-permute-start(bf16[2,3,80,128]{3,2,1,0:T(8,128)(2,1)S(1)} %get-tuple-element.50), channel_id=1, source_target_pairs={{0,2},{1,3},{2,0},{3,1},{4,6},{5,7},{6,4},{7,5},{8,10},{9,11},{10,... | collective-permute-start | bytes 368648 | tf_op jit(solution)/shard_map/ppermute | solution.py:293
  33.5 5.2 %collective-permute-start.10 = (bf16[3,80,128]{2,1,0:T(8,128)(2,1)S(1)}, bf16[3,80,128]{2,1,0:T(8,128)(2,1)S(1)}, u32[]{:S(2)}, u32[]{:S(2)}) collective-permute-start(bf16[3,80,128]{2,1,0:T(8,128)(2,1)S(1)} %fusion.3), channel_id=1, source_target_pairs={{0,16},{8,24},{16,0},{24,8},{1,17},{9,25},{17,1},{25,9},{2,18},{10... | collective-permute-start | bytes 184328 | tf_op jit(solution)/shard_map/ppermute | solution.py:304
  38.7 4.3 %collective-permute-start.11 = (bf16[3,80,128]{2,1,0:T(8,128)(2,1)S(1)}, bf16[3,80,128]{2,1,0:T(8,128)(2,1)S(1)}, u32[]{:S(2)}, u32[]{:S(2)}) collective-permute-start(bf16[3,80,128]{2,1,0:T(8,128)(2,1)S(1)} %fusion.2), channel_id=1, source_target_pairs={{0,2},{1,3},{2,0},{3,1},{4,6},{5,7},{6,4},{7,5},{8,10},{9,11},{10,... | collective-permute-start | bytes 184328 | tf_op jit(solution)/shard_map/ppermute | solution.py:312
  40.0 4.2 %collective-permute-start.12 = (bf16[3,80,128]{2,1,0:T(8,128)(2,1)S(1)}, bf16[3,80,128]{2,1,0:T(8,128)(2,1)S(1)}, u32[]{:S(2)}, u32[]{:S(2)}) collective-permute-start(bf16[3,80,128]{2,1,0:T(8,128)(2,1)S(1)} %fusion.2), channel_id=1, source_target_pairs={{0,4},{1,5},{2,6},{3,7},{4,0},{5,1},{6,2},{7,3},{8,12},{9,13},{10,... | collective-permute-start | bytes 184328 | tf_op jit(solution)/shard_map/ppermute | solution.py:312
  41.9 5.1 %collective-permute-start.13 = (bf16[3,80,128]{2,1,0:T(8,128)(2,1)S(1)}, bf16[3,80,128]{2,1,0:T(8,128)(2,1)S(1)}, u32[]{:S(2)}, u32[]{:S(2)}) collective-permute-start(bf16[3,80,128]{2,1,0:T(8,128)(2,1)S(1)} %fusion.2), channel_id=1, source_target_pairs={{0,6},{1,7},{2,4},{3,5},{4,2},{5,3},{6,0},{7,1},{8,14},{9,15},{10,... | collective-permute-start | bytes 184328 | tf_op jit(solution)/shard_map/ppermute | solution.py:312
  47.0 1.6 %collective-permute-start.14 = (bf16[4,3,80,128]{3,2,1,0:T(8,128)(2,1)S(1)}, bf16[4,3,80,128]{3,2,1,0:T(8,128)(2,1)S(1)}, u32[]{:S(2)}, u32[]{:S(2)}) collective-permute-start(bf16[4,3,80,128]{3,2,1,0:T(8,128)(2,1)S(1)} %pad_maximum_fusion.parts_ref), channel_id=1, source_target_pairs={{0,1},{1,0},{2,3},{3,2},{4,5},{5,4},{6,7},{7,6},{8,9},{9,8},{10,11... | collective-permute-start | bytes 737288 | tf_op jit(solution)/shard_map/ppermute | solution.py:314

commit v6 on v5

--- a/solution.py
+++ b/solution.py
@@ -75,42 +75,52 @@
         term_ref[a] = lax.dot_general(act_s[...], taps_s[:, at : at + rows * width], NT, preferred_element_type=F32)
 
 
-def pair_kernel(term_ref, act_edge_ref, grad_edge_ref, their_pre_ref, their_grad_ref, near_ref, *refs):
-    out_refs, (act_s, taps_s, term_s) = refs[: PLANE * NEAR], refs[PLANE * NEAR :]
+def pair_kernel(term_ref, act_edge_ref, grad_edge_ref, their_pre_ref, their_grad_ref, out_ref, act_s, taps_s):
     rows, chans, width = their_pre_ref.shape
     half = chans // PAIR
-    outers, _, block, _ = out_refs[0].shape
     core = my_core()
     first = core == 0
     mine = pl.ds(pl.multiple_of(core * half, half), half)
+    zero = jnp.zeros((half, width), BF16)
+    zero_act = jnp.zeros((chans, width), BF16)
     taps_s[3 * half :, :] = jnp.zeros((taps_s.shape[0] - 3 * half, taps_s.shape[1]), BF16)
+    act_s[:, :width] = jnp.where(first, zero_act, act_edge_ref[0])
     for r in range(rows):
-        act_s[:, (2 + r) * width : (3 + r) * width] = silu(their_pre_ref[r])
-    near_act = silu(near_ref[1])
-    their_top = act_s[:, 2 * width : 3 * width]
-    their_end = act_s[:, (rows + 1) * width : (rows + 2) * width]
-    extra = ((0, their_top, act_edge_ref[0]), (1, act_edge_ref[0], near_act))
-    extra += ((rows + 2, act_edge_ref[1], their_end), (rows + 3, near_act, act_edge_ref[1]))
-    for slot, if_first, if_second in extra:
-        act_s[:, slot * width : (slot + 1) * width] = jnp.where(first, if_first, if_second)
-    near_grad = near_ref[0, mine, :]
-    their_top, their_end = their_grad_ref[0, mine, :], their_grad_ref[rows - 1, mine, :]
-    zero = jnp.zeros((half, width), BF16)
-    put_taps(taps_s, 0, jnp.where(first, grad_edge_ref[1], their_end))
-    put_taps(taps_s, 1, jnp.where(first, near_grad, grad_edge_ref[1]))
-    put_taps(taps_s, 2, zero)
+        act_s[:, (1 + r) * width : (2 + r) * width] = silu(their_pre_ref[r])
+    act_s[:, (rows + 1) * width :] = jnp.where(first, act_edge_ref[1], zero_act)
+    put_taps(taps_s, 0, their_grad_ref[rows - 1, mine, :])
+    put_taps(taps_s, 1, jnp.where(first, grad_edge_ref[1], zero))
     for r in range(rows):
-        put_taps(taps_s, 3 + r, their_grad_ref[r, mine, :])
-    put_taps(taps_s, rows + 3, zero)
-    put_taps(taps_s, rows + 4, jnp.where(first, their_top, grad_edge_ref[0]))
-    put_taps(taps_s, rows + 5, jnp.where(first, grad_edge_ref[0], near_grad))
-    for a, (left, right, at) in enumerate(((2, rows + 4, 4), (2, rows + 2, 3), (0, rows + 2, 0))):
-        term = term_ref[a] + lax.dot_general(
+        put_taps(taps_s, 2 + r, their_grad_ref[r, mine, :])
+    put_taps(taps_s, rows + 2, jnp.where(first, zero, grad_edge_ref[0]))
+    put_taps(taps_s, rows + 3, their_grad_ref[0, mine, :])
+    for a, (left, right, at) in enumerate(((1, rows + 2, 3), (1, rows + 1, 2), (0, rows + 1, 0))):
+        out_ref[a] = term_ref[a] + lax.dot_general(
             act_s[:, left * width : right * width],
             taps_s[:, at * width : (at + right - left) * width],
             NT,
             preferred_element_type=F32,
         )
+
+
+def edge_kernel(term_ref, act_edge_ref, grad_edge_ref, near_ref, *refs):
+    out_refs, (taps_s, term_s) = refs[: PLANE * NEAR], refs[PLANE * NEAR :]
+    _, chans, width = near_ref.shape
+    half = chans // PAIR
+    outers, _, block, _ = out_refs[0].shape
+    core = my_core()
+    first = core == 0
+    near_act = silu(near_ref[1])
+    near_grad = near_ref[0, pl.ds(pl.multiple_of(core * half, half), half), :]
+    taps_s[3 * half :, :] = jnp.zeros((taps_s.shape[0] - 3 * half, taps_s.shape[1]), BF16)
+    put_taps(taps_s, 0, jnp.where(first, grad_edge_ref[0], near_grad))
+    put_taps(taps_s, 1, jnp.where(first, near_grad, grad_edge_ref[1]))
+    acts = {0: jnp.where(first, near_act, act_edge_ref[1]), 2: jnp.where(first, act_edge_ref[0], near_act)}
+    for a in range(3):
+        term = term_ref[a]
+        if a in acts:
+            taps = taps_s[:, a // 2 * width : (a // 2 + 1) * width]
+            term += lax.dot_general(acts[a], taps, NT, preferred_element_type=F32)
         for p in range(PLANE):
             for z in range(NEAR * outers):
                 term_s[z % NEAR * PLANE + p, z // NEAR, a] = term[
@@ -157,27 +167,29 @@
 
 
 def pick_kernel(after_ref, out_ref):
-    taps = 9
-    block = out_ref.shape[0] // taps
-    k = lax.broadcasted_iota(jnp.int32, (block, taps * block), 0)
-    j = lax.broadcasted_iota(jnp.int32, (block, taps * block), 1)
-    for t in range(taps):
-        out_ref[t * block : (t + 1) * block, :] = jnp.where(j - taps * k == t, 1.0, 0.0).astype(BF16)
+    group = out_ref.shape[0] // 9
+    k = lax.broadcasted_iota(jnp.int32, (group, 9 * group), 0)
+    j = lax.broadcasted_iota(jnp.int32, (group, 9 * group), 1)
+    for t in range(9):
+        out_ref[t * group : (t + 1) * group, :] = jnp.where(j - 9 * k == t, 1.0, 0.0)
 
 
 def place_kernel(flip, parts_ref, pick_ref, *refs):
-    out_hbm, wide_s, rows_s, out_s, sem = refs[-5:]
+    out_hbm, wide_s, out_s, sem = refs[-4:]
     _, _, block, _ = parts_ref.shape
     half = out_s.shape[0]
+    width = pick_ref.shape[0]
+    group = width // 9
     for k in range(PLANE):
         lanes = pl.ds(pl.multiple_of((plane_index() ^ k) * LANES, LANES), LANES)
         wide_s[:, :, lanes] = parts_ref[k].astype(F32)
-    for a in range(3):
-        for b in range(3):
-            t = 3 * a + b
-            rows_s[t * block : (t + 1) * block, :] = wide_s[a, :, b * half : (b + 1) * half]
-    dims = (((0,), (0,)), ((), ()))
-    out_s[...] = lax.dot_general(rows_s[...].astype(BF16), pick_ref[...], dims, preferred_element_type=F32)
+    pick = pick_ref[...].astype(BF16)
+    for g in range(block // group):
+        rows = [wide_s[t // 3, g * group : (g + 1) * group, t % 3 * half : (t % 3 + 1) * half] for t in range(9)]
+        rows = jnp.concatenate(rows, axis=0).astype(BF16)
+        out_s[:, g * width : (g + 1) * width] = lax.dot_general(
+            rows, pick, (((0,), (0,)), ((), ())), preferred_element_type=F32
+        )
     count = sem.shape[0]
     step = half // count
     first = (my_core() ^ flip) * half
@@ -198,6 +210,7 @@
     outer = space // inner
     block = chans // blocks
     half = chans // PAIR
+    group = 16 if block % 16 == 0 else block
     far = blocks // NEAR
     factor = float(images * rows * width * space * blocks) ** (-0.5)
     params = pltpu.CompilerParams(vmem_limit_bytes=VMEM_LIMIT)
@@ -214,15 +227,19 @@
         return [(i, j) for i, j in moves if 0 <= j < space]
 
     near_row = lax.ppermute(edge, "space", inside(beyond))
+    _, my_pre, my_grad = lax.optimization_barrier((edge, pre, grad))
+    their_grad = lax.ppermute(my_grad, "space", pairs)
+    their_pre = lax.ppermute(my_pre, "space", pairs)
     pick = pl.pallas_call(
         pick_kernel,
-        out_shape=jax.ShapeDtypeStruct((9 * block, 9 * block), BF16),
+        out_shape=jax.ShapeDtypeStruct((9 * group, 9 * group), F32),
         in_specs=[anywhere()],
         out_specs=vmem(),
         compiler_params=params,
         cost_estimate=pl.CostEstimate(flops=flops, bytes_accessed=4000000, transcendentals=0),
         name="pick_rows",
     )(edge)
+    pick, own_pre, own_grad = lax.optimization_barrier((pick, pre, grad))
     own, act_edge, grad_edge = pl.pallas_call(
         own_kernel,
         out_shape=(
@@ -239,12 +256,8 @@
         compiler_params=params,
         cost_estimate=pl.CostEstimate(flops=flops, bytes_accessed=4000000, transcendentals=rows * width * chans),
         name="own_terms",
-    )(pre, grad)
-    near_row, pick, own, act_edge, grad_edge, my_pre, my_grad = lax.optimization_barrier(
-        (near_row, pick, own, act_edge, grad_edge, pre, grad)
-    )
-    their_grad = lax.ppermute(my_grad, "space", pairs)
-    their_pre = lax.ppermute(my_pre, "space", pairs)
+    )(own_pre, own_grad)
+
     def input_part(side, edge_rows, *before):
         count = rows // 2
         return pl.pallas_call(
@@ -265,26 +278,36 @@
             name="input_grad",
         )(pre, grad, edge_rows, kernel, *before)
 
-    in_grad = input_part(0, near_row)
-    their_grad, their_pre, in_grad = lax.optimization_barrier((their_grad, their_pre, in_grad))
     piece = jax.ShapeDtypeStruct((far, 3, block, LANES), BF16)
-    terms = pl.pallas_call(
+    term = pl.pallas_call(
         pair_kernel,
-        out_shape=(piece,) * (NEAR * PLANE),
-        in_specs=[vmem()] * 6,
-        out_specs=(vmem(),) * (NEAR * PLANE),
+        out_shape=jax.ShapeDtypeStruct((3, chans, PLANE * LANES), F32),
+        in_specs=[vmem()] * 5,
+        out_specs=vmem(),
         scratch_shapes=[
-            pltpu.VMEM((chans, (rows + 4) * width), BF16),
-            pltpu.VMEM((PLANE * LANES, (rows + 6) * width), BF16),
-            pltpu.VMEM((NEAR * PLANE, far, 3, block, LANES), BF16),
+            pltpu.VMEM((chans, (rows + 2) * width), BF16),
+            pltpu.VMEM((PLANE * LANES, (rows + 4) * width), BF16),
         ],
         compiler_params=params,
         cost_estimate=pl.CostEstimate(flops=flops, bytes_accessed=4000000, transcendentals=rows * width * chans),
         name="pair_terms",
-    )(own, act_edge, grad_edge, their_pre, their_grad, near_row)
+    )(own, act_edge, grad_edge, their_pre, their_grad)
+    terms = pl.pallas_call(
+        edge_kernel,
+        out_shape=(piece,) * (NEAR * PLANE),
+        in_specs=[vmem()] * 4,
+        out_specs=(vmem(),) * (NEAR * PLANE),
+        scratch_shapes=[
+            pltpu.VMEM((PLANE * LANES, 2 * width), BF16),
+            pltpu.VMEM((NEAR * PLANE, far, 3, block, LANES), BF16),
+        ],
+        compiler_params=params,
+        cost_estimate=pl.CostEstimate(flops=flops // 8, bytes_accessed=4000000, transcendentals=width * chans),
+        name="edge_terms",
+    )(term, act_edge, grad_edge, near_row)
 
     got = [terms[0]]
-    for k in range(NEAR * PLANE - 1, 0, -1):
+    for k in (3, 4, 7, 5, 6, 2, 1):
         moves = []
         for z in range(blocks):
             for i in range(space):
@@ -293,15 +316,16 @@
         got.append(lax.ppermute(terms[k], ("dp", "space"), moves))
 
 
+    in_grad = input_part(0, near_row)
+    *got, in_grad = lax.optimization_barrier((*got, in_grad))
     their_edge = lax.dynamic_index_in_dim(their_grad, my_core() * (rows - 1), 0)
-    in_grad = input_part(1, their_edge, in_grad)
-    *got, in_grad = lax.optimization_barrier((*got, in_grad))
-
     near_sum = sum(part.astype(F32) for part in got)
     others = []
     for k in range(1, far):
         moves = [(z, z ^ (k * NEAR)) for z in range(blocks)]
         others.append(lax.ppermute(near_sum[k].astype(BF16), "dp", moves))
+    in_grad = input_part(1, their_edge, in_grad)
+    *others, in_grad = lax.optimization_barrier((*others, in_grad))
     total = near_sum[0] + sum(other.astype(F32) for other in others)
     total = total * factor
     if outer > 1:
@@ -321,7 +345,6 @@
             out_specs=anywhere(),
             scratch_shapes=[
                 pltpu.VMEM((3, block, PLANE * LANES), F32),
-                pltpu.VMEM((9 * block, half), F32),
                 pltpu.VMEM((half, 9 * block), F32),
                 pltpu.SemaphoreType.DMA((4,)),
             ],

time: 50.3 us -> 45.3 us (0.901)
  starting transfers between devices: 25.5 us -> 22 us
  waiting for transfers between devices: 10.6 us -> 9.03 us
    ppermute x1, starting transfers between devices: 6.13 us -> 0.08 us  [shards(): their_grad = lax.ppermute(my_grad, 'space', pairs)]
    ppermute x7, starting transfers between devices: 12.3 us -> 14.5 us  [shards(): got.append(lax.ppermute(terms[k], ('dp', 'space'), moves))]
    ppermute x1, waiting for transfers between devices: 2.54 us -> 1.05 us  [shards(): others.append(lax.ppermute(near_sum[k].astype(BF16), 'dp', moves))]
    ppermute x3, waiting for transfers between devices: 4.71 us -> 3.5 us  [shards(): lax.ppermute(final, 'space', [(i, i ^ k * PAIR) for i in range(space)])]
    ppermute x7, waiting for transfers between devices: 3.35 us -> 3.93 us  [shards(): got.append(lax.ppermute(terms[k], ('dp', 'space'), moves))]
    ppermute x1, waiting for transfers between devices: 0.01 us -> 0.53 us  [shards(): their_grad = lax.ppermute(my_grad, 'space', pairs)]
    ppermute x1, starting transfers between devices: 0.01 us -> 0.52 us  [shards(): their_pre = lax.ppermute(my_pre, 'space', pairs)]
    pallas_call x2 -> x3, Pallas kernels: 2.02 us -> 2.23 us  [the longest x1 1.7 us: shards(): pl.pallas_call(pair_kernel, out_shape=jax.ShapeDtypeStruct((3, chans, PLA...]
  transfers between devices with their start and end apart: 15 -> 15, of which waited for: 7 -> 9; matrix products, arithmetic and copies ran while one was open for 0% -> 0% of each run, Pallas kernels for 17% -> 22%
where the time goes in v6:
time: 45.3 us; the launch traced here: 45.1 us
  starting transfers between devices  22 us (49%)
  Pallas kernels  12 us (26%)
  waiting for transfers between devices  9.03 us (20%)
  local copies, waits for them, and re-layouts  0.99 us (2%)
  between operations  0.82 us (2%)
    ppermute x7, starting transfers between devices, shards(): got.append(lax.ppermute(terms[k], ('dp', 'space'), moves))  14.5 us
    pallas_call x2, Pallas kernels, input_part(): pl.pallas_call(functools.partial(input_kernel, side), out_shape=jax.Shape...  5.18 us
    ppermute x7, waiting for transfers between devices, shards(): got.append(lax.ppermute(terms[k], ('dp', 'space'), moves))  3.93 us
    ppermute x3, starting transfers between devices, shards(): lax.ppermute(final, 'space', [(i, i ^ k * PAIR) for i in range(space)])  3.55 us
    ppermute x3, waiting for transfers between devices, shards(): lax.ppermute(final, 'space', [(i, i ^ k * PAIR) for i in range(space)])  3.5 us
    pallas_call x2, Pallas kernels, place(): pl.pallas_call(functools.partial(place_kernel, flip), out_shape=jax.Shape...  3.03 us
    ppermute x1, starting transfers between devices, shards(): others.append(lax.ppermute(near_sum[k].astype(BF16), 'dp', moves))  2.65 us
    pallas_call x1, Pallas kernels, shards(): pl.pallas_call(pair_kernel, out_shape=jax.ShapeDtypeStruct((3, chans, PLA...  1.7 us
  transfers between devices with their start and end apart: 15, of which 9 were waited for; matrix products, arithmetic and copies ran while one was open for 0% of the time, Pallas kernels for 22%

profile of v6, /device:TPU:0, one launch (start us, length us, event | category | flops | bytes accessed | tf_op | source)
XLA Modules:
  0.0 45.1 jit_solution(16781370989542853341)
XLA Ops:
  0.6 0.9 %dynamic-slice_bitcast_fusion = (bf16[1,320,128]{2,1,0:T(8,128)(2,1)S(1)}, bf16[1,320,128]{2,1,0:T(8,128)(2,1)S(1)}) fusion(bf16[1,8,128,320]{2,3,1,0:T(8,128)(2,1)} %param.3, s32[]{:T(128)S(6)} %select_n.7, bf16[1,8,128,320]{2,3,1,0:T(8,128)(2,1)} %param.4), kind=kLoop, calls=%fused_computation.8 | loop fusion | bytes 327684 | tf_op jit(solution)/shard_map/jit(dynamic_index_in_dim)/dynamic_slice | solution.py:222
  1.6 0.5 %collective-permute-start = (bf16[8,320,128]{2,1,0:T(8,128)(2,1)}, bf16[8,320,128]{2,1,0:T(8,128)(2,1)S(1)}, u32[]{:S(2)}, u32[]{:S(2)}) collective-permute-start(bf16[8,320,128]{2,1,0:T(8,128)(2,1)} %bitcast.32), channel_id=1, source_target_pairs={{0,1},{1,0},{2,3},{3,2},{4,5},{5,4},{6,7},{7,6},{8,9},{9,8},{10,11... | collective-permute-start | bytes 1966088 | tf_op jit(solution)/shard_map/ppermute | solution.py:232
  2.2 0.7 %collective-permute-start.2 = (bf16[2,320,128]{2,1,0:T(8,128)(2,1)S(1)}, bf16[2,320,128]{2,1,0:T(8,128)(2,1)S(1)}, u32[]{:S(2)}, u32[]{:S(2)}) collective-permute-start(bf16[2,320,128]{2,1,0:T(8,128)(2,1)S(1)} %pad_maximum_fusion.1.after_ref), channel_id=1, source_target_pairs={{1,2},{2,1},{3,4},{4,3},{5,6},{6,5},{9,10},{10,9},{11,12},{12,11},... | collective-permute-start | bytes 491528 | tf_op jit(solution)/shard_map/ppermute | solution.py:229
  2.9 1.5 %own_terms.1 = (f32[3,320,512]{2,1,0:T(8,128)S(1)}, bf16[2,320,128]{2,1,0:T(8,128)(2,1)S(1)}, bf16[2,160,128]{2,1,0:T(8,128)(2,1)S(1)}) custom-call(bf16[8,320,128]{2,1,0:T(8,128)(2,1)S(1)} %bitcast.33, bf16[8,320,128]{2,1,0:T(8,128)(2,1)S(1)} %bitcast.37), custom_call_target="tpu_custom_call" | custom-call | flops 1887436800 | bytes 4000000 | tf_op jit(solution)/shard_map/own_terms/pallas_call | solution.py:243
  4.5 0.5 %collective-permute-done.1.their_grad_ref = bf16[8,320,128]{2,1,0:T(8,128)(2,1)S(1)} collective-permute-done((bf16[8,320,128]{2,1,0:T(8,128)(2,1)}, bf16[8,320,128]{2,1,0:T(8,128)(2,1)S(1)}, u32[]{:S(2)}, u32[]{:S(2)}) %collective-permute-start.1) | collective-permute-done | bytes 655392 | tf_op jit(solution)/shard_map/ppermute | solution.py:231
  5.0 1.7 %pair_terms.1.term_ref = f32[3,320,512]{2,1,0:T(8,128)S(1)} custom-call(f32[3,320,512]{2,1,0:T(8,128)S(1)} %get-tuple-element.31.term_ref, bf16[2,320,128]{2,1,0:T(8,128)(2,1)S(1)} %get-tuple-element.32.act_edge_ref, bf16[2,160,128]{2,1,0:T(8,128)(2,1)S(1)} %get-tuple-element.33.grad_edge_ref, bf16[8,320,128]{2,1,0:T(8,128)(2,1)S(1)} %collective-permute-done.their_pre_ref, ...), custom_call_target="tpu_custom_call" | custom-call | flops 1887436800 | bytes 4000000 | tf_op jit(solution)/shard_map/pair_terms/pallas_call | solution.py:282
  6.8 0.5 %edge_terms.1 = (bf16[2,3,80,128]{3,2,1,0:T(8,128)(2,1)S(1)}, bf16[2,3,80,128]{3,2,1,0:T(8,128)(2,1)S(1)}, bf16[2,3,80,128]{3,2,1,0:T(8,128)(2,1)S(1)}, bf16[2,3...) custom-call(f32[3,320,512]{2,1,0:T(8,128)S(1)} %pair_terms.1.term_re, ...), custom_call_target="tpu_custom_call" | custom-call | flops 235929600 | bytes 4000000 | tf_op jit(solution)/shard_map/edge_terms/pallas_call | solution.py:295
  7.3 7.6 %collective-permute-start.3 = (bf16[2,3,80,128]{3,2,1,0:T(8,128)(2,1)S(1)}, bf16[2,3,80,128]{3,2,1,0:T(8,128)(2,1)S(1)}, u32[]{:S(2)}, u32[]{:S(2)}) collective-permute-start(bf16[2,3,80,128]{3,2,1,0:T(8,128)(2,1)S(1)} %get-tuple-element.37), channel_id=1, source_target_pairs={{0,6},{1,7},{2,4},{3,5},{4,2},{5,3},{6,0},{7,1},{8,14},{9,15},{10,... | collective-permute-start | bytes 368648 | tf_op jit(solution)/shard_map/ppermute | solution.py:316
  14.9 1.6 %collective-permute-start.4 = (bf16[2,3,80,128]{3,2,1,0:T(8,128)(2,1)S(1)}, bf16[2,3,80,128]{3,2,1,0:T(8,128)(2,1)S(1)}, u32[]{:S(2)}, u32[]{:S(2)}) collective-permute-start(bf16[2,3,80,128]{3,2,1,0:T(8,128)(2,1)S(1)} %get-tuple-element.38), channel_id=1, source_target_pairs={{0,8},{1,9},{2,10},{3,11},{4,12},{5,13},{6,14},{7,15},{8,0},{9,1},... | collective-permute-start | bytes 368648 | tf_op jit(solution)/shard_map/ppermute | solution.py:316
  16.4 1.9 %collective-permute-start.6 = (bf16[2,3,80,128]{3,2,1,0:T(8,128)(2,1)S(1)}, bf16[2,3,80,128]{3,2,1,0:T(8,128)(2,1)S(1)}, u32[]{:S(2)}, u32[]{:S(2)}) collective-permute-start(bf16[2,3,80,128]{3,2,1,0:T(8,128)(2,1)S(1)} %get-tuple-element.40), channel_id=1, source_target_pairs={{0,10},{1,11},{2,8},{3,9},{4,14},{5,15},{6,12},{7,13},{8,2},{9,3},... | collective-permute-start | bytes 368648 | tf_op jit(solution)/shard_map/ppermute | solution.py:316
  18.4 2.4 %collective-permute-start.7 = (bf16[2,3,80,128]{3,2,1,0:T(8,128)(2,1)S(1)}, bf16[2,3,80,128]{3,2,1,0:T(8,128)(2,1)S(1)}, u32[]{:S(2)}, u32[]{:S(2)}) collective-permute-start(bf16[2,3,80,128]{3,2,1,0:T(8,128)(2,1)S(1)} %get-tuple-element.41), channel_id=1, source_target_pairs={{0,12},{1,13},{2,14},{3,15},{4,8},{5,9},{6,10},{7,11},{8,4},{9,5},... | collective-permute-start | bytes 368648 | tf_op jit(solution)/shard_map/ppermute | solution.py:316
  20.8 1.0 %collective-permute-start.9 = (bf16[2,3,80,128]{3,2,1,0:T(8,128)(2,1)S(1)}, bf16[2,3,80,128]{3,2,1,0:T(8,128)(2,1)S(1)}, u32[]{:S(2)}, u32[]{:S(2)}) collective-permute-start(bf16[2,3,80,128]{3,2,1,0:T(8,128)(2,1)S(1)} %get-tuple-element.43), channel_id=1, source_target_pairs={{0,2},{1,3},{2,0},{3,1},{4,6},{5,7},{6,4},{7,5},{8,10},{9,11},{10,... | collective-permute-start | bytes 368648 | tf_op jit(solution)/shard_map/ppermute | solution.py:316
  21.8 2.6 %input_grad.2.refs_0_ = bf16[8,320,128]{2,1,0:T(8,128)(2,1)} custom-call(bf16[8,320,128]{2,1,0:T(8,128)(2,1)S(1)} %bitcast.34, bf16[8,320,128]{2,1,0:T(8,128)(2,1)S(1)} %bitcast.38, bf16[2,320,128]{2,1,0:T(8,128)(2,1)S(1)} %collective-permute-done.2.near_ref.edge_ref, bf16[3,3,320,320]{3,2,1,0:T(8,128)(2,1)S(1)} %copy-done), custom_call_target="tpu_custom_call" | custom-call | flops 943718400 | bytes 3000000 | tf_op jit(solution)/shard_map/input_grad/pallas_call | solution.py:263
  24.8 3.0 %collective-permute-done.7 = bf16[2,3,80,128]{3,2,1,0:T(8,128)(2,1)S(1)} collective-permute-done((bf16[2,3,80,128]{3,2,1,0:T(8,128)(2,1)S(1)}, bf16[2,3,80,128]{3,2,1,0:T(8,128)(2,1)S(1)}, u32[]{:S(2)}, u32[]{:S(2)}) %collective-permute-start.7) | collective-permute-done | bytes 122912 | tf_op jit(solution)/shard_map/ppermute | solution.py:316
  27.8 0.5 %collective-permute-done.8 = bf16[2,3,80,128]{3,2,1,0:T(8,128)(2,1)S(1)} collective-permute-done((bf16[2,3,80,128]{3,2,1,0:T(8,128)(2,1)S(1)}, bf16[2,3,80,128]{3,2,1,0:T(8,128)(2,1)S(1)}, u32[]{:S(2)}, u32[]{:S(2)}) %collective-permute-start.8) | collective-permute-done | bytes 122912 | tf_op jit(solution)/shard_map/ppermute | solution.py:316
  28.5 2.7 %collective-permute-start.10 = (bf16[3,80,128]{2,1,0:T(8,128)(2,1)S(1)}, bf16[3,80,128]{2,1,0:T(8,128)(2,1)S(1)}, u32[]{:S(2)}, u32[]{:S(2)}) collective-permute-start(bf16[3,80,128]{2,1,0:T(8,128)(2,1)S(1)} %fusion.3), channel_id=1, source_target_pairs={{0,16},{8,24},{16,0},{24,8},{1,17},{9,25},{17,1},{25,9},{2,18},{10... | collective-permute-start | bytes 184328 | tf_op jit(solution)/shard_map/ppermute | solution.py:326
  31.2 2.6 %input_grad.3 = bf16[8,320,128]{2,1,0:T(8,128)(2,1)} custom-call(bf16[8,320,128]{2,1,0:T(8,128)(2,1)S(1)} %bitcast.35, bf16[8,320,128]{2,1,0:T(8,128)(2,1)S(1)} %bitcast.39, bf16[1,320,128]{2,1,0:T(8,128)(2,1)S(1)} %constant_dynamic-slice_fusion.edge_ref, bf16[3,3,320,320]{3,2,1,0:T(8,128)(2,1)S(1)} %copy-done, ...), custom_call_target="tpu_custom_call", output_to_operand_aliasing={{}: (4, {})} | custom-call | flops 943718400 | bytes 3000000 | tf_op jit(solution)/shard_map/input_grad/pallas_call | solution.py:263
  33.8 1.1 %collective-permute-done.10 = bf16[3,80,128]{2,1,0:T(8,128)(2,1)S(1)} collective-permute-done((bf16[3,80,128]{2,1,0:T(8,128)(2,1)S(1)}, bf16[3,80,128]{2,1,0:T(8,128)(2,1)S(1)}, u32[]{:S(2)}, u32[]{:S(2)}) %collective-permute-start.10) | collective-permute-done | bytes 61472 | tf_op jit(solution)/shard_map/ppermute | solution.py:326
  35.3 1.5 %collective-permute-start.12 = (bf16[3,80,128]{2,1,0:T(8,128)(2,1)S(1)}, bf16[3,80,128]{2,1,0:T(8,128)(2,1)S(1)}, u32[]{:S(2)}, u32[]{:S(2)}) collective-permute-start(bf16[3,80,128]{2,1,0:T(8,128)(2,1)S(1)} %fusion.2), channel_id=1, source_target_pairs={{0,4},{1,5},{2,6},{3,7},{4,0},{5,1},{6,2},{7,3},{8,12},{9,13},{10,... | collective-permute-start | bytes 184328 | tf_op jit(solution)/shard_map/ppermute | solution.py:336
  36.8 1.6 %collective-permute-start.13 = (bf16[3,80,128]{2,1,0:T(8,128)(2,1)S(1)}, bf16[3,80,128]{2,1,0:T(8,128)(2,1)S(1)}, u32[]{:S(2)}, u32[]{:S(2)}) collective-permute-start(bf16[3,80,128]{2,1,0:T(8,128)(2,1)S(1)} %fusion.2), channel_id=1, source_target_pairs={{0,6},{1,7},{2,4},{3,5},{4,2},{5,3},{6,0},{7,1},{8,14},{9,15},{10,... | collective-permute-start | bytes 184328 | tf_op jit(solution)/shard_map/ppermute | solution.py:336
  38.4 1.1 %collective-permute-done.11 = bf16[3,80,128]{2,1,0:T(8,128)(2,1)S(1)} collective-permute-done((bf16[3,80,128]{2,1,0:T(8,128)(2,1)S(1)}, bf16[3,80,128]{2,1,0:T(8,128)(2,1)S(1)}, u32[]{:S(2)}, u32[]{:S(2)}) %collective-permute-start.11) | collective-permute-done | bytes 61472 | tf_op jit(solution)/shard_map/ppermute | solution.py:336
  39.7 2.2 %collective-permute-done.13 = bf16[3,80,128]{2,1,0:T(8,128)(2,1)S(1)} collective-permute-done((bf16[3,80,128]{2,1,0:T(8,128)(2,1)S(1)}, bf16[3,80,128]{2,1,0:T(8,128)(2,1)S(1)}, u32[]{:S(2)}, u32[]{:S(2)}) %collective-permute-start.13) | collective-permute-done | bytes 61472 | tf_op jit(solution)/shard_map/ppermute | solution.py:336
  42.0 1.5 %place_rows.2.refs_0_ = f32[320,720]{1,0:T(8,128)} custom-call(bf16[4,3,80,128]{3,2,1,0:T(8,128)(2,1)S(1)} %pad_maximum_fusion.parts_ref, f32[144,144]{1,0:T(8,128)S(1)} %pick_rows.1.pick_ref), custom_call_target="tpu_custom_call" | custom-call | flops 165888000 | bytes 1000000 | tf_op jit(solution)/shard_map/place_rows/pallas_call | solution.py:341
  43.6 1.5 %place_rows.3 = f32[320,720]{1,0:T(8,128)} custom-call(bf16[4,3,80,128]{3,2,1,0:T(8,128)(2,1)S(1)} %collective-permute-done.14.parts_ref, f32[144,144]{1,0:T(8,128)S(1)} %pick_rows.1.pick_ref, f32[320,720]{1,0:T(8,128)} %place_rows.2.refs_0_), custom_call_target="tpu_custom_call", output_to_operand_aliasing={{}: (2, {})} | custom-call | flops 165888000 | bytes 1000000 | tf_op jit(solution)/shard_map/place_rows/pallas_call | solution.py:341
  (27 shorter events, 1.6 us)
Async XLA Ops:
  1.6 1.3 %copy-start.1 = (bf16[1,8,128,320]{2,3,1,0:T(8,128)(2,1)S(1)}, bf16[1,8,128,320]{2,3,1,0:T(8,128)(2,1)}, u32[]{:S(2)}) copy-start(bf16[1,8,128,320]{2,3,1,0:T(8,128)(2,1)} %param.3) | copy-start | bytes 1966084
  1.6 1.3 %copy-start.2 = (bf16[1,8,128,320]{2,3,1,0:T(8,128)(2,1)S(1)}, bf16[1,8,128,320]{2,3,1,0:T(8,128)(2,1)}, u32[]{:S(2)}) copy-start(bf16[1,8,128,320]{2,3,1,0:T(8,128)(2,1)} %param.4) | copy-start | bytes 1966084
  1.6 2.8 %collective-permute-start = (bf16[8,320,128]{2,1,0:T(8,128)(2,1)}, bf16[8,320,128]{2,1,0:T(8,128)(2,1)S(1)}, u32[]{:S(2)}, u32[]{:S(2)}) collective-permute-start(bf16[8,320,128]{2,1,0:T(8,128)(2,1)} %bitcast.32), channel_id=1, source_target_pairs={{0,1},{1,0},{2,3},{3,2},{4,5},{5,4},{6,7},{7,6},{8,9},{9,8},{10,11... | collective-permute-start | bytes 1966088 | tf_op jit(solution)/shard_map/ppermute | solution.py:232
  2.2 2.9 %collective-permute-start.1 = (bf16[8,320,128]{2,1,0:T(8,128)(2,1)}, bf16[8,320,128]{2,1,0:T(8,128)(2,1)S(1)}, u32[]{:S(2)}, u32[]{:S(2)}) collective-permute-start(bf16[8,320,128]{2,1,0:T(8,128)(2,1)} %bitcast.36), channel_id=1, source_target_pairs={{0,1},{1,0},{2,3},{3,2},{4,5},{5,4},{6,7},{7,6},{8,9},{9,8},{10,11... | collective-permute-start | bytes 1966088 | tf_op jit(solution)/shard_map/ppermute | solution.py:231
  2.2 4.5 %collective-permute-start.2 = (bf16[2,320,128]{2,1,0:T(8,128)(2,1)S(1)}, bf16[2,320,128]{2,1,0:T(8,128)(2,1)S(1)}, u32[]{:S(2)}, u32[]{:S(2)}) collective-permute-start(bf16[2,320,128]{2,1,0:T(8,128)(2,1)S(1)} %pad_maximum_fusion.1.after_ref), channel_id=1, source_target_pairs={{1,2},{2,1},{3,4},{4,3},{5,6},{6,5},{9,10},{10,9},{11,12},{12,11},... | collective-permute-start | bytes 491528 | tf_op jit(solution)/shard_map/ppermute | solution.py:229
  6.7 15.1 %copy-start = (bf16[3,3,320,320]{3,2,1,0:T(8,128)(2,1)S(1)}, bf16[3,3,320,320]{3,2,1,0:T(8,128)(2,1)}, u32[]{:S(2)}) copy-start(bf16[3,3,320,320]{3,2,1,0:T(8,128)(2,1)} %kernel_ref.3) | copy-start | bytes 5529604
  7.3 13.4 %collective-permute-start.3 = (bf16[2,3,80,128]{3,2,1,0:T(8,128)(2,1)S(1)}, bf16[2,3,80,128]{3,2,1,0:T(8,128)(2,1)S(1)}, u32[]{:S(2)}, u32[]{:S(2)}) collective-permute-start(bf16[2,3,80,128]{3,2,1,0:T(8,128)(2,1)S(1)} %get-tuple-element.37), channel_id=1, source_target_pairs={{0,6},{1,7},{2,4},{3,5},{4,2},{5,3},{6,0},{7,1},{8,14},{9,15},{10,... | collective-permute-start | bytes 368648 | tf_op jit(solution)/shard_map/ppermute | solution.py:316
  14.9 6.0 %collective-permute-start.4 = (bf16[2,3,80,128]{3,2,1,0:T(8,128)(2,1)S(1)}, bf16[2,3,80,128]{3,2,1,0:T(8,128)(2,1)S(1)}, u32[]{:S(2)}, u32[]{:S(2)}) collective-permute-start(bf16[2,3,80,128]{3,2,1,0:T(8,128)(2,1)S(1)} %get-tuple-element.38), channel_id=1, source_target_pairs={{0,8},{1,9},{2,10},{3,11},{4,12},{5,13},{6,14},{7,15},{8,0},{9,1},... | collective-permute-start | bytes 368648 | tf_op jit(solution)/shard_map/ppermute | solution.py:316
  16.4 8.2 %collective-permute-start.5 = (bf16[2,3,80,128]{3,2,1,0:T(8,128)(2,1)S(1)}, bf16[2,3,80,128]{3,2,1,0:T(8,128)(2,1)S(1)}, u32[]{:S(2)}, u32[]{:S(2)}) collective-permute-start(bf16[2,3,80,128]{3,2,1,0:T(8,128)(2,1)S(1)} %get-tuple-element.39), channel_id=1, source_target_pairs={{0,14},{1,15},{2,12},{3,13},{4,10},{5,11},{6,8},{7,9},{8,6},{9,7},... | collective-permute-start | bytes 368648 | tf_op jit(solution)/shard_map/ppermute | solution.py:316
  16.4 8.4 %collective-permute-start.6 = (bf16[2,3,80,128]{3,2,1,0:T(8,128)(2,1)S(1)}, bf16[2,3,80,128]{3,2,1,0:T(8,128)(2,1)S(1)}, u32[]{:S(2)}, u32[]{:S(2)}) collective-permute-start(bf16[2,3,80,128]{3,2,1,0:T(8,128)(2,1)S(1)} %get-tuple-element.40), channel_id=1, source_target_pairs={{0,10},{1,11},{2,8},{3,9},{4,14},{5,15},{6,12},{7,13},{8,2},{9,3},... | collective-permute-start | bytes 368648 | tf_op jit(solution)/shard_map/ppermute | solution.py:316
  18.4 9.4 %collective-permute-start.7 = (bf16[2,3,80,128]{3,2,1,0:T(8,128)(2,1)S(1)}, bf16[2,3,80,128]{3,2,1,0:T(8,128)(2,1)S(1)}, u32[]{:S(2)}, u32[]{:S(2)}) collective-permute-start(bf16[2,3,80,128]{3,2,1,0:T(8,128)(2,1)S(1)} %get-tuple-element.41), channel_id=1, source_target_pairs={{0,12},{1,13},{2,14},{3,15},{4,8},{5,9},{6,10},{7,11},{8,4},{9,5},... | collective-permute-start | bytes 368648 | tf_op jit(solution)/shard_map/ppermute | solution.py:316
  20.7 7.6 %collective-permute-start.8 = (bf16[2,3,80,128]{3,2,1,0:T(8,128)(2,1)S(1)}, bf16[2,3,80,128]{3,2,1,0:T(8,128)(2,1)S(1)}, u32[]{:S(2)}, u32[]{:S(2)}) collective-permute-start(bf16[2,3,80,128]{3,2,1,0:T(8,128)(2,1)S(1)} %get-tuple-element.42), channel_id=1, source_target_pairs={{0,4},{1,5},{2,6},{3,7},{4,0},{5,1},{6,2},{7,3},{8,12},{9,13},{10,... | collective-permute-start | bytes 368648 | tf_op jit(solution)/shard_map/ppermute | solution.py:316
  20.8 7.5 %collective-permute-start.9 = (bf16[2,3,80,128]{3,2,1,0:T(8,128)(2,1)S(1)}, bf16[2,3,80,128]{3,2,1,0:T(8,128)(2,1)S(1)}, u32[]{:S(2)}, u32[]{:S(2)}) collective-permute-start(bf16[2,3,80,128]{3,2,1,0:T(8,128)(2,1)S(1)} %get-tuple-element.43), channel_id=1, source_target_pairs={{0,2},{1,3},{2,0},{3,1},{4,6},{5,7},{6,4},{7,5},{8,10},{9,11},{10,... | collective-permute-start | bytes 368648 | tf_op jit(solution)/shard_map/ppermute | solution.py:316
  28.5 6.3 %collective-permute-start.10 = (bf16[3,80,128]{2,1,0:T(8,128)(2,1)S(1)}, bf16[3,80,128]{2,1,0:T(8,128)(2,1)S(1)}, u32[]{:S(2)}, u32[]{:S(2)}) collective-permute-start(bf16[3,80,128]{2,1,0:T(8,128)(2,1)S(1)} %fusion.3), channel_id=1, source_target_pairs={{0,16},{8,24},{16,0},{24,8},{1,17},{9,25},{17,1},{25,9},{2,18},{10... | collective-permute-start | bytes 184328 | tf_op jit(solution)/shard_map/ppermute | solution.py:326
  34.8 4.6 %collective-permute-start.11 = (bf16[3,80,128]{2,1,0:T(8,128)(2,1)S(1)}, bf16[3,80,128]{2,1,0:T(8,128)(2,1)S(1)}, u32[]{:S(2)}, u32[]{:S(2)}) collective-permute-start(bf16[3,80,128]{2,1,0:T(8,128)(2,1)S(1)} %fusion.2), channel_id=1, source_target_pairs={{0,2},{1,3},{2,0},{3,1},{4,6},{5,7},{6,4},{7,5},{8,10},{9,11},{10,... | collective-permute-start | bytes 184328 | tf_op jit(solution)/shard_map/ppermute | solution.py:336
  35.3 4.5 %collective-permute-start.12 = (bf16[3,80,128]{2,1,0:T(8,128)(2,1)S(1)}, bf16[3,80,128]{2,1,0:T(8,128)(2,1)S(1)}, u32[]{:S(2)}, u32[]{:S(2)}) collective-permute-start(bf16[3,80,128]{2,1,0:T(8,128)(2,1)S(1)} %fusion.2), channel_id=1, source_target_pairs={{0,4},{1,5},{2,6},{3,7},{4,0},{5,1},{6,2},{7,3},{8,12},{9,13},{10,... | collective-permute-start | bytes 184328 | tf_op jit(solution)/shard_map/ppermute | solution.py:336
  36.8 5.1 %collective-permute-start.13 = (bf16[3,80,128]{2,1,0:T(8,128)(2,1)S(1)}, bf16[3,80,128]{2,1,0:T(8,128)(2,1)S(1)}, u32[]{:S(2)}, u32[]{:S(2)}) collective-permute-start(bf16[3,80,128]{2,1,0:T(8,128)(2,1)S(1)} %fusion.2), channel_id=1, source_target_pairs={{0,6},{1,7},{2,4},{3,5},{4,2},{5,3},{6,0},{7,1},{8,14},{9,15},{10,... | collective-permute-start | bytes 184328 | tf_op jit(solution)/shard_map/ppermute | solution.py:336
  41.9 1.6 %collective-permute-start.14 = (bf16[4,3,80,128]{3,2,1,0:T(8,128)(2,1)S(1)}, bf16[4,3,80,128]{3,2,1,0:T(8,128)(2,1)S(1)}, u32[]{:S(2)}, u32[]{:S(2)}) collective-permute-start(bf16[4,3,80,128]{3,2,1,0:T(8,128)(2,1)S(1)} %pad_maximum_fusion.parts_ref), channel_id=1, source_target_pairs={{0,1},{1,0},{2,3},{3,2},{4,5},{5,4},{6,7},{7,6},{8,9},{9,8},{10,11... | collective-permute-start | bytes 737288 | tf_op jit(solution)/shard_map/ppermute | solution.py:338

commit v7 on v6

--- a/solution.py
+++ b/solution.py
@@ -166,16 +166,20 @@
         copy.wait()
 
 
-def pick_kernel(after_ref, out_ref):
-    group = out_ref.shape[0] // 9
-    k = lax.broadcasted_iota(jnp.int32, (group, 9 * group), 0)
-    j = lax.broadcasted_iota(jnp.int32, (group, 9 * group), 1)
+def pick_kernel(out_ref):
+    size = out_ref.shape[0]
+    group = size // 9
+    j = lax.broadcasted_iota(jnp.int32, (size, size), 0)
+    k = lax.broadcasted_iota(jnp.int32, (size, size), 1)
+    pick = jnp.zeros((size, size), F32)
     for t in range(9):
-        out_ref[t * group : (t + 1) * group, :] = jnp.where(j - 9 * k == t, 1.0, 0.0)
+        c = k - t * group
+        pick = jnp.where((c >= 0) & (c < group) & (j == 9 * c + t), 1.0, pick)
+    out_ref[...] = pick
 
 
 def place_kernel(flip, parts_ref, pick_ref, *refs):
-    out_hbm, wide_s, out_s, sem = refs[-4:]
+    out_hbm, wide_s, turned_s, out_s, sem = refs[-5:]
     _, _, block, _ = parts_ref.shape
     half = out_s.shape[0]
     width = pick_ref.shape[0]
@@ -187,9 +191,11 @@
     for g in range(block // group):
         rows = [wide_s[t // 3, g * group : (g + 1) * group, t % 3 * half : (t % 3 + 1) * half] for t in range(9)]
         rows = jnp.concatenate(rows, axis=0).astype(BF16)
-        out_s[:, g * width : (g + 1) * width] = lax.dot_general(
-            rows, pick, (((0,), (0,)), ((), ())), preferred_element_type=F32
-        )
+        turned_s[g * width : (g + 1) * width, :] = jnp.dot(pick, rows, preferred_element_type=F32)
+    i = lax.broadcasted_iota(jnp.int32, (half, half), 0)
+    j = lax.broadcasted_iota(jnp.int32, (half, half), 1)
+    same = jnp.where(i == j, 1.0, 0.0).astype(BF16)
+    out_s[...] = lax.dot_general(same, turned_s[...].astype(BF16), NT, preferred_element_type=F32)
     count = sem.shape[0]
     step = half // count
     first = (my_core() ^ flip) * half
@@ -218,27 +224,22 @@
 
     pre = jnp.swapaxes(pre_act[0], 1, 2)
     grad = jnp.swapaxes(out_grad[0], 1, 2)
-    row = my_core() * (rows - 1)
-    edge = jnp.stack([lax.dynamic_index_in_dim(grad, row, 0, False), lax.dynamic_index_in_dim(pre, row, 0, False)])
-    beyond = [(i, i + 1 if i % 2 else i - 1) for i in range(space)]
+    beyond = [(i, i - PAIR if i % 2 else i + PAIR) for i in range(space)]
     pairs = [(i, i + 1 - 2 * (i % 2)) for i in range(space)]
 
     def inside(moves):
         return [(i, j) for i, j in moves if 0 <= j < space]
 
-    near_row = lax.ppermute(edge, "space", inside(beyond))
-    _, my_pre, my_grad = lax.optimization_barrier((edge, pre, grad))
-    their_grad = lax.ppermute(my_grad, "space", pairs)
-    their_pre = lax.ppermute(my_pre, "space", pairs)
+    their_grad = lax.ppermute(grad, "space", pairs)
+    their_pre = lax.ppermute(pre, "space", pairs)
     pick = pl.pallas_call(
         pick_kernel,
         out_shape=jax.ShapeDtypeStruct((9 * group, 9 * group), F32),
-        in_specs=[anywhere()],
         out_specs=vmem(),
         compiler_params=params,
         cost_estimate=pl.CostEstimate(flops=flops, bytes_accessed=4000000, transcendentals=0),
         name="pick_rows",
-    )(edge)
+    )()
     pick, own_pre, own_grad = lax.optimization_barrier((pick, pre, grad))
     own, act_edge, grad_edge = pl.pallas_call(
         own_kernel,
@@ -257,6 +258,12 @@
         cost_estimate=pl.CostEstimate(flops=flops, bytes_accessed=4000000, transcendentals=rows * width * chans),
         name="own_terms",
     )(own_pre, own_grad)
+
+    row = (1 - my_core()) * (rows - 1)
+    ready = lax.optimization_barrier((own, act_edge, grad_edge, their_grad, their_pre))
+    own, act_edge, grad_edge, their_grad, their_pre = ready
+    outer_row = jnp.stack([lax.dynamic_index_in_dim(x, row, 0, False) for x in (their_grad, their_pre)])
+    near_row = lax.ppermute(outer_row, "space", inside(beyond))
 
     def input_part(side, edge_rows, *before):
         count = rows // 2
@@ -345,8 +352,9 @@
             out_specs=anywhere(),
             scratch_shapes=[
                 pltpu.VMEM((3, block, PLANE * LANES), F32),
+                pltpu.VMEM((9 * block, half), F32),
                 pltpu.VMEM((half, 9 * block), F32),
-                pltpu.SemaphoreType.DMA((4,)),
+                pltpu.SemaphoreType.DMA((10,)),
             ],
             input_output_aliases={2: 0} if before else {},
             compiler_params=params,

time: 45.3 us -> 46.2 us (1.020)
  starting transfers between devices: 22 us -> 23.2 us
    ppermute x3, starting transfers between devices: 1.25 us -> 5.43 us  [the longest x1 4.83 us: shards(): near_row = lax.ppermute(outer_row, 'space', inside(beyond))]
    ppermute x7, starting transfers between devices: 14.5 us -> 11.5 us  [shards(): got.append(lax.ppermute(terms[k], ('dp', 'space'), moves))]
    unnamed x6, local copies, waits for them, and re-layouts: 0.02 us -> 1.2 us
    dynamic_slice x1 -> x0, local copies, waits for them, and re-layouts: 0.95 us -> none  [shards(): lax.dynamic_index_in_dim(pre, row, 0, False)]
    ppermute x7, waiting for transfers between devices: 3.93 us -> 3.12 us  [shards(): got.append(lax.ppermute(terms[k], ('dp', 'space'), moves))]
    ppermute x1, waiting for transfers between devices: 1.05 us -> 0.31 us  [shards(): others.append(lax.ppermute(near_sum[k].astype(BF16), 'dp', moves))]
    ppermute x3, waiting for transfers between devices: 3.5 us -> 4.06 us  [shards(): lax.ppermute(final, 'space', [(i, i ^ k * PAIR) for i in range(space)])]
    ppermute x3, waiting for transfers between devices: 0.54 us -> 1.08 us  [the longest x1 1.07 us: shards(): near_row = lax.ppermute(outer_row, 'space', inside(beyond))]
  transfers between devices with their start and end apart: 15 -> 15, of which waited for: 9 -> 8; matrix products, arithmetic and copies ran while one was open for 0% -> 0% of each run, Pallas kernels for 22% -> 22%
where the time goes in v7:
time: 46.2 us; the launch traced here: 46 us
  starting transfers between devices  23.2 us (50%)
  Pallas kernels  12 us (26%)
  waiting for transfers between devices  8.58 us (19%)
  local copies, waits for them, and re-layouts  1.24 us (3%)
  between operations  0.78 us (2%)
    ppermute x7, starting transfers between devices, shards(): got.append(lax.ppermute(terms[k], ('dp', 'space'), moves))  11.5 us
    pallas_call x2, Pallas kernels, input_part(): pl.pallas_call(functools.partial(input_kernel, side), out_shape=jax.Shape...  5.2 us
    ppermute x1, starting transfers between devices, shards(): near_row = lax.ppermute(outer_row, 'space', inside(beyond))  4.83 us
    ppermute x3, waiting for transfers between devices, shards(): lax.ppermute(final, 'space', [(i, i ^ k * PAIR) for i in range(space)])  4.06 us
    ppermute x3, starting transfers between devices, shards(): lax.ppermute(final, 'space', [(i, i ^ k * PAIR) for i in range(space)])  3.55 us
    ppermute x7, waiting for transfers between devices, shards(): got.append(lax.ppermute(terms[k], ('dp', 'space'), moves))  3.12 us
    pallas_call x2, Pallas kernels, place(): pl.pallas_call(functools.partial(place_kernel, flip), out_shape=jax.Shape...  2.94 us
    ppermute x1, starting transfers between devices, shards(): others.append(lax.ppermute(near_sum[k].astype(BF16), 'dp', moves))  2.65 us
  transfers between devices with their start and end apart: 15, of which 8 were waited for; matrix products, arithmetic and copies ran while one was open for 0% of the time, Pallas kernels for 22%

profile of v7, /device:TPU:0, one launch (start us, length us, event | category | flops | bytes accessed | tf_op | source)
XLA Modules:
  0.0 46.0 jit_solution(6431725282853459459)
XLA Ops:
  0.6 0.5 %collective-permute-start = (bf16[8,320,128]{2,1,0:T(8,128)(2,1)}, bf16[8,320,128]{2,1,0:T(8,128)(2,1)S(1)}, u32[]{:S(2)}, u32[]{:S(2)}) collective-permute-start(bf16[8,320,128]{2,1,0:T(8,128)(2,1)} %bitcast.28), channel_id=1, source_target_pairs={{0,1},{1,0},{2,3},{3,2},{4,5},{5,4},{6,7},{7,6},{8,9},{9,8},{10,11... | collective-permute-start | bytes 1966088 | tf_op jit(solution)/shard_map/ppermute | solution.py:233
  1.3 1.0 %copy-done.1 = bf16[1,8,128,320]{2,3,1,0:T(8,128)(2,1)S(1)} copy-done((bf16[1,8,128,320]{2,3,1,0:T(8,128)(2,1)S(1)}, bf16[1,8,128,320]{2,3,1,0:T(8,128)(2,1)}, u32[]{:S(2)}) %copy-start.1) | copy-done | bytes 655384
  2.5 1.5 %own_terms.1 = (f32[3,320,512]{2,1,0:T(8,128)S(1)}, bf16[2,320,128]{2,1,0:T(8,128)(2,1)S(1)}, bf16[2,160,128]{2,1,0:T(8,128)(2,1)S(1)}) custom-call(bf16[8,320,128]{2,1,0:T(8,128)(2,1)S(1)} %bitcast.25, bf16[8,320,128]{2,1,0:T(8,128)(2,1)S(1)} %bitcast.29), custom_call_target="tpu_custom_call" | custom-call | flops 1887436800 | bytes 4000000 | tf_op jit(solution)/shard_map/own_terms/pallas_call | solution.py:244
  4.1 4.8 %collective-permute-start.2 = (bf16[2,320,128]{2,1,0:T(8,128)(2,1)S(1)}, bf16[2,320,128]{2,1,0:T(8,128)(2,1)S(1)}, u32[]{:S(2)}, u32[]{:S(2)}) collective-permute-start(bf16[2,320,128]{2,1,0:T(8,128)(2,1)S(1)} %pad_maximum_fusion.1), channel_id=1, source_target_pairs={{0,2},{2,4},{3,1},{4,6},{5,3},{7,5},{8,10},{10,12},{11,9},{12,14},... | collective-permute-start | bytes 491528 | tf_op jit(solution)/shard_map/ppermute | solution.py:266
  9.0 1.7 %pair_terms.1.term_ref = f32[3,320,512]{2,1,0:T(8,128)S(1)} custom-call(f32[3,320,512]{2,1,0:T(8,128)S(1)} %get-tuple-element.37.term_ref, bf16[2,320,128]{2,1,0:T(8,128)(2,1)S(1)} %get-tuple-element.38.act_edge_ref, bf16[2,160,128]{2,1,0:T(8,128)(2,1)S(1)} %get-tuple-element.39.grad_edge_ref, bf16[8,320,128]{2,1,0:T(8,128)(2,1)S(1)} %collective-permute-done.1.their_pre_ref, ...), custom_call_target="tpu_custom_call" | custom-call | flops 1887436800 | bytes 4000000 | tf_op jit(solution)/shard_map/pair_terms/pallas_call | solution.py:289
  10.7 1.1 %collective-permute-done.2.near_ref.edge_ref = bf16[2,320,128]{2,1,0:T(8,128)(2,1)S(1)} collective-permute-done((bf16[2,320,128]{2,1,0:T(8,128)(2,1)S(1)}, bf16[2,320,128]{2,1,0:T(8,128)(2,1)S(1)}, u32[]{:S(2)}, u32[]{:S(2)}) %collective-permute-start.2) | collective-permute-done | bytes 163872 | tf_op jit(solution)/shard_map/ppermute | solution.py:266
  11.8 0.5 %edge_terms.1 = (bf16[2,3,80,128]{3,2,1,0:T(8,128)(2,1)S(1)}, bf16[2,3,80,128]{3,2,1,0:T(8,128)(2,1)S(1)}, bf16[2,3,80,128]{3,2,1,0:T(8,128)(2,1)S(1)}, bf16[2,3...) custom-call(f32[3,320,512]{2,1,0:T(8,128)S(1)} %pair_terms.1.term_re, ...), custom_call_target="tpu_custom_call" | custom-call | flops 235929600 | bytes 4000000 | tf_op jit(solution)/shard_map/edge_terms/pallas_call | solution.py:302
  12.3 4.3 %collective-permute-start.3 = (bf16[2,3,80,128]{3,2,1,0:T(8,128)(2,1)S(1)}, bf16[2,3,80,128]{3,2,1,0:T(8,128)(2,1)S(1)}, u32[]{:S(2)}, u32[]{:S(2)}) collective-permute-start(bf16[2,3,80,128]{3,2,1,0:T(8,128)(2,1)S(1)} %get-tuple-element.43), channel_id=1, source_target_pairs={{0,6},{1,7},{2,4},{3,5},{4,2},{5,3},{6,0},{7,1},{8,14},{9,15},{10,... | collective-permute-start | bytes 368648 | tf_op jit(solution)/shard_map/ppermute | solution.py:323
  16.6 1.6 %collective-permute-start.4 = (bf16[2,3,80,128]{3,2,1,0:T(8,128)(2,1)S(1)}, bf16[2,3,80,128]{3,2,1,0:T(8,128)(2,1)S(1)}, u32[]{:S(2)}, u32[]{:S(2)}) collective-permute-start(bf16[2,3,80,128]{3,2,1,0:T(8,128)(2,1)S(1)} %get-tuple-element.44), channel_id=1, source_target_pairs={{0,8},{1,9},{2,10},{3,11},{4,12},{5,13},{6,14},{7,15},{8,0},{9,1},... | collective-permute-start | bytes 368648 | tf_op jit(solution)/shard_map/ppermute | solution.py:323
  18.2 2.1 %collective-permute-start.6 = (bf16[2,3,80,128]{3,2,1,0:T(8,128)(2,1)S(1)}, bf16[2,3,80,128]{3,2,1,0:T(8,128)(2,1)S(1)}, u32[]{:S(2)}, u32[]{:S(2)}) collective-permute-start(bf16[2,3,80,128]{3,2,1,0:T(8,128)(2,1)S(1)} %get-tuple-element.46), channel_id=1, source_target_pairs={{0,10},{1,11},{2,8},{3,9},{4,14},{5,15},{6,12},{7,13},{8,2},{9,3},... | collective-permute-start | bytes 368648 | tf_op jit(solution)/shard_map/ppermute | solution.py:323
  20.2 2.2 %collective-permute-start.7 = (bf16[2,3,80,128]{3,2,1,0:T(8,128)(2,1)S(1)}, bf16[2,3,80,128]{3,2,1,0:T(8,128)(2,1)S(1)}, u32[]{:S(2)}, u32[]{:S(2)}) collective-permute-start(bf16[2,3,80,128]{3,2,1,0:T(8,128)(2,1)S(1)} %get-tuple-element.47), channel_id=1, source_target_pairs={{0,12},{1,13},{2,14},{3,15},{4,8},{5,9},{6,10},{7,11},{8,4},{9,5},... | collective-permute-start | bytes 368648 | tf_op jit(solution)/shard_map/ppermute | solution.py:323
  22.6 1.2 %collective-permute-start.9 = (bf16[2,3,80,128]{3,2,1,0:T(8,128)(2,1)S(1)}, bf16[2,3,80,128]{3,2,1,0:T(8,128)(2,1)S(1)}, u32[]{:S(2)}, u32[]{:S(2)}) collective-permute-start(bf16[2,3,80,128]{3,2,1,0:T(8,128)(2,1)S(1)} %get-tuple-element.49), channel_id=1, source_target_pairs={{0,2},{1,3},{2,0},{3,1},{4,6},{5,7},{6,4},{7,5},{8,10},{9,11},{10,... | collective-permute-start | bytes 368648 | tf_op jit(solution)/shard_map/ppermute | solution.py:323
  23.8 2.6 %input_grad.2.refs_0_ = bf16[8,320,128]{2,1,0:T(8,128)(2,1)} custom-call(bf16[8,320,128]{2,1,0:T(8,128)(2,1)S(1)} %bitcast.26, bf16[8,320,128]{2,1,0:T(8,128)(2,1)S(1)} %bitcast.30, bf16[2,320,128]{2,1,0:T(8,128)(2,1)S(1)} %collective-permute-done.2.near_ref.edge_ref, bf16[3,3,320,320]{3,2,1,0:T(8,128)(2,1)S(1)} %copy-done), custom_call_target="tpu_custom_call" | custom-call | flops 943718400 | bytes 3000000 | tf_op jit(solution)/shard_map/input_grad/pallas_call | solution.py:270
  26.4 1.1 %collective-permute-done.6 = bf16[2,3,80,128]{3,2,1,0:T(8,128)(2,1)S(1)} collective-permute-done((bf16[2,3,80,128]{3,2,1,0:T(8,128)(2,1)S(1)}, bf16[2,3,80,128]{3,2,1,0:T(8,128)(2,1)S(1)}, u32[]{:S(2)}, u32[]{:S(2)}) %collective-permute-start.6) | collective-permute-done | bytes 122912 | tf_op jit(solution)/shard_map/ppermute | solution.py:323
  27.5 1.8 %collective-permute-done.7 = bf16[2,3,80,128]{3,2,1,0:T(8,128)(2,1)S(1)} collective-permute-done((bf16[2,3,80,128]{3,2,1,0:T(8,128)(2,1)S(1)}, bf16[2,3,80,128]{3,2,1,0:T(8,128)(2,1)S(1)}, u32[]{:S(2)}, u32[]{:S(2)}) %collective-permute-start.7) | collective-permute-done | bytes 122912 | tf_op jit(solution)/shard_map/ppermute | solution.py:323
  29.7 2.6 %collective-permute-start.10 = (bf16[3,80,128]{2,1,0:T(8,128)(2,1)S(1)}, bf16[3,80,128]{2,1,0:T(8,128)(2,1)S(1)}, u32[]{:S(2)}, u32[]{:S(2)}) collective-permute-start(bf16[3,80,128]{2,1,0:T(8,128)(2,1)S(1)} %fusion.3), channel_id=1, source_target_pairs={{0,16},{8,24},{16,0},{24,8},{1,17},{9,25},{17,1},{25,9},{2,18},{10... | collective-permute-start | bytes 184328 | tf_op jit(solution)/shard_map/ppermute | solution.py:333
  32.3 2.6 %input_grad.3 = bf16[8,320,128]{2,1,0:T(8,128)(2,1)} custom-call(bf16[8,320,128]{2,1,0:T(8,128)(2,1)S(1)} %bitcast.27, bf16[8,320,128]{2,1,0:T(8,128)(2,1)S(1)} %bitcast.31, bf16[1,320,128]{2,1,0:T(8,128)(2,1)S(1)} %get-tuple-element.62.edge_ref, bf16[3,3,320,320]{3,2,1,0:T(8,128)(2,1)S(1)} %copy-done, ...), custom_call_target="tpu_custom_call", output_to_operand_aliasing={{}: (4, {})} | custom-call | flops 943718400 | bytes 3000000 | tf_op jit(solution)/shard_map/input_grad/pallas_call | solution.py:270
  35.3 2.4 %collective-permute-start.13 = (bf16[3,80,128]{2,1,0:T(8,128)(2,1)S(1)}, bf16[3,80,128]{2,1,0:T(8,128)(2,1)S(1)}, u32[]{:S(2)}, u32[]{:S(2)}) collective-permute-start(bf16[3,80,128]{2,1,0:T(8,128)(2,1)S(1)} %fusion.2), channel_id=1, source_target_pairs={{0,6},{1,7},{2,4},{3,5},{4,2},{5,3},{6,0},{7,1},{8,14},{9,15},{10,... | collective-permute-start | bytes 184328 | tf_op jit(solution)/shard_map/ppermute | solution.py:343
  37.7 1.0 %collective-permute-start.12 = (bf16[3,80,128]{2,1,0:T(8,128)(2,1)S(1)}, bf16[3,80,128]{2,1,0:T(8,128)(2,1)S(1)}, u32[]{:S(2)}, u32[]{:S(2)}) collective-permute-start(bf16[3,80,128]{2,1,0:T(8,128)(2,1)S(1)} %fusion.2), channel_id=1, source_target_pairs={{0,4},{1,5},{2,6},{3,7},{4,0},{5,1},{6,2},{7,3},{8,12},{9,13},{10,... | collective-permute-start | bytes 184328 | tf_op jit(solution)/shard_map/ppermute | solution.py:343
  38.8 2.0 %collective-permute-done.13 = bf16[3,80,128]{2,1,0:T(8,128)(2,1)S(1)} collective-permute-done((bf16[3,80,128]{2,1,0:T(8,128)(2,1)S(1)}, bf16[3,80,128]{2,1,0:T(8,128)(2,1)S(1)}, u32[]{:S(2)}, u32[]{:S(2)}) %collective-permute-start.13) | collective-permute-done | bytes 61472 | tf_op jit(solution)/shard_map/ppermute | solution.py:343
  40.8 1.1 %collective-permute-done.12 = bf16[3,80,128]{2,1,0:T(8,128)(2,1)S(1)} collective-permute-done((bf16[3,80,128]{2,1,0:T(8,128)(2,1)S(1)}, bf16[3,80,128]{2,1,0:T(8,128)(2,1)S(1)}, u32[]{:S(2)}, u32[]{:S(2)}) %collective-permute-start.12) | collective-permute-done | bytes 61472 | tf_op jit(solution)/shard_map/ppermute | solution.py:343
  41.9 1.0 %collective-permute-done.11 = bf16[3,80,128]{2,1,0:T(8,128)(2,1)S(1)} collective-permute-done((bf16[3,80,128]{2,1,0:T(8,128)(2,1)S(1)}, bf16[3,80,128]{2,1,0:T(8,128)(2,1)S(1)}, u32[]{:S(2)}, u32[]{:S(2)}) %collective-permute-start.11) | collective-permute-done | bytes 61472 | tf_op jit(solution)/shard_map/ppermute | solution.py:343
  43.0 1.5 %place_rows.2.refs_0_ = f32[320,720]{1,0:T(8,128)} custom-call(bf16[4,3,80,128]{3,2,1,0:T(8,128)(2,1)S(1)} %pad_maximum_fusion.parts_ref, f32[144,144]{1,0:T(8,128)S(1)} %pick_rows.1.pick_ref), custom_call_target="tpu_custom_call" | custom-call | flops 165888000 | bytes 1000000 | tf_op jit(solution)/shard_map/place_rows/pallas_call | solution.py:348
  44.5 1.5 %place_rows.3 = f32[320,720]{1,0:T(8,128)} custom-call(bf16[4,3,80,128]{3,2,1,0:T(8,128)(2,1)S(1)} %collective-permute-done.14.parts_ref, f32[144,144]{1,0:T(8,128)S(1)} %pick_rows.1.pick_ref, f32[320,720]{1,0:T(8,128)} %place_rows.2.refs_0_), custom_call_target="tpu_custom_call", output_to_operand_aliasing={{}: (2, {})} | custom-call | flops 165888000 | bytes 1000000 | tf_op jit(solution)/shard_map/place_rows/pallas_call | solution.py:348
  (26 shorter events, 1.5 us)
Async XLA Ops:
  0.6 3.4 %collective-permute-start = (bf16[8,320,128]{2,1,0:T(8,128)(2,1)}, bf16[8,320,128]{2,1,0:T(8,128)(2,1)S(1)}, u32[]{:S(2)}, u32[]{:S(2)}) collective-permute-start(bf16[8,320,128]{2,1,0:T(8,128)(2,1)} %bitcast.28), channel_id=1, source_target_pairs={{0,1},{1,0},{2,3},{3,2},{4,5},{5,4},{6,7},{7,6},{8,9},{9,8},{10,11... | collective-permute-start | bytes 1966088 | tf_op jit(solution)/shard_map/ppermute | solution.py:233
  1.1 2.9 %collective-permute-start.1 = (bf16[8,320,128]{2,1,0:T(8,128)(2,1)}, bf16[8,320,128]{2,1,0:T(8,128)(2,1)S(1)}, u32[]{:S(2)}, u32[]{:S(2)}) collective-permute-start(bf16[8,320,128]{2,1,0:T(8,128)(2,1)} %bitcast.24), channel_id=1, source_target_pairs={{0,1},{1,0},{2,3},{3,2},{4,5},{5,4},{6,7},{7,6},{8,9},{9,8},{10,11... | collective-permute-start | bytes 1966088 | tf_op jit(solution)/shard_map/ppermute | solution.py:234
  1.2 1.1 %copy-start.1 = (bf16[1,8,128,320]{2,3,1,0:T(8,128)(2,1)S(1)}, bf16[1,8,128,320]{2,3,1,0:T(8,128)(2,1)}, u32[]{:S(2)}) copy-start(bf16[1,8,128,320]{2,3,1,0:T(8,128)(2,1)} %param.3) | copy-start | bytes 1966084
  1.2 1.3 %copy-start.2 = (bf16[1,8,128,320]{2,3,1,0:T(8,128)(2,1)S(1)}, bf16[1,8,128,320]{2,3,1,0:T(8,128)(2,1)}, u32[]{:S(2)}) copy-start(bf16[1,8,128,320]{2,3,1,0:T(8,128)(2,1)} %param.4) | copy-start | bytes 1966084
  4.1 7.6 %collective-permute-start.2 = (bf16[2,320,128]{2,1,0:T(8,128)(2,1)S(1)}, bf16[2,320,128]{2,1,0:T(8,128)(2,1)S(1)}, u32[]{:S(2)}, u32[]{:S(2)}) collective-permute-start(bf16[2,320,128]{2,1,0:T(8,128)(2,1)S(1)} %pad_maximum_fusion.1), channel_id=1, source_target_pairs={{0,2},{2,4},{3,1},{4,6},{5,3},{7,5},{8,10},{10,12},{11,9},{12,14},... | collective-permute-start | bytes 491528 | tf_op jit(solution)/shard_map/ppermute | solution.py:266
  10.7 13.1 %copy-start = (bf16[3,3,320,320]{3,2,1,0:T(8,128)(2,1)S(1)}, bf16[3,3,320,320]{3,2,1,0:T(8,128)(2,1)}, u32[]{:S(2)}) copy-start(bf16[3,3,320,320]{3,2,1,0:T(8,128)(2,1)} %kernel_ref.3) | copy-start | bytes 5529604
  12.3 10.2 %collective-permute-start.3 = (bf16[2,3,80,128]{3,2,1,0:T(8,128)(2,1)S(1)}, bf16[2,3,80,128]{3,2,1,0:T(8,128)(2,1)S(1)}, u32[]{:S(2)}, u32[]{:S(2)}) collective-permute-start(bf16[2,3,80,128]{3,2,1,0:T(8,128)(2,1)S(1)} %get-tuple-element.43), channel_id=1, source_target_pairs={{0,6},{1,7},{2,4},{3,5},{4,2},{5,3},{6,0},{7,1},{8,14},{9,15},{10,... | collective-permute-start | bytes 368648 | tf_op jit(solution)/shard_map/ppermute | solution.py:323
  16.6 6.0 %collective-permute-start.4 = (bf16[2,3,80,128]{3,2,1,0:T(8,128)(2,1)S(1)}, bf16[2,3,80,128]{3,2,1,0:T(8,128)(2,1)S(1)}, u32[]{:S(2)}, u32[]{:S(2)}) collective-permute-start(bf16[2,3,80,128]{3,2,1,0:T(8,128)(2,1)S(1)} %get-tuple-element.44), channel_id=1, source_target_pairs={{0,8},{1,9},{2,10},{3,11},{4,12},{5,13},{6,14},{7,15},{8,0},{9,1},... | collective-permute-start | bytes 368648 | tf_op jit(solution)/shard_map/ppermute | solution.py:323
  18.2 8.2 %collective-permute-start.5 = (bf16[2,3,80,128]{3,2,1,0:T(8,128)(2,1)S(1)}, bf16[2,3,80,128]{3,2,1,0:T(8,128)(2,1)S(1)}, u32[]{:S(2)}, u32[]{:S(2)}) collective-permute-start(bf16[2,3,80,128]{3,2,1,0:T(8,128)(2,1)S(1)} %get-tuple-element.45), channel_id=1, source_target_pairs={{0,14},{1,15},{2,12},{3,13},{4,10},{5,11},{6,8},{7,9},{8,6},{9,7},... | collective-permute-start | bytes 368648 | tf_op jit(solution)/shard_map/ppermute | solution.py:323
  18.2 9.4 %collective-permute-start.6 = (bf16[2,3,80,128]{3,2,1,0:T(8,128)(2,1)S(1)}, bf16[2,3,80,128]{3,2,1,0:T(8,128)(2,1)S(1)}, u32[]{:S(2)}, u32[]{:S(2)}) collective-permute-start(bf16[2,3,80,128]{3,2,1,0:T(8,128)(2,1)S(1)} %get-tuple-element.46), channel_id=1, source_target_pairs={{0,10},{1,11},{2,8},{3,9},{4,14},{5,15},{6,12},{7,13},{8,2},{9,3},... | collective-permute-start | bytes 368648 | tf_op jit(solution)/shard_map/ppermute | solution.py:323
  20.2 9.1 %collective-permute-start.7 = (bf16[2,3,80,128]{3,2,1,0:T(8,128)(2,1)S(1)}, bf16[2,3,80,128]{3,2,1,0:T(8,128)(2,1)S(1)}, u32[]{:S(2)}, u32[]{:S(2)}) collective-permute-start(bf16[2,3,80,128]{3,2,1,0:T(8,128)(2,1)S(1)} %get-tuple-element.47), channel_id=1, source_target_pairs={{0,12},{1,13},{2,14},{3,15},{4,8},{5,9},{6,10},{7,11},{8,4},{9,5},... | collective-permute-start | bytes 368648 | tf_op jit(solution)/shard_map/ppermute | solution.py:323
  22.4 7.1 %collective-permute-start.8 = (bf16[2,3,80,128]{3,2,1,0:T(8,128)(2,1)S(1)}, bf16[2,3,80,128]{3,2,1,0:T(8,128)(2,1)S(1)}, u32[]{:S(2)}, u32[]{:S(2)}) collective-permute-start(bf16[2,3,80,128]{3,2,1,0:T(8,128)(2,1)S(1)} %get-tuple-element.48), channel_id=1, source_target_pairs={{0,4},{1,5},{2,6},{3,7},{4,0},{5,1},{6,2},{7,3},{8,12},{9,13},{10,... | collective-permute-start | bytes 368648 | tf_op jit(solution)/shard_map/ppermute | solution.py:323
  22.6 7.0 %collective-permute-start.9 = (bf16[2,3,80,128]{3,2,1,0:T(8,128)(2,1)S(1)}, bf16[2,3,80,128]{3,2,1,0:T(8,128)(2,1)S(1)}, u32[]{:S(2)}, u32[]{:S(2)}) collective-permute-start(bf16[2,3,80,128]{3,2,1,0:T(8,128)(2,1)S(1)} %get-tuple-element.49), channel_id=1, source_target_pairs={{0,2},{1,3},{2,0},{3,1},{4,6},{5,7},{6,4},{7,5},{8,10},{9,11},{10,... | collective-permute-start | bytes 368648 | tf_op jit(solution)/shard_map/ppermute | solution.py:323
  29.7 5.6 %collective-permute-start.10 = (bf16[3,80,128]{2,1,0:T(8,128)(2,1)S(1)}, bf16[3,80,128]{2,1,0:T(8,128)(2,1)S(1)}, u32[]{:S(2)}, u32[]{:S(2)}) collective-permute-start(bf16[3,80,128]{2,1,0:T(8,128)(2,1)S(1)} %fusion.3), channel_id=1, source_target_pairs={{0,16},{8,24},{16,0},{24,8},{1,17},{9,25},{17,1},{25,9},{2,18},{10... | collective-permute-start | bytes 184328 | tf_op jit(solution)/shard_map/ppermute | solution.py:333
  35.3 5.6 %collective-permute-start.13 = (bf16[3,80,128]{2,1,0:T(8,128)(2,1)S(1)}, bf16[3,80,128]{2,1,0:T(8,128)(2,1)S(1)}, u32[]{:S(2)}, u32[]{:S(2)}) collective-permute-start(bf16[3,80,128]{2,1,0:T(8,128)(2,1)S(1)} %fusion.2), channel_id=1, source_target_pairs={{0,6},{1,7},{2,4},{3,5},{4,2},{5,3},{6,0},{7,1},{8,14},{9,15},{10,... | collective-permute-start | bytes 184328 | tf_op jit(solution)/shard_map/ppermute | solution.py:343
  37.7 4.2 %collective-permute-start.12 = (bf16[3,80,128]{2,1,0:T(8,128)(2,1)S(1)}, bf16[3,80,128]{2,1,0:T(8,128)(2,1)S(1)}, u32[]{:S(2)}, u32[]{:S(2)}) collective-permute-start(bf16[3,80,128]{2,1,0:T(8,128)(2,1)S(1)} %fusion.2), channel_id=1, source_target_pairs={{0,4},{1,5},{2,6},{3,7},{4,0},{5,1},{6,2},{7,3},{8,12},{9,13},{10,... | collective-permute-start | bytes 184328 | tf_op jit(solution)/shard_map/ppermute | solution.py:343
  38.7 4.2 %collective-permute-start.11 = (bf16[3,80,128]{2,1,0:T(8,128)(2,1)S(1)}, bf16[3,80,128]{2,1,0:T(8,128)(2,1)S(1)}, u32[]{:S(2)}, u32[]{:S(2)}) collective-permute-start(bf16[3,80,128]{2,1,0:T(8,128)(2,1)S(1)} %fusion.2), channel_id=1, source_target_pairs={{0,2},{1,3},{2,0},{3,1},{4,6},{5,7},{6,4},{7,5},{8,10},{9,11},{10,... | collective-permute-start | bytes 184328 | tf_op jit(solution)/shard_map/ppermute | solution.py:343
  42.9 1.6 %collective-permute-start.14 = (bf16[4,3,80,128]{3,2,1,0:T(8,128)(2,1)S(1)}, bf16[4,3,80,128]{3,2,1,0:T(8,128)(2,1)S(1)}, u32[]{:S(2)}, u32[]{:S(2)}) collective-permute-start(bf16[4,3,80,128]{3,2,1,0:T(8,128)(2,1)S(1)} %pad_maximum_fusion.parts_ref), channel_id=1, source_target_pairs={{0,1},{1,0},{2,3},{3,2},{4,5},{5,4},{6,7},{7,6},{8,9},{9,8},{10,11... | collective-permute-start | bytes 737288 | tf_op jit(solution)/shard_map/ppermute | solution.py:345

commit v8 on v7

--- a/solution.py
+++ b/solution.py
@@ -166,7 +166,7 @@
         copy.wait()
 
 
-def pick_kernel(out_ref):
+def pick_kernel(after_ref, out_ref):
     size = out_ref.shape[0]
     group = size // 9
     j = lax.broadcasted_iota(jnp.int32, (size, size), 0)
@@ -224,22 +224,27 @@
 
     pre = jnp.swapaxes(pre_act[0], 1, 2)
     grad = jnp.swapaxes(out_grad[0], 1, 2)
-    beyond = [(i, i - PAIR if i % 2 else i + PAIR) for i in range(space)]
+    row = my_core() * (rows - 1)
+    edge = jnp.stack([lax.dynamic_index_in_dim(grad, row, 0, False), lax.dynamic_index_in_dim(pre, row, 0, False)])
+    beyond = [(i, i + 1 if i % 2 else i - 1) for i in range(space)]
     pairs = [(i, i + 1 - 2 * (i % 2)) for i in range(space)]
 
     def inside(moves):
         return [(i, j) for i, j in moves if 0 <= j < space]
 
-    their_grad = lax.ppermute(grad, "space", pairs)
-    their_pre = lax.ppermute(pre, "space", pairs)
+    near_row = lax.ppermute(edge, "space", inside(beyond))
+    _, my_pre, my_grad = lax.optimization_barrier((edge, pre, grad))
+    their_grad = lax.ppermute(my_grad, "space", pairs)
+    their_pre = lax.ppermute(my_pre, "space", pairs)
     pick = pl.pallas_call(
         pick_kernel,
         out_shape=jax.ShapeDtypeStruct((9 * group, 9 * group), F32),
+        in_specs=[anywhere()],
         out_specs=vmem(),
         compiler_params=params,
         cost_estimate=pl.CostEstimate(flops=flops, bytes_accessed=4000000, transcendentals=0),
         name="pick_rows",
-    )()
+    )(edge)
     pick, own_pre, own_grad = lax.optimization_barrier((pick, pre, grad))
     own, act_edge, grad_edge = pl.pallas_call(
         own_kernel,
@@ -258,12 +263,6 @@
         cost_estimate=pl.CostEstimate(flops=flops, bytes_accessed=4000000, transcendentals=rows * width * chans),
         name="own_terms",
     )(own_pre, own_grad)
-
-    row = (1 - my_core()) * (rows - 1)
-    ready = lax.optimization_barrier((own, act_edge, grad_edge, their_grad, their_pre))
-    own, act_edge, grad_edge, their_grad, their_pre = ready
-    outer_row = jnp.stack([lax.dynamic_index_in_dim(x, row, 0, False) for x in (their_grad, their_pre)])
-    near_row = lax.ppermute(outer_row, "space", inside(beyond))
 
     def input_part(side, edge_rows, *before):
         count = rows // 2
@@ -314,7 +313,7 @@
     )(term, act_edge, grad_edge, near_row)
 
     got = [terms[0]]
-    for k in (3, 4, 7, 5, 6, 2, 1):
+    for k in (4, 6, 1, 7, 5, 3, 2):
         moves = []
         for z in range(blocks):
             for i in range(space):
@@ -323,16 +322,15 @@
         got.append(lax.ppermute(terms[k], ("dp", "space"), moves))
 
 
-    in_grad = input_part(0, near_row)
+    their_edge = lax.dynamic_index_in_dim(their_grad, my_core() * (rows - 1), 0)
+    got[1], got[2], near_row, their_edge = lax.optimization_barrier((got[1], got[2], near_row, their_edge))
+    in_grad = input_part(1, their_edge, input_part(0, near_row))
     *got, in_grad = lax.optimization_barrier((*got, in_grad))
-    their_edge = lax.dynamic_index_in_dim(their_grad, my_core() * (rows - 1), 0)
     near_sum = sum(part.astype(F32) for part in got)
     others = []
     for k in range(1, far):
         moves = [(z, z ^ (k * NEAR)) for z in range(blocks)]
         others.append(lax.ppermute(near_sum[k].astype(BF16), "dp", moves))
-    in_grad = input_part(1, their_edge, in_grad)
-    *others, in_grad = lax.optimization_barrier((*others, in_grad))
     total = near_sum[0] + sum(other.astype(F32) for other in others)
     total = total * factor
     if outer > 1:

time: 46.2 us -> 45.4 us (0.983)
  starting transfers between devices: 23.2 us -> 22.4 us
    ppermute x3, starting transfers between devices: 5.43 us -> 1.25 us  [the longest x1 0.66 us: shards(): near_row = lax.ppermute(edge, 'space', inside(beyond))]
    ppermute x7, starting transfers between devices: 11.5 us -> 14.8 us  [shards(): got.append(lax.ppermute(terms[k], ('dp', 'space'), moves))]
    ppermute x1, waiting for transfers between devices: 0.31 us -> 3.57 us  [shards(): others.append(lax.ppermute(near_sum[k].astype(BF16), 'dp', moves))]
    ppermute x3, waiting for transfers between devices: 4.06 us -> 2.2 us  [shards(): lax.ppermute(final, 'space', [(i, i ^ k * PAIR) for i in range(space)])]
    unnamed x6, local copies, waits for them, and re-layouts: 1.2 us -> 0.02 us
    dynamic_slice x0 -> x1, local copies, waits for them, and re-layouts: none -> 0.95 us  [shards(): lax.dynamic_index_in_dim(pre, row, 0, False)]
    ppermute x3, waiting for transfers between devices: 1.08 us -> 0.47 us  [the longest x1 0.47 us: shards(): their_grad = lax.ppermute(my_grad, 'space', pairs)]
    ppermute x7, waiting for transfers between devices: 3.12 us -> 2.59 us  [shards(): got.append(lax.ppermute(terms[k], ('dp', 'space'), moves))]
  transfers between devices with their start and end apart: 15 -> 15, of which waited for: 8 -> 7; matrix products, arithmetic and copies ran while one was open for 0% -> 0% of each run, Pallas kernels for 22% -> 22%
where the time goes in v8:
time: 45.4 us; the launch traced here: 45.2 us
  starting transfers between devices  22.4 us (49%)
  Pallas kernels  12 us (26%)
  waiting for transfers between devices  8.84 us (19%)
  local copies, waits for them, and re-layouts  0.98 us (2%)
  between operations  0.83 us (2%)
    ppermute x7, starting transfers between devices, shards(): got.append(lax.ppermute(terms[k], ('dp', 'space'), moves))  14.8 us
    pallas_call x2, Pallas kernels, input_part(): pl.pallas_call(functools.partial(input_kernel, side), out_shape=jax.Shape...  5.2 us
    ppermute x1, waiting for transfers between devices, shards(): others.append(lax.ppermute(near_sum[k].astype(BF16), 'dp', moves))  3.57 us
    ppermute x3, starting transfers between devices, shards(): lax.ppermute(final, 'space', [(i, i ^ k * PAIR) for i in range(space)])  3.55 us
    pallas_call x2, Pallas kernels, place(): pl.pallas_call(functools.partial(place_kernel, flip), out_shape=jax.Shape...  2.94 us
    ppermute x1, starting transfers between devices, shards(): others.append(lax.ppermute(near_sum[k].astype(BF16), 'dp', moves))  2.65 us
    ppermute x7, waiting for transfers between devices, shards(): got.append(lax.ppermute(terms[k], ('dp', 'space'), moves))  2.59 us
    ppermute x3, waiting for transfers between devices, shards(): lax.ppermute(final, 'space', [(i, i ^ k * PAIR) for i in range(space)])  2.2 us
  transfers between devices with their start and end apart: 15, of which 7 were waited for; matrix products, arithmetic and copies ran while one was open for 0% of the time, Pallas kernels for 22%

profile of v8, /device:TPU:0, one launch (start us, length us, event | category | flops | bytes accessed | tf_op | source)
XLA Modules:
  0.0 45.2 jit_solution(4670610024067599786)
XLA Ops:
  0.6 0.9 %dynamic-slice_bitcast_fusion = (bf16[1,320,128]{2,1,0:T(8,128)(2,1)S(1)}, bf16[1,320,128]{2,1,0:T(8,128)(2,1)S(1)}) fusion(bf16[1,8,128,320]{2,3,1,0:T(8,128)(2,1)} %param.3, s32[]{:T(128)S(6)} %select_n.7, bf16[1,8,128,320]{2,3,1,0:T(8,128)(2,1)} %param.4), kind=kLoop, calls=%fused_computation.8 | loop fusion | bytes 327684 | tf_op jit(solution)/shard_map/jit(dynamic_index_in_dim)/dynamic_slice | solution.py:228
  1.6 0.5 %collective-permute-start = (bf16[8,320,128]{2,1,0:T(8,128)(2,1)}, bf16[8,320,128]{2,1,0:T(8,128)(2,1)S(1)}, u32[]{:S(2)}, u32[]{:S(2)}) collective-permute-start(bf16[8,320,128]{2,1,0:T(8,128)(2,1)} %bitcast.32), channel_id=1, source_target_pairs={{0,1},{1,0},{2,3},{3,2},{4,5},{5,4},{6,7},{7,6},{8,9},{9,8},{10,11... | collective-permute-start | bytes 1966088 | tf_op jit(solution)/shard_map/ppermute | solution.py:238
  2.2 0.7 %collective-permute-start.2 = (bf16[2,320,128]{2,1,0:T(8,128)(2,1)S(1)}, bf16[2,320,128]{2,1,0:T(8,128)(2,1)S(1)}, u32[]{:S(2)}, u32[]{:S(2)}) collective-permute-start(bf16[2,320,128]{2,1,0:T(8,128)(2,1)S(1)} %pad_maximum_fusion.1.after_ref), channel_id=1, source_target_pairs={{1,2},{2,1},{3,4},{4,3},{5,6},{6,5},{9,10},{10,9},{11,12},{12,11},... | collective-permute-start | bytes 491528 | tf_op jit(solution)/shard_map/ppermute | solution.py:235
  3.0 1.5 %own_terms.1 = (f32[3,320,512]{2,1,0:T(8,128)S(1)}, bf16[2,320,128]{2,1,0:T(8,128)(2,1)S(1)}, bf16[2,160,128]{2,1,0:T(8,128)(2,1)S(1)}) custom-call(bf16[8,320,128]{2,1,0:T(8,128)(2,1)S(1)} %bitcast.33, bf16[8,320,128]{2,1,0:T(8,128)(2,1)S(1)} %bitcast.37), custom_call_target="tpu_custom_call" | custom-call | flops 1887436800 | bytes 4000000 | tf_op jit(solution)/shard_map/own_terms/pallas_call | solution.py:249
  4.6 0.5 %collective-permute-done.1.their_grad_ref = bf16[8,320,128]{2,1,0:T(8,128)(2,1)S(1)} collective-permute-done((bf16[8,320,128]{2,1,0:T(8,128)(2,1)}, bf16[8,320,128]{2,1,0:T(8,128)(2,1)S(1)}, u32[]{:S(2)}, u32[]{:S(2)}) %collective-permute-start.1) | collective-permute-done | bytes 655392 | tf_op jit(solution)/shard_map/ppermute | solution.py:237
  5.0 1.7 %pair_terms.1.term_ref = f32[3,320,512]{2,1,0:T(8,128)S(1)} custom-call(f32[3,320,512]{2,1,0:T(8,128)S(1)} %get-tuple-element.33.term_ref, bf16[2,320,128]{2,1,0:T(8,128)(2,1)S(1)} %get-tuple-element.34.act_edge_ref, bf16[2,160,128]{2,1,0:T(8,128)(2,1)S(1)} %get-tuple-element.35.grad_edge_ref, bf16[8,320,128]{2,1,0:T(8,128)(2,1)S(1)} %collective-permute-done.their_pre_ref, ...), custom_call_target="tpu_custom_call" | custom-call | flops 1887436800 | bytes 4000000 | tf_op jit(solution)/shard_map/pair_terms/pallas_call | solution.py:288
  6.8 0.5 %edge_terms.1 = (bf16[2,3,80,128]{3,2,1,0:T(8,128)(2,1)S(1)}, bf16[2,3,80,128]{3,2,1,0:T(8,128)(2,1)S(1)}, bf16[2,3,80,128]{3,2,1,0:T(8,128)(2,1)S(1)}, bf16[2,3...) custom-call(f32[3,320,512]{2,1,0:T(8,128)S(1)} %pair_terms.1.term_re, ...), custom_call_target="tpu_custom_call" | custom-call | flops 235929600 | bytes 4000000 | tf_op jit(solution)/shard_map/edge_terms/pallas_call | solution.py:301
  7.3 3.0 %collective-permute-start.3 = (bf16[2,3,80,128]{3,2,1,0:T(8,128)(2,1)S(1)}, bf16[2,3,80,128]{3,2,1,0:T(8,128)(2,1)S(1)}, u32[]{:S(2)}, u32[]{:S(2)}) collective-permute-start(bf16[2,3,80,128]{3,2,1,0:T(8,128)(2,1)S(1)} %get-tuple-element.39), channel_id=1, source_target_pairs={{0,8},{1,9},{2,10},{3,11},{4,12},{5,13},{6,14},{7,15},{8,0},{9,1},... | collective-permute-start | bytes 368648 | tf_op jit(solution)/shard_map/ppermute | solution.py:322
  10.3 5.3 %collective-permute-start.4 = (bf16[2,3,80,128]{3,2,1,0:T(8,128)(2,1)S(1)}, bf16[2,3,80,128]{3,2,1,0:T(8,128)(2,1)S(1)}, u32[]{:S(2)}, u32[]{:S(2)}) collective-permute-start(bf16[2,3,80,128]{3,2,1,0:T(8,128)(2,1)S(1)} %get-tuple-element.40), channel_id=1, source_target_pairs={{0,12},{1,13},{2,14},{3,15},{4,8},{5,9},{6,10},{7,11},{8,4},{9,5},... | collective-permute-start | bytes 368648 | tf_op jit(solution)/shard_map/ppermute | solution.py:322
  15.6 1.3 %collective-permute-start.5 = (bf16[2,3,80,128]{3,2,1,0:T(8,128)(2,1)S(1)}, bf16[2,3,80,128]{3,2,1,0:T(8,128)(2,1)S(1)}, u32[]{:S(2)}, u32[]{:S(2)}) collective-permute-start(bf16[2,3,80,128]{3,2,1,0:T(8,128)(2,1)S(1)} %get-tuple-element.43), channel_id=1, source_target_pairs={{0,2},{1,3},{2,0},{3,1},{4,6},{5,7},{6,4},{7,5},{8,10},{9,11},{10,... | collective-permute-start | bytes 368648 | tf_op jit(solution)/shard_map/ppermute | solution.py:322
  17.1 2.3 %collective-permute-start.7 = (bf16[2,3,80,128]{3,2,1,0:T(8,128)(2,1)S(1)}, bf16[2,3,80,128]{3,2,1,0:T(8,128)(2,1)S(1)}, u32[]{:S(2)}, u32[]{:S(2)}) collective-permute-start(bf16[2,3,80,128]{3,2,1,0:T(8,128)(2,1)S(1)} %get-tuple-element.45), channel_id=1, source_target_pairs={{0,10},{1,11},{2,8},{3,9},{4,14},{5,15},{6,12},{7,13},{8,2},{9,3},... | collective-permute-start | bytes 368648 | tf_op jit(solution)/shard_map/ppermute | solution.py:322
  19.4 2.1 %collective-permute-start.8 = (bf16[2,3,80,128]{3,2,1,0:T(8,128)(2,1)S(1)}, bf16[2,3,80,128]{3,2,1,0:T(8,128)(2,1)S(1)}, u32[]{:S(2)}, u32[]{:S(2)}) collective-permute-start(bf16[2,3,80,128]{3,2,1,0:T(8,128)(2,1)S(1)} %get-tuple-element.46), channel_id=1, source_target_pairs={{0,6},{1,7},{2,4},{3,5},{4,2},{5,3},{6,0},{7,1},{8,14},{9,15},{10,... | collective-permute-start | bytes 368648 | tf_op jit(solution)/shard_map/ppermute | solution.py:322
  21.5 0.6 %collective-permute-done.4 = bf16[2,3,80,128]{3,2,1,0:T(8,128)(2,1)S(1)} collective-permute-done((bf16[2,3,80,128]{3,2,1,0:T(8,128)(2,1)S(1)}, bf16[2,3,80,128]{3,2,1,0:T(8,128)(2,1)S(1)}, u32[]{:S(2)}, u32[]{:S(2)}) %collective-permute-start.4) | collective-permute-done | bytes 122912 | tf_op jit(solution)/shard_map/ppermute | solution.py:322
  22.1 0.6 %collective-permute-start.9 = (bf16[2,3,80,128]{3,2,1,0:T(8,128)(2,1)S(1)}, bf16[2,3,80,128]{3,2,1,0:T(8,128)(2,1)S(1)}, u32[]{:S(2)}, u32[]{:S(2)}) collective-permute-start(bf16[2,3,80,128]{3,2,1,0:T(8,128)(2,1)S(1)} %get-tuple-element.47), channel_id=1, source_target_pairs={{0,4},{1,5},{2,6},{3,7},{4,0},{5,1},{6,2},{7,3},{8,12},{9,13},{10,... | collective-permute-start | bytes 368648 | tf_op jit(solution)/shard_map/ppermute | solution.py:322
  22.7 2.6 %input_grad.2.refs_0_ = bf16[8,320,128]{2,1,0:T(8,128)(2,1)} custom-call(bf16[8,320,128]{2,1,0:T(8,128)(2,1)S(1)} %bitcast.34, bf16[8,320,128]{2,1,0:T(8,128)(2,1)S(1)} %bitcast.38, bf16[2,320,128]{2,1,0:T(8,128)(2,1)S(1)} %collective-permute-done.2.near_ref.edge_ref, bf16[3,3,320,320]{3,2,1,0:T(8,128)(2,1)S(1)} %copy-done), custom_call_target="tpu_custom_call" | custom-call | flops 943718400 | bytes 3000000 | tf_op jit(solution)/shard_map/input_grad/pallas_call | solution.py:269
  25.3 2.6 %input_grad.3 = bf16[8,320,128]{2,1,0:T(8,128)(2,1)} custom-call(bf16[8,320,128]{2,1,0:T(8,128)(2,1)S(1)} %bitcast.35, bf16[8,320,128]{2,1,0:T(8,128)(2,1)S(1)} %bitcast.39, bf16[1,320,128]{2,1,0:T(8,128)(2,1)S(1)} %constant_dynamic-slice_fusion.edge_ref, bf16[3,3,320,320]{3,2,1,0:T(8,128)(2,1)S(1)} %copy-done, ...), custom_call_target="tpu_custom_call", output_to_operand_aliasing={{}: (4, {})} | custom-call | flops 943718400 | bytes 3000000 | tf_op jit(solution)/shard_map/input_grad/pallas_call | solution.py:269
  28.0 2.0 %collective-permute-done.8 = bf16[2,3,80,128]{3,2,1,0:T(8,128)(2,1)S(1)} collective-permute-done((bf16[2,3,80,128]{3,2,1,0:T(8,128)(2,1)S(1)}, bf16[2,3,80,128]{3,2,1,0:T(8,128)(2,1)S(1)}, u32[]{:S(2)}, u32[]{:S(2)}) %collective-permute-start.8) | collective-permute-done | bytes 122912 | tf_op jit(solution)/shard_map/ppermute | solution.py:322
  30.1 2.7 %collective-permute-start.10 = (bf16[3,80,128]{2,1,0:T(8,128)(2,1)S(1)}, bf16[3,80,128]{2,1,0:T(8,128)(2,1)S(1)}, u32[]{:S(2)}, u32[]{:S(2)}) collective-permute-start(bf16[3,80,128]{2,1,0:T(8,128)(2,1)S(1)} %fusion.3), channel_id=1, source_target_pairs={{0,16},{8,24},{16,0},{24,8},{1,17},{9,25},{17,1},{25,9},{2,18},{10... | collective-permute-start | bytes 184328 | tf_op jit(solution)/shard_map/ppermute | solution.py:333
  32.8 3.6 %collective-permute-done.10 = bf16[3,80,128]{2,1,0:T(8,128)(2,1)S(1)} collective-permute-done((bf16[3,80,128]{2,1,0:T(8,128)(2,1)S(1)}, bf16[3,80,128]{2,1,0:T(8,128)(2,1)S(1)}, u32[]{:S(2)}, u32[]{:S(2)}) %collective-permute-start.10) | collective-permute-done | bytes 61472 | tf_op jit(solution)/shard_map/ppermute | solution.py:333
  37.0 2.9 %collective-permute-start.13 = (bf16[3,80,128]{2,1,0:T(8,128)(2,1)S(1)}, bf16[3,80,128]{2,1,0:T(8,128)(2,1)S(1)}, u32[]{:S(2)}, u32[]{:S(2)}) collective-permute-start(bf16[3,80,128]{2,1,0:T(8,128)(2,1)S(1)} %fusion.2), channel_id=1, source_target_pairs={{0,6},{1,7},{2,4},{3,5},{4,2},{5,3},{6,0},{7,1},{8,14},{9,15},{10,... | collective-permute-start | bytes 184328 | tf_op jit(solution)/shard_map/ppermute | solution.py:341
  39.9 0.7 %collective-permute-done.11 = bf16[3,80,128]{2,1,0:T(8,128)(2,1)S(1)} collective-permute-done((bf16[3,80,128]{2,1,0:T(8,128)(2,1)S(1)}, bf16[3,80,128]{2,1,0:T(8,128)(2,1)S(1)}, u32[]{:S(2)}, u32[]{:S(2)}) %collective-permute-start.11) | collective-permute-done | bytes 61472 | tf_op jit(solution)/shard_map/ppermute | solution.py:341
  40.8 1.3 %collective-permute-done.13 = bf16[3,80,128]{2,1,0:T(8,128)(2,1)S(1)} collective-permute-done((bf16[3,80,128]{2,1,0:T(8,128)(2,1)S(1)}, bf16[3,80,128]{2,1,0:T(8,128)(2,1)S(1)}, u32[]{:S(2)}, u32[]{:S(2)}) %collective-permute-start.13) | collective-permute-done | bytes 61472 | tf_op jit(solution)/shard_map/ppermute | solution.py:341
  42.2 1.5 %place_rows.2.refs_0_ = f32[320,720]{1,0:T(8,128)} custom-call(bf16[4,3,80,128]{3,2,1,0:T(8,128)(2,1)S(1)} %pad_maximum_fusion.parts_ref, f32[144,144]{1,0:T(8,128)S(1)} %pick_rows.1.pick_ref), custom_call_target="tpu_custom_call" | custom-call | flops 165888000 | bytes 1000000 | tf_op jit(solution)/shard_map/place_rows/pallas_call | solution.py:346
  43.7 1.5 %place_rows.3 = f32[320,720]{1,0:T(8,128)} custom-call(bf16[4,3,80,128]{3,2,1,0:T(8,128)(2,1)S(1)} %collective-permute-done.14.parts_ref, f32[144,144]{1,0:T(8,128)S(1)} %pick_rows.1.pick_ref, f32[320,720]{1,0:T(8,128)} %place_rows.2.refs_0_), custom_call_target="tpu_custom_call", output_to_operand_aliasing={{}: (2, {})} | custom-call | flops 165888000 | bytes 1000000 | tf_op jit(solution)/shard_map/place_rows/pallas_call | solution.py:346
  (27 shorter events, 1.5 us)
Async XLA Ops:
  1.6 1.4 %copy-start.1 = (bf16[1,8,128,320]{2,3,1,0:T(8,128)(2,1)S(1)}, bf16[1,8,128,320]{2,3,1,0:T(8,128)(2,1)}, u32[]{:S(2)}) copy-start(bf16[1,8,128,320]{2,3,1,0:T(8,128)(2,1)} %param.3) | copy-start | bytes 1966084
  1.6 1.4 %copy-start.2 = (bf16[1,8,128,320]{2,3,1,0:T(8,128)(2,1)S(1)}, bf16[1,8,128,320]{2,3,1,0:T(8,128)(2,1)}, u32[]{:S(2)}) copy-start(bf16[1,8,128,320]{2,3,1,0:T(8,128)(2,1)} %param.4) | copy-start | bytes 1966084
  1.6 2.9 %collective-permute-start = (bf16[8,320,128]{2,1,0:T(8,128)(2,1)}, bf16[8,320,128]{2,1,0:T(8,128)(2,1)S(1)}, u32[]{:S(2)}, u32[]{:S(2)}) collective-permute-start(bf16[8,320,128]{2,1,0:T(8,128)(2,1)} %bitcast.32), channel_id=1, source_target_pairs={{0,1},{1,0},{2,3},{3,2},{4,5},{5,4},{6,7},{7,6},{8,9},{9,8},{10,11... | collective-permute-start | bytes 1966088 | tf_op jit(solution)/shard_map/ppermute | solution.py:238
  2.2 2.9 %collective-permute-start.1 = (bf16[8,320,128]{2,1,0:T(8,128)(2,1)}, bf16[8,320,128]{2,1,0:T(8,128)(2,1)S(1)}, u32[]{:S(2)}, u32[]{:S(2)}) collective-permute-start(bf16[8,320,128]{2,1,0:T(8,128)(2,1)} %bitcast.36), channel_id=1, source_target_pairs={{0,1},{1,0},{2,3},{3,2},{4,5},{5,4},{6,7},{7,6},{8,9},{9,8},{10,11... | collective-permute-start | bytes 1966088 | tf_op jit(solution)/shard_map/ppermute | solution.py:237
  2.2 4.5 %collective-permute-start.2 = (bf16[2,320,128]{2,1,0:T(8,128)(2,1)S(1)}, bf16[2,320,128]{2,1,0:T(8,128)(2,1)S(1)}, u32[]{:S(2)}, u32[]{:S(2)}) collective-permute-start(bf16[2,320,128]{2,1,0:T(8,128)(2,1)S(1)} %pad_maximum_fusion.1.after_ref), channel_id=1, source_target_pairs={{1,2},{2,1},{3,4},{4,3},{5,6},{6,5},{9,10},{10,9},{11,12},{12,11},... | collective-permute-start | bytes 491528 | tf_op jit(solution)/shard_map/ppermute | solution.py:235
  6.7 16.0 %copy-start = (bf16[3,3,320,320]{3,2,1,0:T(8,128)(2,1)S(1)}, bf16[3,3,320,320]{3,2,1,0:T(8,128)(2,1)}, u32[]{:S(2)}) copy-start(bf16[3,3,320,320]{3,2,1,0:T(8,128)(2,1)} %kernel_ref.3) | copy-start | bytes 5529604
  7.3 12.1 %collective-permute-start.3 = (bf16[2,3,80,128]{3,2,1,0:T(8,128)(2,1)S(1)}, bf16[2,3,80,128]{3,2,1,0:T(8,128)(2,1)S(1)}, u32[]{:S(2)}, u32[]{:S(2)}) collective-permute-start(bf16[2,3,80,128]{3,2,1,0:T(8,128)(2,1)S(1)} %get-tuple-element.39), channel_id=1, source_target_pairs={{0,8},{1,9},{2,10},{3,11},{4,12},{5,13},{6,14},{7,15},{8,0},{9,1},... | collective-permute-start | bytes 368648 | tf_op jit(solution)/shard_map/ppermute | solution.py:322
  10.3 11.8 %collective-permute-start.4 = (bf16[2,3,80,128]{3,2,1,0:T(8,128)(2,1)S(1)}, bf16[2,3,80,128]{3,2,1,0:T(8,128)(2,1)S(1)}, u32[]{:S(2)}, u32[]{:S(2)}) collective-permute-start(bf16[2,3,80,128]{3,2,1,0:T(8,128)(2,1)S(1)} %get-tuple-element.40), channel_id=1, source_target_pairs={{0,12},{1,13},{2,14},{3,15},{4,8},{5,9},{6,10},{7,11},{8,4},{9,5},... | collective-permute-start | bytes 368648 | tf_op jit(solution)/shard_map/ppermute | solution.py:322
  15.6 12.4 %collective-permute-start.5 = (bf16[2,3,80,128]{3,2,1,0:T(8,128)(2,1)S(1)}, bf16[2,3,80,128]{3,2,1,0:T(8,128)(2,1)S(1)}, u32[]{:S(2)}, u32[]{:S(2)}) collective-permute-start(bf16[2,3,80,128]{3,2,1,0:T(8,128)(2,1)S(1)} %get-tuple-element.43), channel_id=1, source_target_pairs={{0,2},{1,3},{2,0},{3,1},{4,6},{5,7},{6,4},{7,5},{8,10},{9,11},{10,... | collective-permute-start | bytes 368648 | tf_op jit(solution)/shard_map/ppermute | solution.py:322
  16.9 11.1 %collective-permute-start.6 = (bf16[2,3,80,128]{3,2,1,0:T(8,128)(2,1)S(1)}, bf16[2,3,80,128]{3,2,1,0:T(8,128)(2,1)S(1)}, u32[]{:S(2)}, u32[]{:S(2)}) collective-permute-start(bf16[2,3,80,128]{3,2,1,0:T(8,128)(2,1)S(1)} %get-tuple-element.44), channel_id=1, source_target_pairs={{0,14},{1,15},{2,12},{3,13},{4,10},{5,11},{6,8},{7,9},{8,6},{9,7},... | collective-permute-start | bytes 368648 | tf_op jit(solution)/shard_map/ppermute | solution.py:322
  17.1 10.9 %collective-permute-start.7 = (bf16[2,3,80,128]{3,2,1,0:T(8,128)(2,1)S(1)}, bf16[2,3,80,128]{3,2,1,0:T(8,128)(2,1)S(1)}, u32[]{:S(2)}, u32[]{:S(2)}) collective-permute-start(bf16[2,3,80,128]{3,2,1,0:T(8,128)(2,1)S(1)} %get-tuple-element.45), channel_id=1, source_target_pairs={{0,10},{1,11},{2,8},{3,9},{4,14},{5,15},{6,12},{7,13},{8,2},{9,3},... | collective-permute-start | bytes 368648 | tf_op jit(solution)/shard_map/ppermute | solution.py:322
  19.4 10.6 %collective-permute-start.8 = (bf16[2,3,80,128]{3,2,1,0:T(8,128)(2,1)S(1)}, bf16[2,3,80,128]{3,2,1,0:T(8,128)(2,1)S(1)}, u32[]{:S(2)}, u32[]{:S(2)}) collective-permute-start(bf16[2,3,80,128]{3,2,1,0:T(8,128)(2,1)S(1)} %get-tuple-element.46), channel_id=1, source_target_pairs={{0,6},{1,7},{2,4},{3,5},{4,2},{5,3},{6,0},{7,1},{8,14},{9,15},{10,... | collective-permute-start | bytes 368648 | tf_op jit(solution)/shard_map/ppermute | solution.py:322
  22.1 7.9 %collective-permute-start.9 = (bf16[2,3,80,128]{3,2,1,0:T(8,128)(2,1)S(1)}, bf16[2,3,80,128]{3,2,1,0:T(8,128)(2,1)S(1)}, u32[]{:S(2)}, u32[]{:S(2)}) collective-permute-start(bf16[2,3,80,128]{3,2,1,0:T(8,128)(2,1)S(1)} %get-tuple-element.47), channel_id=1, source_target_pairs={{0,4},{1,5},{2,6},{3,7},{4,0},{5,1},{6,2},{7,3},{8,12},{9,13},{10,... | collective-permute-start | bytes 368648 | tf_op jit(solution)/shard_map/ppermute | solution.py:322
  30.1 6.2 %collective-permute-start.10 = (bf16[3,80,128]{2,1,0:T(8,128)(2,1)S(1)}, bf16[3,80,128]{2,1,0:T(8,128)(2,1)S(1)}, u32[]{:S(2)}, u32[]{:S(2)}) collective-permute-start(bf16[3,80,128]{2,1,0:T(8,128)(2,1)S(1)} %fusion.3), channel_id=1, source_target_pairs={{0,16},{8,24},{16,0},{24,8},{1,17},{9,25},{17,1},{25,9},{2,18},{10... | collective-permute-start | bytes 184328 | tf_op jit(solution)/shard_map/ppermute | solution.py:333
  36.4 4.3 %collective-permute-start.11 = (bf16[3,80,128]{2,1,0:T(8,128)(2,1)S(1)}, bf16[3,80,128]{2,1,0:T(8,128)(2,1)S(1)}, u32[]{:S(2)}, u32[]{:S(2)}) collective-permute-start(bf16[3,80,128]{2,1,0:T(8,128)(2,1)S(1)} %fusion.2), channel_id=1, source_target_pairs={{0,2},{1,3},{2,0},{3,1},{4,6},{5,7},{6,4},{7,5},{8,10},{9,11},{10,... | collective-permute-start | bytes 184328 | tf_op jit(solution)/shard_map/ppermute | solution.py:341
  36.6 4.2 %collective-permute-start.12 = (bf16[3,80,128]{2,1,0:T(8,128)(2,1)S(1)}, bf16[3,80,128]{2,1,0:T(8,128)(2,1)S(1)}, u32[]{:S(2)}, u32[]{:S(2)}) collective-permute-start(bf16[3,80,128]{2,1,0:T(8,128)(2,1)S(1)} %fusion.2), channel_id=1, source_target_pairs={{0,4},{1,5},{2,6},{3,7},{4,0},{5,1},{6,2},{7,3},{8,12},{9,13},{10,... | collective-permute-start | bytes 184328 | tf_op jit(solution)/shard_map/ppermute | solution.py:341
  37.0 5.1 %collective-permute-start.13 = (bf16[3,80,128]{2,1,0:T(8,128)(2,1)S(1)}, bf16[3,80,128]{2,1,0:T(8,128)(2,1)S(1)}, u32[]{:S(2)}, u32[]{:S(2)}) collective-permute-start(bf16[3,80,128]{2,1,0:T(8,128)(2,1)S(1)} %fusion.2), channel_id=1, source_target_pairs={{0,6},{1,7},{2,4},{3,5},{4,2},{5,3},{6,0},{7,1},{8,14},{9,15},{10,... | collective-permute-start | bytes 184328 | tf_op jit(solution)/shard_map/ppermute | solution.py:341
  42.2 1.6 %collective-permute-start.14 = (bf16[4,3,80,128]{3,2,1,0:T(8,128)(2,1)S(1)}, bf16[4,3,80,128]{3,2,1,0:T(8,128)(2,1)S(1)}, u32[]{:S(2)}, u32[]{:S(2)}) collective-permute-start(bf16[4,3,80,128]{3,2,1,0:T(8,128)(2,1)S(1)} %pad_maximum_fusion.parts_ref), channel_id=1, source_target_pairs={{0,1},{1,0},{2,3},{3,2},{4,5},{5,4},{6,7},{7,6},{8,9},{9,8},{10,11... | collective-permute-start | bytes 737288 | tf_op jit(solution)/shard_map/ppermute | solution.py:343

commit v9 on v8

--- a/solution.py
+++ b/solution.py
@@ -103,11 +103,18 @@
         )
 
 
+def sends(outers):
+    whole, split = (4, 6, 1), (7, 5, 3, 2)
+    return (
+        [(k, 0, outers) for k in whole] + [(k, 1, outers) for k in split] + [(k, 0, 1) for k in split]
+    )
+
+
 def edge_kernel(term_ref, act_edge_ref, grad_edge_ref, near_ref, *refs):
-    out_refs, (taps_s, term_s) = refs[: PLANE * NEAR], refs[PLANE * NEAR :]
+    out_refs, (own_ref, taps_s, term_s) = refs[:-3], refs[-3:]
     _, chans, width = near_ref.shape
     half = chans // PAIR
-    outers, _, block, _ = out_refs[0].shape
+    outers, _, block, _ = own_ref.shape
     core = my_core()
     first = core == 0
     near_act = silu(near_ref[1])
@@ -123,13 +130,13 @@
             term += lax.dot_general(acts[a], taps, NT, preferred_element_type=F32)
         for p in range(PLANE):
             for z in range(NEAR * outers):
-                term_s[z % NEAR * PLANE + p, z // NEAR, a] = term[
-                    z * block : (z + 1) * block, p * LANES : (p + 1) * LANES
-                ].astype(term_s.dtype)
+                term_s[z % NEAR * PLANE + p, z // NEAR, a] = term[z * block : (z + 1) * block, p * LANES : (p + 1) * LANES]
     at, outer_at = near_index(), lax.axis_index("dp") // NEAR
-    for k, out_ref in enumerate(out_refs):
-        for j in range(outers):
-            out_ref[j] = term_s[at ^ k, outer_at ^ j]
+    for j in range(outers):
+        own_ref[j] = term_s[at, outer_at ^ j]
+    for (k, first_j, last_j), out_ref in zip(sends(outers), out_refs):
+        for j in range(first_j, last_j):
+            out_ref[j - first_j] = term_s[at ^ k, outer_at ^ j].astype(out_ref.dtype)
 
 
 def input_kernel(side, pre_ref, grad_ref, edge_ref, kernel_ref, *refs):
@@ -284,7 +291,9 @@
             name="input_grad",
         )(pre, grad, edge_rows, kernel, *before)
 
-    piece = jax.ShapeDtypeStruct((far, 3, block, LANES), BF16)
+    order = sends(far)
+    pieces = [jax.ShapeDtypeStruct((last_j - first_j, 3, block, LANES), BF16) for _, first_j, last_j in order]
+    pieces.append(jax.ShapeDtypeStruct((far, 3, block, LANES), F32))
     term = pl.pallas_call(
         pair_kernel,
         out_shape=jax.ShapeDtypeStruct((3, chans, PLANE * LANES), F32),
@@ -298,40 +307,44 @@
         cost_estimate=pl.CostEstimate(flops=flops, bytes_accessed=4000000, transcendentals=rows * width * chans),
         name="pair_terms",
     )(own, act_edge, grad_edge, their_pre, their_grad)
-    terms = pl.pallas_call(
+    *terms, own_piece = pl.pallas_call(
         edge_kernel,
-        out_shape=(piece,) * (NEAR * PLANE),
+        out_shape=tuple(pieces),
         in_specs=[vmem()] * 4,
-        out_specs=(vmem(),) * (NEAR * PLANE),
+        out_specs=(vmem(),) * len(pieces),
         scratch_shapes=[
             pltpu.VMEM((PLANE * LANES, 2 * width), BF16),
-            pltpu.VMEM((NEAR * PLANE, far, 3, block, LANES), BF16),
+            pltpu.VMEM((NEAR * PLANE, far, 3, block, LANES), F32),
         ],
         compiler_params=params,
         cost_estimate=pl.CostEstimate(flops=flops // 8, bytes_accessed=4000000, transcendentals=width * chans),
         name="edge_terms",
     )(term, act_edge, grad_edge, near_row)
 
-    got = [terms[0]]
-    for k in (4, 6, 1, 7, 5, 3, 2):
+    got = []
+    for (k, _, _), term in zip(order, terms):
         moves = []
         for z in range(blocks):
             for i in range(space):
                 to_z, to_i = z ^ (k // PLANE), i ^ (k % PLANE * PAIR)
                 moves.append((z * space + i, to_z * space + to_i))
-        got.append(lax.ppermute(terms[k], ("dp", "space"), moves))
+        got.append(lax.ppermute(term, ("dp", "space"), moves))
 
 
     their_edge = lax.dynamic_index_in_dim(their_grad, my_core() * (rows - 1), 0)
-    got[1], got[2], near_row, their_edge = lax.optimization_barrier((got[1], got[2], near_row, their_edge))
-    in_grad = input_part(1, their_edge, input_part(0, near_row))
-    *got, in_grad = lax.optimization_barrier((*got, in_grad))
-    near_sum = sum(part.astype(F32) for part in got)
+    got[0], got[1], near_row, their_edge = lax.optimization_barrier((got[0], got[1], near_row, their_edge))
+    in_grad = input_part(0, near_row)
+    *first_got, in_grad = lax.optimization_barrier((*got[:7], in_grad))
+    got[:7] = first_got
+    travel = own_piece[1:] + sum(part[-(far - 1) :].astype(F32) for part in got[:7])
     others = []
     for k in range(1, far):
         moves = [(z, z ^ (k * NEAR)) for z in range(blocks)]
-        others.append(lax.ppermute(near_sum[k].astype(BF16), "dp", moves))
-    total = near_sum[0] + sum(other.astype(F32) for other in others)
+        others.append(lax.ppermute(travel[k - 1].astype(BF16), "dp", moves))
+    in_grad = input_part(1, their_edge, in_grad)
+    *others, in_grad = lax.optimization_barrier((*others, in_grad))
+    total = own_piece[0] + sum(part[0].astype(F32) for part in got[:3] + got[7:])
+    total = total + sum(other.astype(F32) for other in others)
     total = total * factor
     if outer > 1:
         total = lax.psum(total, "space", axis_index_groups=[[o * inner + i for o in range(outer)] for i in range(inner)])

time: 45.4 us -> 47.1 us (1.037)
  starting transfers between devices: 22.4 us -> 28.6 us
  waiting for transfers between devices: 8.84 us -> 4.29 us
    ppermute x8 -> x12, starting transfers between devices: 17.5 us -> 23.7 us  [the longest x11 21.1 us: shards(): got.append(lax.ppermute(term, ('dp', 'space'), moves))]
    ppermute x8 -> x12, waiting for transfers between devices: 6.15 us -> 0.61 us  [the longest x11 0.61 us: shards(): got.append(lax.ppermute(term, ('dp', 'space'), moves))]
    ppermute x3, waiting for transfers between devices: 2.2 us -> 3.19 us  [shards(): lax.ppermute(final, 'space', [(i, i ^ k * PAIR) for i in range(space)])]
  transfers between devices with their start and end apart: 15 -> 19, of which waited for: 7 -> 5; matrix products, arithmetic and copies ran while one was open for 0% -> 0% of each run, Pallas kernels for 22% -> 21%
where the time goes in v9:
time: 47.1 us; the launch traced here: 46.9 us
  starting transfers between devices  28.6 us (61%)
  Pallas kernels  12 us (25%)
  waiting for transfers between devices  4.29 us (9%)
  local copies, waits for them, and re-layouts  0.97 us (2%)
  between operations  0.85 us (2%)
    ppermute x11, starting transfers between devices, shards(): got.append(lax.ppermute(term, ('dp', 'space'), moves))  21.1 us
    pallas_call x2, Pallas kernels, input_part(): pl.pallas_call(functools.partial(input_kernel, side), out_shape=jax.Shape...  5.18 us
    ppermute x3, starting transfers between devices, shards(): lax.ppermute(final, 'space', [(i, i ^ k * PAIR) for i in range(space)])  3.55 us
    ppermute x3, waiting for transfers between devices, shards(): lax.ppermute(final, 'space', [(i, i ^ k * PAIR) for i in range(space)])  3.19 us
    pallas_call x2, Pallas kernels, place(): pl.pallas_call(functools.partial(place_kernel, flip), out_shape=jax.Shape...  2.94 us
    ppermute x1, starting transfers between devices, shards(): others.append(lax.ppermute(travel[k - 1].astype(BF16), 'dp', moves))  2.65 us
    pallas_call x1, Pallas kernels, shards(): pl.pallas_call(pair_kernel, out_shape=jax.ShapeDtypeStruct((3, chans, PLA...  1.7 us
    pallas_call x1, Pallas kernels, shards(): pl.pallas_call(own_kernel, out_shape=(jax.ShapeDtypeStruct((3, chans, PLA...  1.53 us
  transfers between devices with their start and end apart: 19, of which 5 were waited for; matrix products, arithmetic and copies ran while one was open for 0% of the time, Pallas kernels for 21%

profile of v9, /device:TPU:0, one launch (start us, length us, event | category | flops | bytes accessed | tf_op | source)
XLA Modules:
  0.0 46.9 jit_solution(1052998239521605043)
XLA Ops:
  0.6 0.9 %dynamic-slice_bitcast_fusion = (bf16[1,320,128]{2,1,0:T(8,128)(2,1)S(1)}, bf16[1,320,128]{2,1,0:T(8,128)(2,1)S(1)}) fusion(bf16[1,8,128,320]{2,3,1,0:T(8,128)(2,1)} %param.3, s32[]{:T(128)S(6)} %select_n.7, bf16[1,8,128,320]{2,3,1,0:T(8,128)(2,1)} %param.4), kind=kLoop, calls=%fused_computation.6 | loop fusion | bytes 327684 | tf_op jit(solution)/shard_map/jit(dynamic_index_in_dim)/dynamic_slice | solution.py:235
  2.2 0.7 %collective-permute-start.2 = (bf16[2,320,128]{2,1,0:T(8,128)(2,1)S(1)}, bf16[2,320,128]{2,1,0:T(8,128)(2,1)S(1)}, u32[]{:S(2)}, u32[]{:S(2)}) collective-permute-start(bf16[2,320,128]{2,1,0:T(8,128)(2,1)S(1)} %pad_maximum_fusion.1.after_ref), channel_id=1, source_target_pairs={{1,2},{2,1},{3,4},{4,3},{5,6},{6,5},{9,10},{10,9},{11,12},{12,11},... | collective-permute-start | bytes 491528 | tf_op jit(solution)/shard_map/ppermute | solution.py:242
  3.0 1.5 %own_terms.1 = (f32[3,320,512]{2,1,0:T(8,128)S(1)}, bf16[2,320,128]{2,1,0:T(8,128)(2,1)S(1)}, bf16[2,160,128]{2,1,0:T(8,128)(2,1)S(1)}) custom-call(bf16[8,320,128]{2,1,0:T(8,128)(2,1)S(1)} %bitcast.31, bf16[8,320,128]{2,1,0:T(8,128)(2,1)S(1)} %bitcast.35), custom_call_target="tpu_custom_call" | custom-call | flops 1887436800 | bytes 4000000 | tf_op jit(solution)/shard_map/own_terms/pallas_call | solution.py:256
  5.0 1.7 %pair_terms.1.term_ref = f32[3,320,512]{2,1,0:T(8,128)S(1)} custom-call(f32[3,320,512]{2,1,0:T(8,128)S(1)} %get-tuple-element.38.term_ref, bf16[2,320,128]{2,1,0:T(8,128)(2,1)S(1)} %get-tuple-element.39.act_edge_ref, bf16[2,160,128]{2,1,0:T(8,128)(2,1)S(1)} %get-tuple-element.40.grad_edge_ref, bf16[8,320,128]{2,1,0:T(8,128)(2,1)S(1)} %collective-permute-done.their_pre_ref, ...), custom_call_target="tpu_custom_call" | custom-call | flops 1887436800 | bytes 4000000 | tf_op jit(solution)/shard_map/pair_terms/pallas_call | solution.py:297
  6.8 0.5 %edge_terms.1 = (bf16[2,3,80,128]{3,2,1,0:T(8,128)(2,1)S(1)}, bf16[2,3,80,128]{3,2,1,0:T(8,128)(2,1)S(1)}, bf16[2,3,80,128]{3,2,1,0:T(8,128)(2,1)S(1)}, bf16[1,3...) custom-call(f32[3,320,512]{2,1,0:T(8,128)S(1)} %pair_terms.1.term_re, ...), custom_call_target="tpu_custom_call" | custom-call | flops 235929600 | bytes 4000000 | tf_op jit(solution)/shard_map/edge_terms/pallas_call | solution.py:310
  7.3 3.0 %collective-permute-start.3 = (bf16[2,3,80,128]{3,2,1,0:T(8,128)(2,1)S(1)}, bf16[2,3,80,128]{3,2,1,0:T(8,128)(2,1)S(1)}, u32[]{:S(2)}, u32[]{:S(2)}) collective-permute-start(bf16[2,3,80,128]{3,2,1,0:T(8,128)(2,1)S(1)} %get-tuple-element.44), channel_id=1, source_target_pairs={{0,8},{1,9},{2,10},{3,11},{4,12},{5,13},{6,14},{7,15},{8,0},{9,1},... | collective-permute-start | bytes 368648 | tf_op jit(solution)/shard_map/ppermute | solution.py:331
  10.3 5.3 %collective-permute-start.4 = (bf16[2,3,80,128]{3,2,1,0:T(8,128)(2,1)S(1)}, bf16[2,3,80,128]{3,2,1,0:T(8,128)(2,1)S(1)}, u32[]{:S(2)}, u32[]{:S(2)}) collective-permute-start(bf16[2,3,80,128]{3,2,1,0:T(8,128)(2,1)S(1)} %get-tuple-element.45), channel_id=1, source_target_pairs={{0,12},{1,13},{2,14},{3,15},{4,8},{5,9},{6,10},{7,11},{8,4},{9,5},... | collective-permute-start | bytes 368648 | tf_op jit(solution)/shard_map/ppermute | solution.py:331
  15.6 1.3 %collective-permute-start.5 = (bf16[2,3,80,128]{3,2,1,0:T(8,128)(2,1)S(1)}, bf16[2,3,80,128]{3,2,1,0:T(8,128)(2,1)S(1)}, u32[]{:S(2)}, u32[]{:S(2)}) collective-permute-start(bf16[2,3,80,128]{3,2,1,0:T(8,128)(2,1)S(1)} %get-tuple-element.48), channel_id=1, source_target_pairs={{0,2},{1,3},{2,0},{3,1},{4,6},{5,7},{6,4},{7,5},{8,10},{9,11},{10,... | collective-permute-start | bytes 368648 | tf_op jit(solution)/shard_map/ppermute | solution.py:331
  17.1 2.3 %collective-permute-start.7 = (bf16[1,3,80,128]{3,2,1,0:T(8,128)(2,1)S(1)}, bf16[1,3,80,128]{3,2,1,0:T(8,128)(2,1)S(1)}, u32[]{:S(2)}, u32[]{:S(2)}) collective-permute-start(bf16[1,3,80,128]{3,2,1,0:T(8,128)(2,1)S(1)} %get-tuple-element.50), channel_id=1, source_target_pairs={{0,10},{1,11},{2,8},{3,9},{4,14},{5,15},{6,12},{7,13},{8,2},{9,3},... | collective-permute-start | bytes 184328 | tf_op jit(solution)/shard_map/ppermute | solution.py:331
  19.4 2.1 %collective-permute-start.8 = (bf16[1,3,80,128]{3,2,1,0:T(8,128)(2,1)S(1)}, bf16[1,3,80,128]{3,2,1,0:T(8,128)(2,1)S(1)}, u32[]{:S(2)}, u32[]{:S(2)}) collective-permute-start(bf16[1,3,80,128]{3,2,1,0:T(8,128)(2,1)S(1)} %get-tuple-element.51), channel_id=1, source_target_pairs={{0,6},{1,7},{2,4},{3,5},{4,2},{5,3},{6,0},{7,1},{8,14},{9,15},{10,... | collective-permute-start | bytes 184328 | tf_op jit(solution)/shard_map/ppermute | solution.py:331
  21.6 0.6 %collective-permute-done.4 = bf16[2,3,80,128]{3,2,1,0:T(8,128)(2,1)S(1)} collective-permute-done((bf16[2,3,80,128]{3,2,1,0:T(8,128)(2,1)S(1)}, bf16[2,3,80,128]{3,2,1,0:T(8,128)(2,1)S(1)}, u32[]{:S(2)}, u32[]{:S(2)}) %collective-permute-start.4) | collective-permute-done | bytes 122912 | tf_op jit(solution)/shard_map/ppermute | solution.py:331
  22.6 2.6 %input_grad.2.refs_0_ = bf16[8,320,128]{2,1,0:T(8,128)(2,1)} custom-call(bf16[8,320,128]{2,1,0:T(8,128)(2,1)S(1)} %bitcast.32, bf16[8,320,128]{2,1,0:T(8,128)(2,1)S(1)} %bitcast.36, bf16[2,320,128]{2,1,0:T(8,128)(2,1)S(1)} %collective-permute-done.2.near_ref.edge_ref, bf16[3,3,320,320]{3,2,1,0:T(8,128)(2,1)S(1)} %copy-done), custom_call_target="tpu_custom_call" | custom-call | flops 943718400 | bytes 3000000 | tf_op jit(solution)/shard_map/input_grad/pallas_call | solution.py:276
  25.2 3.8 %collective-permute-start.11 = (bf16[1,3,80,128]{3,2,1,0:T(8,128)(2,1)S(1)}, bf16[1,3,80,128]{3,2,1,0:T(8,128)(2,1)S(1)}, u32[]{:S(2)}, u32[]{:S(2)}) collective-permute-start(bf16[1,3,80,128]{3,2,1,0:T(8,128)(2,1)S(1)} %get-tuple-element.64), channel_id=1, source_target_pairs={{0,14},{1,15},{2,12},{3,13},{4,10},{5,11},{6,8},{7,9},{8,6},{9,7},... | collective-permute-start | bytes 184328 | tf_op jit(solution)/shard_map/ppermute | solution.py:331
  29.2 0.8 %collective-permute-start.13 = (bf16[1,3,80,128]{3,2,1,0:T(8,128)(2,1)S(1)}, bf16[1,3,80,128]{3,2,1,0:T(8,128)(2,1)S(1)}, u32[]{:S(2)}, u32[]{:S(2)}) collective-permute-start(bf16[1,3,80,128]{3,2,1,0:T(8,128)(2,1)S(1)} %get-tuple-element.66), channel_id=1, source_target_pairs={{0,6},{1,7},{2,4},{3,5},{4,2},{5,3},{6,0},{7,1},{8,14},{9,15},{10,... | collective-permute-start | bytes 184328 | tf_op jit(solution)/shard_map/ppermute | solution.py:331
  30.0 1.6 %collective-permute-start.14 = (bf16[1,3,80,128]{3,2,1,0:T(8,128)(2,1)S(1)}, bf16[1,3,80,128]{3,2,1,0:T(8,128)(2,1)S(1)}, u32[]{:S(2)}, u32[]{:S(2)}) collective-permute-start(bf16[1,3,80,128]{3,2,1,0:T(8,128)(2,1)S(1)} %get-tuple-element.67), channel_id=1, source_target_pairs={{0,4},{1,5},{2,6},{3,7},{4,0},{5,1},{6,2},{7,3},{8,12},{9,13},{10,... | collective-permute-start | bytes 184328 | tf_op jit(solution)/shard_map/ppermute | solution.py:331
  31.7 2.6 %collective-permute-start.10 = (bf16[3,80,128]{2,1,0:T(8,128)(2,1)S(1)}, bf16[3,80,128]{2,1,0:T(8,128)(2,1)S(1)}, u32[]{:S(2)}, u32[]{:S(2)}) collective-permute-start(bf16[3,80,128]{2,1,0:T(8,128)(2,1)S(1)} %fusion.2), channel_id=1, source_target_pairs={{0,16},{8,24},{16,0},{24,8},{1,17},{9,25},{17,1},{25,9},{2,18},{10... | collective-permute-start | bytes 184328 | tf_op jit(solution)/shard_map/ppermute | solution.py:343
  34.3 2.6 %input_grad.3 = bf16[8,320,128]{2,1,0:T(8,128)(2,1)} custom-call(bf16[8,320,128]{2,1,0:T(8,128)(2,1)S(1)} %bitcast.33, bf16[8,320,128]{2,1,0:T(8,128)(2,1)S(1)} %bitcast.37, bf16[1,320,128]{2,1,0:T(8,128)(2,1)S(1)} %constant_dynamic-slice_fusion.edge_ref, bf16[3,3,320,320]{3,2,1,0:T(8,128)(2,1)S(1)} %copy-done, ...), custom_call_target="tpu_custom_call", output_to_operand_aliasing={{}: (4, {})} | custom-call | flops 943718400 | bytes 3000000 | tf_op jit(solution)/shard_map/input_grad/pallas_call | solution.py:276
  37.1 1.2 %collective-permute-start.15 = (bf16[3,80,128]{2,1,0:T(8,128)(2,1)S(1)}, bf16[3,80,128]{2,1,0:T(8,128)(2,1)S(1)}, u32[]{:S(2)}, u32[]{:S(2)}) collective-permute-start(bf16[3,80,128]{2,1,0:T(8,128)(2,1)S(1)} %fusion.1), channel_id=1, source_target_pairs={{0,2},{1,3},{2,0},{3,1},{4,6},{5,7},{6,4},{7,5},{8,10},{9,11},{10,... | collective-permute-start | bytes 184328 | tf_op jit(solution)/shard_map/ppermute | solution.py:354
  38.7 1.9 %collective-permute-start.17 = (bf16[3,80,128]{2,1,0:T(8,128)(2,1)S(1)}, bf16[3,80,128]{2,1,0:T(8,128)(2,1)S(1)}, u32[]{:S(2)}, u32[]{:S(2)}) collective-permute-start(bf16[3,80,128]{2,1,0:T(8,128)(2,1)S(1)} %fusion.1), channel_id=1, source_target_pairs={{0,6},{1,7},{2,4},{3,5},{4,2},{5,3},{6,0},{7,1},{8,14},{9,15},{10,... | collective-permute-start | bytes 184328 | tf_op jit(solution)/shard_map/ppermute | solution.py:354
  40.6 0.7 %collective-permute-done.15 = bf16[3,80,128]{2,1,0:T(8,128)(2,1)S(1)} collective-permute-done((bf16[3,80,128]{2,1,0:T(8,128)(2,1)S(1)}, bf16[3,80,128]{2,1,0:T(8,128)(2,1)S(1)}, u32[]{:S(2)}, u32[]{:S(2)}) %collective-permute-start.15) | collective-permute-done | bytes 61472 | tf_op jit(solution)/shard_map/ppermute | solution.py:354
  41.4 1.1 %collective-permute-done.16 = bf16[3,80,128]{2,1,0:T(8,128)(2,1)S(1)} collective-permute-done((bf16[3,80,128]{2,1,0:T(8,128)(2,1)S(1)}, bf16[3,80,128]{2,1,0:T(8,128)(2,1)S(1)}, u32[]{:S(2)}, u32[]{:S(2)}) %collective-permute-start.16) | collective-permute-done | bytes 61472 | tf_op jit(solution)/shard_map/ppermute | solution.py:354
  42.5 1.3 %collective-permute-done.17 = bf16[3,80,128]{2,1,0:T(8,128)(2,1)S(1)} collective-permute-done((bf16[3,80,128]{2,1,0:T(8,128)(2,1)S(1)}, bf16[3,80,128]{2,1,0:T(8,128)(2,1)S(1)}, u32[]{:S(2)}, u32[]{:S(2)}) %collective-permute-start.17) | collective-permute-done | bytes 61472 | tf_op jit(solution)/shard_map/ppermute | solution.py:354
  43.9 1.5 %place_rows.2.refs_0_ = f32[320,720]{1,0:T(8,128)} custom-call(bf16[4,3,80,128]{3,2,1,0:T(8,128)(2,1)S(1)} %pad_maximum_fusion.parts_ref, f32[144,144]{1,0:T(8,128)S(1)} %pick_rows.1.pick_ref), custom_call_target="tpu_custom_call" | custom-call | flops 165888000 | bytes 1000000 | tf_op jit(solution)/shard_map/place_rows/pallas_call | solution.py:359
  45.4 1.5 %place_rows.3 = f32[320,720]{1,0:T(8,128)} custom-call(bf16[4,3,80,128]{3,2,1,0:T(8,128)(2,1)S(1)} %collective-permute-done.18.parts_ref, f32[144,144]{1,0:T(8,128)S(1)} %pick_rows.1.pick_ref, f32[320,720]{1,0:T(8,128)} %place_rows.2.refs_0_), custom_call_target="tpu_custom_call", output_to_operand_aliasing={{}: (2, {})} | custom-call | flops 165888000 | bytes 1000000 | tf_op jit(solution)/shard_map/place_rows/pallas_call | solution.py:359
  (34 shorter events, 2.8 us)
Async XLA Ops:
  1.6 1.4 %copy-start.1 = (bf16[1,8,128,320]{2,3,1,0:T(8,128)(2,1)S(1)}, bf16[1,8,128,320]{2,3,1,0:T(8,128)(2,1)}, u32[]{:S(2)}) copy-start(bf16[1,8,128,320]{2,3,1,0:T(8,128)(2,1)} %param.3) | copy-start | bytes 1966084
  1.6 1.4 %copy-start.2 = (bf16[1,8,128,320]{2,3,1,0:T(8,128)(2,1)S(1)}, bf16[1,8,128,320]{2,3,1,0:T(8,128)(2,1)}, u32[]{:S(2)}) copy-start(bf16[1,8,128,320]{2,3,1,0:T(8,128)(2,1)} %param.4) | copy-start | bytes 1966084
  1.6 2.9 %collective-permute-start = (bf16[8,320,128]{2,1,0:T(8,128)(2,1)}, bf16[8,320,128]{2,1,0:T(8,128)(2,1)S(1)}, u32[]{:S(2)}, u32[]{:S(2)}) collective-permute-start(bf16[8,320,128]{2,1,0:T(8,128)(2,1)} %bitcast.30), channel_id=1, source_target_pairs={{0,1},{1,0},{2,3},{3,2},{4,5},{5,4},{6,7},{7,6},{8,9},{9,8},{10,11... | collective-permute-start | bytes 1966088 | tf_op jit(solution)/shard_map/ppermute | solution.py:245
  2.2 2.9 %collective-permute-start.1 = (bf16[8,320,128]{2,1,0:T(8,128)(2,1)}, bf16[8,320,128]{2,1,0:T(8,128)(2,1)S(1)}, u32[]{:S(2)}, u32[]{:S(2)}) collective-permute-start(bf16[8,320,128]{2,1,0:T(8,128)(2,1)} %bitcast.34), channel_id=1, source_target_pairs={{0,1},{1,0},{2,3},{3,2},{4,5},{5,4},{6,7},{7,6},{8,9},{9,8},{10,11... | collective-permute-start | bytes 1966088 | tf_op jit(solution)/shard_map/ppermute | solution.py:244
  2.2 4.5 %collective-permute-start.2 = (bf16[2,320,128]{2,1,0:T(8,128)(2,1)S(1)}, bf16[2,320,128]{2,1,0:T(8,128)(2,1)S(1)}, u32[]{:S(2)}, u32[]{:S(2)}) collective-permute-start(bf16[2,320,128]{2,1,0:T(8,128)(2,1)S(1)} %pad_maximum_fusion.1.after_ref), channel_id=1, source_target_pairs={{1,2},{2,1},{3,4},{4,3},{5,6},{6,5},{9,10},{10,9},{11,12},{12,11},... | collective-permute-start | bytes 491528 | tf_op jit(solution)/shard_map/ppermute | solution.py:242
  6.7 15.8 %copy-start = (bf16[3,3,320,320]{3,2,1,0:T(8,128)(2,1)S(1)}, bf16[3,3,320,320]{3,2,1,0:T(8,128)(2,1)}, u32[]{:S(2)}) copy-start(bf16[3,3,320,320]{3,2,1,0:T(8,128)(2,1)} %kernel_ref.3) | copy-start | bytes 5529604
  7.3 12.1 %collective-permute-start.3 = (bf16[2,3,80,128]{3,2,1,0:T(8,128)(2,1)S(1)}, bf16[2,3,80,128]{3,2,1,0:T(8,128)(2,1)S(1)}, u32[]{:S(2)}, u32[]{:S(2)}) collective-permute-start(bf16[2,3,80,128]{3,2,1,0:T(8,128)(2,1)S(1)} %get-tuple-element.44), channel_id=1, source_target_pairs={{0,8},{1,9},{2,10},{3,11},{4,12},{5,13},{6,14},{7,15},{8,0},{9,1},... | collective-permute-start | bytes 368648 | tf_op jit(solution)/shard_map/ppermute | solution.py:331
  10.3 11.8 %collective-permute-start.4 = (bf16[2,3,80,128]{3,2,1,0:T(8,128)(2,1)S(1)}, bf16[2,3,80,128]{3,2,1,0:T(8,128)(2,1)S(1)}, u32[]{:S(2)}, u32[]{:S(2)}) collective-permute-start(bf16[2,3,80,128]{3,2,1,0:T(8,128)(2,1)S(1)} %get-tuple-element.45), channel_id=1, source_target_pairs={{0,12},{1,13},{2,14},{3,15},{4,8},{5,9},{6,10},{7,11},{8,4},{9,5},... | collective-permute-start | bytes 368648 | tf_op jit(solution)/shard_map/ppermute | solution.py:331
  15.6 16.0 %collective-permute-start.5 = (bf16[2,3,80,128]{3,2,1,0:T(8,128)(2,1)S(1)}, bf16[2,3,80,128]{3,2,1,0:T(8,128)(2,1)S(1)}, u32[]{:S(2)}, u32[]{:S(2)}) collective-permute-start(bf16[2,3,80,128]{3,2,1,0:T(8,128)(2,1)S(1)} %get-tuple-element.48), channel_id=1, source_target_pairs={{0,2},{1,3},{2,0},{3,1},{4,6},{5,7},{6,4},{7,5},{8,10},{9,11},{10,... | collective-permute-start | bytes 368648 | tf_op jit(solution)/shard_map/ppermute | solution.py:331
  16.9 8.3 %collective-permute-start.6 = (bf16[1,3,80,128]{3,2,1,0:T(8,128)(2,1)S(1)}, bf16[1,3,80,128]{3,2,1,0:T(8,128)(2,1)S(1)}, u32[]{:S(2)}, u32[]{:S(2)}) collective-permute-start(bf16[1,3,80,128]{3,2,1,0:T(8,128)(2,1)S(1)} %get-tuple-element.49), channel_id=1, source_target_pairs={{0,14},{1,15},{2,12},{3,13},{4,10},{5,11},{6,8},{7,9},{8,6},{9,7},... | collective-permute-start | bytes 184328 | tf_op jit(solution)/shard_map/ppermute | solution.py:331
  17.1 11.8 %collective-permute-start.7 = (bf16[1,3,80,128]{3,2,1,0:T(8,128)(2,1)S(1)}, bf16[1,3,80,128]{3,2,1,0:T(8,128)(2,1)S(1)}, u32[]{:S(2)}, u32[]{:S(2)}) collective-permute-start(bf16[1,3,80,128]{3,2,1,0:T(8,128)(2,1)S(1)} %get-tuple-element.50), channel_id=1, source_target_pairs={{0,10},{1,11},{2,8},{3,9},{4,14},{5,15},{6,12},{7,13},{8,2},{9,3},... | collective-permute-start | bytes 184328 | tf_op jit(solution)/shard_map/ppermute | solution.py:331
  19.4 9.8 %collective-permute-start.8 = (bf16[1,3,80,128]{3,2,1,0:T(8,128)(2,1)S(1)}, bf16[1,3,80,128]{3,2,1,0:T(8,128)(2,1)S(1)}, u32[]{:S(2)}, u32[]{:S(2)}) collective-permute-start(bf16[1,3,80,128]{3,2,1,0:T(8,128)(2,1)S(1)} %get-tuple-element.51), channel_id=1, source_target_pairs={{0,6},{1,7},{2,4},{3,5},{4,2},{5,3},{6,0},{7,1},{8,14},{9,15},{10,... | collective-permute-start | bytes 184328 | tf_op jit(solution)/shard_map/ppermute | solution.py:331
  22.1 7.9 %collective-permute-start.9 = (bf16[1,3,80,128]{3,2,1,0:T(8,128)(2,1)S(1)}, bf16[1,3,80,128]{3,2,1,0:T(8,128)(2,1)S(1)}, u32[]{:S(2)}, u32[]{:S(2)}) collective-permute-start(bf16[1,3,80,128]{3,2,1,0:T(8,128)(2,1)S(1)} %get-tuple-element.52), channel_id=1, source_target_pairs={{0,4},{1,5},{2,6},{3,7},{4,0},{5,1},{6,2},{7,3},{8,12},{9,13},{10,... | collective-permute-start | bytes 184328 | tf_op jit(solution)/shard_map/ppermute | solution.py:331
  25.2 11.8 %collective-permute-start.11 = (bf16[1,3,80,128]{3,2,1,0:T(8,128)(2,1)S(1)}, bf16[1,3,80,128]{3,2,1,0:T(8,128)(2,1)S(1)}, u32[]{:S(2)}, u32[]{:S(2)}) collective-permute-start(bf16[1,3,80,128]{3,2,1,0:T(8,128)(2,1)S(1)} %get-tuple-element.64), channel_id=1, source_target_pairs={{0,14},{1,15},{2,12},{3,13},{4,10},{5,11},{6,8},{7,9},{8,6},{9,7},... | collective-permute-start | bytes 184328 | tf_op jit(solution)/shard_map/ppermute | solution.py:331
  28.9 8.0 %collective-permute-start.12 = (bf16[1,3,80,128]{3,2,1,0:T(8,128)(2,1)S(1)}, bf16[1,3,80,128]{3,2,1,0:T(8,128)(2,1)S(1)}, u32[]{:S(2)}, u32[]{:S(2)}) collective-permute-start(bf16[1,3,80,128]{3,2,1,0:T(8,128)(2,1)S(1)} %get-tuple-element.65), channel_id=1, source_target_pairs={{0,10},{1,11},{2,8},{3,9},{4,14},{5,15},{6,12},{7,13},{8,2},{9,3},... | collective-permute-start | bytes 184328 | tf_op jit(solution)/shard_map/ppermute | solution.py:331
  29.2 7.8 %collective-permute-start.13 = (bf16[1,3,80,128]{3,2,1,0:T(8,128)(2,1)S(1)}, bf16[1,3,80,128]{3,2,1,0:T(8,128)(2,1)S(1)}, u32[]{:S(2)}, u32[]{:S(2)}) collective-permute-start(bf16[1,3,80,128]{3,2,1,0:T(8,128)(2,1)S(1)} %get-tuple-element.66), channel_id=1, source_target_pairs={{0,6},{1,7},{2,4},{3,5},{4,2},{5,3},{6,0},{7,1},{8,14},{9,15},{10,... | collective-permute-start | bytes 184328 | tf_op jit(solution)/shard_map/ppermute | solution.py:331
  30.0 7.0 %collective-permute-start.14 = (bf16[1,3,80,128]{3,2,1,0:T(8,128)(2,1)S(1)}, bf16[1,3,80,128]{3,2,1,0:T(8,128)(2,1)S(1)}, u32[]{:S(2)}, u32[]{:S(2)}) collective-permute-start(bf16[1,3,80,128]{3,2,1,0:T(8,128)(2,1)S(1)} %get-tuple-element.67), channel_id=1, source_target_pairs={{0,4},{1,5},{2,6},{3,7},{4,0},{5,1},{6,2},{7,3},{8,12},{9,13},{10,... | collective-permute-start | bytes 184328 | tf_op jit(solution)/shard_map/ppermute | solution.py:331
  31.7 5.3 %collective-permute-start.10 = (bf16[3,80,128]{2,1,0:T(8,128)(2,1)S(1)}, bf16[3,80,128]{2,1,0:T(8,128)(2,1)S(1)}, u32[]{:S(2)}, u32[]{:S(2)}) collective-permute-start(bf16[3,80,128]{2,1,0:T(8,128)(2,1)S(1)} %fusion.2), channel_id=1, source_target_pairs={{0,16},{8,24},{16,0},{24,8},{1,17},{9,25},{17,1},{25,9},{2,18},{10... | collective-permute-start | bytes 184328 | tf_op jit(solution)/shard_map/ppermute | solution.py:343
  37.1 4.3 %collective-permute-start.15 = (bf16[3,80,128]{2,1,0:T(8,128)(2,1)S(1)}, bf16[3,80,128]{2,1,0:T(8,128)(2,1)S(1)}, u32[]{:S(2)}, u32[]{:S(2)}) collective-permute-start(bf16[3,80,128]{2,1,0:T(8,128)(2,1)S(1)} %fusion.1), channel_id=1, source_target_pairs={{0,2},{1,3},{2,0},{3,1},{4,6},{5,7},{6,4},{7,5},{8,10},{9,11},{10,... | collective-permute-start | bytes 184328 | tf_op jit(solution)/shard_map/ppermute | solution.py:354
  38.3 4.2 %collective-permute-start.16 = (bf16[3,80,128]{2,1,0:T(8,128)(2,1)S(1)}, bf16[3,80,128]{2,1,0:T(8,128)(2,1)S(1)}, u32[]{:S(2)}, u32[]{:S(2)}) collective-permute-start(bf16[3,80,128]{2,1,0:T(8,128)(2,1)S(1)} %fusion.1), channel_id=1, source_target_pairs={{0,4},{1,5},{2,6},{3,7},{4,0},{5,1},{6,2},{7,3},{8,12},{9,13},{10,... | collective-permute-start | bytes 184328 | tf_op jit(solution)/shard_map/ppermute | solution.py:354
  38.7 5.1 %collective-permute-start.17 = (bf16[3,80,128]{2,1,0:T(8,128)(2,1)S(1)}, bf16[3,80,128]{2,1,0:T(8,128)(2,1)S(1)}, u32[]{:S(2)}, u32[]{:S(2)}) collective-permute-start(bf16[3,80,128]{2,1,0:T(8,128)(2,1)S(1)} %fusion.1), channel_id=1, source_target_pairs={{0,6},{1,7},{2,4},{3,5},{4,2},{5,3},{6,0},{7,1},{8,14},{9,15},{10,... | collective-permute-start | bytes 184328 | tf_op jit(solution)/shard_map/ppermute | solution.py:354
  43.9 1.6 %collective-permute-start.18 = (bf16[4,3,80,128]{3,2,1,0:T(8,128)(2,1)S(1)}, bf16[4,3,80,128]{3,2,1,0:T(8,128)(2,1)S(1)}, u32[]{:S(2)}, u32[]{:S(2)}) collective-permute-start(bf16[4,3,80,128]{3,2,1,0:T(8,128)(2,1)S(1)} %pad_maximum_fusion.parts_ref), channel_id=1, source_target_pairs={{0,1},{1,0},{2,3},{3,2},{4,5},{5,4},{6,7},{7,6},{8,9},{9,8},{10,11... | collective-permute-start | bytes 737288 | tf_op jit(solution)/shard_map/ppermute | solution.py:356

commit v10 on v8

--- a/solution.py
+++ b/solution.py
@@ -57,50 +57,39 @@
     return lax.rem(lax.axis_index("space"), PAIR)
 
 
-def own_kernel(pre_ref, grad_ref, term_ref, act_edge_ref, grad_edge_ref, act_s, taps_s):
+def chip_kernel(pre_ref, grad_ref, their_pre_ref, their_grad_ref, out_ref, act_edge_ref, grad_edge_ref, act_s, taps_s):
     rows, chans, width = pre_ref.shape
-    half = chans // PAIR
-    mine = pl.ds(pl.multiple_of(my_core() * half, half), half)
-    zero = jnp.zeros((half, width), BF16)
-    taps_s[3 * half :, :] = jnp.zeros((taps_s.shape[0] - 3 * half, taps_s.shape[1]), BF16)
-    for r in range(rows + 2):
-        put_taps(taps_s, r, grad_ref[r - 1, mine, :] if 0 < r <= rows else zero)
-    for r in range(rows):
-        act_s[:, r * width : (r + 1) * width] = silu(pre_ref[r])
-    for i, r in enumerate((0, rows - 1)):
-        act_edge_ref[i] = act_s[:, r * width : (r + 1) * width]
-        grad_edge_ref[i] = grad_ref[r, mine, :]
-    for a in range(3):
-        at = (2 - a) * width
-        term_ref[a] = lax.dot_general(act_s[...], taps_s[:, at : at + rows * width], NT, preferred_element_type=F32)
-
-
-def pair_kernel(term_ref, act_edge_ref, grad_edge_ref, their_pre_ref, their_grad_ref, out_ref, act_s, taps_s):
-    rows, chans, width = their_pre_ref.shape
     half = chans // PAIR
     core = my_core()
     first = core == 0
     mine = pl.ds(pl.multiple_of(core * half, half), half)
     zero = jnp.zeros((half, width), BF16)
-    zero_act = jnp.zeros((chans, width), BF16)
     taps_s[3 * half :, :] = jnp.zeros((taps_s.shape[0] - 3 * half, taps_s.shape[1]), BF16)
-    act_s[:, :width] = jnp.where(first, zero_act, act_edge_ref[0])
-    for r in range(rows):
-        act_s[:, (1 + r) * width : (2 + r) * width] = silu(their_pre_ref[r])
-    act_s[:, (rows + 1) * width :] = jnp.where(first, act_edge_ref[1], zero_act)
-    put_taps(taps_s, 0, their_grad_ref[rows - 1, mine, :])
-    put_taps(taps_s, 1, jnp.where(first, grad_edge_ref[1], zero))
-    for r in range(rows):
-        put_taps(taps_s, 2 + r, their_grad_ref[r, mine, :])
-    put_taps(taps_s, rows + 2, jnp.where(first, zero, grad_edge_ref[0]))
-    put_taps(taps_s, rows + 3, their_grad_ref[0, mine, :])
-    for a, (left, right, at) in enumerate(((1, rows + 2, 3), (1, rows + 1, 2), (0, rows + 1, 0))):
-        out_ref[a] = term_ref[a] + lax.dot_general(
-            act_s[:, left * width : right * width],
-            taps_s[:, at * width : (at + right - left) * width],
-            NT,
-            preferred_element_type=F32,
-        )
+    for part, (ref, other_ref, upper) in enumerate(((grad_ref, their_grad_ref, first), (their_grad_ref, grad_ref, ~first))):
+        at = part * (rows + 2)
+        put_taps(taps_s, at, jnp.where(upper, zero, other_ref[rows - 1, mine, :]))
+        for r in range(rows):
+            put_taps(taps_s, at + r + 1, ref[r, mine, :])
+        put_taps(taps_s, at + rows + 1, jnp.where(upper, other_ref[0, mine, :], zero))
+    for part, ref in enumerate((pre_ref, their_pre_ref)):
+        for r in range(rows):
+            act_s[:, (part * rows + r) * width : (part * rows + r + 1) * width] = silu(ref[r])
+    for i, r in enumerate((0, rows - 1)):
+        act_edge_ref[i] = act_s[:, r * width : (r + 1) * width]
+        grad_edge_ref[i] = grad_ref[r, mine, :]
+    for a in range(3):
+        terms = []
+        for part in range(PAIR):
+            at = (part * (rows + 2) + 2 - a) * width
+            terms.append(
+                lax.dot_general(
+                    act_s[:, part * rows * width : (part + 1) * rows * width],
+                    taps_s[:, at : at + rows * width],
+                    NT,
+                    preferred_element_type=F32,
+                )
+            )
+        out_ref[a] = terms[0] + terms[1]
 
 
 def edge_kernel(term_ref, act_edge_ref, grad_edge_ref, near_ref, *refs):
@@ -123,13 +112,11 @@
             term += lax.dot_general(acts[a], taps, NT, preferred_element_type=F32)
         for p in range(PLANE):
             for z in range(NEAR * outers):
-                term_s[z % NEAR * PLANE + p, z // NEAR, a] = term[
-                    z * block : (z + 1) * block, p * LANES : (p + 1) * LANES
-                ].astype(term_s.dtype)
+                term_s[z % NEAR * PLANE + p, z // NEAR, a] = term[z * block : (z + 1) * block, p * LANES : (p + 1) * LANES]
     at, outer_at = near_index(), lax.axis_index("dp") // NEAR
     for k, out_ref in enumerate(out_refs):
         for j in range(outers):
-            out_ref[j] = term_s[at ^ k, outer_at ^ j]
+            out_ref[j] = term_s[at ^ k, outer_at ^ j].astype(out_ref.dtype)
 
 
 def input_kernel(side, pre_ref, grad_ref, edge_ref, kernel_ref, *refs):
@@ -192,17 +179,18 @@
         rows = [wide_s[t // 3, g * group : (g + 1) * group, t % 3 * half : (t % 3 + 1) * half] for t in range(9)]
         rows = jnp.concatenate(rows, axis=0).astype(BF16)
         turned_s[g * width : (g + 1) * width, :] = jnp.dot(pick, rows, preferred_element_type=F32)
-    i = lax.broadcasted_iota(jnp.int32, (half, half), 0)
-    j = lax.broadcasted_iota(jnp.int32, (half, half), 1)
-    same = jnp.where(i == j, 1.0, 0.0).astype(BF16)
-    out_s[...] = lax.dot_general(same, turned_s[...].astype(BF16), NT, preferred_element_type=F32)
-    count = sem.shape[0]
-    step = half // count
+    turned = turned_s[...].astype(BF16)
+    step = half // sem.shape[0]
     first = (my_core() ^ flip) * half
     copies = []
-    for i in range(count):
-        to = pl.ds(pl.multiple_of(first + i * step, 8), step)
-        copies.append(pltpu.make_async_copy(out_s.at[pl.ds(i * step, step)], out_hbm.at[to], sem.at[i]))
+    for n in range(sem.shape[0]):
+        i = lax.broadcasted_iota(jnp.int32, (step, half), 0)
+        j = lax.broadcasted_iota(jnp.int32, (step, half), 1)
+        same = jnp.where(i + n * step == j, 1.0, 0.0).astype(BF16)
+        here = slice(n * step, (n + 1) * step)
+        out_s[here, :] = lax.dot_general(same, turned, NT, preferred_element_type=F32)
+        to = pl.ds(pl.multiple_of(first + n * step, 8), step)
+        copies.append(pltpu.make_async_copy(out_s.at[here], out_hbm.at[to], sem.at[n]))
         copies[-1].start()
     for copy in copies:
         copy.wait()
@@ -246,24 +234,6 @@
         name="pick_rows",
     )(edge)
     pick, own_pre, own_grad = lax.optimization_barrier((pick, pre, grad))
-    own, act_edge, grad_edge = pl.pallas_call(
-        own_kernel,
-        out_shape=(
-            jax.ShapeDtypeStruct((3, chans, PLANE * LANES), F32),
-            jax.ShapeDtypeStruct((2, chans, width), BF16),
-            jax.ShapeDtypeStruct((2, half, width), BF16),
-        ),
-        in_specs=[vmem()] * 2,
-        out_specs=(vmem(),) * 3,
-        scratch_shapes=[
-            pltpu.VMEM((chans, rows * width), BF16),
-            pltpu.VMEM((PLANE * LANES, (rows + 2) * width), BF16),
-        ],
-        compiler_params=params,
-        cost_estimate=pl.CostEstimate(flops=flops, bytes_accessed=4000000, transcendentals=rows * width * chans),
-        name="own_terms",
-    )(own_pre, own_grad)
-
     def input_part(side, edge_rows, *before):
         count = rows // 2
         return pl.pallas_call(
@@ -285,27 +255,31 @@
         )(pre, grad, edge_rows, kernel, *before)
 
     piece = jax.ShapeDtypeStruct((far, 3, block, LANES), BF16)
-    term = pl.pallas_call(
-        pair_kernel,
-        out_shape=jax.ShapeDtypeStruct((3, chans, PLANE * LANES), F32),
-        in_specs=[vmem()] * 5,
-        out_specs=vmem(),
+    term, act_edge, grad_edge = pl.pallas_call(
+        chip_kernel,
+        out_shape=(
+            jax.ShapeDtypeStruct((3, chans, PLANE * LANES), F32),
+            jax.ShapeDtypeStruct((2, chans, width), BF16),
+            jax.ShapeDtypeStruct((2, half, width), BF16),
+        ),
+        in_specs=[vmem()] * 4,
+        out_specs=(vmem(),) * 3,
         scratch_shapes=[
-            pltpu.VMEM((chans, (rows + 2) * width), BF16),
-            pltpu.VMEM((PLANE * LANES, (rows + 4) * width), BF16),
+            pltpu.VMEM((chans, PAIR * rows * width), BF16),
+            pltpu.VMEM((PLANE * LANES, PAIR * (rows + 2) * width), BF16),
         ],
         compiler_params=params,
-        cost_estimate=pl.CostEstimate(flops=flops, bytes_accessed=4000000, transcendentals=rows * width * chans),
-        name="pair_terms",
-    )(own, act_edge, grad_edge, their_pre, their_grad)
+        cost_estimate=pl.CostEstimate(flops=2 * flops, bytes_accessed=4000000, transcendentals=2 * rows * width * chans),
+        name="chip_terms",
+    )(own_pre, own_grad, their_pre, their_grad)
     terms = pl.pallas_call(
         edge_kernel,
-        out_shape=(piece,) * (NEAR * PLANE),
+        out_shape=(jax.ShapeDtypeStruct(piece.shape, F32),) + (piece,) * (NEAR * PLANE - 1),
         in_specs=[vmem()] * 4,
         out_specs=(vmem(),) * (NEAR * PLANE),
         scratch_shapes=[
             pltpu.VMEM((PLANE * LANES, 2 * width), BF16),
-            pltpu.VMEM((NEAR * PLANE, far, 3, block, LANES), BF16),
+            pltpu.VMEM((NEAR * PLANE, far, 3, block, LANES), F32),
         ],
         compiler_params=params,
         cost_estimate=pl.CostEstimate(flops=flops // 8, bytes_accessed=4000000, transcendentals=width * chans),
@@ -352,7 +326,7 @@
                 pltpu.VMEM((3, block, PLANE * LANES), F32),
                 pltpu.VMEM((9 * block, half), F32),
                 pltpu.VMEM((half, 9 * block), F32),
-                pltpu.SemaphoreType.DMA((10,)),
+                pltpu.SemaphoreType.DMA((2,)),
             ],
             input_output_aliases={2: 0} if before else {},
             compiler_params=params,

time: 45.4 us -> 45.5 us (level)
  waiting for transfers between devices: 8.84 us -> 10.6 us
  starting transfers between devices: 22.4 us -> 21.1 us
    ppermute x7, starting transfers between devices: 14.8 us -> 13.6 us  [shards(): got.append(lax.ppermute(terms[k], ('dp', 'space'), moves))]
    ppermute x1, waiting for transfers between devices: 0.01 us -> 1.1 us  [shards(): their_pre = lax.ppermute(my_pre, 'space', pairs)]
    ppermute x1, waiting for transfers between devices: 0.47 us -> 0.94 us  [shards(): their_grad = lax.ppermute(my_grad, 'space', pairs)]
    pallas_call x3 -> x2, Pallas kernels: 3.74 us -> 3.48 us  [the longest x1 2.93 us: shards(): pl.pallas_call(chip_kernel, out_shape=(jax.ShapeDtypeStruct((3, chans, PL...]
  transfers between devices with their start and end apart: 15 -> 15, of which waited for: 7 -> 8; matrix products, arithmetic and copies ran while one was open for 0% -> 0% of each run, Pallas kernels for 22% -> 21%
where the time goes in v10:
time: 45.5 us; the launch traced here: 45.3 us
  starting transfers between devices  21.1 us (46%)
  Pallas kernels  11.6 us (25%)
  waiting for transfers between devices  10.6 us (23%)
  local copies, waits for them, and re-layouts  0.98 us (2%)
  between operations  0.81 us (2%)
    ppermute x7, starting transfers between devices, shards(): got.append(lax.ppermute(terms[k], ('dp', 'space'), moves))  13.6 us
    pallas_call x2, Pallas kernels, input_part(): pl.pallas_call(functools.partial(input_kernel, side), out_shape=jax.Shape...  5.21 us
    ppermute x1, waiting for transfers between devices, shards(): others.append(lax.ppermute(near_sum[k].astype(BF16), 'dp', moves))  3.57 us
    ppermute x3, starting transfers between devices, shards(): lax.ppermute(final, 'space', [(i, i ^ k * PAIR) for i in range(space)])  3.55 us
    pallas_call x1, Pallas kernels, shards(): pl.pallas_call(chip_kernel, out_shape=(jax.ShapeDtypeStruct((3, chans, PL...  2.93 us
    pallas_call x2, Pallas kernels, place(): pl.pallas_call(functools.partial(place_kernel, flip), out_shape=jax.Shape...  2.81 us
    ppermute x1, starting transfers between devices, shards(): others.append(lax.ppermute(near_sum[k].astype(BF16), 'dp', moves))  2.65 us
    ppermute x7, waiting for transfers between devices, shards(): got.append(lax.ppermute(terms[k], ('dp', 'space'), moves))  2.57 us
  transfers between devices with their start and end apart: 15, of which 8 were waited for; matrix products, arithmetic and copies ran while one was open for 0% of the time, Pallas kernels for 21%

profile of v10, /device:TPU:0, one launch (start us, length us, event | category | flops | bytes accessed | tf_op | source)
XLA Modules:
  0.0 45.3 jit_solution(15115995876786116040)
XLA Ops:
  0.6 0.9 %dynamic-slice_bitcast_fusion = (bf16[1,320,128]{2,1,0:T(8,128)(2,1)S(1)}, bf16[1,320,128]{2,1,0:T(8,128)(2,1)S(1)}) fusion(bf16[1,8,128,320]{2,3,1,0:T(8,128)(2,1)} %param.3, s32[]{:T(128)S(6)} %select_n.7, bf16[1,8,128,320]{2,3,1,0:T(8,128)(2,1)} %param.4), kind=kLoop, calls=%fused_computation.8 | loop fusion | bytes 327684 | tf_op jit(solution)/shard_map/jit(dynamic_index_in_dim)/dynamic_slice | solution.py:216
  2.2 0.7 %collective-permute-start.2 = (bf16[2,320,128]{2,1,0:T(8,128)(2,1)S(1)}, bf16[2,320,128]{2,1,0:T(8,128)(2,1)S(1)}, u32[]{:S(2)}, u32[]{:S(2)}) collective-permute-start(bf16[2,320,128]{2,1,0:T(8,128)(2,1)S(1)} %pad_maximum_fusion.1.after_ref), channel_id=1, source_target_pairs={{1,2},{2,1},{3,4},{4,3},{5,6},{6,5},{9,10},{10,9},{11,12},{12,11},... | collective-permute-start | bytes 491528 | tf_op jit(solution)/shard_map/ppermute | solution.py:223
  3.0 1.1 %collective-permute-done.their_pre_ref = bf16[8,320,128]{2,1,0:T(8,128)(2,1)S(1)} collective-permute-done((bf16[8,320,128]{2,1,0:T(8,128)(2,1)}, bf16[8,320,128]{2,1,0:T(8,128)(2,1)S(1)}, u32[]{:S(2)}, u32[]{:S(2)}) %collective-permute-start) | collective-permute-done | bytes 655392 | tf_op jit(solution)/shard_map/ppermute | solution.py:226
  4.1 0.9 %collective-permute-done.1.their_grad_ref = bf16[8,320,128]{2,1,0:T(8,128)(2,1)S(1)} collective-permute-done((bf16[8,320,128]{2,1,0:T(8,128)(2,1)}, bf16[8,320,128]{2,1,0:T(8,128)(2,1)S(1)}, u32[]{:S(2)}, u32[]{:S(2)}) %collective-permute-start.1) | collective-permute-done | bytes 655392 | tf_op jit(solution)/shard_map/ppermute | solution.py:225
  5.0 2.9 %chip_terms.1 = (f32[3,320,512]{2,1,0:T(8,128)S(1)}, bf16[2,320,128]{2,1,0:T(8,128)(2,1)S(1)}, bf16[2,160,128]{2,1,0:T(8,128)(2,1)S(1)}) custom-call(bf16[8,320,128]{2,1,0:T(8,128)(2,1)S(1)} %bitcast.33, bf16[8,320,128]{2,1,0:T(8,128)(2,1)S(1)} %bitcast.37, bf16[8,320,128]{2,1,0:T(8,128)(2,1)S(1)} %collective-permute-done.their_pre_ref, ...), custom_call_target="tpu_custom_call" | custom-call | flops 3774873600 | bytes 4000000 | tf_op jit(solution)/shard_map/chip_terms/pallas_call | solution.py:258
  8.0 0.5 %edge_terms.1 = (f32[2,3,80,128]{3,2,1,0:T(8,128)S(1)}, bf16[2,3,80,128]{3,2,1,0:T(8,128)(2,1)S(1)}, bf16[2,3,80,128]{3,2,1,0:T(8,128)(2,1)S(1)}, bf16[2,3,80,12...) custom-call(f32[3,320,512]{2,1,0:T(8,128)S(1)} %get-tuple-element.35, ...), custom_call_target="tpu_custom_call" | custom-call | flops 235929600 | bytes 4000000 | tf_op jit(solution)/shard_map/edge_terms/pallas_call | solution.py:275
  8.5 3.0 %collective-permute-start.3 = (bf16[2,3,80,128]{3,2,1,0:T(8,128)(2,1)S(1)}, bf16[2,3,80,128]{3,2,1,0:T(8,128)(2,1)S(1)}, u32[]{:S(2)}, u32[]{:S(2)}) collective-permute-start(bf16[2,3,80,128]{3,2,1,0:T(8,128)(2,1)S(1)} %get-tuple-element.39), channel_id=1, source_target_pairs={{0,8},{1,9},{2,10},{3,11},{4,12},{5,13},{6,14},{7,15},{8,0},{9,1},... | collective-permute-start | bytes 368648 | tf_op jit(solution)/shard_map/ppermute | solution.py:296
  11.6 4.1 %collective-permute-start.4 = (bf16[2,3,80,128]{3,2,1,0:T(8,128)(2,1)S(1)}, bf16[2,3,80,128]{3,2,1,0:T(8,128)(2,1)S(1)}, u32[]{:S(2)}, u32[]{:S(2)}) collective-permute-start(bf16[2,3,80,128]{3,2,1,0:T(8,128)(2,1)S(1)} %get-tuple-element.40), channel_id=1, source_target_pairs={{0,12},{1,13},{2,14},{3,15},{4,8},{5,9},{6,10},{7,11},{8,4},{9,5},... | collective-permute-start | bytes 368648 | tf_op jit(solution)/shard_map/ppermute | solution.py:296
  15.6 1.3 %collective-permute-start.5 = (bf16[2,3,80,128]{3,2,1,0:T(8,128)(2,1)S(1)}, bf16[2,3,80,128]{3,2,1,0:T(8,128)(2,1)S(1)}, u32[]{:S(2)}, u32[]{:S(2)}) collective-permute-start(bf16[2,3,80,128]{3,2,1,0:T(8,128)(2,1)S(1)} %get-tuple-element.43), channel_id=1, source_target_pairs={{0,2},{1,3},{2,0},{3,1},{4,6},{5,7},{6,4},{7,5},{8,10},{9,11},{10,... | collective-permute-start | bytes 368648 | tf_op jit(solution)/shard_map/ppermute | solution.py:296
  17.1 2.3 %collective-permute-start.7 = (bf16[2,3,80,128]{3,2,1,0:T(8,128)(2,1)S(1)}, bf16[2,3,80,128]{3,2,1,0:T(8,128)(2,1)S(1)}, u32[]{:S(2)}, u32[]{:S(2)}) collective-permute-start(bf16[2,3,80,128]{3,2,1,0:T(8,128)(2,1)S(1)} %get-tuple-element.45), channel_id=1, source_target_pairs={{0,10},{1,11},{2,8},{3,9},{4,14},{5,15},{6,12},{7,13},{8,2},{9,3},... | collective-permute-start | bytes 368648 | tf_op jit(solution)/shard_map/ppermute | solution.py:296
  19.4 2.1 %collective-permute-start.8 = (bf16[2,3,80,128]{3,2,1,0:T(8,128)(2,1)S(1)}, bf16[2,3,80,128]{3,2,1,0:T(8,128)(2,1)S(1)}, u32[]{:S(2)}, u32[]{:S(2)}) collective-permute-start(bf16[2,3,80,128]{3,2,1,0:T(8,128)(2,1)S(1)} %get-tuple-element.46), channel_id=1, source_target_pairs={{0,6},{1,7},{2,4},{3,5},{4,2},{5,3},{6,0},{7,1},{8,14},{9,15},{10,... | collective-permute-start | bytes 368648 | tf_op jit(solution)/shard_map/ppermute | solution.py:296
  21.6 0.6 %collective-permute-done.4 = bf16[2,3,80,128]{3,2,1,0:T(8,128)(2,1)S(1)} collective-permute-done((bf16[2,3,80,128]{3,2,1,0:T(8,128)(2,1)S(1)}, bf16[2,3,80,128]{3,2,1,0:T(8,128)(2,1)S(1)}, u32[]{:S(2)}, u32[]{:S(2)}) %collective-permute-start.4) | collective-permute-done | bytes 122912 | tf_op jit(solution)/shard_map/ppermute | solution.py:296
  22.1 0.6 %collective-permute-start.9 = (bf16[2,3,80,128]{3,2,1,0:T(8,128)(2,1)S(1)}, bf16[2,3,80,128]{3,2,1,0:T(8,128)(2,1)S(1)}, u32[]{:S(2)}, u32[]{:S(2)}) collective-permute-start(bf16[2,3,80,128]{3,2,1,0:T(8,128)(2,1)S(1)} %get-tuple-element.47), channel_id=1, source_target_pairs={{0,4},{1,5},{2,6},{3,7},{4,0},{5,1},{6,2},{7,3},{8,12},{9,13},{10,... | collective-permute-start | bytes 368648 | tf_op jit(solution)/shard_map/ppermute | solution.py:296
  22.8 2.6 %input_grad.2.refs_0_ = bf16[8,320,128]{2,1,0:T(8,128)(2,1)} custom-call(bf16[8,320,128]{2,1,0:T(8,128)(2,1)S(1)} %bitcast.34, bf16[8,320,128]{2,1,0:T(8,128)(2,1)S(1)} %bitcast.38, bf16[2,320,128]{2,1,0:T(8,128)(2,1)S(1)} %collective-permute-done.2.near_ref.edge_ref, bf16[3,3,320,320]{3,2,1,0:T(8,128)(2,1)S(1)} %copy-done), custom_call_target="tpu_custom_call" | custom-call | flops 943718400 | bytes 3000000 | tf_op jit(solution)/shard_map/input_grad/pallas_call | solution.py:239
  25.4 2.6 %input_grad.3 = bf16[8,320,128]{2,1,0:T(8,128)(2,1)} custom-call(bf16[8,320,128]{2,1,0:T(8,128)(2,1)S(1)} %bitcast.35, bf16[8,320,128]{2,1,0:T(8,128)(2,1)S(1)} %bitcast.39, bf16[1,320,128]{2,1,0:T(8,128)(2,1)S(1)} %constant_dynamic-slice_fusion.edge_ref, bf16[3,3,320,320]{3,2,1,0:T(8,128)(2,1)S(1)} %copy-done, ...), custom_call_target="tpu_custom_call", output_to_operand_aliasing={{}: (4, {})} | custom-call | flops 943718400 | bytes 3000000 | tf_op jit(solution)/shard_map/input_grad/pallas_call | solution.py:239
  28.0 2.0 %collective-permute-done.8 = bf16[2,3,80,128]{3,2,1,0:T(8,128)(2,1)S(1)} collective-permute-done((bf16[2,3,80,128]{3,2,1,0:T(8,128)(2,1)S(1)}, bf16[2,3,80,128]{3,2,1,0:T(8,128)(2,1)S(1)}, u32[]{:S(2)}, u32[]{:S(2)}) %collective-permute-start.8) | collective-permute-done | bytes 122912 | tf_op jit(solution)/shard_map/ppermute | solution.py:296
  30.1 2.7 %collective-permute-start.10 = (bf16[3,80,128]{2,1,0:T(8,128)(2,1)S(1)}, bf16[3,80,128]{2,1,0:T(8,128)(2,1)S(1)}, u32[]{:S(2)}, u32[]{:S(2)}) collective-permute-start(bf16[3,80,128]{2,1,0:T(8,128)(2,1)S(1)} %fusion.3), channel_id=1, source_target_pairs={{0,16},{8,24},{16,0},{24,8},{1,17},{9,25},{17,1},{25,9},{2,18},{10... | collective-permute-start | bytes 184328 | tf_op jit(solution)/shard_map/ppermute | solution.py:307
  32.8 3.6 %collective-permute-done.10 = bf16[3,80,128]{2,1,0:T(8,128)(2,1)S(1)} collective-permute-done((bf16[3,80,128]{2,1,0:T(8,128)(2,1)S(1)}, bf16[3,80,128]{2,1,0:T(8,128)(2,1)S(1)}, u32[]{:S(2)}, u32[]{:S(2)}) %collective-permute-start.10) | collective-permute-done | bytes 61472 | tf_op jit(solution)/shard_map/ppermute | solution.py:307
  36.5 1.6 %collective-permute-start.12 = (bf16[3,80,128]{2,1,0:T(8,128)(2,1)S(1)}, bf16[3,80,128]{2,1,0:T(8,128)(2,1)S(1)}, u32[]{:S(2)}, u32[]{:S(2)}) collective-permute-start(bf16[3,80,128]{2,1,0:T(8,128)(2,1)S(1)} %fusion.2), channel_id=1, source_target_pairs={{0,4},{1,5},{2,6},{3,7},{4,0},{5,1},{6,2},{7,3},{8,12},{9,13},{10,... | collective-permute-start | bytes 184328 | tf_op jit(solution)/shard_map/ppermute | solution.py:315
  38.1 1.9 %collective-permute-start.11 = (bf16[3,80,128]{2,1,0:T(8,128)(2,1)S(1)}, bf16[3,80,128]{2,1,0:T(8,128)(2,1)S(1)}, u32[]{:S(2)}, u32[]{:S(2)}) collective-permute-start(bf16[3,80,128]{2,1,0:T(8,128)(2,1)S(1)} %fusion.2), channel_id=1, source_target_pairs={{0,2},{1,3},{2,0},{3,1},{4,6},{5,7},{6,4},{7,5},{8,10},{9,11},{10,... | collective-permute-start | bytes 184328 | tf_op jit(solution)/shard_map/ppermute | solution.py:315
  39.9 1.6 %collective-permute-done.13 = bf16[3,80,128]{2,1,0:T(8,128)(2,1)S(1)} collective-permute-done((bf16[3,80,128]{2,1,0:T(8,128)(2,1)S(1)}, bf16[3,80,128]{2,1,0:T(8,128)(2,1)S(1)}, u32[]{:S(2)}, u32[]{:S(2)}) %collective-permute-start.13) | collective-permute-done | bytes 61472 | tf_op jit(solution)/shard_map/ppermute | solution.py:315
  41.6 0.7 %collective-permute-done.11 = bf16[3,80,128]{2,1,0:T(8,128)(2,1)S(1)} collective-permute-done((bf16[3,80,128]{2,1,0:T(8,128)(2,1)S(1)}, bf16[3,80,128]{2,1,0:T(8,128)(2,1)S(1)}, u32[]{:S(2)}, u32[]{:S(2)}) %collective-permute-start.11) | collective-permute-done | bytes 61472 | tf_op jit(solution)/shard_map/ppermute | solution.py:315
  42.4 1.4 %place_rows.2.refs_0_ = f32[320,720]{1,0:T(8,128)} custom-call(bf16[4,3,80,128]{3,2,1,0:T(8,128)(2,1)S(1)} %pad_maximum_fusion.parts_ref, f32[144,144]{1,0:T(8,128)S(1)} %pick_rows.1.pick_ref), custom_call_target="tpu_custom_call" | custom-call | flops 165888000 | bytes 1000000 | tf_op jit(solution)/shard_map/place_rows/pallas_call | solution.py:320
  43.9 1.4 %place_rows.3 = f32[320,720]{1,0:T(8,128)} custom-call(bf16[4,3,80,128]{3,2,1,0:T(8,128)(2,1)S(1)} %collective-permute-done.14.parts_ref, f32[144,144]{1,0:T(8,128)S(1)} %pick_rows.1.pick_ref, f32[320,720]{1,0:T(8,128)} %place_rows.2.refs_0_), custom_call_target="tpu_custom_call", output_to_operand_aliasing={{}: (2, {})} | custom-call | flops 165888000 | bytes 1000000 | tf_op jit(solution)/shard_map/place_rows/pallas_call | solution.py:320
  (26 shorter events, 1.4 us)
Async XLA Ops:
  1.6 3.4 %copy-start.1 = (bf16[1,8,128,320]{2,3,1,0:T(8,128)(2,1)S(1)}, bf16[1,8,128,320]{2,3,1,0:T(8,128)(2,1)}, u32[]{:S(2)}) copy-start(bf16[1,8,128,320]{2,3,1,0:T(8,128)(2,1)} %param.3) | copy-start | bytes 1966084
  1.6 3.4 %copy-start.2 = (bf16[1,8,128,320]{2,3,1,0:T(8,128)(2,1)S(1)}, bf16[1,8,128,320]{2,3,1,0:T(8,128)(2,1)}, u32[]{:S(2)}) copy-start(bf16[1,8,128,320]{2,3,1,0:T(8,128)(2,1)} %param.4) | copy-start | bytes 1966084
  1.6 2.5 %collective-permute-start = (bf16[8,320,128]{2,1,0:T(8,128)(2,1)}, bf16[8,320,128]{2,1,0:T(8,128)(2,1)S(1)}, u32[]{:S(2)}, u32[]{:S(2)}) collective-permute-start(bf16[8,320,128]{2,1,0:T(8,128)(2,1)} %bitcast.32), channel_id=1, source_target_pairs={{0,1},{1,0},{2,3},{3,2},{4,5},{5,4},{6,7},{7,6},{8,9},{9,8},{10,11... | collective-permute-start | bytes 1966088 | tf_op jit(solution)/shard_map/ppermute | solution.py:226
  2.2 2.9 %collective-permute-start.1 = (bf16[8,320,128]{2,1,0:T(8,128)(2,1)}, bf16[8,320,128]{2,1,0:T(8,128)(2,1)S(1)}, u32[]{:S(2)}, u32[]{:S(2)}) collective-permute-start(bf16[8,320,128]{2,1,0:T(8,128)(2,1)} %bitcast.36), channel_id=1, source_target_pairs={{0,1},{1,0},{2,3},{3,2},{4,5},{5,4},{6,7},{7,6},{8,9},{9,8},{10,11... | collective-permute-start | bytes 1966088 | tf_op jit(solution)/shard_map/ppermute | solution.py:225
  2.2 5.8 %collective-permute-start.2 = (bf16[2,320,128]{2,1,0:T(8,128)(2,1)S(1)}, bf16[2,320,128]{2,1,0:T(8,128)(2,1)S(1)}, u32[]{:S(2)}, u32[]{:S(2)}) collective-permute-start(bf16[2,320,128]{2,1,0:T(8,128)(2,1)S(1)} %pad_maximum_fusion.1.after_ref), channel_id=1, source_target_pairs={{1,2},{2,1},{3,4},{4,3},{5,6},{6,5},{9,10},{10,9},{11,12},{12,11},... | collective-permute-start | bytes 491528 | tf_op jit(solution)/shard_map/ppermute | solution.py:223
  8.0 14.8 %copy-start = (bf16[3,3,320,320]{3,2,1,0:T(8,128)(2,1)S(1)}, bf16[3,3,320,320]{3,2,1,0:T(8,128)(2,1)}, u32[]{:S(2)}) copy-start(bf16[3,3,320,320]{3,2,1,0:T(8,128)(2,1)} %kernel_ref.3) | copy-start | bytes 5529604
  8.5 10.9 %collective-permute-start.3 = (bf16[2,3,80,128]{3,2,1,0:T(8,128)(2,1)S(1)}, bf16[2,3,80,128]{3,2,1,0:T(8,128)(2,1)S(1)}, u32[]{:S(2)}, u32[]{:S(2)}) collective-permute-start(bf16[2,3,80,128]{3,2,1,0:T(8,128)(2,1)S(1)} %get-tuple-element.39), channel_id=1, source_target_pairs={{0,8},{1,9},{2,10},{3,11},{4,12},{5,13},{6,14},{7,15},{8,0},{9,1},... | collective-permute-start | bytes 368648 | tf_op jit(solution)/shard_map/ppermute | solution.py:296
  11.6 10.6 %collective-permute-start.4 = (bf16[2,3,80,128]{3,2,1,0:T(8,128)(2,1)S(1)}, bf16[2,3,80,128]{3,2,1,0:T(8,128)(2,1)S(1)}, u32[]{:S(2)}, u32[]{:S(2)}) collective-permute-start(bf16[2,3,80,128]{3,2,1,0:T(8,128)(2,1)S(1)} %get-tuple-element.40), channel_id=1, source_target_pairs={{0,12},{1,13},{2,14},{3,15},{4,8},{5,9},{6,10},{7,11},{8,4},{9,5},... | collective-permute-start | bytes 368648 | tf_op jit(solution)/shard_map/ppermute | solution.py:296
  15.6 12.4 %collective-permute-start.5 = (bf16[2,3,80,128]{3,2,1,0:T(8,128)(2,1)S(1)}, bf16[2,3,80,128]{3,2,1,0:T(8,128)(2,1)S(1)}, u32[]{:S(2)}, u32[]{:S(2)}) collective-permute-start(bf16[2,3,80,128]{3,2,1,0:T(8,128)(2,1)S(1)} %get-tuple-element.43), channel_id=1, source_target_pairs={{0,2},{1,3},{2,0},{3,1},{4,6},{5,7},{6,4},{7,5},{8,10},{9,11},{10,... | collective-permute-start | bytes 368648 | tf_op jit(solution)/shard_map/ppermute | solution.py:296
  16.9 11.1 %collective-permute-start.6 = (bf16[2,3,80,128]{3,2,1,0:T(8,128)(2,1)S(1)}, bf16[2,3,80,128]{3,2,1,0:T(8,128)(2,1)S(1)}, u32[]{:S(2)}, u32[]{:S(2)}) collective-permute-start(bf16[2,3,80,128]{3,2,1,0:T(8,128)(2,1)S(1)} %get-tuple-element.44), channel_id=1, source_target_pairs={{0,14},{1,15},{2,12},{3,13},{4,10},{5,11},{6,8},{7,9},{8,6},{9,7},... | collective-permute-start | bytes 368648 | tf_op jit(solution)/shard_map/ppermute | solution.py:296
  17.1 10.9 %collective-permute-start.7 = (bf16[2,3,80,128]{3,2,1,0:T(8,128)(2,1)S(1)}, bf16[2,3,80,128]{3,2,1,0:T(8,128)(2,1)S(1)}, u32[]{:S(2)}, u32[]{:S(2)}) collective-permute-start(bf16[2,3,80,128]{3,2,1,0:T(8,128)(2,1)S(1)} %get-tuple-element.45), channel_id=1, source_target_pairs={{0,10},{1,11},{2,8},{3,9},{4,14},{5,15},{6,12},{7,13},{8,2},{9,3},... | collective-permute-start | bytes 368648 | tf_op jit(solution)/shard_map/ppermute | solution.py:296
  19.4 10.6 %collective-permute-start.8 = (bf16[2,3,80,128]{3,2,1,0:T(8,128)(2,1)S(1)}, bf16[2,3,80,128]{3,2,1,0:T(8,128)(2,1)S(1)}, u32[]{:S(2)}, u32[]{:S(2)}) collective-permute-start(bf16[2,3,80,128]{3,2,1,0:T(8,128)(2,1)S(1)} %get-tuple-element.46), channel_id=1, source_target_pairs={{0,6},{1,7},{2,4},{3,5},{4,2},{5,3},{6,0},{7,1},{8,14},{9,15},{10,... | collective-permute-start | bytes 368648 | tf_op jit(solution)/shard_map/ppermute | solution.py:296
  22.1 7.9 %collective-permute-start.9 = (bf16[2,3,80,128]{3,2,1,0:T(8,128)(2,1)S(1)}, bf16[2,3,80,128]{3,2,1,0:T(8,128)(2,1)S(1)}, u32[]{:S(2)}, u32[]{:S(2)}) collective-permute-start(bf16[2,3,80,128]{3,2,1,0:T(8,128)(2,1)S(1)} %get-tuple-element.47), channel_id=1, source_target_pairs={{0,4},{1,5},{2,6},{3,7},{4,0},{5,1},{6,2},{7,3},{8,12},{9,13},{10,... | collective-permute-start | bytes 368648 | tf_op jit(solution)/shard_map/ppermute | solution.py:296
  30.1 6.2 %collective-permute-start.10 = (bf16[3,80,128]{2,1,0:T(8,128)(2,1)S(1)}, bf16[3,80,128]{2,1,0:T(8,128)(2,1)S(1)}, u32[]{:S(2)}, u32[]{:S(2)}) collective-permute-start(bf16[3,80,128]{2,1,0:T(8,128)(2,1)S(1)} %fusion.3), channel_id=1, source_target_pairs={{0,16},{8,24},{16,0},{24,8},{1,17},{9,25},{17,1},{25,9},{2,18},{10... | collective-permute-start | bytes 184328 | tf_op jit(solution)/shard_map/ppermute | solution.py:307
  36.4 5.2 %collective-permute-start.13 = (bf16[3,80,128]{2,1,0:T(8,128)(2,1)S(1)}, bf16[3,80,128]{2,1,0:T(8,128)(2,1)S(1)}, u32[]{:S(2)}, u32[]{:S(2)}) collective-permute-start(bf16[3,80,128]{2,1,0:T(8,128)(2,1)S(1)} %fusion.2), channel_id=1, source_target_pairs={{0,6},{1,7},{2,4},{3,5},{4,2},{5,3},{6,0},{7,1},{8,14},{9,15},{10,... | collective-permute-start | bytes 184328 | tf_op jit(solution)/shard_map/ppermute | solution.py:315
  36.5 5.1 %collective-permute-start.12 = (bf16[3,80,128]{2,1,0:T(8,128)(2,1)S(1)}, bf16[3,80,128]{2,1,0:T(8,128)(2,1)S(1)}, u32[]{:S(2)}, u32[]{:S(2)}) collective-permute-start(bf16[3,80,128]{2,1,0:T(8,128)(2,1)S(1)} %fusion.2), channel_id=1, source_target_pairs={{0,4},{1,5},{2,6},{3,7},{4,0},{5,1},{6,2},{7,3},{8,12},{9,13},{10,... | collective-permute-start | bytes 184328 | tf_op jit(solution)/shard_map/ppermute | solution.py:315
  38.1 4.2 %collective-permute-start.11 = (bf16[3,80,128]{2,1,0:T(8,128)(2,1)S(1)}, bf16[3,80,128]{2,1,0:T(8,128)(2,1)S(1)}, u32[]{:S(2)}, u32[]{:S(2)}) collective-permute-start(bf16[3,80,128]{2,1,0:T(8,128)(2,1)S(1)} %fusion.2), channel_id=1, source_target_pairs={{0,2},{1,3},{2,0},{3,1},{4,6},{5,7},{6,4},{7,5},{8,10},{9,11},{10,... | collective-permute-start | bytes 184328 | tf_op jit(solution)/shard_map/ppermute | solution.py:315
  42.4 1.6 %collective-permute-start.14 = (bf16[4,3,80,128]{3,2,1,0:T(8,128)(2,1)S(1)}, bf16[4,3,80,128]{3,2,1,0:T(8,128)(2,1)S(1)}, u32[]{:S(2)}, u32[]{:S(2)}) collective-permute-start(bf16[4,3,80,128]{3,2,1,0:T(8,128)(2,1)S(1)} %pad_maximum_fusion.parts_ref), channel_id=1, source_target_pairs={{0,1},{1,0},{2,3},{3,2},{4,5},{5,4},{6,7},{7,6},{8,9},{9,8},{10,11... | collective-permute-start | bytes 737288 | tf_op jit(solution)/shard_map/ppermute | solution.py:317

commit v11 on v10

--- a/solution.py
+++ b/solution.py
@@ -287,7 +287,7 @@
     )(term, act_edge, grad_edge, near_row)
 
     got = [terms[0]]
-    for k in (4, 6, 1, 7, 5, 3, 2):
+    for k in (4, 1, 2, 7, 3, 5, 6):
         moves = []
         for z in range(blocks):
             for i in range(space):

time: 45.5 us -> 45.7 us (level)
  waiting for transfers between devices: 10.6 us -> 11.1 us
    ppermute x3, waiting for transfers between devices: 2.36 us -> 3.72 us  [shards(): lax.ppermute(final, 'space', [(i, i ^ k * PAIR) for i in range(space)])]
    ppermute x1, waiting for transfers between devices: 3.57 us -> 2.79 us  [shards(): others.append(lax.ppermute(near_sum[k].astype(BF16), 'dp', moves))]
  transfers between devices with their start and end apart: 15 -> 15, of which waited for: 8 -> 9; matrix products, arithmetic and copies ran while one was open for 0% -> 0% of each run, Pallas kernels for 21% -> 21%
where the time goes in v11:
time: 45.7 us; the launch traced here: 45.5 us
  starting transfers between devices  20.8 us (46%)
  Pallas kernels  11.6 us (25%)
  waiting for transfers between devices  11.1 us (24%)
  local copies, waits for them, and re-layouts  0.98 us (2%)
  between operations  0.8 us (2%)
    ppermute x7, starting transfers between devices, shards(): got.append(lax.ppermute(terms[k], ('dp', 'space'), moves))  13.3 us
    pallas_call x2, Pallas kernels, input_part(): pl.pallas_call(functools.partial(input_kernel, side), out_shape=jax.Shape...  5.21 us
    ppermute x3, waiting for transfers between devices, shards(): lax.ppermute(final, 'space', [(i, i ^ k * PAIR) for i in range(space)])  3.72 us
    ppermute x3, starting transfers between devices, shards(): lax.ppermute(final, 'space', [(i, i ^ k * PAIR) for i in range(space)])  3.55 us
    pallas_call x1, Pallas kernels, shards(): pl.pallas_call(chip_kernel, out_shape=(jax.ShapeDtypeStruct((3, chans, PL...  2.93 us
    pallas_call x2, Pallas kernels, place(): pl.pallas_call(functools.partial(place_kernel, flip), out_shape=jax.Shape...  2.81 us
    ppermute x1, waiting for transfers between devices, shards(): others.append(lax.ppermute(near_sum[k].astype(BF16), 'dp', moves))  2.79 us
    ppermute x1, starting transfers between devices, shards(): others.append(lax.ppermute(near_sum[k].astype(BF16), 'dp', moves))  2.65 us
  transfers between devices with their start and end apart: 15, of which 9 were waited for; matrix products, arithmetic and copies ran while one was open for 0% of the time, Pallas kernels for 21%

profile of v11, /device:TPU:0, one launch (start us, length us, event | category | flops | bytes accessed | tf_op | source)
XLA Modules:
  0.0 45.5 jit_solution(16730065737174397037)
XLA Ops:
  0.6 0.9 %dynamic-slice_bitcast_fusion = (bf16[1,320,128]{2,1,0:T(8,128)(2,1)S(1)}, bf16[1,320,128]{2,1,0:T(8,128)(2,1)S(1)}) fusion(bf16[1,8,128,320]{2,3,1,0:T(8,128)(2,1)} %param.3, s32[]{:T(128)S(6)} %select_n.7, bf16[1,8,128,320]{2,3,1,0:T(8,128)(2,1)} %param.4), kind=kLoop, calls=%fused_computation.8 | loop fusion | bytes 327684 | tf_op jit(solution)/shard_map/jit(dynamic_index_in_dim)/dynamic_slice | solution.py:216
  1.6 0.5 %collective-permute-start = (bf16[8,320,128]{2,1,0:T(8,128)(2,1)}, bf16[8,320,128]{2,1,0:T(8,128)(2,1)S(1)}, u32[]{:S(2)}, u32[]{:S(2)}) collective-permute-start(bf16[8,320,128]{2,1,0:T(8,128)(2,1)} %bitcast.32), channel_id=1, source_target_pairs={{0,1},{1,0},{2,3},{3,2},{4,5},{5,4},{6,7},{7,6},{8,9},{9,8},{10,11... | collective-permute-start | bytes 1966088 | tf_op jit(solution)/shard_map/ppermute | solution.py:226
  2.2 0.7 %collective-permute-start.2 = (bf16[2,320,128]{2,1,0:T(8,128)(2,1)S(1)}, bf16[2,320,128]{2,1,0:T(8,128)(2,1)S(1)}, u32[]{:S(2)}, u32[]{:S(2)}) collective-permute-start(bf16[2,320,128]{2,1,0:T(8,128)(2,1)S(1)} %pad_maximum_fusion.1.after_ref), channel_id=1, source_target_pairs={{1,2},{2,1},{3,4},{4,3},{5,6},{6,5},{9,10},{10,9},{11,12},{12,11},... | collective-permute-start | bytes 491528 | tf_op jit(solution)/shard_map/ppermute | solution.py:223
  3.0 1.1 %collective-permute-done.their_pre_ref = bf16[8,320,128]{2,1,0:T(8,128)(2,1)S(1)} collective-permute-done((bf16[8,320,128]{2,1,0:T(8,128)(2,1)}, bf16[8,320,128]{2,1,0:T(8,128)(2,1)S(1)}, u32[]{:S(2)}, u32[]{:S(2)}) %collective-permute-start) | collective-permute-done | bytes 655392 | tf_op jit(solution)/shard_map/ppermute | solution.py:226
  4.1 0.9 %collective-permute-done.1.their_grad_ref = bf16[8,320,128]{2,1,0:T(8,128)(2,1)S(1)} collective-permute-done((bf16[8,320,128]{2,1,0:T(8,128)(2,1)}, bf16[8,320,128]{2,1,0:T(8,128)(2,1)S(1)}, u32[]{:S(2)}, u32[]{:S(2)}) %collective-permute-start.1) | collective-permute-done | bytes 655392 | tf_op jit(solution)/shard_map/ppermute | solution.py:225
  5.0 2.9 %chip_terms.1 = (f32[3,320,512]{2,1,0:T(8,128)S(1)}, bf16[2,320,128]{2,1,0:T(8,128)(2,1)S(1)}, bf16[2,160,128]{2,1,0:T(8,128)(2,1)S(1)}) custom-call(bf16[8,320,128]{2,1,0:T(8,128)(2,1)S(1)} %bitcast.33, bf16[8,320,128]{2,1,0:T(8,128)(2,1)S(1)} %bitcast.37, bf16[8,320,128]{2,1,0:T(8,128)(2,1)S(1)} %collective-permute-done.their_pre_ref, ...), custom_call_target="tpu_custom_call" | custom-call | flops 3774873600 | bytes 4000000 | tf_op jit(solution)/shard_map/chip_terms/pallas_call | solution.py:258
  8.0 0.5 %edge_terms.1 = (f32[2,3,80,128]{3,2,1,0:T(8,128)S(1)}, bf16[2,3,80,128]{3,2,1,0:T(8,128)(2,1)S(1)}, bf16[2,3,80,128]{3,2,1,0:T(8,128)(2,1)S(1)}, bf16[2,3,80,12...) custom-call(f32[3,320,512]{2,1,0:T(8,128)S(1)} %get-tuple-element.35, ...), custom_call_target="tpu_custom_call" | custom-call | flops 235929600 | bytes 4000000 | tf_op jit(solution)/shard_map/edge_terms/pallas_call | solution.py:275
  8.5 3.0 %collective-permute-start.3 = (bf16[2,3,80,128]{3,2,1,0:T(8,128)(2,1)S(1)}, bf16[2,3,80,128]{3,2,1,0:T(8,128)(2,1)S(1)}, u32[]{:S(2)}, u32[]{:S(2)}) collective-permute-start(bf16[2,3,80,128]{3,2,1,0:T(8,128)(2,1)S(1)} %get-tuple-element.39), channel_id=1, source_target_pairs={{0,8},{1,9},{2,10},{3,11},{4,12},{5,13},{6,14},{7,15},{8,0},{9,1},... | collective-permute-start | bytes 368648 | tf_op jit(solution)/shard_map/ppermute | solution.py:296
  11.6 2.4 %collective-permute-start.4 = (bf16[2,3,80,128]{3,2,1,0:T(8,128)(2,1)S(1)}, bf16[2,3,80,128]{3,2,1,0:T(8,128)(2,1)S(1)}, u32[]{:S(2)}, u32[]{:S(2)}) collective-permute-start(bf16[2,3,80,128]{3,2,1,0:T(8,128)(2,1)S(1)} %get-tuple-element.40), channel_id=1, source_target_pairs={{0,2},{1,3},{2,0},{3,1},{4,6},{5,7},{6,4},{7,5},{8,10},{9,11},{10,... | collective-permute-start | bytes 368648 | tf_op jit(solution)/shard_map/ppermute | solution.py:296
  14.0 3.1 %collective-permute-start.5 = (bf16[2,3,80,128]{3,2,1,0:T(8,128)(2,1)S(1)}, bf16[2,3,80,128]{3,2,1,0:T(8,128)(2,1)S(1)}, u32[]{:S(2)}, u32[]{:S(2)}) collective-permute-start(bf16[2,3,80,128]{3,2,1,0:T(8,128)(2,1)S(1)} %get-tuple-element.43), channel_id=1, source_target_pairs={{0,4},{1,5},{2,6},{3,7},{4,0},{5,1},{6,2},{7,3},{8,12},{9,13},{10,... | collective-permute-start | bytes 368648 | tf_op jit(solution)/shard_map/ppermute | solution.py:296
  17.1 2.8 %collective-permute-start.7 = (bf16[2,3,80,128]{3,2,1,0:T(8,128)(2,1)S(1)}, bf16[2,3,80,128]{3,2,1,0:T(8,128)(2,1)S(1)}, u32[]{:S(2)}, u32[]{:S(2)}) collective-permute-start(bf16[2,3,80,128]{3,2,1,0:T(8,128)(2,1)S(1)} %get-tuple-element.45), channel_id=1, source_target_pairs={{0,6},{1,7},{2,4},{3,5},{4,2},{5,3},{6,0},{7,1},{8,14},{9,15},{10,... | collective-permute-start | bytes 368648 | tf_op jit(solution)/shard_map/ppermute | solution.py:296
  19.9 2.0 %collective-permute-start.8 = (bf16[2,3,80,128]{3,2,1,0:T(8,128)(2,1)S(1)}, bf16[2,3,80,128]{3,2,1,0:T(8,128)(2,1)S(1)}, u32[]{:S(2)}, u32[]{:S(2)}) collective-permute-start(bf16[2,3,80,128]{3,2,1,0:T(8,128)(2,1)S(1)} %get-tuple-element.46), channel_id=1, source_target_pairs={{0,10},{1,11},{2,8},{3,9},{4,14},{5,15},{6,12},{7,13},{8,2},{9,3},... | collective-permute-start | bytes 368648 | tf_op jit(solution)/shard_map/ppermute | solution.py:296
  21.9 2.6 %input_grad.2.refs_0_ = bf16[8,320,128]{2,1,0:T(8,128)(2,1)} custom-call(bf16[8,320,128]{2,1,0:T(8,128)(2,1)S(1)} %bitcast.34, bf16[8,320,128]{2,1,0:T(8,128)(2,1)S(1)} %bitcast.38, bf16[2,320,128]{2,1,0:T(8,128)(2,1)S(1)} %collective-permute-done.2.near_ref.edge_ref, bf16[3,3,320,320]{3,2,1,0:T(8,128)(2,1)S(1)} %copy-done), custom_call_target="tpu_custom_call" | custom-call | flops 943718400 | bytes 3000000 | tf_op jit(solution)/shard_map/input_grad/pallas_call | solution.py:239
  24.5 2.6 %input_grad.3 = bf16[8,320,128]{2,1,0:T(8,128)(2,1)} custom-call(bf16[8,320,128]{2,1,0:T(8,128)(2,1)S(1)} %bitcast.35, bf16[8,320,128]{2,1,0:T(8,128)(2,1)S(1)} %bitcast.39, bf16[1,320,128]{2,1,0:T(8,128)(2,1)S(1)} %constant_dynamic-slice_fusion.edge_ref, bf16[3,3,320,320]{3,2,1,0:T(8,128)(2,1)S(1)} %copy-done, ...), custom_call_target="tpu_custom_call", output_to_operand_aliasing={{}: (4, {})} | custom-call | flops 943718400 | bytes 3000000 | tf_op jit(solution)/shard_map/input_grad/pallas_call | solution.py:239
  27.1 2.2 %collective-permute-done.7 = bf16[2,3,80,128]{3,2,1,0:T(8,128)(2,1)S(1)} collective-permute-done((bf16[2,3,80,128]{3,2,1,0:T(8,128)(2,1)S(1)}, bf16[2,3,80,128]{3,2,1,0:T(8,128)(2,1)S(1)}, u32[]{:S(2)}, u32[]{:S(2)}) %collective-permute-start.7) | collective-permute-done | bytes 122912 | tf_op jit(solution)/shard_map/ppermute | solution.py:296
  29.7 2.7 %collective-permute-start.10 = (bf16[3,80,128]{2,1,0:T(8,128)(2,1)S(1)}, bf16[3,80,128]{2,1,0:T(8,128)(2,1)S(1)}, u32[]{:S(2)}, u32[]{:S(2)}) collective-permute-start(bf16[3,80,128]{2,1,0:T(8,128)(2,1)S(1)} %fusion.3), channel_id=1, source_target_pairs={{0,16},{8,24},{16,0},{24,8},{1,17},{9,25},{17,1},{25,9},{2,18},{10... | collective-permute-start | bytes 184328 | tf_op jit(solution)/shard_map/ppermute | solution.py:307
  32.4 2.8 %collective-permute-done.10 = bf16[3,80,128]{2,1,0:T(8,128)(2,1)S(1)} collective-permute-done((bf16[3,80,128]{2,1,0:T(8,128)(2,1)S(1)}, bf16[3,80,128]{2,1,0:T(8,128)(2,1)S(1)}, u32[]{:S(2)}, u32[]{:S(2)}) %collective-permute-start.10) | collective-permute-done | bytes 61472 | tf_op jit(solution)/shard_map/ppermute | solution.py:307
  35.2 1.9 %collective-permute-start.13 = (bf16[3,80,128]{2,1,0:T(8,128)(2,1)S(1)}, bf16[3,80,128]{2,1,0:T(8,128)(2,1)S(1)}, u32[]{:S(2)}, u32[]{:S(2)}) collective-permute-start(bf16[3,80,128]{2,1,0:T(8,128)(2,1)S(1)} %fusion.2), channel_id=1, source_target_pairs={{0,6},{1,7},{2,4},{3,5},{4,2},{5,3},{6,0},{7,1},{8,14},{9,15},{10,... | collective-permute-start | bytes 184328 | tf_op jit(solution)/shard_map/ppermute | solution.py:315
  37.1 1.1 %collective-permute-start.12 = (bf16[3,80,128]{2,1,0:T(8,128)(2,1)S(1)}, bf16[3,80,128]{2,1,0:T(8,128)(2,1)S(1)}, u32[]{:S(2)}, u32[]{:S(2)}) collective-permute-start(bf16[3,80,128]{2,1,0:T(8,128)(2,1)S(1)} %fusion.2), channel_id=1, source_target_pairs={{0,4},{1,5},{2,6},{3,7},{4,0},{5,1},{6,2},{7,3},{8,12},{9,13},{10,... | collective-permute-start | bytes 184328 | tf_op jit(solution)/shard_map/ppermute | solution.py:315
  38.8 1.6 %collective-permute-done.13 = bf16[3,80,128]{2,1,0:T(8,128)(2,1)S(1)} collective-permute-done((bf16[3,80,128]{2,1,0:T(8,128)(2,1)S(1)}, bf16[3,80,128]{2,1,0:T(8,128)(2,1)S(1)}, u32[]{:S(2)}, u32[]{:S(2)}) %collective-permute-start.13) | collective-permute-done | bytes 61472 | tf_op jit(solution)/shard_map/ppermute | solution.py:315
  40.4 1.0 %collective-permute-done.12 = bf16[3,80,128]{2,1,0:T(8,128)(2,1)S(1)} collective-permute-done((bf16[3,80,128]{2,1,0:T(8,128)(2,1)S(1)}, bf16[3,80,128]{2,1,0:T(8,128)(2,1)S(1)}, u32[]{:S(2)}, u32[]{:S(2)}) %collective-permute-start.12) | collective-permute-done | bytes 61472 | tf_op jit(solution)/shard_map/ppermute | solution.py:315
  41.4 1.1 %collective-permute-done.11 = bf16[3,80,128]{2,1,0:T(8,128)(2,1)S(1)} collective-permute-done((bf16[3,80,128]{2,1,0:T(8,128)(2,1)S(1)}, bf16[3,80,128]{2,1,0:T(8,128)(2,1)S(1)}, u32[]{:S(2)}, u32[]{:S(2)}) %collective-permute-start.11) | collective-permute-done | bytes 61472 | tf_op jit(solution)/shard_map/ppermute | solution.py:315
  42.6 1.4 %place_rows.2.refs_0_ = f32[320,720]{1,0:T(8,128)} custom-call(bf16[4,3,80,128]{3,2,1,0:T(8,128)(2,1)S(1)} %pad_maximum_fusion.parts_ref, f32[144,144]{1,0:T(8,128)S(1)} %pick_rows.1.pick_ref), custom_call_target="tpu_custom_call" | custom-call | flops 165888000 | bytes 1000000 | tf_op jit(solution)/shard_map/place_rows/pallas_call | solution.py:320
  44.1 1.4 %place_rows.3 = f32[320,720]{1,0:T(8,128)} custom-call(bf16[4,3,80,128]{3,2,1,0:T(8,128)(2,1)S(1)} %collective-permute-done.14.parts_ref, f32[144,144]{1,0:T(8,128)S(1)} %pick_rows.1.pick_ref, f32[320,720]{1,0:T(8,128)} %place_rows.2.refs_0_), custom_call_target="tpu_custom_call", output_to_operand_aliasing={{}: (2, {})} | custom-call | flops 165888000 | bytes 1000000 | tf_op jit(solution)/shard_map/place_rows/pallas_call | solution.py:320
  (26 shorter events, 1.4 us)
Async XLA Ops:
  1.6 3.4 %copy-start.1 = (bf16[1,8,128,320]{2,3,1,0:T(8,128)(2,1)S(1)}, bf16[1,8,128,320]{2,3,1,0:T(8,128)(2,1)}, u32[]{:S(2)}) copy-start(bf16[1,8,128,320]{2,3,1,0:T(8,128)(2,1)} %param.3) | copy-start | bytes 1966084
  1.6 3.4 %copy-start.2 = (bf16[1,8,128,320]{2,3,1,0:T(8,128)(2,1)S(1)}, bf16[1,8,128,320]{2,3,1,0:T(8,128)(2,1)}, u32[]{:S(2)}) copy-start(bf16[1,8,128,320]{2,3,1,0:T(8,128)(2,1)} %param.4) | copy-start | bytes 1966084
  1.6 2.5 %collective-permute-start = (bf16[8,320,128]{2,1,0:T(8,128)(2,1)}, bf16[8,320,128]{2,1,0:T(8,128)(2,1)S(1)}, u32[]{:S(2)}, u32[]{:S(2)}) collective-permute-start(bf16[8,320,128]{2,1,0:T(8,128)(2,1)} %bitcast.32), channel_id=1, source_target_pairs={{0,1},{1,0},{2,3},{3,2},{4,5},{5,4},{6,7},{7,6},{8,9},{9,8},{10,11... | collective-permute-start | bytes 1966088 | tf_op jit(solution)/shard_map/ppermute | solution.py:226
  2.2 2.9 %collective-permute-start.1 = (bf16[8,320,128]{2,1,0:T(8,128)(2,1)}, bf16[8,320,128]{2,1,0:T(8,128)(2,1)S(1)}, u32[]{:S(2)}, u32[]{:S(2)}) collective-permute-start(bf16[8,320,128]{2,1,0:T(8,128)(2,1)} %bitcast.36), channel_id=1, source_target_pairs={{0,1},{1,0},{2,3},{3,2},{4,5},{5,4},{6,7},{7,6},{8,9},{9,8},{10,11... | collective-permute-start | bytes 1966088 | tf_op jit(solution)/shard_map/ppermute | solution.py:225
  2.2 5.8 %collective-permute-start.2 = (bf16[2,320,128]{2,1,0:T(8,128)(2,1)S(1)}, bf16[2,320,128]{2,1,0:T(8,128)(2,1)S(1)}, u32[]{:S(2)}, u32[]{:S(2)}) collective-permute-start(bf16[2,320,128]{2,1,0:T(8,128)(2,1)S(1)} %pad_maximum_fusion.1.after_ref), channel_id=1, source_target_pairs={{1,2},{2,1},{3,4},{4,3},{5,6},{6,5},{9,10},{10,9},{11,12},{12,11},... | collective-permute-start | bytes 491528 | tf_op jit(solution)/shard_map/ppermute | solution.py:223
  8.0 13.9 %copy-start = (bf16[3,3,320,320]{3,2,1,0:T(8,128)(2,1)S(1)}, bf16[3,3,320,320]{3,2,1,0:T(8,128)(2,1)}, u32[]{:S(2)}) copy-start(bf16[3,3,320,320]{3,2,1,0:T(8,128)(2,1)} %kernel_ref.3) | copy-start | bytes 5529604
  8.5 11.3 %collective-permute-start.3 = (bf16[2,3,80,128]{3,2,1,0:T(8,128)(2,1)S(1)}, bf16[2,3,80,128]{3,2,1,0:T(8,128)(2,1)S(1)}, u32[]{:S(2)}, u32[]{:S(2)}) collective-permute-start(bf16[2,3,80,128]{3,2,1,0:T(8,128)(2,1)S(1)} %get-tuple-element.39), channel_id=1, source_target_pairs={{0,8},{1,9},{2,10},{3,11},{4,12},{5,13},{6,14},{7,15},{8,0},{9,1},... | collective-permute-start | bytes 368648 | tf_op jit(solution)/shard_map/ppermute | solution.py:296
  11.6 10.3 %collective-permute-start.4 = (bf16[2,3,80,128]{3,2,1,0:T(8,128)(2,1)S(1)}, bf16[2,3,80,128]{3,2,1,0:T(8,128)(2,1)S(1)}, u32[]{:S(2)}, u32[]{:S(2)}) collective-permute-start(bf16[2,3,80,128]{3,2,1,0:T(8,128)(2,1)S(1)} %get-tuple-element.40), channel_id=1, source_target_pairs={{0,2},{1,3},{2,0},{3,1},{4,6},{5,7},{6,4},{7,5},{8,10},{9,11},{10,... | collective-permute-start | bytes 368648 | tf_op jit(solution)/shard_map/ppermute | solution.py:296
  14.0 13.2 %collective-permute-start.5 = (bf16[2,3,80,128]{3,2,1,0:T(8,128)(2,1)S(1)}, bf16[2,3,80,128]{3,2,1,0:T(8,128)(2,1)S(1)}, u32[]{:S(2)}, u32[]{:S(2)}) collective-permute-start(bf16[2,3,80,128]{3,2,1,0:T(8,128)(2,1)S(1)} %get-tuple-element.43), channel_id=1, source_target_pairs={{0,4},{1,5},{2,6},{3,7},{4,0},{5,1},{6,2},{7,3},{8,12},{9,13},{10,... | collective-permute-start | bytes 368648 | tf_op jit(solution)/shard_map/ppermute | solution.py:296
  17.0 10.1 %collective-permute-start.6 = (bf16[2,3,80,128]{3,2,1,0:T(8,128)(2,1)S(1)}, bf16[2,3,80,128]{3,2,1,0:T(8,128)(2,1)S(1)}, u32[]{:S(2)}, u32[]{:S(2)}) collective-permute-start(bf16[2,3,80,128]{3,2,1,0:T(8,128)(2,1)S(1)} %get-tuple-element.44), channel_id=1, source_target_pairs={{0,14},{1,15},{2,12},{3,13},{4,10},{5,11},{6,8},{7,9},{8,6},{9,7},... | collective-permute-start | bytes 368648 | tf_op jit(solution)/shard_map/ppermute | solution.py:296
  17.1 12.3 %collective-permute-start.7 = (bf16[2,3,80,128]{3,2,1,0:T(8,128)(2,1)S(1)}, bf16[2,3,80,128]{3,2,1,0:T(8,128)(2,1)S(1)}, u32[]{:S(2)}, u32[]{:S(2)}) collective-permute-start(bf16[2,3,80,128]{3,2,1,0:T(8,128)(2,1)S(1)} %get-tuple-element.45), channel_id=1, source_target_pairs={{0,6},{1,7},{2,4},{3,5},{4,2},{5,3},{6,0},{7,1},{8,14},{9,15},{10,... | collective-permute-start | bytes 368648 | tf_op jit(solution)/shard_map/ppermute | solution.py:296
  19.9 9.5 %collective-permute-start.8 = (bf16[2,3,80,128]{3,2,1,0:T(8,128)(2,1)S(1)}, bf16[2,3,80,128]{3,2,1,0:T(8,128)(2,1)S(1)}, u32[]{:S(2)}, u32[]{:S(2)}) collective-permute-start(bf16[2,3,80,128]{3,2,1,0:T(8,128)(2,1)S(1)} %get-tuple-element.46), channel_id=1, source_target_pairs={{0,10},{1,11},{2,8},{3,9},{4,14},{5,15},{6,12},{7,13},{8,2},{9,3},... | collective-permute-start | bytes 368648 | tf_op jit(solution)/shard_map/ppermute | solution.py:296
  21.9 7.7 %collective-permute-start.9 = (bf16[2,3,80,128]{3,2,1,0:T(8,128)(2,1)S(1)}, bf16[2,3,80,128]{3,2,1,0:T(8,128)(2,1)S(1)}, u32[]{:S(2)}, u32[]{:S(2)}) collective-permute-start(bf16[2,3,80,128]{3,2,1,0:T(8,128)(2,1)S(1)} %get-tuple-element.47), channel_id=1, source_target_pairs={{0,12},{1,13},{2,14},{3,15},{4,8},{5,9},{6,10},{7,11},{8,4},{9,5},... | collective-permute-start | bytes 368648 | tf_op jit(solution)/shard_map/ppermute | solution.py:296
  29.7 5.4 %collective-permute-start.10 = (bf16[3,80,128]{2,1,0:T(8,128)(2,1)S(1)}, bf16[3,80,128]{2,1,0:T(8,128)(2,1)S(1)}, u32[]{:S(2)}, u32[]{:S(2)}) collective-permute-start(bf16[3,80,128]{2,1,0:T(8,128)(2,1)S(1)} %fusion.3), channel_id=1, source_target_pairs={{0,16},{8,24},{16,0},{24,8},{1,17},{9,25},{17,1},{25,9},{2,18},{10... | collective-permute-start | bytes 184328 | tf_op jit(solution)/shard_map/ppermute | solution.py:307
  35.2 5.2 %collective-permute-start.13 = (bf16[3,80,128]{2,1,0:T(8,128)(2,1)S(1)}, bf16[3,80,128]{2,1,0:T(8,128)(2,1)S(1)}, u32[]{:S(2)}, u32[]{:S(2)}) collective-permute-start(bf16[3,80,128]{2,1,0:T(8,128)(2,1)S(1)} %fusion.2), channel_id=1, source_target_pairs={{0,6},{1,7},{2,4},{3,5},{4,2},{5,3},{6,0},{7,1},{8,14},{9,15},{10,... | collective-permute-start | bytes 184328 | tf_op jit(solution)/shard_map/ppermute | solution.py:315
  37.1 4.2 %collective-permute-start.12 = (bf16[3,80,128]{2,1,0:T(8,128)(2,1)S(1)}, bf16[3,80,128]{2,1,0:T(8,128)(2,1)S(1)}, u32[]{:S(2)}, u32[]{:S(2)}) collective-permute-start(bf16[3,80,128]{2,1,0:T(8,128)(2,1)S(1)} %fusion.2), channel_id=1, source_target_pairs={{0,4},{1,5},{2,6},{3,7},{4,0},{5,1},{6,2},{7,3},{8,12},{9,13},{10,... | collective-permute-start | bytes 184328 | tf_op jit(solution)/shard_map/ppermute | solution.py:315
  38.3 4.2 %collective-permute-start.11 = (bf16[3,80,128]{2,1,0:T(8,128)(2,1)S(1)}, bf16[3,80,128]{2,1,0:T(8,128)(2,1)S(1)}, u32[]{:S(2)}, u32[]{:S(2)}) collective-permute-start(bf16[3,80,128]{2,1,0:T(8,128)(2,1)S(1)} %fusion.2), channel_id=1, source_target_pairs={{0,2},{1,3},{2,0},{3,1},{4,6},{5,7},{6,4},{7,5},{8,10},{9,11},{10,... | collective-permute-start | bytes 184328 | tf_op jit(solution)/shard_map/ppermute | solution.py:315
  42.5 1.6 %collective-permute-start.14 = (bf16[4,3,80,128]{3,2,1,0:T(8,128)(2,1)S(1)}, bf16[4,3,80,128]{3,2,1,0:T(8,128)(2,1)S(1)}, u32[]{:S(2)}, u32[]{:S(2)}) collective-permute-start(bf16[4,3,80,128]{3,2,1,0:T(8,128)(2,1)S(1)} %pad_maximum_fusion.parts_ref), channel_id=1, source_target_pairs={{0,1},{1,0},{2,3},{3,2},{4,5},{5,4},{6,7},{7,6},{8,9},{9,8},{10,11... | collective-permute-start | bytes 737288 | tf_op jit(solution)/shard_map/ppermute | solution.py:317

commit v12 on v11

--- a/solution.py
+++ b/solution.py
@@ -15,6 +15,14 @@
 NEAR = 2
 VMEM_LIMIT = 16 * 1024 * 1024
 NT = (((1,), (1,)), ((), ()))
+
+
+FIRST_ORDER = ((4, 2, 1, 7, 3, 6, 5), (4, 1, 2, 7, 3, 5, 6))
+SPREAD_ORDER = ((2, 1, 3), (1, 2, 3))
+
+
+def by_core(orders, core, slot):
+    return jnp.where(core == 0, orders[0][slot], orders[1][slot])
 
 
 def vmem():
@@ -114,7 +122,8 @@
             for z in range(NEAR * outers):
                 term_s[z % NEAR * PLANE + p, z // NEAR, a] = term[z * block : (z + 1) * block, p * LANES : (p + 1) * LANES]
     at, outer_at = near_index(), lax.axis_index("dp") // NEAR
-    for k, out_ref in enumerate(out_refs):
+    for slot, out_ref in enumerate(out_refs):
+        k = by_core(FIRST_ORDER, core, slot - 1) if slot else 0
         for j in range(outers):
             out_ref[j] = term_s[at ^ k, outer_at ^ j].astype(out_ref.dtype)
 
@@ -171,9 +180,11 @@
     half = out_s.shape[0]
     width = pick_ref.shape[0]
     group = width // 9
-    for k in range(PLANE):
+    whose = my_core() ^ flip
+    for slot in range(PLANE):
+        k = by_core(SPREAD_ORDER, whose, slot - 1) if slot else 0
         lanes = pl.ds(pl.multiple_of((plane_index() ^ k) * LANES, LANES), LANES)
-        wide_s[:, :, lanes] = parts_ref[k].astype(F32)
+        wide_s[:, :, lanes] = parts_ref[slot].astype(F32)
     pick = pick_ref[...].astype(BF16)
     for g in range(block // group):
         rows = [wide_s[t // 3, g * group : (g + 1) * group, t % 3 * half : (t % 3 + 1) * half] for t in range(9)]
@@ -181,7 +192,7 @@
         turned_s[g * width : (g + 1) * width, :] = jnp.dot(pick, rows, preferred_element_type=F32)
     turned = turned_s[...].astype(BF16)
     step = half // sem.shape[0]
-    first = (my_core() ^ flip) * half
+    first = whose * half
     copies = []
     for n in range(sem.shape[0]):
         i = lax.broadcasted_iota(jnp.int32, (step, half), 0)
@@ -287,14 +298,14 @@
     )(term, act_edge, grad_edge, near_row)
 
     got = [terms[0]]
-    for k in (4, 1, 2, 7, 3, 5, 6):
+    for slot in range(NEAR * PLANE - 1):
         moves = []
         for z in range(blocks):
             for i in range(space):
+                k = FIRST_ORDER[i % PAIR][slot]
                 to_z, to_i = z ^ (k // PLANE), i ^ (k % PLANE * PAIR)
                 moves.append((z * space + i, to_z * space + to_i))
-        got.append(lax.ppermute(terms[k], ("dp", "space"), moves))
-
+        got.append(lax.ppermute(terms[slot + 1], ("dp", "space"), moves))
 
     their_edge = lax.dynamic_index_in_dim(their_grad, my_core() * (rows - 1), 0)
     got[1], got[2], near_row, their_edge = lax.optimization_barrier((got[1], got[2], near_row, their_edge))
@@ -311,8 +322,9 @@
         total = lax.psum(total, "space", axis_index_groups=[[o * inner + i for o in range(outer)] for i in range(inner)])
     final = total.astype(BF16)
     parts = [final]
-    for k in range(1, PLANE):
-        parts.append(lax.ppermute(final, "space", [(i, i ^ (k * PAIR)) for i in range(space)]))
+    for slot in range(PLANE - 1):
+        moves = [(i, i ^ (SPREAD_ORDER[i % PAIR][slot] * PAIR)) for i in range(space)]
+        parts.append(lax.ppermute(final, "space", moves))
     parts = jnp.stack(parts)
     their_parts = lax.ppermute(parts, "space", pairs)
 

time: 45.7 us -> 45.9 us (level)
  no operation moved by 1% of the time
where the time goes in v12:
time: 45.9 us; the launch traced here: 45.7 us
  starting transfers between devices  20.9 us (46%)
  Pallas kernels  11.6 us (25%)
  waiting for transfers between devices  11.2 us (24%)
  local copies, waits for them, and re-layouts  0.98 us (2%)
  between operations  0.8 us (2%)
    ppermute x7, starting transfers between devices, shards(): got.append(lax.ppermute(terms[slot + 1], ('dp', 'space'), moves))  13.4 us
    pallas_call x2, Pallas kernels, input_part(): pl.pallas_call(functools.partial(input_kernel, side), out_shape=jax.Shape...  5.19 us
    ppermute x3, waiting for transfers between devices, shards(): parts.append(lax.ppermute(final, 'space', moves))  4.08 us
    ppermute x3, starting transfers between devices, shards(): parts.append(lax.ppermute(final, 'space', moves))  3.55 us
    ppermute x1, waiting for transfers between devices, shards(): others.append(lax.ppermute(near_sum[k].astype(BF16), 'dp', moves))  3.21 us
    pallas_call x1, Pallas kernels, shards(): pl.pallas_call(chip_kernel, out_shape=(jax.ShapeDtypeStruct((3, chans, PL...  2.93 us
    pallas_call x2, Pallas kernels, place(): pl.pallas_call(functools.partial(place_kernel, flip), out_shape=jax.Shape...  2.81 us
    ppermute x1, starting transfers between devices, shards(): others.append(lax.ppermute(near_sum[k].astype(BF16), 'dp', moves))  2.63 us
  transfers between devices with their start and end apart: 15, of which 9 were waited for; matrix products, arithmetic and copies ran while one was open for 0% of the time, Pallas kernels for 21%

profile of v12, /device:TPU:0, one launch (start us, length us, event | category | flops | bytes accessed | tf_op | source)
XLA Modules:
  0.0 45.7 jit_solution(5422017489205901452)
XLA Ops:
  0.6 0.9 %dynamic-slice_bitcast_fusion = (bf16[1,320,128]{2,1,0:T(8,128)(2,1)S(1)}, bf16[1,320,128]{2,1,0:T(8,128)(2,1)S(1)}) fusion(bf16[1,8,128,320]{2,3,1,0:T(8,128)(2,1)} %param.3, s32[]{:T(128)S(6)} %select_n.7, bf16[1,8,128,320]{2,3,1,0:T(8,128)(2,1)} %param.4), kind=kLoop, calls=%fused_computation.8 | loop fusion | bytes 327684 | tf_op jit(solution)/shard_map/jit(dynamic_index_in_dim)/dynamic_slice | solution.py:227
  2.2 0.7 %collective-permute-start.2 = (bf16[2,320,128]{2,1,0:T(8,128)(2,1)S(1)}, bf16[2,320,128]{2,1,0:T(8,128)(2,1)S(1)}, u32[]{:S(2)}, u32[]{:S(2)}) collective-permute-start(bf16[2,320,128]{2,1,0:T(8,128)(2,1)S(1)} %pad_maximum_fusion.1.after_ref), channel_id=1, source_target_pairs={{1,2},{2,1},{3,4},{4,3},{5,6},{6,5},{9,10},{10,9},{11,12},{12,11},... | collective-permute-start | bytes 491528 | tf_op jit(solution)/shard_map/ppermute | solution.py:234
  3.0 1.1 %collective-permute-done.their_pre_ref = bf16[8,320,128]{2,1,0:T(8,128)(2,1)S(1)} collective-permute-done((bf16[8,320,128]{2,1,0:T(8,128)(2,1)}, bf16[8,320,128]{2,1,0:T(8,128)(2,1)S(1)}, u32[]{:S(2)}, u32[]{:S(2)}) %collective-permute-start) | collective-permute-done | bytes 655392 | tf_op jit(solution)/shard_map/ppermute | solution.py:237
  4.1 0.9 %collective-permute-done.1.their_grad_ref = bf16[8,320,128]{2,1,0:T(8,128)(2,1)S(1)} collective-permute-done((bf16[8,320,128]{2,1,0:T(8,128)(2,1)}, bf16[8,320,128]{2,1,0:T(8,128)(2,1)S(1)}, u32[]{:S(2)}, u32[]{:S(2)}) %collective-permute-start.1) | collective-permute-done | bytes 655392 | tf_op jit(solution)/shard_map/ppermute | solution.py:236
  5.0 2.9 %chip_terms.1 = (f32[3,320,512]{2,1,0:T(8,128)S(1)}, bf16[2,320,128]{2,1,0:T(8,128)(2,1)S(1)}, bf16[2,160,128]{2,1,0:T(8,128)(2,1)S(1)}) custom-call(bf16[8,320,128]{2,1,0:T(8,128)(2,1)S(1)} %bitcast.33, bf16[8,320,128]{2,1,0:T(8,128)(2,1)S(1)} %bitcast.37, bf16[8,320,128]{2,1,0:T(8,128)(2,1)S(1)} %collective-permute-done.their_pre_ref, ...), custom_call_target="tpu_custom_call" | custom-call | flops 3774873600 | bytes 4000000 | tf_op jit(solution)/shard_map/chip_terms/pallas_call | solution.py:269
  8.0 0.5 %edge_terms.1 = (f32[2,3,80,128]{3,2,1,0:T(8,128)S(1)}, bf16[2,3,80,128]{3,2,1,0:T(8,128)(2,1)S(1)}, bf16[2,3,80,128]{3,2,1,0:T(8,128)(2,1)S(1)}, bf16[2,3,80,12...) custom-call(f32[3,320,512]{2,1,0:T(8,128)S(1)} %get-tuple-element.35, ...), custom_call_target="tpu_custom_call" | custom-call | flops 235929600 | bytes 4000000 | tf_op jit(solution)/shard_map/edge_terms/pallas_call | solution.py:286
  8.5 3.0 %collective-permute-start.3 = (bf16[2,3,80,128]{3,2,1,0:T(8,128)(2,1)S(1)}, bf16[2,3,80,128]{3,2,1,0:T(8,128)(2,1)S(1)}, u32[]{:S(2)}, u32[]{:S(2)}) collective-permute-start(bf16[2,3,80,128]{3,2,1,0:T(8,128)(2,1)S(1)} %get-tuple-element.39), channel_id=1, source_target_pairs={{0,8},{1,9},{2,10},{3,11},{4,12},{5,13},{6,14},{7,15},{8,0},{9,1},... | collective-permute-start | bytes 368648 | tf_op jit(solution)/shard_map/ppermute | solution.py:308
  11.6 4.4 %collective-permute-start.4 = (bf16[2,3,80,128]{3,2,1,0:T(8,128)(2,1)S(1)}, bf16[2,3,80,128]{3,2,1,0:T(8,128)(2,1)S(1)}, u32[]{:S(2)}, u32[]{:S(2)}) collective-permute-start(bf16[2,3,80,128]{3,2,1,0:T(8,128)(2,1)S(1)} %get-tuple-element.40), channel_id=1, source_target_pairs={{0,4},{1,3},{2,6},{3,1},{4,0},{5,7},{6,2},{7,5},{8,12},{9,11},{10,... | collective-permute-start | bytes 368648 | tf_op jit(solution)/shard_map/ppermute | solution.py:308
  15.9 1.1 %collective-permute-start.5 = (bf16[2,3,80,128]{3,2,1,0:T(8,128)(2,1)S(1)}, bf16[2,3,80,128]{3,2,1,0:T(8,128)(2,1)S(1)}, u32[]{:S(2)}, u32[]{:S(2)}) collective-permute-start(bf16[2,3,80,128]{3,2,1,0:T(8,128)(2,1)S(1)} %get-tuple-element.43), channel_id=1, source_target_pairs={{0,2},{1,5},{2,0},{3,7},{4,6},{5,1},{6,4},{7,3},{8,10},{9,13},{10,... | collective-permute-start | bytes 368648 | tf_op jit(solution)/shard_map/ppermute | solution.py:308
  17.1 2.8 %collective-permute-start.7 = (bf16[2,3,80,128]{3,2,1,0:T(8,128)(2,1)S(1)}, bf16[2,3,80,128]{3,2,1,0:T(8,128)(2,1)S(1)}, u32[]{:S(2)}, u32[]{:S(2)}) collective-permute-start(bf16[2,3,80,128]{3,2,1,0:T(8,128)(2,1)S(1)} %get-tuple-element.45), channel_id=1, source_target_pairs={{0,6},{1,7},{2,4},{3,5},{4,2},{5,3},{6,0},{7,1},{8,14},{9,15},{10,... | collective-permute-start | bytes 368648 | tf_op jit(solution)/shard_map/ppermute | solution.py:308
  19.9 1.1 %collective-permute-start.8 = (bf16[2,3,80,128]{3,2,1,0:T(8,128)(2,1)S(1)}, bf16[2,3,80,128]{3,2,1,0:T(8,128)(2,1)S(1)}, u32[]{:S(2)}, u32[]{:S(2)}) collective-permute-start(bf16[2,3,80,128]{3,2,1,0:T(8,128)(2,1)S(1)} %get-tuple-element.46), channel_id=1, source_target_pairs={{0,12},{1,11},{2,14},{3,9},{4,8},{5,15},{6,10},{7,13},{8,4},{9,3},... | collective-permute-start | bytes 368648 | tf_op jit(solution)/shard_map/ppermute | solution.py:308
  21.0 1.0 %collective-permute-start.9 = (bf16[2,3,80,128]{3,2,1,0:T(8,128)(2,1)S(1)}, bf16[2,3,80,128]{3,2,1,0:T(8,128)(2,1)S(1)}, u32[]{:S(2)}, u32[]{:S(2)}) collective-permute-start(bf16[2,3,80,128]{3,2,1,0:T(8,128)(2,1)S(1)} %get-tuple-element.47), channel_id=1, source_target_pairs={{0,10},{1,13},{2,8},{3,15},{4,14},{5,9},{6,12},{7,11},{8,2},{9,5},... | collective-permute-start | bytes 368648 | tf_op jit(solution)/shard_map/ppermute | solution.py:308
  22.0 2.6 %input_grad.2.refs_0_ = bf16[8,320,128]{2,1,0:T(8,128)(2,1)} custom-call(bf16[8,320,128]{2,1,0:T(8,128)(2,1)S(1)} %bitcast.34, bf16[8,320,128]{2,1,0:T(8,128)(2,1)S(1)} %bitcast.38, bf16[2,320,128]{2,1,0:T(8,128)(2,1)S(1)} %collective-permute-done.2.near_ref.edge_ref, bf16[3,3,320,320]{3,2,1,0:T(8,128)(2,1)S(1)} %copy-done), custom_call_target="tpu_custom_call" | custom-call | flops 943718400 | bytes 3000000 | tf_op jit(solution)/shard_map/input_grad/pallas_call | solution.py:250
  24.6 2.6 %input_grad.3 = bf16[8,320,128]{2,1,0:T(8,128)(2,1)} custom-call(bf16[8,320,128]{2,1,0:T(8,128)(2,1)S(1)} %bitcast.35, bf16[8,320,128]{2,1,0:T(8,128)(2,1)S(1)} %bitcast.39, bf16[1,320,128]{2,1,0:T(8,128)(2,1)S(1)} %constant_dynamic-slice_fusion.edge_ref, bf16[3,3,320,320]{3,2,1,0:T(8,128)(2,1)S(1)} %copy-done, ...), custom_call_target="tpu_custom_call", output_to_operand_aliasing={{}: (4, {})} | custom-call | flops 943718400 | bytes 3000000 | tf_op jit(solution)/shard_map/input_grad/pallas_call | solution.py:250
  27.2 1.5 %collective-permute-done.7 = bf16[2,3,80,128]{3,2,1,0:T(8,128)(2,1)S(1)} collective-permute-done((bf16[2,3,80,128]{3,2,1,0:T(8,128)(2,1)S(1)}, bf16[2,3,80,128]{3,2,1,0:T(8,128)(2,1)S(1)}, u32[]{:S(2)}, u32[]{:S(2)}) %collective-permute-start.7) | collective-permute-done | bytes 122912 | tf_op jit(solution)/shard_map/ppermute | solution.py:308
  29.2 2.6 %collective-permute-start.10 = (bf16[3,80,128]{2,1,0:T(8,128)(2,1)S(1)}, bf16[3,80,128]{2,1,0:T(8,128)(2,1)S(1)}, u32[]{:S(2)}, u32[]{:S(2)}) collective-permute-start(bf16[3,80,128]{2,1,0:T(8,128)(2,1)S(1)} %fusion.3), channel_id=1, source_target_pairs={{0,16},{8,24},{16,0},{24,8},{1,17},{9,25},{17,1},{25,9},{2,18},{10... | collective-permute-start | bytes 184328 | tf_op jit(solution)/shard_map/ppermute | solution.py:318
  31.8 3.2 %collective-permute-done.10 = bf16[3,80,128]{2,1,0:T(8,128)(2,1)S(1)} collective-permute-done((bf16[3,80,128]{2,1,0:T(8,128)(2,1)S(1)}, bf16[3,80,128]{2,1,0:T(8,128)(2,1)S(1)}, u32[]{:S(2)}, u32[]{:S(2)}) %collective-permute-start.10) | collective-permute-done | bytes 61472 | tf_op jit(solution)/shard_map/ppermute | solution.py:318
  35.0 2.1 %collective-permute-start.13 = (bf16[3,80,128]{2,1,0:T(8,128)(2,1)S(1)}, bf16[3,80,128]{2,1,0:T(8,128)(2,1)S(1)}, u32[]{:S(2)}, u32[]{:S(2)}) collective-permute-start(bf16[3,80,128]{2,1,0:T(8,128)(2,1)S(1)} %fusion.2), channel_id=1, source_target_pairs={{0,6},{1,7},{2,4},{3,5},{4,2},{5,3},{6,0},{7,1},{8,14},{9,15},{10,... | collective-permute-start | bytes 184328 | tf_op jit(solution)/shard_map/ppermute | solution.py:327
  37.2 1.3 %collective-permute-start.12 = (bf16[3,80,128]{2,1,0:T(8,128)(2,1)S(1)}, bf16[3,80,128]{2,1,0:T(8,128)(2,1)S(1)}, u32[]{:S(2)}, u32[]{:S(2)}) collective-permute-start(bf16[3,80,128]{2,1,0:T(8,128)(2,1)S(1)} %fusion.2), channel_id=1, source_target_pairs={{0,2},{1,5},{2,0},{3,7},{4,6},{5,1},{6,4},{7,3},{8,10},{9,13},{10,... | collective-permute-start | bytes 184328 | tf_op jit(solution)/shard_map/ppermute | solution.py:327
  38.6 1.6 %collective-permute-done.13 = bf16[3,80,128]{2,1,0:T(8,128)(2,1)S(1)} collective-permute-done((bf16[3,80,128]{2,1,0:T(8,128)(2,1)S(1)}, bf16[3,80,128]{2,1,0:T(8,128)(2,1)S(1)}, u32[]{:S(2)}, u32[]{:S(2)}) %collective-permute-start.13) | collective-permute-done | bytes 61472 | tf_op jit(solution)/shard_map/ppermute | solution.py:327
  40.2 1.2 %collective-permute-done.12 = bf16[3,80,128]{2,1,0:T(8,128)(2,1)S(1)} collective-permute-done((bf16[3,80,128]{2,1,0:T(8,128)(2,1)S(1)}, bf16[3,80,128]{2,1,0:T(8,128)(2,1)S(1)}, u32[]{:S(2)}, u32[]{:S(2)}) %collective-permute-start.12) | collective-permute-done | bytes 61472 | tf_op jit(solution)/shard_map/ppermute | solution.py:327
  41.4 1.3 %collective-permute-done.11 = bf16[3,80,128]{2,1,0:T(8,128)(2,1)S(1)} collective-permute-done((bf16[3,80,128]{2,1,0:T(8,128)(2,1)S(1)}, bf16[3,80,128]{2,1,0:T(8,128)(2,1)S(1)}, u32[]{:S(2)}, u32[]{:S(2)}) %collective-permute-start.11) | collective-permute-done | bytes 61472 | tf_op jit(solution)/shard_map/ppermute | solution.py:327
  42.8 1.4 %place_rows.2.refs_0_ = f32[320,720]{1,0:T(8,128)} custom-call(bf16[4,3,80,128]{3,2,1,0:T(8,128)(2,1)S(1)} %pad_maximum_fusion.parts_ref, f32[144,144]{1,0:T(8,128)S(1)} %pick_rows.1.pick_ref), custom_call_target="tpu_custom_call" | custom-call | flops 165888000 | bytes 1000000 | tf_op jit(solution)/shard_map/place_rows/pallas_call | solution.py:332
  44.3 1.4 %place_rows.3 = f32[320,720]{1,0:T(8,128)} custom-call(bf16[4,3,80,128]{3,2,1,0:T(8,128)(2,1)S(1)} %collective-permute-done.14.parts_ref, f32[144,144]{1,0:T(8,128)S(1)} %pick_rows.1.pick_ref, f32[320,720]{1,0:T(8,128)} %place_rows.2.refs_0_), custom_call_target="tpu_custom_call", output_to_operand_aliasing={{}: (2, {})} | custom-call | flops 165888000 | bytes 1000000 | tf_op jit(solution)/shard_map/place_rows/pallas_call | solution.py:332
  (26 shorter events, 1.6 us)
Async XLA Ops:
  1.6 3.4 %copy-start.1 = (bf16[1,8,128,320]{2,3,1,0:T(8,128)(2,1)S(1)}, bf16[1,8,128,320]{2,3,1,0:T(8,128)(2,1)}, u32[]{:S(2)}) copy-start(bf16[1,8,128,320]{2,3,1,0:T(8,128)(2,1)} %param.3) | copy-start | bytes 1966084
  1.6 3.4 %copy-start.2 = (bf16[1,8,128,320]{2,3,1,0:T(8,128)(2,1)S(1)}, bf16[1,8,128,320]{2,3,1,0:T(8,128)(2,1)}, u32[]{:S(2)}) copy-start(bf16[1,8,128,320]{2,3,1,0:T(8,128)(2,1)} %param.4) | copy-start | bytes 1966084
  1.6 2.5 %collective-permute-start = (bf16[8,320,128]{2,1,0:T(8,128)(2,1)}, bf16[8,320,128]{2,1,0:T(8,128)(2,1)S(1)}, u32[]{:S(2)}, u32[]{:S(2)}) collective-permute-start(bf16[8,320,128]{2,1,0:T(8,128)(2,1)} %bitcast.32), channel_id=1, source_target_pairs={{0,1},{1,0},{2,3},{3,2},{4,5},{5,4},{6,7},{7,6},{8,9},{9,8},{10,11... | collective-permute-start | bytes 1966088 | tf_op jit(solution)/shard_map/ppermute | solution.py:237
  2.2 2.9 %collective-permute-start.1 = (bf16[8,320,128]{2,1,0:T(8,128)(2,1)}, bf16[8,320,128]{2,1,0:T(8,128)(2,1)S(1)}, u32[]{:S(2)}, u32[]{:S(2)}) collective-permute-start(bf16[8,320,128]{2,1,0:T(8,128)(2,1)} %bitcast.36), channel_id=1, source_target_pairs={{0,1},{1,0},{2,3},{3,2},{4,5},{5,4},{6,7},{7,6},{8,9},{9,8},{10,11... | collective-permute-start | bytes 1966088 | tf_op jit(solution)/shard_map/ppermute | solution.py:236
  2.2 5.8 %collective-permute-start.2 = (bf16[2,320,128]{2,1,0:T(8,128)(2,1)S(1)}, bf16[2,320,128]{2,1,0:T(8,128)(2,1)S(1)}, u32[]{:S(2)}, u32[]{:S(2)}) collective-permute-start(bf16[2,320,128]{2,1,0:T(8,128)(2,1)S(1)} %pad_maximum_fusion.1.after_ref), channel_id=1, source_target_pairs={{1,2},{2,1},{3,4},{4,3},{5,6},{6,5},{9,10},{10,9},{11,12},{12,11},... | collective-permute-start | bytes 491528 | tf_op jit(solution)/shard_map/ppermute | solution.py:234
  8.0 14.0 %copy-start = (bf16[3,3,320,320]{3,2,1,0:T(8,128)(2,1)S(1)}, bf16[3,3,320,320]{3,2,1,0:T(8,128)(2,1)}, u32[]{:S(2)}) copy-start(bf16[3,3,320,320]{3,2,1,0:T(8,128)(2,1)} %kernel_ref.3) | copy-start | bytes 5529604
  8.5 11.3 %collective-permute-start.3 = (bf16[2,3,80,128]{3,2,1,0:T(8,128)(2,1)S(1)}, bf16[2,3,80,128]{3,2,1,0:T(8,128)(2,1)S(1)}, u32[]{:S(2)}, u32[]{:S(2)}) collective-permute-start(bf16[2,3,80,128]{3,2,1,0:T(8,128)(2,1)S(1)} %get-tuple-element.39), channel_id=1, source_target_pairs={{0,8},{1,9},{2,10},{3,11},{4,12},{5,13},{6,14},{7,15},{8,0},{9,1},... | collective-permute-start | bytes 368648 | tf_op jit(solution)/shard_map/ppermute | solution.py:308
  11.6 9.4 %collective-permute-start.4 = (bf16[2,3,80,128]{3,2,1,0:T(8,128)(2,1)S(1)}, bf16[2,3,80,128]{3,2,1,0:T(8,128)(2,1)S(1)}, u32[]{:S(2)}, u32[]{:S(2)}) collective-permute-start(bf16[2,3,80,128]{3,2,1,0:T(8,128)(2,1)S(1)} %get-tuple-element.40), channel_id=1, source_target_pairs={{0,4},{1,3},{2,6},{3,1},{4,0},{5,7},{6,2},{7,5},{8,12},{9,11},{10,... | collective-permute-start | bytes 368648 | tf_op jit(solution)/shard_map/ppermute | solution.py:308
  15.9 11.2 %collective-permute-start.5 = (bf16[2,3,80,128]{3,2,1,0:T(8,128)(2,1)S(1)}, bf16[2,3,80,128]{3,2,1,0:T(8,128)(2,1)S(1)}, u32[]{:S(2)}, u32[]{:S(2)}) collective-permute-start(bf16[2,3,80,128]{3,2,1,0:T(8,128)(2,1)S(1)} %get-tuple-element.43), channel_id=1, source_target_pairs={{0,2},{1,5},{2,0},{3,7},{4,6},{5,1},{6,4},{7,3},{8,10},{9,13},{10,... | collective-permute-start | bytes 368648 | tf_op jit(solution)/shard_map/ppermute | solution.py:308
  17.0 10.2 %collective-permute-start.6 = (bf16[2,3,80,128]{3,2,1,0:T(8,128)(2,1)S(1)}, bf16[2,3,80,128]{3,2,1,0:T(8,128)(2,1)S(1)}, u32[]{:S(2)}, u32[]{:S(2)}) collective-permute-start(bf16[2,3,80,128]{3,2,1,0:T(8,128)(2,1)S(1)} %get-tuple-element.44), channel_id=1, source_target_pairs={{0,14},{1,15},{2,12},{3,13},{4,10},{5,11},{6,8},{7,9},{8,6},{9,7},... | collective-permute-start | bytes 368648 | tf_op jit(solution)/shard_map/ppermute | solution.py:308
  17.1 11.6 %collective-permute-start.7 = (bf16[2,3,80,128]{3,2,1,0:T(8,128)(2,1)S(1)}, bf16[2,3,80,128]{3,2,1,0:T(8,128)(2,1)S(1)}, u32[]{:S(2)}, u32[]{:S(2)}) collective-permute-start(bf16[2,3,80,128]{3,2,1,0:T(8,128)(2,1)S(1)} %get-tuple-element.45), channel_id=1, source_target_pairs={{0,6},{1,7},{2,4},{3,5},{4,2},{5,3},{6,0},{7,1},{8,14},{9,15},{10,... | collective-permute-start | bytes 368648 | tf_op jit(solution)/shard_map/ppermute | solution.py:308
  19.9 9.2 %collective-permute-start.8 = (bf16[2,3,80,128]{3,2,1,0:T(8,128)(2,1)S(1)}, bf16[2,3,80,128]{3,2,1,0:T(8,128)(2,1)S(1)}, u32[]{:S(2)}, u32[]{:S(2)}) collective-permute-start(bf16[2,3,80,128]{3,2,1,0:T(8,128)(2,1)S(1)} %get-tuple-element.46), channel_id=1, source_target_pairs={{0,12},{1,11},{2,14},{3,9},{4,8},{5,15},{6,10},{7,13},{8,4},{9,3},... | collective-permute-start | bytes 368648 | tf_op jit(solution)/shard_map/ppermute | solution.py:308
  21.0 8.1 %collective-permute-start.9 = (bf16[2,3,80,128]{3,2,1,0:T(8,128)(2,1)S(1)}, bf16[2,3,80,128]{3,2,1,0:T(8,128)(2,1)S(1)}, u32[]{:S(2)}, u32[]{:S(2)}) collective-permute-start(bf16[2,3,80,128]{3,2,1,0:T(8,128)(2,1)S(1)} %get-tuple-element.47), channel_id=1, source_target_pairs={{0,10},{1,13},{2,8},{3,15},{4,14},{5,9},{6,12},{7,11},{8,2},{9,5},... | collective-permute-start | bytes 368648 | tf_op jit(solution)/shard_map/ppermute | solution.py:308
  29.2 5.8 %collective-permute-start.10 = (bf16[3,80,128]{2,1,0:T(8,128)(2,1)S(1)}, bf16[3,80,128]{2,1,0:T(8,128)(2,1)S(1)}, u32[]{:S(2)}, u32[]{:S(2)}) collective-permute-start(bf16[3,80,128]{2,1,0:T(8,128)(2,1)S(1)} %fusion.3), channel_id=1, source_target_pairs={{0,16},{8,24},{16,0},{24,8},{1,17},{9,25},{17,1},{25,9},{2,18},{10... | collective-permute-start | bytes 184328 | tf_op jit(solution)/shard_map/ppermute | solution.py:318
  35.0 5.2 %collective-permute-start.13 = (bf16[3,80,128]{2,1,0:T(8,128)(2,1)S(1)}, bf16[3,80,128]{2,1,0:T(8,128)(2,1)S(1)}, u32[]{:S(2)}, u32[]{:S(2)}) collective-permute-start(bf16[3,80,128]{2,1,0:T(8,128)(2,1)S(1)} %fusion.2), channel_id=1, source_target_pairs={{0,6},{1,7},{2,4},{3,5},{4,2},{5,3},{6,0},{7,1},{8,14},{9,15},{10,... | collective-permute-start | bytes 184328 | tf_op jit(solution)/shard_map/ppermute | solution.py:327
  37.2 4.2 %collective-permute-start.12 = (bf16[3,80,128]{2,1,0:T(8,128)(2,1)S(1)}, bf16[3,80,128]{2,1,0:T(8,128)(2,1)S(1)}, u32[]{:S(2)}, u32[]{:S(2)}) collective-permute-start(bf16[3,80,128]{2,1,0:T(8,128)(2,1)S(1)} %fusion.2), channel_id=1, source_target_pairs={{0,2},{1,5},{2,0},{3,7},{4,6},{5,1},{6,4},{7,3},{8,10},{9,13},{10,... | collective-permute-start | bytes 184328 | tf_op jit(solution)/shard_map/ppermute | solution.py:327
  38.5 4.2 %collective-permute-start.11 = (bf16[3,80,128]{2,1,0:T(8,128)(2,1)S(1)}, bf16[3,80,128]{2,1,0:T(8,128)(2,1)S(1)}, u32[]{:S(2)}, u32[]{:S(2)}) collective-permute-start(bf16[3,80,128]{2,1,0:T(8,128)(2,1)S(1)} %fusion.2), channel_id=1, source_target_pairs={{0,4},{1,3},{2,6},{3,1},{4,0},{5,7},{6,2},{7,5},{8,12},{9,11},{10,... | collective-permute-start | bytes 184328 | tf_op jit(solution)/shard_map/ppermute | solution.py:327
  42.7 1.6 %collective-permute-start.14 = (bf16[4,3,80,128]{3,2,1,0:T(8,128)(2,1)S(1)}, bf16[4,3,80,128]{3,2,1,0:T(8,128)(2,1)S(1)}, u32[]{:S(2)}, u32[]{:S(2)}) collective-permute-start(bf16[4,3,80,128]{3,2,1,0:T(8,128)(2,1)S(1)} %pad_maximum_fusion.parts_ref), channel_id=1, source_target_pairs={{0,1},{1,0},{2,3},{3,2},{4,5},{5,4},{6,7},{7,6},{8,9},{9,8},{10,11... | collective-permute-start | bytes 737288 | tf_op jit(solution)/shard_map/ppermute | solution.py:329

commit v13 on v11

--- a/solution.py
+++ b/solution.py
@@ -119,7 +119,13 @@
             out_ref[j] = term_s[at ^ k, outer_at ^ j].astype(out_ref.dtype)
 
 
-def input_kernel(side, pre_ref, grad_ref, edge_ref, kernel_ref, *refs):
+def input_kernel(side, on_core, *refs):
+    @pl.when(my_core() == on_core)
+    def _():
+        input_rows(side, *refs)
+
+
+def input_rows(side, pre_ref, grad_ref, edge_ref, kernel_ref, *refs):
     out_hbm, taps_s, out_s, sem = refs[-4:]
     rows, chans, width = pre_ref.shape
     count = rows // 2
@@ -234,10 +240,10 @@
         name="pick_rows",
     )(edge)
     pick, own_pre, own_grad = lax.optimization_barrier((pick, pre, grad))
-    def input_part(side, edge_rows, *before):
+    def input_part(side, on_core, edge_rows, *before):
         count = rows // 2
         return pl.pallas_call(
-            functools.partial(input_kernel, side),
+            functools.partial(input_kernel, side, on_core),
             out_shape=jax.ShapeDtypeStruct((rows, chans, width), BF16),
             in_specs=[vmem()] * 4 + [anywhere()] * len(before),
             out_specs=anywhere(),
@@ -272,6 +278,10 @@
         cost_estimate=pl.CostEstimate(flops=2 * flops, bytes_accessed=4000000, transcendentals=2 * rows * width * chans),
         name="chip_terms",
     )(own_pre, own_grad, their_pre, their_grad)
+    ready = lax.optimization_barrier((term, act_edge, grad_edge, their_grad))
+    term, act_edge, grad_edge, their_grad = ready
+    their_edge = lax.dynamic_index_in_dim(their_grad, my_core() * (rows - 1), 0)
+    in_grad = input_part(1, 1, their_edge)
     terms = pl.pallas_call(
         edge_kernel,
         out_shape=(jax.ShapeDtypeStruct(piece.shape, F32),) + (piece,) * (NEAR * PLANE - 1),
@@ -286,6 +296,9 @@
         name="edge_terms",
     )(term, act_edge, grad_edge, near_row)
 
+    in_grad = input_part(0, 1, near_row, in_grad)
+    *terms, in_grad = lax.optimization_barrier((*terms, in_grad))
+
     got = [terms[0]]
     for k in (4, 1, 2, 7, 3, 5, 6):
         moves = []
@@ -296,15 +309,17 @@
         got.append(lax.ppermute(terms[k], ("dp", "space"), moves))
 
 
-    their_edge = lax.dynamic_index_in_dim(their_grad, my_core() * (rows - 1), 0)
     got[1], got[2], near_row, their_edge = lax.optimization_barrier((got[1], got[2], near_row, their_edge))
-    in_grad = input_part(1, their_edge, input_part(0, near_row))
+    in_grad = input_part(0, 0, near_row, in_grad)
     *got, in_grad = lax.optimization_barrier((*got, in_grad))
+
     near_sum = sum(part.astype(F32) for part in got)
     others = []
     for k in range(1, far):
         moves = [(z, z ^ (k * NEAR)) for z in range(blocks)]
         others.append(lax.ppermute(near_sum[k].astype(BF16), "dp", moves))
+    in_grad = input_part(1, 0, their_edge, in_grad)
+    *others, in_grad = lax.optimization_barrier((*others, in_grad))
     total = near_sum[0] + sum(other.astype(F32) for other in others)
     total = total * factor
     if outer > 1:

time: 45.7 us -> 46.7 us (1.022)
  starting transfers between devices: 20.8 us -> 21.3 us
  waiting for transfers between devices: 11.1 us -> 11.6 us
    ppermute x7, waiting for transfers between devices: 2.45 us -> 5.28 us  [shards(): got.append(lax.ppermute(terms[k], ('dp', 'space'), moves))]
    ppermute x1, waiting for transfers between devices: 2.79 us -> 1.29 us  [shards(): others.append(lax.ppermute(near_sum[k].astype(BF16), 'dp', moves))]
    ppermute x3, waiting for transfers between devices: 3.72 us -> 2.95 us  [shards(): lax.ppermute(final, 'space', [(i, i ^ k * PAIR) for i in range(space)])]
    ppermute x1, starting transfers between devices: 2.65 us -> 3.24 us  [shards(): others.append(lax.ppermute(near_sum[k].astype(BF16), 'dp', moves))]
    pallas_call x2 -> x4, Pallas kernels: 5.21 us -> 5.25 us  [input_part(): pl.pallas_call(functools.partial(input_kernel, side, on_core), out_shape=...]
  transfers between devices with their start and end apart: 15 -> 15, of which waited for: 9 -> 7; matrix products, arithmetic and copies ran while one was open for 0% -> 0% of each run, Pallas kernels for 21% -> 21%
where the time goes in v13:
time: 46.7 us; the launch traced here: 46.6 us
  starting transfers between devices  21.3 us (46%)
  Pallas kernels  11.6 us (25%)
  waiting for transfers between devices  11.6 us (25%)
  local copies, waits for them, and re-layouts  0.99 us (2%)
  between operations  0.82 us (2%)
    ppermute x7, starting transfers between devices, shards(): got.append(lax.ppermute(terms[k], ('dp', 'space'), moves))  13.2 us
    ppermute x7, waiting for transfers between devices, shards(): got.append(lax.ppermute(terms[k], ('dp', 'space'), moves))  5.28 us
    pallas_call x4, Pallas kernels, input_part(): pl.pallas_call(functools.partial(input_kernel, side, on_core), out_shape=...  5.25 us
    ppermute x3, starting transfers between devices, shards(): lax.ppermute(final, 'space', [(i, i ^ k * PAIR) for i in range(space)])  3.55 us
    ppermute x1, starting transfers between devices, shards(): others.append(lax.ppermute(near_sum[k].astype(BF16), 'dp', moves))  3.24 us
    ppermute x3, waiting for transfers between devices, shards(): lax.ppermute(final, 'space', [(i, i ^ k * PAIR) for i in range(space)])  2.95 us
    pallas_call x1, Pallas kernels, shards(): pl.pallas_call(chip_kernel, out_shape=(jax.ShapeDtypeStruct((3, chans, PL...  2.93 us
    pallas_call x2, Pallas kernels, place(): pl.pallas_call(functools.partial(place_kernel, flip), out_shape=jax.Shape...  2.81 us
  transfers between devices with their start and end apart: 15, of which 7 were waited for; matrix products, arithmetic and copies ran while one was open for 0% of the time, Pallas kernels for 21%

profile of v13, /device:TPU:0, one launch (start us, length us, event | category | flops | bytes accessed | tf_op | source)
XLA Modules:
  0.0 46.6 jit_solution(8223322044896184730)
XLA Ops:
  0.6 0.9 %dynamic-slice_bitcast_fusion = (bf16[1,320,128]{2,1,0:T(8,128)(2,1)S(1)}, bf16[1,320,128]{2,1,0:T(8,128)(2,1)S(1)}) fusion(bf16[1,8,128,320]{2,3,1,0:T(8,128)(2,1)} %param.3, s32[]{:T(128)S(6)} %select_n.7, bf16[1,8,128,320]{2,3,1,0:T(8,128)(2,1)} %param.4), kind=kLoop, calls=%fused_computation.8 | loop fusion | bytes 327684 | tf_op jit(solution)/shard_map/jit(dynamic_index_in_dim)/dynamic_slice | solution.py:222
  1.6 0.5 %collective-permute-start = (bf16[8,320,128]{2,1,0:T(8,128)(2,1)}, bf16[8,320,128]{2,1,0:T(8,128)(2,1)S(1)}, u32[]{:S(2)}, u32[]{:S(2)}) collective-permute-start(bf16[8,320,128]{2,1,0:T(8,128)(2,1)} %bitcast.32), channel_id=1, source_target_pairs={{0,1},{1,0},{2,3},{3,2},{4,5},{5,4},{6,7},{7,6},{8,9},{9,8},{10,11... | collective-permute-start | bytes 1966088 | tf_op jit(solution)/shard_map/ppermute | solution.py:232
  2.2 0.7 %collective-permute-start.2 = (bf16[2,320,128]{2,1,0:T(8,128)(2,1)S(1)}, bf16[2,320,128]{2,1,0:T(8,128)(2,1)S(1)}, u32[]{:S(2)}, u32[]{:S(2)}) collective-permute-start(bf16[2,320,128]{2,1,0:T(8,128)(2,1)S(1)} %pad_maximum_fusion.1.after_ref), channel_id=1, source_target_pairs={{1,2},{2,1},{3,4},{4,3},{5,6},{6,5},{9,10},{10,9},{11,12},{12,11},... | collective-permute-start | bytes 491528 | tf_op jit(solution)/shard_map/ppermute | solution.py:229
  3.0 1.1 %collective-permute-done.their_pre_ref = bf16[8,320,128]{2,1,0:T(8,128)(2,1)S(1)} collective-permute-done((bf16[8,320,128]{2,1,0:T(8,128)(2,1)}, bf16[8,320,128]{2,1,0:T(8,128)(2,1)S(1)}, u32[]{:S(2)}, u32[]{:S(2)}) %collective-permute-start) | collective-permute-done | bytes 655392 | tf_op jit(solution)/shard_map/ppermute | solution.py:232
  4.1 0.9 %collective-permute-done.1.their_grad_ref = bf16[8,320,128]{2,1,0:T(8,128)(2,1)S(1)} collective-permute-done((bf16[8,320,128]{2,1,0:T(8,128)(2,1)}, bf16[8,320,128]{2,1,0:T(8,128)(2,1)S(1)}, u32[]{:S(2)}, u32[]{:S(2)}) %collective-permute-start.1) | collective-permute-done | bytes 655392 | tf_op jit(solution)/shard_map/ppermute | solution.py:231
  5.0 2.9 %chip_terms.1 = (f32[3,320,512]{2,1,0:T(8,128)S(1)}, bf16[2,320,128]{2,1,0:T(8,128)(2,1)S(1)}, bf16[2,160,128]{2,1,0:T(8,128)(2,1)S(1)}) custom-call(bf16[8,320,128]{2,1,0:T(8,128)(2,1)S(1)} %bitcast.33, bf16[8,320,128]{2,1,0:T(8,128)(2,1)S(1)} %bitcast.39, bf16[8,320,128]{2,1,0:T(8,128)(2,1)S(1)} %collective-permute-done.their_pre_ref, ...), custom_call_target="tpu_custom_call" | custom-call | flops 3774873600 | bytes 4000000 | tf_op jit(solution)/shard_map/chip_terms/pallas_call | solution.py:264
  8.1 0.5 %edge_terms.1 = (f32[2,3,80,128]{3,2,1,0:T(8,128)S(1)}, bf16[2,3,80,128]{3,2,1,0:T(8,128)(2,1)S(1)}, bf16[2,3,80,128]{3,2,1,0:T(8,128)(2,1)S(1)}, bf16[2,3,80,12...) custom-call(f32[3,320,512]{2,1,0:T(8,128)S(1)} %get-tuple-element.53, ...), custom_call_target="tpu_custom_call" | custom-call | flops 235929600 | bytes 4000000 | tf_op jit(solution)/shard_map/edge_terms/pallas_call | solution.py:285
  8.7 3.0 %collective-permute-start.3 = (bf16[2,3,80,128]{3,2,1,0:T(8,128)(2,1)S(1)}, bf16[2,3,80,128]{3,2,1,0:T(8,128)(2,1)S(1)}, u32[]{:S(2)}, u32[]{:S(2)}) collective-permute-start(bf16[2,3,80,128]{3,2,1,0:T(8,128)(2,1)S(1)} %get-tuple-element.66), channel_id=1, source_target_pairs={{0,8},{1,9},{2,10},{3,11},{4,12},{5,13},{6,14},{7,15},{8,0},{9,1},... | collective-permute-start | bytes 368648 | tf_op jit(solution)/shard_map/ppermute | solution.py:309
  11.7 2.3 %collective-permute-start.4 = (bf16[2,3,80,128]{3,2,1,0:T(8,128)(2,1)S(1)}, bf16[2,3,80,128]{3,2,1,0:T(8,128)(2,1)S(1)}, u32[]{:S(2)}, u32[]{:S(2)}) collective-permute-start(bf16[2,3,80,128]{3,2,1,0:T(8,128)(2,1)S(1)} %get-tuple-element.67), channel_id=1, source_target_pairs={{0,2},{1,3},{2,0},{3,1},{4,6},{5,7},{6,4},{7,5},{8,10},{9,11},{10,... | collective-permute-start | bytes 368648 | tf_op jit(solution)/shard_map/ppermute | solution.py:309
  14.0 3.1 %collective-permute-start.5 = (bf16[2,3,80,128]{3,2,1,0:T(8,128)(2,1)S(1)}, bf16[2,3,80,128]{3,2,1,0:T(8,128)(2,1)S(1)}, u32[]{:S(2)}, u32[]{:S(2)}) collective-permute-start(bf16[2,3,80,128]{3,2,1,0:T(8,128)(2,1)S(1)} %get-tuple-element.70), channel_id=1, source_target_pairs={{0,4},{1,5},{2,6},{3,7},{4,0},{5,1},{6,2},{7,3},{8,12},{9,13},{10,... | collective-permute-start | bytes 368648 | tf_op jit(solution)/shard_map/ppermute | solution.py:309
  17.1 2.8 %collective-permute-start.7 = (bf16[2,3,80,128]{3,2,1,0:T(8,128)(2,1)S(1)}, bf16[2,3,80,128]{3,2,1,0:T(8,128)(2,1)S(1)}, u32[]{:S(2)}, u32[]{:S(2)}) collective-permute-start(bf16[2,3,80,128]{3,2,1,0:T(8,128)(2,1)S(1)} %get-tuple-element.72), channel_id=1, source_target_pairs={{0,6},{1,7},{2,4},{3,5},{4,2},{5,3},{6,0},{7,1},{8,14},{9,15},{10,... | collective-permute-start | bytes 368648 | tf_op jit(solution)/shard_map/ppermute | solution.py:309
  19.9 1.9 %collective-permute-start.8 = (bf16[2,3,80,128]{3,2,1,0:T(8,128)(2,1)S(1)}, bf16[2,3,80,128]{3,2,1,0:T(8,128)(2,1)S(1)}, u32[]{:S(2)}, u32[]{:S(2)}) collective-permute-start(bf16[2,3,80,128]{3,2,1,0:T(8,128)(2,1)S(1)} %get-tuple-element.73), channel_id=1, source_target_pairs={{0,10},{1,11},{2,8},{3,9},{4,14},{5,15},{6,12},{7,13},{8,2},{9,3},... | collective-permute-start | bytes 368648 | tf_op jit(solution)/shard_map/ppermute | solution.py:309
  21.8 2.6 %input_grad.6.refs_4_ = bf16[8,320,128]{2,1,0:T(8,128)(2,1)} custom-call(bf16[8,320,128]{2,1,0:T(8,128)(2,1)S(1)} %bitcast.36, bf16[8,320,128]{2,1,0:T(8,128)(2,1)S(1)} %bitcast.42, bf16[2,320,128]{2,1,0:T(8,128)(2,1)S(1)} %collective-permute-done.2.near_ref.refs_2_, bf16[3,3,320,320]{3,2,1,0:T(8,128)(2,1)S(1)} %copy-done, ...), custom_call_target="tpu_custom_call", output_to_operand_aliasing={{}: (4, {})} | custom-call | flops 943718400 | bytes 3000000 | tf_op jit(solution)/shard_map/input_grad/pallas_call | solution.py:245
  24.5 5.3 %collective-permute-done.7 = bf16[2,3,80,128]{3,2,1,0:T(8,128)(2,1)S(1)} collective-permute-done((bf16[2,3,80,128]{3,2,1,0:T(8,128)(2,1)S(1)}, bf16[2,3,80,128]{3,2,1,0:T(8,128)(2,1)S(1)}, u32[]{:S(2)}, u32[]{:S(2)}) %collective-permute-start.7) | collective-permute-done | bytes 122912 | tf_op jit(solution)/shard_map/ppermute | solution.py:309
  29.7 0.1 convert_add_fusion
  29.9 3.2 %collective-permute-start.10 = (bf16[3,80,128]{2,1,0:T(8,128)(2,1)S(1)}, bf16[3,80,128]{2,1,0:T(8,128)(2,1)S(1)}, u32[]{:S(2)}, u32[]{:S(2)}) collective-permute-start(bf16[3,80,128]{2,1,0:T(8,128)(2,1)S(1)} %fusion.3), channel_id=1, source_target_pairs={{0,16},{8,24},{16,0},{24,8},{1,17},{9,25},{17,1},{25,9},{2,18},{10... | collective-permute-start | bytes 184328 | tf_op jit(solution)/shard_map/ppermute | solution.py:320
  33.1 2.6 %input_grad.7 = bf16[8,320,128]{2,1,0:T(8,128)(2,1)} custom-call(bf16[8,320,128]{2,1,0:T(8,128)(2,1)S(1)} %bitcast.37, bf16[8,320,128]{2,1,0:T(8,128)(2,1)S(1)} %bitcast.43, bf16[1,320,128]{2,1,0:T(8,128)(2,1)S(1)} %constant_dynamic-slice_fusion.refs_2_, bf16[3,3,320,320]{3,2,1,0:T(8,128)(2,1)S(1)} %copy-done, ...), custom_call_target="tpu_custom_call", output_to_operand_aliasing={{}: (4, {})} | custom-call | flops 943718400 | bytes 3000000 | tf_op jit(solution)/shard_map/input_grad/pallas_call | solution.py:245
  35.7 1.3 %collective-permute-done.10 = bf16[3,80,128]{2,1,0:T(8,128)(2,1)S(1)} collective-permute-done((bf16[3,80,128]{2,1,0:T(8,128)(2,1)S(1)}, bf16[3,80,128]{2,1,0:T(8,128)(2,1)S(1)}, u32[]{:S(2)}, u32[]{:S(2)}) %collective-permute-start.10) | collective-permute-done | bytes 61472 | tf_op jit(solution)/shard_map/ppermute | solution.py:320
  37.0 2.2 %collective-permute-start.13 = (bf16[3,80,128]{2,1,0:T(8,128)(2,1)S(1)}, bf16[3,80,128]{2,1,0:T(8,128)(2,1)S(1)}, u32[]{:S(2)}, u32[]{:S(2)}) collective-permute-start(bf16[3,80,128]{2,1,0:T(8,128)(2,1)S(1)} %fusion.2), channel_id=1, source_target_pairs={{0,6},{1,7},{2,4},{3,5},{4,2},{5,3},{6,0},{7,1},{8,14},{9,15},{10,... | collective-permute-start | bytes 184328 | tf_op jit(solution)/shard_map/ppermute | solution.py:330
  39.3 1.3 %collective-permute-start.11 = (bf16[3,80,128]{2,1,0:T(8,128)(2,1)S(1)}, bf16[3,80,128]{2,1,0:T(8,128)(2,1)S(1)}, u32[]{:S(2)}, u32[]{:S(2)}) collective-permute-start(bf16[3,80,128]{2,1,0:T(8,128)(2,1)S(1)} %fusion.2), channel_id=1, source_target_pairs={{0,2},{1,3},{2,0},{3,1},{4,6},{5,7},{6,4},{7,5},{8,10},{9,11},{10,... | collective-permute-start | bytes 184328 | tf_op jit(solution)/shard_map/ppermute | solution.py:330
  40.6 1.7 %collective-permute-done.13 = bf16[3,80,128]{2,1,0:T(8,128)(2,1)S(1)} collective-permute-done((bf16[3,80,128]{2,1,0:T(8,128)(2,1)S(1)}, bf16[3,80,128]{2,1,0:T(8,128)(2,1)S(1)}, u32[]{:S(2)}, u32[]{:S(2)}) %collective-permute-start.13) | collective-permute-done | bytes 61472 | tf_op jit(solution)/shard_map/ppermute | solution.py:330
  42.3 1.3 %collective-permute-done.12 = bf16[3,80,128]{2,1,0:T(8,128)(2,1)S(1)} collective-permute-done((bf16[3,80,128]{2,1,0:T(8,128)(2,1)S(1)}, bf16[3,80,128]{2,1,0:T(8,128)(2,1)S(1)}, u32[]{:S(2)}, u32[]{:S(2)}) %collective-permute-start.12) | collective-permute-done | bytes 61472 | tf_op jit(solution)/shard_map/ppermute | solution.py:330
  43.7 1.4 %place_rows.2.refs_0_ = f32[320,720]{1,0:T(8,128)} custom-call(bf16[4,3,80,128]{3,2,1,0:T(8,128)(2,1)S(1)} %pad_maximum_fusion.parts_ref, f32[144,144]{1,0:T(8,128)S(1)} %pick_rows.1.pick_ref), custom_call_target="tpu_custom_call" | custom-call | flops 165888000 | bytes 1000000 | tf_op jit(solution)/shard_map/place_rows/pallas_call | solution.py:335
  45.2 1.4 %place_rows.3 = f32[320,720]{1,0:T(8,128)} custom-call(bf16[4,3,80,128]{3,2,1,0:T(8,128)(2,1)S(1)} %collective-permute-done.14.parts_ref, f32[144,144]{1,0:T(8,128)S(1)} %pick_rows.1.pick_ref, f32[320,720]{1,0:T(8,128)} %place_rows.2.refs_0_), custom_call_target="tpu_custom_call", output_to_operand_aliasing={{}: (2, {})} | custom-call | flops 165888000 | bytes 1000000 | tf_op jit(solution)/shard_map/place_rows/pallas_call | solution.py:335
  (28 shorter events, 0.6 us)
Async XLA Ops:
  1.6 3.4 %copy-start.1 = (bf16[1,8,128,320]{2,3,1,0:T(8,128)(2,1)S(1)}, bf16[1,8,128,320]{2,3,1,0:T(8,128)(2,1)}, u32[]{:S(2)}) copy-start(bf16[1,8,128,320]{2,3,1,0:T(8,128)(2,1)} %param.3) | copy-start | bytes 1966084
  1.6 3.4 %copy-start.2 = (bf16[1,8,128,320]{2,3,1,0:T(8,128)(2,1)S(1)}, bf16[1,8,128,320]{2,3,1,0:T(8,128)(2,1)}, u32[]{:S(2)}) copy-start(bf16[1,8,128,320]{2,3,1,0:T(8,128)(2,1)} %param.4) | copy-start | bytes 1966084
  1.6 2.5 %collective-permute-start = (bf16[8,320,128]{2,1,0:T(8,128)(2,1)}, bf16[8,320,128]{2,1,0:T(8,128)(2,1)S(1)}, u32[]{:S(2)}, u32[]{:S(2)}) collective-permute-start(bf16[8,320,128]{2,1,0:T(8,128)(2,1)} %bitcast.32), channel_id=1, source_target_pairs={{0,1},{1,0},{2,3},{3,2},{4,5},{5,4},{6,7},{7,6},{8,9},{9,8},{10,11... | collective-permute-start | bytes 1966088 | tf_op jit(solution)/shard_map/ppermute | solution.py:232
  2.2 2.9 %collective-permute-start.1 = (bf16[8,320,128]{2,1,0:T(8,128)(2,1)}, bf16[8,320,128]{2,1,0:T(8,128)(2,1)S(1)}, u32[]{:S(2)}, u32[]{:S(2)}) collective-permute-start(bf16[8,320,128]{2,1,0:T(8,128)(2,1)} %bitcast.38), channel_id=1, source_target_pairs={{0,1},{1,0},{2,3},{3,2},{4,5},{5,4},{6,7},{7,6},{8,9},{9,8},{10,11... | collective-permute-start | bytes 1966088 | tf_op jit(solution)/shard_map/ppermute | solution.py:231
  2.2 5.8 %collective-permute-start.2 = (bf16[2,320,128]{2,1,0:T(8,128)(2,1)S(1)}, bf16[2,320,128]{2,1,0:T(8,128)(2,1)S(1)}, u32[]{:S(2)}, u32[]{:S(2)}) collective-permute-start(bf16[2,320,128]{2,1,0:T(8,128)(2,1)S(1)} %pad_maximum_fusion.1.after_ref), channel_id=1, source_target_pairs={{1,2},{2,1},{3,4},{4,3},{5,6},{6,5},{9,10},{10,9},{11,12},{12,11},... | collective-permute-start | bytes 491528 | tf_op jit(solution)/shard_map/ppermute | solution.py:229
  3.0 5.0 %copy-start = (bf16[3,3,320,320]{3,2,1,0:T(8,128)(2,1)S(1)}, bf16[3,3,320,320]{3,2,1,0:T(8,128)(2,1)}, u32[]{:S(2)}) copy-start(bf16[3,3,320,320]{3,2,1,0:T(8,128)(2,1)} %refs_3_.7) | copy-start | bytes 5529604
  8.7 11.2 %collective-permute-start.3 = (bf16[2,3,80,128]{3,2,1,0:T(8,128)(2,1)S(1)}, bf16[2,3,80,128]{3,2,1,0:T(8,128)(2,1)S(1)}, u32[]{:S(2)}, u32[]{:S(2)}) collective-permute-start(bf16[2,3,80,128]{3,2,1,0:T(8,128)(2,1)S(1)} %get-tuple-element.66), channel_id=1, source_target_pairs={{0,8},{1,9},{2,10},{3,11},{4,12},{5,13},{6,14},{7,15},{8,0},{9,1},... | collective-permute-start | bytes 368648 | tf_op jit(solution)/shard_map/ppermute | solution.py:309
  11.7 10.2 %collective-permute-start.4 = (bf16[2,3,80,128]{3,2,1,0:T(8,128)(2,1)S(1)}, bf16[2,3,80,128]{3,2,1,0:T(8,128)(2,1)S(1)}, u32[]{:S(2)}, u32[]{:S(2)}) collective-permute-start(bf16[2,3,80,128]{3,2,1,0:T(8,128)(2,1)S(1)} %get-tuple-element.67), channel_id=1, source_target_pairs={{0,2},{1,3},{2,0},{3,1},{4,6},{5,7},{6,4},{7,5},{8,10},{9,11},{10,... | collective-permute-start | bytes 368648 | tf_op jit(solution)/shard_map/ppermute | solution.py:309
  14.0 10.4 %collective-permute-start.5 = (bf16[2,3,80,128]{3,2,1,0:T(8,128)(2,1)S(1)}, bf16[2,3,80,128]{3,2,1,0:T(8,128)(2,1)S(1)}, u32[]{:S(2)}, u32[]{:S(2)}) collective-permute-start(bf16[2,3,80,128]{3,2,1,0:T(8,128)(2,1)S(1)} %get-tuple-element.70), channel_id=1, source_target_pairs={{0,4},{1,5},{2,6},{3,7},{4,0},{5,1},{6,2},{7,3},{8,12},{9,13},{10,... | collective-permute-start | bytes 368648 | tf_op jit(solution)/shard_map/ppermute | solution.py:309
  17.1 7.4 %collective-permute-start.6 = (bf16[2,3,80,128]{3,2,1,0:T(8,128)(2,1)S(1)}, bf16[2,3,80,128]{3,2,1,0:T(8,128)(2,1)S(1)}, u32[]{:S(2)}, u32[]{:S(2)}) collective-permute-start(bf16[2,3,80,128]{3,2,1,0:T(8,128)(2,1)S(1)} %get-tuple-element.71), channel_id=1, source_target_pairs={{0,14},{1,15},{2,12},{3,13},{4,10},{5,11},{6,8},{7,9},{8,6},{9,7},... | collective-permute-start | bytes 368648 | tf_op jit(solution)/shard_map/ppermute | solution.py:309
  17.1 12.6 %collective-permute-start.7 = (bf16[2,3,80,128]{3,2,1,0:T(8,128)(2,1)S(1)}, bf16[2,3,80,128]{3,2,1,0:T(8,128)(2,1)S(1)}, u32[]{:S(2)}, u32[]{:S(2)}) collective-permute-start(bf16[2,3,80,128]{3,2,1,0:T(8,128)(2,1)S(1)} %get-tuple-element.72), channel_id=1, source_target_pairs={{0,6},{1,7},{2,4},{3,5},{4,2},{5,3},{6,0},{7,1},{8,14},{9,15},{10,... | collective-permute-start | bytes 368648 | tf_op jit(solution)/shard_map/ppermute | solution.py:309
  19.9 9.8 %collective-permute-start.8 = (bf16[2,3,80,128]{3,2,1,0:T(8,128)(2,1)S(1)}, bf16[2,3,80,128]{3,2,1,0:T(8,128)(2,1)S(1)}, u32[]{:S(2)}, u32[]{:S(2)}) collective-permute-start(bf16[2,3,80,128]{3,2,1,0:T(8,128)(2,1)S(1)} %get-tuple-element.73), channel_id=1, source_target_pairs={{0,10},{1,11},{2,8},{3,9},{4,14},{5,15},{6,12},{7,13},{8,2},{9,3},... | collective-permute-start | bytes 368648 | tf_op jit(solution)/shard_map/ppermute | solution.py:309
  21.8 7.9 %collective-permute-start.9 = (bf16[2,3,80,128]{3,2,1,0:T(8,128)(2,1)S(1)}, bf16[2,3,80,128]{3,2,1,0:T(8,128)(2,1)S(1)}, u32[]{:S(2)}, u32[]{:S(2)}) collective-permute-start(bf16[2,3,80,128]{3,2,1,0:T(8,128)(2,1)S(1)} %get-tuple-element.74), channel_id=1, source_target_pairs={{0,12},{1,13},{2,14},{3,15},{4,8},{5,9},{6,10},{7,11},{8,4},{9,5},... | collective-permute-start | bytes 368648 | tf_op jit(solution)/shard_map/ppermute | solution.py:309
  29.9 7.1 %collective-permute-start.10 = (bf16[3,80,128]{2,1,0:T(8,128)(2,1)S(1)}, bf16[3,80,128]{2,1,0:T(8,128)(2,1)S(1)}, u32[]{:S(2)}, u32[]{:S(2)}) collective-permute-start(bf16[3,80,128]{2,1,0:T(8,128)(2,1)S(1)} %fusion.3), channel_id=1, source_target_pairs={{0,16},{8,24},{16,0},{24,8},{1,17},{9,25},{17,1},{25,9},{2,18},{10... | collective-permute-start | bytes 184328 | tf_op jit(solution)/shard_map/ppermute | solution.py:320
  37.0 5.2 %collective-permute-start.13 = (bf16[3,80,128]{2,1,0:T(8,128)(2,1)S(1)}, bf16[3,80,128]{2,1,0:T(8,128)(2,1)S(1)}, u32[]{:S(2)}, u32[]{:S(2)}) collective-permute-start(bf16[3,80,128]{2,1,0:T(8,128)(2,1)S(1)} %fusion.2), channel_id=1, source_target_pairs={{0,6},{1,7},{2,4},{3,5},{4,2},{5,3},{6,0},{7,1},{8,14},{9,15},{10,... | collective-permute-start | bytes 184328 | tf_op jit(solution)/shard_map/ppermute | solution.py:330
  39.3 4.3 %collective-permute-start.12 = (bf16[3,80,128]{2,1,0:T(8,128)(2,1)S(1)}, bf16[3,80,128]{2,1,0:T(8,128)(2,1)S(1)}, u32[]{:S(2)}, u32[]{:S(2)}) collective-permute-start(bf16[3,80,128]{2,1,0:T(8,128)(2,1)S(1)} %fusion.2), channel_id=1, source_target_pairs={{0,4},{1,5},{2,6},{3,7},{4,0},{5,1},{6,2},{7,3},{8,12},{9,13},{10,... | collective-permute-start | bytes 184328 | tf_op jit(solution)/shard_map/ppermute | solution.py:330
  39.3 4.3 %collective-permute-start.11 = (bf16[3,80,128]{2,1,0:T(8,128)(2,1)S(1)}, bf16[3,80,128]{2,1,0:T(8,128)(2,1)S(1)}, u32[]{:S(2)}, u32[]{:S(2)}) collective-permute-start(bf16[3,80,128]{2,1,0:T(8,128)(2,1)S(1)} %fusion.2), channel_id=1, source_target_pairs={{0,2},{1,3},{2,0},{3,1},{4,6},{5,7},{6,4},{7,5},{8,10},{9,11},{10,... | collective-permute-start | bytes 184328 | tf_op jit(solution)/shard_map/ppermute | solution.py:330
  43.6 1.6 %collective-permute-start.14 = (bf16[4,3,80,128]{3,2,1,0:T(8,128)(2,1)S(1)}, bf16[4,3,80,128]{3,2,1,0:T(8,128)(2,1)S(1)}, u32[]{:S(2)}, u32[]{:S(2)}) collective-permute-start(bf16[4,3,80,128]{3,2,1,0:T(8,128)(2,1)S(1)} %pad_maximum_fusion.parts_ref), channel_id=1, source_target_pairs={{0,1},{1,0},{2,3},{3,2},{4,5},{5,4},{6,7},{7,6},{8,9},{9,8},{10,11... | collective-permute-start | bytes 737288 | tf_op jit(solution)/shard_map/ppermute | solution.py:332

commit v14 on v11

--- a/solution.py
+++ b/solution.py
@@ -171,9 +171,10 @@
     half = out_s.shape[0]
     width = pick_ref.shape[0]
     group = width // 9
-    for k in range(PLANE):
+    for slot in range(PLANE):
+        k = (PLANE - slot) % PLANE
         lanes = pl.ds(pl.multiple_of((plane_index() ^ k) * LANES, LANES), LANES)
-        wide_s[:, :, lanes] = parts_ref[k].astype(F32)
+        wide_s[:, :, lanes] = parts_ref[slot].astype(F32)
     pick = pick_ref[...].astype(BF16)
     for g in range(block // group):
         rows = [wide_s[t // 3, g * group : (g + 1) * group, t % 3 * half : (t % 3 + 1) * half] for t in range(9)]
@@ -310,9 +311,10 @@
     if outer > 1:
         total = lax.psum(total, "space", axis_index_groups=[[o * inner + i for o in range(outer)] for i in range(inner)])
     final = total.astype(BF16)
-    parts = [final]
-    for k in range(1, PLANE):
-        parts.append(lax.ppermute(final, "space", [(i, i ^ (k * PAIR)) for i in range(space)]))
+    spread = {}
+    for k in range(PLANE - 1, 0, -1):
+        spread[k] = lax.ppermute(final, "space", [(i, i ^ (k * PAIR)) for i in range(space)])
+    parts = [final] + [spread[k] for k in range(PLANE - 1, 0, -1)]
     parts = jnp.stack(parts)
     their_parts = lax.ppermute(parts, "space", pairs)
 

time: 45.7 us -> 46 us (level)
  no operation moved by 1% of the time
where the time goes in v14:
time: 46 us; the launch traced here: 45.8 us
  starting transfers between devices  20.8 us (45%)
  Pallas kernels  11.6 us (25%)
  waiting for transfers between devices  11.4 us (25%)
  local copies, waits for them, and re-layouts  0.98 us (2%)
  between operations  0.8 us (2%)
    ppermute x7, starting transfers between devices, shards(): got.append(lax.ppermute(terms[k], ('dp', 'space'), moves))  13.3 us
    pallas_call x2, Pallas kernels, input_part(): pl.pallas_call(functools.partial(input_kernel, side), out_shape=jax.Shape...  5.21 us
    ppermute x3, waiting for transfers between devices, shards(): lax.ppermute(final, 'space', [(i, i ^ k * PAIR) for i in range(space)])  4.08 us
    ppermute x3, starting transfers between devices, shards(): lax.ppermute(final, 'space', [(i, i ^ k * PAIR) for i in range(space)])  3.55 us
    pallas_call x1, Pallas kernels, shards(): pl.pallas_call(chip_kernel, out_shape=(jax.ShapeDtypeStruct((3, chans, PL...  2.93 us
    pallas_call x2, Pallas kernels, place(): pl.pallas_call(functools.partial(place_kernel, flip), out_shape=jax.Shape...  2.81 us
    ppermute x1, waiting for transfers between devices, shards(): others.append(lax.ppermute(near_sum[k].astype(BF16), 'dp', moves))  2.79 us
    ppermute x1, starting transfers between devices, shards(): others.append(lax.ppermute(near_sum[k].astype(BF16), 'dp', moves))  2.65 us
  transfers between devices with their start and end apart: 15, of which 9 were waited for; matrix products, arithmetic and copies ran while one was open for 0% of the time, Pallas kernels for 21%

profile of v14, /device:TPU:0, one launch (start us, length us, event | category | flops | bytes accessed | tf_op | source)
XLA Modules:
  0.0 45.8 jit_solution(14531425467086428770)
XLA Ops:
  0.6 0.9 %dynamic-slice_bitcast_fusion = (bf16[1,320,128]{2,1,0:T(8,128)(2,1)S(1)}, bf16[1,320,128]{2,1,0:T(8,128)(2,1)S(1)}) fusion(bf16[1,8,128,320]{2,3,1,0:T(8,128)(2,1)} %param.3, s32[]{:T(128)S(6)} %select_n.7, bf16[1,8,128,320]{2,3,1,0:T(8,128)(2,1)} %param.4), kind=kLoop, calls=%fused_computation.8 | loop fusion | bytes 327684 | tf_op jit(solution)/shard_map/jit(dynamic_index_in_dim)/dynamic_slice | solution.py:217
  2.2 0.7 %collective-permute-start.2 = (bf16[2,320,128]{2,1,0:T(8,128)(2,1)S(1)}, bf16[2,320,128]{2,1,0:T(8,128)(2,1)S(1)}, u32[]{:S(2)}, u32[]{:S(2)}) collective-permute-start(bf16[2,320,128]{2,1,0:T(8,128)(2,1)S(1)} %pad_maximum_fusion.1.after_ref), channel_id=1, source_target_pairs={{1,2},{2,1},{3,4},{4,3},{5,6},{6,5},{9,10},{10,9},{11,12},{12,11},... | collective-permute-start | bytes 491528 | tf_op jit(solution)/shard_map/ppermute | solution.py:224
  3.0 1.1 %collective-permute-done.their_pre_ref = bf16[8,320,128]{2,1,0:T(8,128)(2,1)S(1)} collective-permute-done((bf16[8,320,128]{2,1,0:T(8,128)(2,1)}, bf16[8,320,128]{2,1,0:T(8,128)(2,1)S(1)}, u32[]{:S(2)}, u32[]{:S(2)}) %collective-permute-start) | collective-permute-done | bytes 655392 | tf_op jit(solution)/shard_map/ppermute | solution.py:227
  4.1 0.9 %collective-permute-done.1.their_grad_ref = bf16[8,320,128]{2,1,0:T(8,128)(2,1)S(1)} collective-permute-done((bf16[8,320,128]{2,1,0:T(8,128)(2,1)}, bf16[8,320,128]{2,1,0:T(8,128)(2,1)S(1)}, u32[]{:S(2)}, u32[]{:S(2)}) %collective-permute-start.1) | collective-permute-done | bytes 655392 | tf_op jit(solution)/shard_map/ppermute | solution.py:226
  5.0 2.9 %chip_terms.1 = (f32[3,320,512]{2,1,0:T(8,128)S(1)}, bf16[2,320,128]{2,1,0:T(8,128)(2,1)S(1)}, bf16[2,160,128]{2,1,0:T(8,128)(2,1)S(1)}) custom-call(bf16[8,320,128]{2,1,0:T(8,128)(2,1)S(1)} %bitcast.33, bf16[8,320,128]{2,1,0:T(8,128)(2,1)S(1)} %bitcast.37, bf16[8,320,128]{2,1,0:T(8,128)(2,1)S(1)} %collective-permute-done.their_pre_ref, ...), custom_call_target="tpu_custom_call" | custom-call | flops 3774873600 | bytes 4000000 | tf_op jit(solution)/shard_map/chip_terms/pallas_call | solution.py:259
  8.0 0.5 %edge_terms.1 = (f32[2,3,80,128]{3,2,1,0:T(8,128)S(1)}, bf16[2,3,80,128]{3,2,1,0:T(8,128)(2,1)S(1)}, bf16[2,3,80,128]{3,2,1,0:T(8,128)(2,1)S(1)}, bf16[2,3,80,12...) custom-call(f32[3,320,512]{2,1,0:T(8,128)S(1)} %get-tuple-element.35, ...), custom_call_target="tpu_custom_call" | custom-call | flops 235929600 | bytes 4000000 | tf_op jit(solution)/shard_map/edge_terms/pallas_call | solution.py:276
  8.5 3.0 %collective-permute-start.3 = (bf16[2,3,80,128]{3,2,1,0:T(8,128)(2,1)S(1)}, bf16[2,3,80,128]{3,2,1,0:T(8,128)(2,1)S(1)}, u32[]{:S(2)}, u32[]{:S(2)}) collective-permute-start(bf16[2,3,80,128]{3,2,1,0:T(8,128)(2,1)S(1)} %get-tuple-element.39), channel_id=1, source_target_pairs={{0,8},{1,9},{2,10},{3,11},{4,12},{5,13},{6,14},{7,15},{8,0},{9,1},... | collective-permute-start | bytes 368648 | tf_op jit(solution)/shard_map/ppermute | solution.py:297
  11.6 2.4 %collective-permute-start.4 = (bf16[2,3,80,128]{3,2,1,0:T(8,128)(2,1)S(1)}, bf16[2,3,80,128]{3,2,1,0:T(8,128)(2,1)S(1)}, u32[]{:S(2)}, u32[]{:S(2)}) collective-permute-start(bf16[2,3,80,128]{3,2,1,0:T(8,128)(2,1)S(1)} %get-tuple-element.40), channel_id=1, source_target_pairs={{0,2},{1,3},{2,0},{3,1},{4,6},{5,7},{6,4},{7,5},{8,10},{9,11},{10,... | collective-permute-start | bytes 368648 | tf_op jit(solution)/shard_map/ppermute | solution.py:297
  14.0 3.1 %collective-permute-start.5 = (bf16[2,3,80,128]{3,2,1,0:T(8,128)(2,1)S(1)}, bf16[2,3,80,128]{3,2,1,0:T(8,128)(2,1)S(1)}, u32[]{:S(2)}, u32[]{:S(2)}) collective-permute-start(bf16[2,3,80,128]{3,2,1,0:T(8,128)(2,1)S(1)} %get-tuple-element.43), channel_id=1, source_target_pairs={{0,4},{1,5},{2,6},{3,7},{4,0},{5,1},{6,2},{7,3},{8,12},{9,13},{10,... | collective-permute-start | bytes 368648 | tf_op jit(solution)/shard_map/ppermute | solution.py:297
  17.1 2.8 %collective-permute-start.7 = (bf16[2,3,80,128]{3,2,1,0:T(8,128)(2,1)S(1)}, bf16[2,3,80,128]{3,2,1,0:T(8,128)(2,1)S(1)}, u32[]{:S(2)}, u32[]{:S(2)}) collective-permute-start(bf16[2,3,80,128]{3,2,1,0:T(8,128)(2,1)S(1)} %get-tuple-element.45), channel_id=1, source_target_pairs={{0,6},{1,7},{2,4},{3,5},{4,2},{5,3},{6,0},{7,1},{8,14},{9,15},{10,... | collective-permute-start | bytes 368648 | tf_op jit(solution)/shard_map/ppermute | solution.py:297
  19.9 2.0 %collective-permute-start.8 = (bf16[2,3,80,128]{3,2,1,0:T(8,128)(2,1)S(1)}, bf16[2,3,80,128]{3,2,1,0:T(8,128)(2,1)S(1)}, u32[]{:S(2)}, u32[]{:S(2)}) collective-permute-start(bf16[2,3,80,128]{3,2,1,0:T(8,128)(2,1)S(1)} %get-tuple-element.46), channel_id=1, source_target_pairs={{0,10},{1,11},{2,8},{3,9},{4,14},{5,15},{6,12},{7,13},{8,2},{9,3},... | collective-permute-start | bytes 368648 | tf_op jit(solution)/shard_map/ppermute | solution.py:297
  21.9 2.6 %input_grad.2.refs_0_ = bf16[8,320,128]{2,1,0:T(8,128)(2,1)} custom-call(bf16[8,320,128]{2,1,0:T(8,128)(2,1)S(1)} %bitcast.34, bf16[8,320,128]{2,1,0:T(8,128)(2,1)S(1)} %bitcast.38, bf16[2,320,128]{2,1,0:T(8,128)(2,1)S(1)} %collective-permute-done.2.near_ref.edge_ref, bf16[3,3,320,320]{3,2,1,0:T(8,128)(2,1)S(1)} %copy-done), custom_call_target="tpu_custom_call" | custom-call | flops 943718400 | bytes 3000000 | tf_op jit(solution)/shard_map/input_grad/pallas_call | solution.py:240
  24.5 2.6 %input_grad.3 = bf16[8,320,128]{2,1,0:T(8,128)(2,1)} custom-call(bf16[8,320,128]{2,1,0:T(8,128)(2,1)S(1)} %bitcast.35, bf16[8,320,128]{2,1,0:T(8,128)(2,1)S(1)} %bitcast.39, bf16[1,320,128]{2,1,0:T(8,128)(2,1)S(1)} %constant_dynamic-slice_fusion.edge_ref, bf16[3,3,320,320]{3,2,1,0:T(8,128)(2,1)S(1)} %copy-done, ...), custom_call_target="tpu_custom_call", output_to_operand_aliasing={{}: (4, {})} | custom-call | flops 943718400 | bytes 3000000 | tf_op jit(solution)/shard_map/input_grad/pallas_call | solution.py:240
  27.1 2.2 %collective-permute-done.7 = bf16[2,3,80,128]{3,2,1,0:T(8,128)(2,1)S(1)} collective-permute-done((bf16[2,3,80,128]{3,2,1,0:T(8,128)(2,1)S(1)}, bf16[2,3,80,128]{3,2,1,0:T(8,128)(2,1)S(1)}, u32[]{:S(2)}, u32[]{:S(2)}) %collective-permute-start.7) | collective-permute-done | bytes 122912 | tf_op jit(solution)/shard_map/ppermute | solution.py:297
  29.7 2.7 %collective-permute-start.10 = (bf16[3,80,128]{2,1,0:T(8,128)(2,1)S(1)}, bf16[3,80,128]{2,1,0:T(8,128)(2,1)S(1)}, u32[]{:S(2)}, u32[]{:S(2)}) collective-permute-start(bf16[3,80,128]{2,1,0:T(8,128)(2,1)S(1)} %fusion.3), channel_id=1, source_target_pairs={{0,16},{8,24},{16,0},{24,8},{1,17},{9,25},{17,1},{25,9},{2,18},{10... | collective-permute-start | bytes 184328 | tf_op jit(solution)/shard_map/ppermute | solution.py:308
  32.4 2.8 %collective-permute-done.10 = bf16[3,80,128]{2,1,0:T(8,128)(2,1)S(1)} collective-permute-done((bf16[3,80,128]{2,1,0:T(8,128)(2,1)S(1)}, bf16[3,80,128]{2,1,0:T(8,128)(2,1)S(1)}, u32[]{:S(2)}, u32[]{:S(2)}) %collective-permute-start.10) | collective-permute-done | bytes 61472 | tf_op jit(solution)/shard_map/ppermute | solution.py:308
  35.2 1.6 %collective-permute-start.13 = (bf16[3,80,128]{2,1,0:T(8,128)(2,1)S(1)}, bf16[3,80,128]{2,1,0:T(8,128)(2,1)S(1)}, u32[]{:S(2)}, u32[]{:S(2)}) collective-permute-start(bf16[3,80,128]{2,1,0:T(8,128)(2,1)S(1)} %fusion.2), channel_id=1, source_target_pairs={{0,2},{1,3},{2,0},{3,1},{4,6},{5,7},{6,4},{7,5},{8,10},{9,11},{10,... | collective-permute-start | bytes 184328 | tf_op jit(solution)/shard_map/ppermute | solution.py:316
  36.8 0.9 %collective-permute-start.12 = (bf16[3,80,128]{2,1,0:T(8,128)(2,1)S(1)}, bf16[3,80,128]{2,1,0:T(8,128)(2,1)S(1)}, u32[]{:S(2)}, u32[]{:S(2)}) collective-permute-start(bf16[3,80,128]{2,1,0:T(8,128)(2,1)S(1)} %fusion.2), channel_id=1, source_target_pairs={{0,4},{1,5},{2,6},{3,7},{4,0},{5,1},{6,2},{7,3},{8,12},{9,13},{10,... | collective-permute-start | bytes 184328 | tf_op jit(solution)/shard_map/ppermute | solution.py:316
  37.7 1.0 %collective-permute-start.11 = (bf16[3,80,128]{2,1,0:T(8,128)(2,1)S(1)}, bf16[3,80,128]{2,1,0:T(8,128)(2,1)S(1)}, u32[]{:S(2)}, u32[]{:S(2)}) collective-permute-start(bf16[3,80,128]{2,1,0:T(8,128)(2,1)S(1)} %fusion.2), channel_id=1, source_target_pairs={{0,6},{1,7},{2,4},{3,5},{4,2},{5,3},{6,0},{7,1},{8,14},{9,15},{10,... | collective-permute-start | bytes 184328 | tf_op jit(solution)/shard_map/ppermute | solution.py:316
  38.8 0.7 %collective-permute-done.13 = bf16[3,80,128]{2,1,0:T(8,128)(2,1)S(1)} collective-permute-done((bf16[3,80,128]{2,1,0:T(8,128)(2,1)S(1)}, bf16[3,80,128]{2,1,0:T(8,128)(2,1)S(1)}, u32[]{:S(2)}, u32[]{:S(2)}) %collective-permute-start.13) | collective-permute-done | bytes 61472 | tf_op jit(solution)/shard_map/ppermute | solution.py:316
  39.5 1.5 %collective-permute-done.12 = bf16[3,80,128]{2,1,0:T(8,128)(2,1)S(1)} collective-permute-done((bf16[3,80,128]{2,1,0:T(8,128)(2,1)S(1)}, bf16[3,80,128]{2,1,0:T(8,128)(2,1)S(1)}, u32[]{:S(2)}, u32[]{:S(2)}) %collective-permute-start.12) | collective-permute-done | bytes 61472 | tf_op jit(solution)/shard_map/ppermute | solution.py:316
  41.0 1.8 %collective-permute-done.11 = bf16[3,80,128]{2,1,0:T(8,128)(2,1)S(1)} collective-permute-done((bf16[3,80,128]{2,1,0:T(8,128)(2,1)S(1)}, bf16[3,80,128]{2,1,0:T(8,128)(2,1)S(1)}, u32[]{:S(2)}, u32[]{:S(2)}) %collective-permute-start.11) | collective-permute-done | bytes 61472 | tf_op jit(solution)/shard_map/ppermute | solution.py:316
  42.9 1.4 %place_rows.2.refs_0_ = f32[320,720]{1,0:T(8,128)} custom-call(bf16[4,3,80,128]{3,2,1,0:T(8,128)(2,1)S(1)} %pad_maximum_fusion.parts_ref, f32[144,144]{1,0:T(8,128)S(1)} %pick_rows.1.pick_ref), custom_call_target="tpu_custom_call" | custom-call | flops 165888000 | bytes 1000000 | tf_op jit(solution)/shard_map/place_rows/pallas_call | solution.py:322
  44.4 1.4 %place_rows.3 = f32[320,720]{1,0:T(8,128)} custom-call(bf16[4,3,80,128]{3,2,1,0:T(8,128)(2,1)S(1)} %collective-permute-done.14.parts_ref, f32[144,144]{1,0:T(8,128)S(1)} %pick_rows.1.pick_ref, f32[320,720]{1,0:T(8,128)} %place_rows.2.refs_0_), custom_call_target="tpu_custom_call", output_to_operand_aliasing={{}: (2, {})} | custom-call | flops 165888000 | bytes 1000000 | tf_op jit(solution)/shard_map/place_rows/pallas_call | solution.py:322
  (26 shorter events, 1.4 us)
Async XLA Ops:
  1.6 3.4 %copy-start.1 = (bf16[1,8,128,320]{2,3,1,0:T(8,128)(2,1)S(1)}, bf16[1,8,128,320]{2,3,1,0:T(8,128)(2,1)}, u32[]{:S(2)}) copy-start(bf16[1,8,128,320]{2,3,1,0:T(8,128)(2,1)} %param.3) | copy-start | bytes 1966084
  1.6 3.4 %copy-start.2 = (bf16[1,8,128,320]{2,3,1,0:T(8,128)(2,1)S(1)}, bf16[1,8,128,320]{2,3,1,0:T(8,128)(2,1)}, u32[]{:S(2)}) copy-start(bf16[1,8,128,320]{2,3,1,0:T(8,128)(2,1)} %param.4) | copy-start | bytes 1966084
  1.6 2.5 %collective-permute-start = (bf16[8,320,128]{2,1,0:T(8,128)(2,1)}, bf16[8,320,128]{2,1,0:T(8,128)(2,1)S(1)}, u32[]{:S(2)}, u32[]{:S(2)}) collective-permute-start(bf16[8,320,128]{2,1,0:T(8,128)(2,1)} %bitcast.32), channel_id=1, source_target_pairs={{0,1},{1,0},{2,3},{3,2},{4,5},{5,4},{6,7},{7,6},{8,9},{9,8},{10,11... | collective-permute-start | bytes 1966088 | tf_op jit(solution)/shard_map/ppermute | solution.py:227
  2.2 2.9 %collective-permute-start.1 = (bf16[8,320,128]{2,1,0:T(8,128)(2,1)}, bf16[8,320,128]{2,1,0:T(8,128)(2,1)S(1)}, u32[]{:S(2)}, u32[]{:S(2)}) collective-permute-start(bf16[8,320,128]{2,1,0:T(8,128)(2,1)} %bitcast.36), channel_id=1, source_target_pairs={{0,1},{1,0},{2,3},{3,2},{4,5},{5,4},{6,7},{7,6},{8,9},{9,8},{10,11... | collective-permute-start | bytes 1966088 | tf_op jit(solution)/shard_map/ppermute | solution.py:226
  2.2 5.8 %collective-permute-start.2 = (bf16[2,320,128]{2,1,0:T(8,128)(2,1)S(1)}, bf16[2,320,128]{2,1,0:T(8,128)(2,1)S(1)}, u32[]{:S(2)}, u32[]{:S(2)}) collective-permute-start(bf16[2,320,128]{2,1,0:T(8,128)(2,1)S(1)} %pad_maximum_fusion.1.after_ref), channel_id=1, source_target_pairs={{1,2},{2,1},{3,4},{4,3},{5,6},{6,5},{9,10},{10,9},{11,12},{12,11},... | collective-permute-start | bytes 491528 | tf_op jit(solution)/shard_map/ppermute | solution.py:224
  8.0 13.9 %copy-start = (bf16[3,3,320,320]{3,2,1,0:T(8,128)(2,1)S(1)}, bf16[3,3,320,320]{3,2,1,0:T(8,128)(2,1)}, u32[]{:S(2)}) copy-start(bf16[3,3,320,320]{3,2,1,0:T(8,128)(2,1)} %kernel_ref.3) | copy-start | bytes 5529604
  8.5 11.3 %collective-permute-start.3 = (bf16[2,3,80,128]{3,2,1,0:T(8,128)(2,1)S(1)}, bf16[2,3,80,128]{3,2,1,0:T(8,128)(2,1)S(1)}, u32[]{:S(2)}, u32[]{:S(2)}) collective-permute-start(bf16[2,3,80,128]{3,2,1,0:T(8,128)(2,1)S(1)} %get-tuple-element.39), channel_id=1, source_target_pairs={{0,8},{1,9},{2,10},{3,11},{4,12},{5,13},{6,14},{7,15},{8,0},{9,1},... | collective-permute-start | bytes 368648 | tf_op jit(solution)/shard_map/ppermute | solution.py:297
  11.6 10.3 %collective-permute-start.4 = (bf16[2,3,80,128]{3,2,1,0:T(8,128)(2,1)S(1)}, bf16[2,3,80,128]{3,2,1,0:T(8,128)(2,1)S(1)}, u32[]{:S(2)}, u32[]{:S(2)}) collective-permute-start(bf16[2,3,80,128]{3,2,1,0:T(8,128)(2,1)S(1)} %get-tuple-element.40), channel_id=1, source_target_pairs={{0,2},{1,3},{2,0},{3,1},{4,6},{5,7},{6,4},{7,5},{8,10},{9,11},{10,... | collective-permute-start | bytes 368648 | tf_op jit(solution)/shard_map/ppermute | solution.py:297
  14.0 13.2 %collective-permute-start.5 = (bf16[2,3,80,128]{3,2,1,0:T(8,128)(2,1)S(1)}, bf16[2,3,80,128]{3,2,1,0:T(8,128)(2,1)S(1)}, u32[]{:S(2)}, u32[]{:S(2)}) collective-permute-start(bf16[2,3,80,128]{3,2,1,0:T(8,128)(2,1)S(1)} %get-tuple-element.43), channel_id=1, source_target_pairs={{0,4},{1,5},{2,6},{3,7},{4,0},{5,1},{6,2},{7,3},{8,12},{9,13},{10,... | collective-permute-start | bytes 368648 | tf_op jit(solution)/shard_map/ppermute | solution.py:297
  17.0 10.1 %collective-permute-start.6 = (bf16[2,3,80,128]{3,2,1,0:T(8,128)(2,1)S(1)}, bf16[2,3,80,128]{3,2,1,0:T(8,128)(2,1)S(1)}, u32[]{:S(2)}, u32[]{:S(2)}) collective-permute-start(bf16[2,3,80,128]{3,2,1,0:T(8,128)(2,1)S(1)} %get-tuple-element.44), channel_id=1, source_target_pairs={{0,14},{1,15},{2,12},{3,13},{4,10},{5,11},{6,8},{7,9},{8,6},{9,7},... | collective-permute-start | bytes 368648 | tf_op jit(solution)/shard_map/ppermute | solution.py:297
  17.1 12.3 %collective-permute-start.7 = (bf16[2,3,80,128]{3,2,1,0:T(8,128)(2,1)S(1)}, bf16[2,3,80,128]{3,2,1,0:T(8,128)(2,1)S(1)}, u32[]{:S(2)}, u32[]{:S(2)}) collective-permute-start(bf16[2,3,80,128]{3,2,1,0:T(8,128)(2,1)S(1)} %get-tuple-element.45), channel_id=1, source_target_pairs={{0,6},{1,7},{2,4},{3,5},{4,2},{5,3},{6,0},{7,1},{8,14},{9,15},{10,... | collective-permute-start | bytes 368648 | tf_op jit(solution)/shard_map/ppermute | solution.py:297
  19.9 9.5 %collective-permute-start.8 = (bf16[2,3,80,128]{3,2,1,0:T(8,128)(2,1)S(1)}, bf16[2,3,80,128]{3,2,1,0:T(8,128)(2,1)S(1)}, u32[]{:S(2)}, u32[]{:S(2)}) collective-permute-start(bf16[2,3,80,128]{3,2,1,0:T(8,128)(2,1)S(1)} %get-tuple-element.46), channel_id=1, source_target_pairs={{0,10},{1,11},{2,8},{3,9},{4,14},{5,15},{6,12},{7,13},{8,2},{9,3},... | collective-permute-start | bytes 368648 | tf_op jit(solution)/shard_map/ppermute | solution.py:297
  21.9 7.7 %collective-permute-start.9 = (bf16[2,3,80,128]{3,2,1,0:T(8,128)(2,1)S(1)}, bf16[2,3,80,128]{3,2,1,0:T(8,128)(2,1)S(1)}, u32[]{:S(2)}, u32[]{:S(2)}) collective-permute-start(bf16[2,3,80,128]{3,2,1,0:T(8,128)(2,1)S(1)} %get-tuple-element.47), channel_id=1, source_target_pairs={{0,12},{1,13},{2,14},{3,15},{4,8},{5,9},{6,10},{7,11},{8,4},{9,5},... | collective-permute-start | bytes 368648 | tf_op jit(solution)/shard_map/ppermute | solution.py:297
  29.7 5.4 %collective-permute-start.10 = (bf16[3,80,128]{2,1,0:T(8,128)(2,1)S(1)}, bf16[3,80,128]{2,1,0:T(8,128)(2,1)S(1)}, u32[]{:S(2)}, u32[]{:S(2)}) collective-permute-start(bf16[3,80,128]{2,1,0:T(8,128)(2,1)S(1)} %fusion.3), channel_id=1, source_target_pairs={{0,16},{8,24},{16,0},{24,8},{1,17},{9,25},{17,1},{25,9},{2,18},{10... | collective-permute-start | bytes 184328 | tf_op jit(solution)/shard_map/ppermute | solution.py:308
  35.2 4.3 %collective-permute-start.13 = (bf16[3,80,128]{2,1,0:T(8,128)(2,1)S(1)}, bf16[3,80,128]{2,1,0:T(8,128)(2,1)S(1)}, u32[]{:S(2)}, u32[]{:S(2)}) collective-permute-start(bf16[3,80,128]{2,1,0:T(8,128)(2,1)S(1)} %fusion.2), channel_id=1, source_target_pairs={{0,2},{1,3},{2,0},{3,1},{4,6},{5,7},{6,4},{7,5},{8,10},{9,11},{10,... | collective-permute-start | bytes 184328 | tf_op jit(solution)/shard_map/ppermute | solution.py:316
  36.8 4.2 %collective-permute-start.12 = (bf16[3,80,128]{2,1,0:T(8,128)(2,1)S(1)}, bf16[3,80,128]{2,1,0:T(8,128)(2,1)S(1)}, u32[]{:S(2)}, u32[]{:S(2)}) collective-permute-start(bf16[3,80,128]{2,1,0:T(8,128)(2,1)S(1)} %fusion.2), channel_id=1, source_target_pairs={{0,4},{1,5},{2,6},{3,7},{4,0},{5,1},{6,2},{7,3},{8,12},{9,13},{10,... | collective-permute-start | bytes 184328 | tf_op jit(solution)/shard_map/ppermute | solution.py:316
  37.7 5.1 %collective-permute-start.11 = (bf16[3,80,128]{2,1,0:T(8,128)(2,1)S(1)}, bf16[3,80,128]{2,1,0:T(8,128)(2,1)S(1)}, u32[]{:S(2)}, u32[]{:S(2)}) collective-permute-start(bf16[3,80,128]{2,1,0:T(8,128)(2,1)S(1)} %fusion.2), channel_id=1, source_target_pairs={{0,6},{1,7},{2,4},{3,5},{4,2},{5,3},{6,0},{7,1},{8,14},{9,15},{10,... | collective-permute-start | bytes 184328 | tf_op jit(solution)/shard_map/ppermute | solution.py:316
  42.9 1.6 %collective-permute-start.14 = (bf16[4,3,80,128]{3,2,1,0:T(8,128)(2,1)S(1)}, bf16[4,3,80,128]{3,2,1,0:T(8,128)(2,1)S(1)}, u32[]{:S(2)}, u32[]{:S(2)}) collective-permute-start(bf16[4,3,80,128]{3,2,1,0:T(8,128)(2,1)S(1)} %pad_maximum_fusion.parts_ref), channel_id=1, source_target_pairs={{0,1},{1,0},{2,3},{3,2},{4,5},{5,4},{6,7},{7,6},{8,9},{9,8},{10,11... | collective-permute-start | bytes 737288 | tf_op jit(solution)/shard_map/ppermute | solution.py:319

commit v15 on v8

--- a/solution.py
+++ b/solution.py
@@ -313,7 +313,7 @@
     )(term, act_edge, grad_edge, near_row)
 
     got = [terms[0]]
-    for k in (4, 6, 1, 7, 5, 3, 2):
+    for k in (4, 1, 2, 7, 3, 5, 6):
         moves = []
         for z in range(blocks):
             for i in range(space):

time: 45.4 us -> 46.1 us (1.015)
  waiting for transfers between devices: 8.84 us -> 9.81 us
    ppermute x3, waiting for transfers between devices: 2.2 us -> 4.07 us  [shards(): lax.ppermute(final, 'space', [(i, i ^ k * PAIR) for i in range(space)])]
    ppermute x1, waiting for transfers between devices: 3.57 us -> 2.8 us  [shards(): others.append(lax.ppermute(near_sum[k].astype(BF16), 'dp', moves))]
where the time goes in v15:
time: 46.1 us; the launch traced here: 45.9 us
  starting transfers between devices  22.1 us (48%)
  Pallas kernels  12 us (26%)
  waiting for transfers between devices  9.81 us (21%)
  local copies, waits for them, and re-layouts  0.98 us (2%)
  between operations  0.83 us (2%)
    ppermute x7, starting transfers between devices, shards(): got.append(lax.ppermute(terms[k], ('dp', 'space'), moves))  14.6 us
    pallas_call x2, Pallas kernels, input_part(): pl.pallas_call(functools.partial(input_kernel, side), out_shape=jax.Shape...  5.21 us
    ppermute x3, waiting for transfers between devices, shards(): lax.ppermute(final, 'space', [(i, i ^ k * PAIR) for i in range(space)])  4.07 us
    ppermute x3, starting transfers between devices, shards(): lax.ppermute(final, 'space', [(i, i ^ k * PAIR) for i in range(space)])  3.55 us
    pallas_call x2, Pallas kernels, place(): pl.pallas_call(functools.partial(place_kernel, flip), out_shape=jax.Shape...  2.94 us
    ppermute x1, waiting for transfers between devices, shards(): others.append(lax.ppermute(near_sum[k].astype(BF16), 'dp', moves))  2.8 us
    ppermute x1, starting transfers between devices, shards(): others.append(lax.ppermute(near_sum[k].astype(BF16), 'dp', moves))  2.65 us
    ppermute x7, waiting for transfers between devices, shards(): got.append(lax.ppermute(terms[k], ('dp', 'space'), moves))  2.46 us
  transfers between devices with their start and end apart: 15, of which 7 were waited for; matrix products, arithmetic and copies ran while one was open for 0% of the time, Pallas kernels for 22%

profile of v15, /device:TPU:0, one launch (start us, length us, event | category | flops | bytes accessed | tf_op | source)
XLA Modules:
  0.0 45.9 jit_solution(10079568673828737702)
XLA Ops:
  0.6 0.9 %dynamic-slice_bitcast_fusion = (bf16[1,320,128]{2,1,0:T(8,128)(2,1)S(1)}, bf16[1,320,128]{2,1,0:T(8,128)(2,1)S(1)}) fusion(bf16[1,8,128,320]{2,3,1,0:T(8,128)(2,1)} %param.3, s32[]{:T(128)S(6)} %select_n.7, bf16[1,8,128,320]{2,3,1,0:T(8,128)(2,1)} %param.4), kind=kLoop, calls=%fused_computation.8 | loop fusion | bytes 327684 | tf_op jit(solution)/shard_map/jit(dynamic_index_in_dim)/dynamic_slice | solution.py:228
  1.6 0.5 %collective-permute-start = (bf16[8,320,128]{2,1,0:T(8,128)(2,1)}, bf16[8,320,128]{2,1,0:T(8,128)(2,1)S(1)}, u32[]{:S(2)}, u32[]{:S(2)}) collective-permute-start(bf16[8,320,128]{2,1,0:T(8,128)(2,1)} %bitcast.32), channel_id=1, source_target_pairs={{0,1},{1,0},{2,3},{3,2},{4,5},{5,4},{6,7},{7,6},{8,9},{9,8},{10,11... | collective-permute-start | bytes 1966088 | tf_op jit(solution)/shard_map/ppermute | solution.py:238
  2.2 0.7 %collective-permute-start.2 = (bf16[2,320,128]{2,1,0:T(8,128)(2,1)S(1)}, bf16[2,320,128]{2,1,0:T(8,128)(2,1)S(1)}, u32[]{:S(2)}, u32[]{:S(2)}) collective-permute-start(bf16[2,320,128]{2,1,0:T(8,128)(2,1)S(1)} %pad_maximum_fusion.1.after_ref), channel_id=1, source_target_pairs={{1,2},{2,1},{3,4},{4,3},{5,6},{6,5},{9,10},{10,9},{11,12},{12,11},... | collective-permute-start | bytes 491528 | tf_op jit(solution)/shard_map/ppermute | solution.py:235
  3.0 1.5 %own_terms.1 = (f32[3,320,512]{2,1,0:T(8,128)S(1)}, bf16[2,320,128]{2,1,0:T(8,128)(2,1)S(1)}, bf16[2,160,128]{2,1,0:T(8,128)(2,1)S(1)}) custom-call(bf16[8,320,128]{2,1,0:T(8,128)(2,1)S(1)} %bitcast.33, bf16[8,320,128]{2,1,0:T(8,128)(2,1)S(1)} %bitcast.37), custom_call_target="tpu_custom_call" | custom-call | flops 1887436800 | bytes 4000000 | tf_op jit(solution)/shard_map/own_terms/pallas_call | solution.py:249
  5.0 1.7 %pair_terms.1.term_ref = f32[3,320,512]{2,1,0:T(8,128)S(1)} custom-call(f32[3,320,512]{2,1,0:T(8,128)S(1)} %get-tuple-element.33.term_ref, bf16[2,320,128]{2,1,0:T(8,128)(2,1)S(1)} %get-tuple-element.34.act_edge_ref, bf16[2,160,128]{2,1,0:T(8,128)(2,1)S(1)} %get-tuple-element.35.grad_edge_ref, bf16[8,320,128]{2,1,0:T(8,128)(2,1)S(1)} %collective-permute-done.their_pre_ref, ...), custom_call_target="tpu_custom_call" | custom-call | flops 1887436800 | bytes 4000000 | tf_op jit(solution)/shard_map/pair_terms/pallas_call | solution.py:288
  6.8 0.5 %edge_terms.1 = (bf16[2,3,80,128]{3,2,1,0:T(8,128)(2,1)S(1)}, bf16[2,3,80,128]{3,2,1,0:T(8,128)(2,1)S(1)}, bf16[2,3,80,128]{3,2,1,0:T(8,128)(2,1)S(1)}, bf16[2,3...) custom-call(f32[3,320,512]{2,1,0:T(8,128)S(1)} %pair_terms.1.term_re, ...), custom_call_target="tpu_custom_call" | custom-call | flops 235929600 | bytes 4000000 | tf_op jit(solution)/shard_map/edge_terms/pallas_call | solution.py:301
  7.3 3.0 %collective-permute-start.3 = (bf16[2,3,80,128]{3,2,1,0:T(8,128)(2,1)S(1)}, bf16[2,3,80,128]{3,2,1,0:T(8,128)(2,1)S(1)}, u32[]{:S(2)}, u32[]{:S(2)}) collective-permute-start(bf16[2,3,80,128]{3,2,1,0:T(8,128)(2,1)S(1)} %get-tuple-element.39), channel_id=1, source_target_pairs={{0,8},{1,9},{2,10},{3,11},{4,12},{5,13},{6,14},{7,15},{8,0},{9,1},... | collective-permute-start | bytes 368648 | tf_op jit(solution)/shard_map/ppermute | solution.py:322
  10.3 3.6 %collective-permute-start.4 = (bf16[2,3,80,128]{3,2,1,0:T(8,128)(2,1)S(1)}, bf16[2,3,80,128]{3,2,1,0:T(8,128)(2,1)S(1)}, u32[]{:S(2)}, u32[]{:S(2)}) collective-permute-start(bf16[2,3,80,128]{3,2,1,0:T(8,128)(2,1)S(1)} %get-tuple-element.40), channel_id=1, source_target_pairs={{0,2},{1,3},{2,0},{3,1},{4,6},{5,7},{6,4},{7,5},{8,10},{9,11},{10,... | collective-permute-start | bytes 368648 | tf_op jit(solution)/shard_map/ppermute | solution.py:322
  13.9 3.1 %collective-permute-start.5 = (bf16[2,3,80,128]{3,2,1,0:T(8,128)(2,1)S(1)}, bf16[2,3,80,128]{3,2,1,0:T(8,128)(2,1)S(1)}, u32[]{:S(2)}, u32[]{:S(2)}) collective-permute-start(bf16[2,3,80,128]{3,2,1,0:T(8,128)(2,1)S(1)} %get-tuple-element.43), channel_id=1, source_target_pairs={{0,4},{1,5},{2,6},{3,7},{4,0},{5,1},{6,2},{7,3},{8,12},{9,13},{10,... | collective-permute-start | bytes 368648 | tf_op jit(solution)/shard_map/ppermute | solution.py:322
  17.1 2.8 %collective-permute-start.7 = (bf16[2,3,80,128]{3,2,1,0:T(8,128)(2,1)S(1)}, bf16[2,3,80,128]{3,2,1,0:T(8,128)(2,1)S(1)}, u32[]{:S(2)}, u32[]{:S(2)}) collective-permute-start(bf16[2,3,80,128]{3,2,1,0:T(8,128)(2,1)S(1)} %get-tuple-element.45), channel_id=1, source_target_pairs={{0,6},{1,7},{2,4},{3,5},{4,2},{5,3},{6,0},{7,1},{8,14},{9,15},{10,... | collective-permute-start | bytes 368648 | tf_op jit(solution)/shard_map/ppermute | solution.py:322
  19.8 2.0 %collective-permute-start.8 = (bf16[2,3,80,128]{3,2,1,0:T(8,128)(2,1)S(1)}, bf16[2,3,80,128]{3,2,1,0:T(8,128)(2,1)S(1)}, u32[]{:S(2)}, u32[]{:S(2)}) collective-permute-start(bf16[2,3,80,128]{3,2,1,0:T(8,128)(2,1)S(1)} %get-tuple-element.46), channel_id=1, source_target_pairs={{0,10},{1,11},{2,8},{3,9},{4,14},{5,15},{6,12},{7,13},{8,2},{9,3},... | collective-permute-start | bytes 368648 | tf_op jit(solution)/shard_map/ppermute | solution.py:322
  21.9 2.6 %input_grad.2.refs_0_ = bf16[8,320,128]{2,1,0:T(8,128)(2,1)} custom-call(bf16[8,320,128]{2,1,0:T(8,128)(2,1)S(1)} %bitcast.34, bf16[8,320,128]{2,1,0:T(8,128)(2,1)S(1)} %bitcast.38, bf16[2,320,128]{2,1,0:T(8,128)(2,1)S(1)} %collective-permute-done.2.near_ref.edge_ref, bf16[3,3,320,320]{3,2,1,0:T(8,128)(2,1)S(1)} %copy-done), custom_call_target="tpu_custom_call" | custom-call | flops 943718400 | bytes 3000000 | tf_op jit(solution)/shard_map/input_grad/pallas_call | solution.py:269
  24.5 2.6 %input_grad.3 = bf16[8,320,128]{2,1,0:T(8,128)(2,1)} custom-call(bf16[8,320,128]{2,1,0:T(8,128)(2,1)S(1)} %bitcast.35, bf16[8,320,128]{2,1,0:T(8,128)(2,1)S(1)} %bitcast.39, bf16[1,320,128]{2,1,0:T(8,128)(2,1)S(1)} %constant_dynamic-slice_fusion.edge_ref, bf16[3,3,320,320]{3,2,1,0:T(8,128)(2,1)S(1)} %copy-done, ...), custom_call_target="tpu_custom_call", output_to_operand_aliasing={{}: (4, {})} | custom-call | flops 943718400 | bytes 3000000 | tf_op jit(solution)/shard_map/input_grad/pallas_call | solution.py:269
  27.1 2.2 %collective-permute-done.7 = bf16[2,3,80,128]{3,2,1,0:T(8,128)(2,1)S(1)} collective-permute-done((bf16[2,3,80,128]{3,2,1,0:T(8,128)(2,1)S(1)}, bf16[2,3,80,128]{3,2,1,0:T(8,128)(2,1)S(1)}, u32[]{:S(2)}, u32[]{:S(2)}) %collective-permute-start.7) | collective-permute-done | bytes 122912 | tf_op jit(solution)/shard_map/ppermute | solution.py:322
  29.7 2.6 %collective-permute-start.10 = (bf16[3,80,128]{2,1,0:T(8,128)(2,1)S(1)}, bf16[3,80,128]{2,1,0:T(8,128)(2,1)S(1)}, u32[]{:S(2)}, u32[]{:S(2)}) collective-permute-start(bf16[3,80,128]{2,1,0:T(8,128)(2,1)S(1)} %fusion.3), channel_id=1, source_target_pairs={{0,16},{8,24},{16,0},{24,8},{1,17},{9,25},{17,1},{25,9},{2,18},{10... | collective-permute-start | bytes 184328 | tf_op jit(solution)/shard_map/ppermute | solution.py:333
  32.4 2.8 %collective-permute-done.10 = bf16[3,80,128]{2,1,0:T(8,128)(2,1)S(1)} collective-permute-done((bf16[3,80,128]{2,1,0:T(8,128)(2,1)S(1)}, bf16[3,80,128]{2,1,0:T(8,128)(2,1)S(1)}, u32[]{:S(2)}, u32[]{:S(2)}) %collective-permute-start.10) | collective-permute-done | bytes 61472 | tf_op jit(solution)/shard_map/ppermute | solution.py:333
  35.2 1.6 %collective-permute-start.11 = (bf16[3,80,128]{2,1,0:T(8,128)(2,1)S(1)}, bf16[3,80,128]{2,1,0:T(8,128)(2,1)S(1)}, u32[]{:S(2)}, u32[]{:S(2)}) collective-permute-start(bf16[3,80,128]{2,1,0:T(8,128)(2,1)S(1)} %fusion.2), channel_id=1, source_target_pairs={{0,2},{1,3},{2,0},{3,1},{4,6},{5,7},{6,4},{7,5},{8,10},{9,11},{10,... | collective-permute-start | bytes 184328 | tf_op jit(solution)/shard_map/ppermute | solution.py:341
  36.8 0.9 %collective-permute-start.12 = (bf16[3,80,128]{2,1,0:T(8,128)(2,1)S(1)}, bf16[3,80,128]{2,1,0:T(8,128)(2,1)S(1)}, u32[]{:S(2)}, u32[]{:S(2)}) collective-permute-start(bf16[3,80,128]{2,1,0:T(8,128)(2,1)S(1)} %fusion.2), channel_id=1, source_target_pairs={{0,4},{1,5},{2,6},{3,7},{4,0},{5,1},{6,2},{7,3},{8,12},{9,13},{10,... | collective-permute-start | bytes 184328 | tf_op jit(solution)/shard_map/ppermute | solution.py:341
  37.7 1.0 %collective-permute-start.13 = (bf16[3,80,128]{2,1,0:T(8,128)(2,1)S(1)}, bf16[3,80,128]{2,1,0:T(8,128)(2,1)S(1)}, u32[]{:S(2)}, u32[]{:S(2)}) collective-permute-start(bf16[3,80,128]{2,1,0:T(8,128)(2,1)S(1)} %fusion.2), channel_id=1, source_target_pairs={{0,6},{1,7},{2,4},{3,5},{4,2},{5,3},{6,0},{7,1},{8,14},{9,15},{10,... | collective-permute-start | bytes 184328 | tf_op jit(solution)/shard_map/ppermute | solution.py:341
  38.7 0.7 %collective-permute-done.11 = bf16[3,80,128]{2,1,0:T(8,128)(2,1)S(1)} collective-permute-done((bf16[3,80,128]{2,1,0:T(8,128)(2,1)S(1)}, bf16[3,80,128]{2,1,0:T(8,128)(2,1)S(1)}, u32[]{:S(2)}, u32[]{:S(2)}) %collective-permute-start.11) | collective-permute-done | bytes 61472 | tf_op jit(solution)/shard_map/ppermute | solution.py:341
  39.5 1.5 %collective-permute-done.12 = bf16[3,80,128]{2,1,0:T(8,128)(2,1)S(1)} collective-permute-done((bf16[3,80,128]{2,1,0:T(8,128)(2,1)S(1)}, bf16[3,80,128]{2,1,0:T(8,128)(2,1)S(1)}, u32[]{:S(2)}, u32[]{:S(2)}) %collective-permute-start.12) | collective-permute-done | bytes 61472 | tf_op jit(solution)/shard_map/ppermute | solution.py:341
  41.0 1.8 %collective-permute-done.13 = bf16[3,80,128]{2,1,0:T(8,128)(2,1)S(1)} collective-permute-done((bf16[3,80,128]{2,1,0:T(8,128)(2,1)S(1)}, bf16[3,80,128]{2,1,0:T(8,128)(2,1)S(1)}, u32[]{:S(2)}, u32[]{:S(2)}) %collective-permute-start.13) | collective-permute-done | bytes 61472 | tf_op jit(solution)/shard_map/ppermute | solution.py:341
  42.9 1.5 %place_rows.2.refs_0_ = f32[320,720]{1,0:T(8,128)} custom-call(bf16[4,3,80,128]{3,2,1,0:T(8,128)(2,1)S(1)} %pad_maximum_fusion.parts_ref, f32[144,144]{1,0:T(8,128)S(1)} %pick_rows.1.pick_ref), custom_call_target="tpu_custom_call" | custom-call | flops 165888000 | bytes 1000000 | tf_op jit(solution)/shard_map/place_rows/pallas_call | solution.py:346
  44.4 1.5 %place_rows.3 = f32[320,720]{1,0:T(8,128)} custom-call(bf16[4,3,80,128]{3,2,1,0:T(8,128)(2,1)S(1)} %collective-permute-done.14.parts_ref, f32[144,144]{1,0:T(8,128)S(1)} %pick_rows.1.pick_ref, f32[320,720]{1,0:T(8,128)} %place_rows.2.refs_0_), custom_call_target="tpu_custom_call", output_to_operand_aliasing={{}: (2, {})} | custom-call | flops 165888000 | bytes 1000000 | tf_op jit(solution)/shard_map/place_rows/pallas_call | solution.py:346
  (27 shorter events, 1.3 us)
Async XLA Ops:
  1.6 1.4 %copy-start.1 = (bf16[1,8,128,320]{2,3,1,0:T(8,128)(2,1)S(1)}, bf16[1,8,128,320]{2,3,1,0:T(8,128)(2,1)}, u32[]{:S(2)}) copy-start(bf16[1,8,128,320]{2,3,1,0:T(8,128)(2,1)} %param.3) | copy-start | bytes 1966084
  1.6 1.4 %copy-start.2 = (bf16[1,8,128,320]{2,3,1,0:T(8,128)(2,1)S(1)}, bf16[1,8,128,320]{2,3,1,0:T(8,128)(2,1)}, u32[]{:S(2)}) copy-start(bf16[1,8,128,320]{2,3,1,0:T(8,128)(2,1)} %param.4) | copy-start | bytes 1966084
  1.6 2.9 %collective-permute-start = (bf16[8,320,128]{2,1,0:T(8,128)(2,1)}, bf16[8,320,128]{2,1,0:T(8,128)(2,1)S(1)}, u32[]{:S(2)}, u32[]{:S(2)}) collective-permute-start(bf16[8,320,128]{2,1,0:T(8,128)(2,1)} %bitcast.32), channel_id=1, source_target_pairs={{0,1},{1,0},{2,3},{3,2},{4,5},{5,4},{6,7},{7,6},{8,9},{9,8},{10,11... | collective-permute-start | bytes 1966088 | tf_op jit(solution)/shard_map/ppermute | solution.py:238
  2.2 2.9 %collective-permute-start.1 = (bf16[8,320,128]{2,1,0:T(8,128)(2,1)}, bf16[8,320,128]{2,1,0:T(8,128)(2,1)S(1)}, u32[]{:S(2)}, u32[]{:S(2)}) collective-permute-start(bf16[8,320,128]{2,1,0:T(8,128)(2,1)} %bitcast.36), channel_id=1, source_target_pairs={{0,1},{1,0},{2,3},{3,2},{4,5},{5,4},{6,7},{7,6},{8,9},{9,8},{10,11... | collective-permute-start | bytes 1966088 | tf_op jit(solution)/shard_map/ppermute | solution.py:237
  2.2 4.5 %collective-permute-start.2 = (bf16[2,320,128]{2,1,0:T(8,128)(2,1)S(1)}, bf16[2,320,128]{2,1,0:T(8,128)(2,1)S(1)}, u32[]{:S(2)}, u32[]{:S(2)}) collective-permute-start(bf16[2,320,128]{2,1,0:T(8,128)(2,1)S(1)} %pad_maximum_fusion.1.after_ref), channel_id=1, source_target_pairs={{1,2},{2,1},{3,4},{4,3},{5,6},{6,5},{9,10},{10,9},{11,12},{12,11},... | collective-permute-start | bytes 491528 | tf_op jit(solution)/shard_map/ppermute | solution.py:235
  6.7 15.1 %copy-start = (bf16[3,3,320,320]{3,2,1,0:T(8,128)(2,1)S(1)}, bf16[3,3,320,320]{3,2,1,0:T(8,128)(2,1)}, u32[]{:S(2)}) copy-start(bf16[3,3,320,320]{3,2,1,0:T(8,128)(2,1)} %kernel_ref.3) | copy-start | bytes 5529604
  7.3 12.5 %collective-permute-start.3 = (bf16[2,3,80,128]{3,2,1,0:T(8,128)(2,1)S(1)}, bf16[2,3,80,128]{3,2,1,0:T(8,128)(2,1)S(1)}, u32[]{:S(2)}, u32[]{:S(2)}) collective-permute-start(bf16[2,3,80,128]{3,2,1,0:T(8,128)(2,1)S(1)} %get-tuple-element.39), channel_id=1, source_target_pairs={{0,8},{1,9},{2,10},{3,11},{4,12},{5,13},{6,14},{7,15},{8,0},{9,1},... | collective-permute-start | bytes 368648 | tf_op jit(solution)/shard_map/ppermute | solution.py:322
  10.3 11.6 %collective-permute-start.4 = (bf16[2,3,80,128]{3,2,1,0:T(8,128)(2,1)S(1)}, bf16[2,3,80,128]{3,2,1,0:T(8,128)(2,1)S(1)}, u32[]{:S(2)}, u32[]{:S(2)}) collective-permute-start(bf16[2,3,80,128]{3,2,1,0:T(8,128)(2,1)S(1)} %get-tuple-element.40), channel_id=1, source_target_pairs={{0,2},{1,3},{2,0},{3,1},{4,6},{5,7},{6,4},{7,5},{8,10},{9,11},{10,... | collective-permute-start | bytes 368648 | tf_op jit(solution)/shard_map/ppermute | solution.py:322
  13.9 13.1 %collective-permute-start.5 = (bf16[2,3,80,128]{3,2,1,0:T(8,128)(2,1)S(1)}, bf16[2,3,80,128]{3,2,1,0:T(8,128)(2,1)S(1)}, u32[]{:S(2)}, u32[]{:S(2)}) collective-permute-start(bf16[2,3,80,128]{3,2,1,0:T(8,128)(2,1)S(1)} %get-tuple-element.43), channel_id=1, source_target_pairs={{0,4},{1,5},{2,6},{3,7},{4,0},{5,1},{6,2},{7,3},{8,12},{9,13},{10,... | collective-permute-start | bytes 368648 | tf_op jit(solution)/shard_map/ppermute | solution.py:322
  17.0 10.1 %collective-permute-start.6 = (bf16[2,3,80,128]{3,2,1,0:T(8,128)(2,1)S(1)}, bf16[2,3,80,128]{3,2,1,0:T(8,128)(2,1)S(1)}, u32[]{:S(2)}, u32[]{:S(2)}) collective-permute-start(bf16[2,3,80,128]{3,2,1,0:T(8,128)(2,1)S(1)} %get-tuple-element.44), channel_id=1, source_target_pairs={{0,14},{1,15},{2,12},{3,13},{4,10},{5,11},{6,8},{7,9},{8,6},{9,7},... | collective-permute-start | bytes 368648 | tf_op jit(solution)/shard_map/ppermute | solution.py:322
  17.1 12.3 %collective-permute-start.7 = (bf16[2,3,80,128]{3,2,1,0:T(8,128)(2,1)S(1)}, bf16[2,3,80,128]{3,2,1,0:T(8,128)(2,1)S(1)}, u32[]{:S(2)}, u32[]{:S(2)}) collective-permute-start(bf16[2,3,80,128]{3,2,1,0:T(8,128)(2,1)S(1)} %get-tuple-element.45), channel_id=1, source_target_pairs={{0,6},{1,7},{2,4},{3,5},{4,2},{5,3},{6,0},{7,1},{8,14},{9,15},{10,... | collective-permute-start | bytes 368648 | tf_op jit(solution)/shard_map/ppermute | solution.py:322
  19.8 9.5 %collective-permute-start.8 = (bf16[2,3,80,128]{3,2,1,0:T(8,128)(2,1)S(1)}, bf16[2,3,80,128]{3,2,1,0:T(8,128)(2,1)S(1)}, u32[]{:S(2)}, u32[]{:S(2)}) collective-permute-start(bf16[2,3,80,128]{3,2,1,0:T(8,128)(2,1)S(1)} %get-tuple-element.46), channel_id=1, source_target_pairs={{0,10},{1,11},{2,8},{3,9},{4,14},{5,15},{6,12},{7,13},{8,2},{9,3},... | collective-permute-start | bytes 368648 | tf_op jit(solution)/shard_map/ppermute | solution.py:322
  21.8 7.7 %collective-permute-start.9 = (bf16[2,3,80,128]{3,2,1,0:T(8,128)(2,1)S(1)}, bf16[2,3,80,128]{3,2,1,0:T(8,128)(2,1)S(1)}, u32[]{:S(2)}, u32[]{:S(2)}) collective-permute-start(bf16[2,3,80,128]{3,2,1,0:T(8,128)(2,1)S(1)} %get-tuple-element.47), channel_id=1, source_target_pairs={{0,12},{1,13},{2,14},{3,15},{4,8},{5,9},{6,10},{7,11},{8,4},{9,5},... | collective-permute-start | bytes 368648 | tf_op jit(solution)/shard_map/ppermute | solution.py:322
  29.7 5.4 %collective-permute-start.10 = (bf16[3,80,128]{2,1,0:T(8,128)(2,1)S(1)}, bf16[3,80,128]{2,1,0:T(8,128)(2,1)S(1)}, u32[]{:S(2)}, u32[]{:S(2)}) collective-permute-start(bf16[3,80,128]{2,1,0:T(8,128)(2,1)S(1)} %fusion.3), channel_id=1, source_target_pairs={{0,16},{8,24},{16,0},{24,8},{1,17},{9,25},{17,1},{25,9},{2,18},{10... | collective-permute-start | bytes 184328 | tf_op jit(solution)/shard_map/ppermute | solution.py:333
  35.2 4.3 %collective-permute-start.11 = (bf16[3,80,128]{2,1,0:T(8,128)(2,1)S(1)}, bf16[3,80,128]{2,1,0:T(8,128)(2,1)S(1)}, u32[]{:S(2)}, u32[]{:S(2)}) collective-permute-start(bf16[3,80,128]{2,1,0:T(8,128)(2,1)S(1)} %fusion.2), channel_id=1, source_target_pairs={{0,2},{1,3},{2,0},{3,1},{4,6},{5,7},{6,4},{7,5},{8,10},{9,11},{10,... | collective-permute-start | bytes 184328 | tf_op jit(solution)/shard_map/ppermute | solution.py:341
  36.8 4.2 %collective-permute-start.12 = (bf16[3,80,128]{2,1,0:T(8,128)(2,1)S(1)}, bf16[3,80,128]{2,1,0:T(8,128)(2,1)S(1)}, u32[]{:S(2)}, u32[]{:S(2)}) collective-permute-start(bf16[3,80,128]{2,1,0:T(8,128)(2,1)S(1)} %fusion.2), channel_id=1, source_target_pairs={{0,4},{1,5},{2,6},{3,7},{4,0},{5,1},{6,2},{7,3},{8,12},{9,13},{10,... | collective-permute-start | bytes 184328 | tf_op jit(solution)/shard_map/ppermute | solution.py:341
  37.7 5.1 %collective-permute-start.13 = (bf16[3,80,128]{2,1,0:T(8,128)(2,1)S(1)}, bf16[3,80,128]{2,1,0:T(8,128)(2,1)S(1)}, u32[]{:S(2)}, u32[]{:S(2)}) collective-permute-start(bf16[3,80,128]{2,1,0:T(8,128)(2,1)S(1)} %fusion.2), channel_id=1, source_target_pairs={{0,6},{1,7},{2,4},{3,5},{4,2},{5,3},{6,0},{7,1},{8,14},{9,15},{10,... | collective-permute-start | bytes 184328 | tf_op jit(solution)/shard_map/ppermute | solution.py:341
  42.8 1.6 %collective-permute-start.14 = (bf16[4,3,80,128]{3,2,1,0:T(8,128)(2,1)S(1)}, bf16[4,3,80,128]{3,2,1,0:T(8,128)(2,1)S(1)}, u32[]{:S(2)}, u32[]{:S(2)}) collective-permute-start(bf16[4,3,80,128]{3,2,1,0:T(8,128)(2,1)S(1)} %pad_maximum_fusion.parts_ref), channel_id=1, source_target_pairs={{0,1},{1,0},{2,3},{3,2},{4,5},{5,4},{6,7},{7,6},{8,9},{9,8},{10,11... | collective-permute-start | bytes 737288 | tf_op jit(solution)/shard_map/ppermute | solution.py:343
